TPU v7x, 32 devices: a whole 2x2x4 slice. The times are simulated.
32 devices in a mesh: group: 4 (over y, core), member: 8 (over z, x).
Axes of the slice: x: 2, y: 2, z: 4, core: 2. Of those that a mesh axis runs over, the one named last changes fastest.
Arguments:
- encoded: float32 [8192, 256], P(('group', 'member'))
- item_table: float32 [131072, 256], P(('group', 'member'))
- target_owner: int32 [8192, 1], P(('group', 'member')), may hold values from 0 to 31; in each aligned block of 256 rows (0 to 255, 256 to 511, ...) at most 32 rows name the same one
- target_local: int32 [8192], P(('group', 'member')), may hold values from 0 to 4095
- negative_ids: int32 [16384], P(('group', 'member')), may hold values from 0 to 131071, as said below
- valid: int32 [8192], P(('group', 'member')), may hold values 0 or 1
Outputs:
- encoded_grad: float32 [8192, 256], P(('group', 'member'))
- table_grad: float32 [131072, 256], P(('group', 'member'))
Inputs may be any that keep to these rules, and one draw needn't show every extreme that they name: `target_owner`: the positions of one device name any one owner at most 32 times; some owner is named exactly 32 times by some device. `negative_ids`: id // 4096 is the owning device; the 512 ids of one device name every owning device exactly 16 times.
All inputs are finite; a program needn't handle non-finite values. No bound on the sum of `valid` on one device may be relied on, other than what follows from the above.
Results may differ from a plain program's by a relative error of at most 0.0003.
Values sent between devices are 32-bit elements; how exact they have to be, the bound alone decides.
No kernel may reach another device: no remote copies, remote signals or barrier semaphores. Data moves between devices by JAX's collectives and lax.ppermute only.
A program may use at most 128 MiB of HBM per device.

v0:
```python
import jax
import jax.numpy as jnp
from jax import lax
from jax.sharding import PartitionSpec as P


def merged(value, axis, combine):
    everything = jax.tree.map(lambda part: lax.all_gather(part, axis), value)
    first = jax.tree.map(lambda part: part[0], everything)

    def hop(k, so_far):
        return combine(so_far, jax.tree.map(lambda part: part[k], everything))

    return lax.fori_loop(1, lax.axis_size(axis), hop, first)


def contract_rows(left, right):
    return lax.dot_general(
        left,
        right,
        (((1,), (1,)), ((), ())),
        precision=lax.Precision.HIGHEST,
        preferred_element_type=jnp.float32,
    )


def contract_first(left, right):
    return lax.dot_general(
        left,
        right,
        (((0,), (0,)), ((), ())),
        precision=lax.Precision.HIGHEST,
        preferred_element_type=jnp.float32,
    )


def slot_ranks(owners, devices):
    onehot = (owners[:, None] == jnp.arange(devices, dtype=jnp.int32)[None, :]).astype(jnp.int32)
    return jnp.sum((jnp.cumsum(onehot, axis=0) - 1) * onehot, axis=1)


def join_stats(first, second):
    larger = jnp.maximum(first[0], second[0])
    return (larger, first[1] * jnp.exp(first[0] - larger) + second[1] * jnp.exp(second[0] - larger))


def shards(encoded, item_table, target_owner, target_local, negative_ids, valid):
    devices = lax.axis_size(("group", "member"))
    tok_dev = encoded.shape[0]
    width = encoded.shape[1]
    rows_dev = item_table.shape[0]
    neg_dev = negative_ids.shape[0]
    slots_target = max(2, 4 * tok_dev // devices)
    slots_negative = neg_dev // devices
    slots_all = slots_target + slots_negative
    owners_target = target_owner[:, 0]
    owners_negative = negative_ids // rows_dev
    local_negative = negative_ids % rows_dev
    rank_target = slot_ranks(owners_target, devices)
    rank_negative = slot_ranks(owners_negative, devices) + slots_target
    empty_index = tok_dev + neg_dev
    slot_source = jnp.full((devices, slots_all), empty_index, jnp.int32)
    slot_source = slot_source.at[owners_target, rank_target].set(
        jnp.arange(tok_dev, dtype=jnp.int32)
    )
    slot_source = slot_source.at[owners_negative, rank_negative].set(
        tok_dev + jnp.arange(neg_dev, dtype=jnp.int32)
    )
    local_all = jnp.concatenate([target_local, local_negative, jnp.zeros((1,), jnp.int32)])
    request = local_all[slot_source]
    asked = lax.all_to_all(request, ("group", "member"), split_axis=0, concat_axis=0, tiled=True)
    found = item_table[asked]
    back = lax.all_to_all(found, ("group", "member"), split_axis=0, concat_axis=0, tiled=True)
    target_rows = back[owners_target, rank_target]
    negative_rows = back[owners_negative, rank_negative]
    weight = valid.astype(jnp.float32)
    positive = jnp.sum(encoded * target_rows, axis=1)
    group_encoded, group_positive, group_weight = (
        lax.all_gather(encoded, "member", axis=0, tiled=True),
        lax.all_gather(positive, "member", axis=0, tiled=True),
        lax.all_gather(weight, "member", axis=0, tiled=True),
    )
    score = contract_rows(group_encoded, negative_rows)
    part_max = jnp.max(score, axis=1)
    part_sum = jnp.sum(jnp.exp(score - part_max[:, None]), axis=1)
    all_max, all_sum = merged((part_max, part_sum), "member", join_stats)
    top = jnp.maximum(all_max, group_positive)
    total = all_sum * jnp.exp(all_max - top) + jnp.exp(group_positive - top)
    prob = jnp.exp(score - top[:, None]) / total[:, None]
    group_own = jnp.exp(group_positive - top) / total
    negative_grad = contract_first(group_weight[:, None] * prob, group_encoded)
    pulled = lax.psum_scatter(
        jnp.dot(
            prob, negative_rows, precision=lax.Precision.HIGHEST, preferred_element_type=jnp.float32
        ),
        "member",
        scatter_dimension=0,
        tiled=True,
    )
    member_index = lax.axis_index("member")
    own = lax.dynamic_slice_in_dim(group_own, member_index * tok_dev, tok_dev, 0)
    encoded_grad = weight[:, None] * ((own - 1.0)[:, None] * target_rows + pulled)
    target_grad = (weight * (own - 1.0))[:, None] * encoded
    stacked = jnp.concatenate(
        [target_grad, negative_grad, jnp.zeros((1, width), jnp.float32)], axis=0
    )
    outgoing = stacked[slot_source]
    incoming = lax.all_to_all(
        outgoing, ("group", "member"), split_axis=0, concat_axis=0, tiled=True
    )
    table_grad = (
        jnp.zeros((rows_dev, width), jnp.float32)
        .at[asked.reshape(-1)]
        .add(incoming.reshape(-1, width))
    )
    return (encoded_grad, table_grad)


def solution(mesh):
    placed = (
        P(("group", "member"), None),
        P(("group", "member"), None),
        P(("group", "member"), None),
        P(("group", "member")),
        P(("group", "member")),
        P(("group", "member")),
    )
    return jax.shard_map(
        shards,
        mesh=mesh,
        in_specs=placed,
        out_specs=(P(("group", "member"), None), P(("group", "member"), None)),
        check_vma=False,
    )
```

profile of v0, /device:TPU:0, one launch (start us, length us, event | category | flops | bytes accessed | tf_op | source)
XLA Modules:
  0.0 319.3 jit_solution(3541265915946919273)
XLA Ops:
  7.2 0.0 all-gather.6.cloned.1.call-start
  7.2 0.7 all-gather.6.cloned.1.call-update
  7.9 0.7 compare_select_fusion.6
  8.6 0.7 fusion.11
  9.3 0.6 reduce-window.14
  9.9 0.2 slice_reduce_fusion.1
  10.1 0.8 fusion.10
  10.9 0.7 or_select_fusion.1
  11.6 1.2 reduce-window.16
  12.8 0.2 slice_reduce_fusion
  13.0 0.1 fusion.7
  13.2 12.7 %scatter_fusion = s32[32,48]{1,0:T(8,128)S(1)} fusion(s32[32,48]{1,0:T(8,128)S(1)} %broadcast_in_dim.10, s32[256]{0:T(256)S(1)} %bitcast.67, s32[256]{0:T(256)S(1)} %iota.20), kind=kCustom, calls=%fused_computation.5 | custom fusion | bytes 5120 | tf_op jit(solution)/shard_map/scatter | solution.py:63
  25.9 25.1 %scatter_fusion.1 = s32[32,48]{1,0:T(8,128)S(1)} fusion(s32[32,48]{1,0:T(8,128)S(1)} %scatter_fusion, s32[512]{0:T(512)S(1)} %bitcast.65, s32[512]{0:T(512)S(1)} %iota_add_fusion), kind=kCustom, calls=%fused_computation.6 | custom fusion | bytes 10240 | tf_op jit(solution)/shard_map/scatter | solution.py:66
  51.1 0.1 reshape.151
  51.1 5.9 %gather_fusion = s32[1536]{0:T(1024)S(1)} fusion(s32[769]{0:T(1024)S(1)} %pad_add_fusion, s32[2048]{0:T(1024)S(1)} %pad_clamp_fusion.1), kind=kCustom, calls=%fused_computation | custom fusion | bytes 18432 | tf_op jit(solution)/shard_map/gather | solution.py:70
  57.0 0.1 all_to_all.14
  57.1 14.2 %all_to_all.22 = s32[32,1,48]{2,1,0:T(1,128)S(1)} all-to-all(s32[32,1,48]{2,1,0:T(1,128)S(1)} %all_to_all.14), channel_id=1, replica_groups=mesh['group'=4,'member'=8] {'group','member'}, dimensions={0} | all-to-all | bytes 12288 | tf_op jit(solution)/shard_map/all_to_all | solution.py:71
  71.3 0.1 reshape.159
  71.4 0.0 copy-start.2
  71.4 6.8 %gather_fusion.1 = f32[1536,256]{1,0:T(8,128)} fusion(f32[4096,256]{1,0:T(8,128)} %param.9, s32[2048]{0:T(1024)S(1)} %pad_clamp_fusion), kind=kCustom, calls=%fused_computation.1 | custom fusion | bytes 3151872 | tf_op jit(solution)/shard_map/gather | solution.py:72
  78.2 2.7 all-to-all-start.1
  80.9 0.0 copy-start
  80.9 0.0 reduce-scatter.2.cloned.1.call-start
  81.0 40.3 %all-gather.3 = f32[8,1,256]{2,1,0:T(1,128)S(1)} all-gather(f32[1,1,256]{2,1,0:T(1,128)S(1)} %bitcast.75), channel_id=1, replica_groups=mesh['group'=4,'member'=8] {'member'}, dimensions={0}, use_global_device_ids=true | all-gather | bytes 9216 | tf_op jit(solution)/shard_map/all_gather | solution.py:81
  121.4 2.0 gather_fusion.2
  123.4 3.9 %gather_fusion.3 = f32[512,256]{1,0:T(8,128)S(1)} fusion(f32[32,48,256]{2,1,0:T(8,128)S(1)} %all-to-all-done.1, s32[512]{0:T(512)S(1)} %bitcast.64), kind=kCustom, calls=%fused_computation.3 | custom fusion | bytes 1052672 | tf_op jit(solution)/shard_map/gather | solution.py:75
  127.3 0.1 multiply_reduce_fusion
  127.4 23.9 %all-gather.2 = f32[8,1,256]{2,1,0:T(1,128)S(1)} all-gather(f32[1,1,256]{2,1,0:T(1,128)S(1)} %bitcast.82), channel_id=1, replica_groups=mesh['group'=4,'member'=8] {'member'}, dimensions={0}, use_global_device_ids=true | all-gather | bytes 9216 | tf_op jit(solution)/shard_map/all_gather | solution.py:80
  151.4 6.8 %fusion.20 = (f32[2048]{0:T(1024)S(1)}, f32[512,2048]{1,0:T(8,128)}) fusion(f32[512,256]{1,0:T(8,128)S(1)} %gather_fusion.3, f32[2048,256]{1,0:T(8,128)} %all-gather.6.cloned.1.call-done), kind=kOutput, calls=%fused_computation.74 | convolution fusion | flops 3222272000 | bytes 6823936 | tf_op jit(solution)/shard_map/dot_general | solution.py:18
  158.2 30.5 %all-gather = f32[16384]{0:T(1024)S(1)} all-gather(f32[2048]{0:T(1024)S(1)} %get-tuple-element.164), channel_id=2, replica_groups=mesh['group'=4,'member'=8] {'member'}, dimensions={0}, use_global_device_ids=true | all-gather | bytes 73728 | tf_op jit(solution)/shard_map/all_gather | solution.py:8
  188.7 2.8 exponential_reduce_fusion
  191.5 30.7 %all-gather.1 = f32[16384]{0:T(1024)S(1)} all-gather(f32[2048]{0:T(1024)S(1)} %exponential_reduce_fusion), channel_id=3, replica_groups=mesh['group'=4,'member'=8] {'member'}, dimensions={0}, use_global_device_ids=true | all-gather | bytes 73728 | tf_op jit(solution)/shard_map/all_gather | solution.py:8
  222.2 0.4 while.17
  222.7 10.5 %fusion.5 = f32[2048,256]{1,0:T(8,128)} fusion(f32[512,256]{1,0:T(8,128)S(1)} %gather_fusion.3, f32[512,2048]{1,0:T(8,128)} %get-tuple-element.165, f32[2048]{0:T(1024)S(1)} %multiply_add_fusion.1, f32[2048]{0:T(1024)S(1)} %get-tuple-element.152), kind=kOutput, calls=%fused_computation.18 | convolution fusion | flops 3223322624 | bytes 6832128 | tf_op jit(solution)/shard_map/dot_general | solution.py:93
  233.1 0.0 reduce-scatter.2.cloned.1.call-update
  233.2 0.1 convert_multiply_fusion
  233.2 0.1 broadcast_multiply_fusion
  233.4 6.1 %fusion = f32[512,256]{1,0:T(8,128)S(1)} fusion(f32[2048,256]{1,0:T(8,128)S(1)} %copy-done.1, f32[2048]{0:T(1024)S(1)} %bitcast.80, f32[512,2048]{1,0:T(8,128)} %get-tuple-element.165, f32[2048]{0:T(1024)S(1)} %multiply_add_fusion.1, f32[2048]{0:T(1024)S(1)} %get-tuple-element.152), kind=kOutput, calls=%fused_computation.11 | convolution fusion | flops 3224371200 | bytes 6840320 | tf_op jit(solution)/shard_map/dot_general | solution.py:28
  239.5 0.2 maximum_maximum_fusion
  239.6 4.6 %gather_fusion.4 = f32[1536,256]{1,0:T(8,128)} fusion(f32[769,256]{1,0:T(8,128)S(1)} %maximum_maximum_fusion, s32[2048]{0:T(1024)S(1)} %pad_clamp_fusion.1), kind=kCustom, calls=%fused_computation.4 | custom fusion | bytes 3151872 | tf_op jit(solution)/shard_map/gather | solution.py:107
  244.3 2.9 all-to-all-start.2
  247.2 0.5 broadcast.322
  247.7 0.7 reduce.11
  248.4 0.1 reshape.147
  248.5 45.9 %all-to-all-done.2 = f32[32,48,256]{2,1,0:T(8,128)S(1)} async-done(((f32[32,48,256]{2,1,0:T(8,128)}), f32[32,48,256]{2,1,0:T(8,128)S(1)}, u32[]{:S(2)}, u32[]{:S(2)}) %all-to-all-start.2) | async-done | bytes 1572896 | tf_op jit(solution)/shard_map/all_to_all | solution.py:108
  294.4 11.7 %scatter_custom_fusion.2 = f32[4096,256]{1,0:T(8,128)} fusion(s32[1536]{0:T(1024)S(1)} %fusion.12, f32[1536,256]{1,0:T(8,128)S(1)} %bitcast.68, f32[]{:T(128)} %constant.110.clone.1), kind=kCustom, calls=%fused_computation.16 | custom fusion | flops 393216 | bytes 4194308 | tf_op jit(solution)/shard_map/scatter-add | solution.py:114
  306.1 4.6 %reduce-scatter.2.cloned.1.call-done = f32[256,256]{1,0:T(8,128)} async-done(((f32[2048,256]{1,0:T(8,128)}), f32[256,256]{1,0:T(8,128)}) %reduce-scatter.2.cloned.1.call-update) | async-done | bytes 262160 | tf_op jit(solution)/shard_map/reduce_scatter | solution.py:92
  310.7 1.8 add_multiply_fusion
  (46 shorter events, 0.5 us)
Async XLA Ops:
  7.2 43.9 %copy-start.3 = (s32[256]{0:T(256)S(1)}, s32[256]{0:T(256)}, u32[]{:S(2)}) copy-start(s32[256]{0:T(256)} %param.11) | copy-start | bytes 3076
  7.2 144.2 %all-gather.6.cloned.1.call-start = ((), (), s32[]{:S(2)}) async-start(), calls=%async_computation.4 | async-start | bytes 2359296 | tf_op jit(solution)/shard_map/all_gather | solution.py:79
  71.4 9.6 %copy-start.2 = (s32[256]{0:T(256)S(1)}, s32[256]{0:T(256)}, u32[]{:S(2)}) copy-start(s32[256]{0:T(256)} %param.13) | copy-start | bytes 3076
  78.2 43.1 %all-to-all-start.1 = ((f32[32,48,256]{2,1,0:T(8,128)}), f32[32,48,256]{2,1,0:T(8,128)S(1)}, u32[]{:S(2)}, u32[]{:S(2)}) async-start(f32[32,48,256]{2,1,0:T(8,128)} %bitcast.14), calls=%async_computation.1 | async-start | bytes 3145728 | tf_op jit(solution)/shard_map/all_to_all | solution.py:73
  80.9 46.4 %copy-start = (f32[256,256]{1,0:T(8,128)S(1)}, f32[256,256]{1,0:T(8,128)}, u32[]{:S(2)}) copy-start(f32[256,256]{1,0:T(8,128)} %param.8) | copy-start | bytes 786436
  80.9 229.8 %reduce-scatter.2.cloned.1.call-start = ((), (), s32[]{:S(2)}) async-start(), calls=%async_computation.5 | async-start | bytes 2359296 | tf_op jit(solution)/shard_map/reduce_scatter | solution.py:92
  222.7 10.7 %copy-start.1 = (f32[2048,256]{1,0:T(8,128)S(1)}, f32[2048,256]{1,0:T(8,128)}, u32[]{:S(2)}) copy-start(f32[2048,256]{1,0:T(8,128)} %all-gather.6.cloned.1.call-done) | copy-start | bytes 6291460
  244.3 50.2 %all-to-all-start.2 = ((f32[32,48,256]{2,1,0:T(8,128)}), f32[32,48,256]{2,1,0:T(8,128)S(1)}, u32[]{:S(2)}, u32[]{:S(2)}) async-start(f32[32,48,256]{2,1,0:T(8,128)} %bitcast.21), calls=%async_computation.3 | async-start | bytes 3145728 | tf_op jit(solution)/shard_map/all_to_all | solution.py:108
Sparse Core Ops, SparseCore 0:
  10.1 51.9 all-gather.5
  233.3 77.3 reduce-scatter.1
where the time goes:
time: 320 us; the launch traced here: 319 us
  blocking collectives  140 us (44%)
  local copies, waits for them, and re-layouts  62.5 us (20%)
  waiting for transfers between devices  51.2 us (16%)
  matrix products  23.3 us (7%)
  other arithmetic  22.4 us (7%)
  between operations  14.3 us (4%)
  starting transfers between devices  5.67 us (2%)
    all_gather x2, blocking collectives, merged(): everything = jax.tree.map(lambda part: lax.all_gather(part, axis), value)  61.2 us
    all_to_all x1, waiting for transfers between devices, shards(): lax.all_to_all(outgoing, ('group', 'member'), split_axis=0, concat_axis=0...  45.9 us
    all_gather x1, blocking collectives, shards(): lax.all_gather(weight, 'member', axis=0, tiled=True)  40.3 us
    scatter x1, local copies, waits for them, and re-layouts, shards(): slot_source.at[owners_negative, rank_negative]  25.1 us
    all_gather x1, blocking collectives, shards(): lax.all_gather(positive, 'member', axis=0, tiled=True)  23.9 us
    all_to_all x1, blocking collectives, shards(): lax.all_to_all(request, ('group', 'member'), split_axis=0, concat_axis=0,...  14.2 us
    scatter x1, local copies, waits for them, and re-layouts, shards(): slot_source.at[owners_target, rank_target]  12.7 us
    scatter-add x1, other arithmetic, shards(): table_grad = jnp.zeros((rows_dev, width), jnp.float32).at[asked.reshape(-...  11.7 us
  transfers between devices with their start and end apart: 4, of which 2 were waited for; matrix products, arithmetic and copies ran while one was open for 27% of the time, Pallas kernels for 0%

commit v1 on v0

v1 whole, which is shorter than its diff:
```python
import functools

import jax
import jax.numpy as jnp
from jax import lax
from jax.experimental import pallas as pl
from jax.experimental.pallas import tpu as pltpu
from jax.sharding import PartitionSpec as P

F32 = jnp.float32
BF16 = jnp.bfloat16
I32 = jnp.int32
LANES = 128
VMEM = pl.BlockSpec(memory_space=pltpu.VMEM)
SMEM = pl.BlockSpec(memory_space=pltpu.SMEM)
MIB = 1 << 20

NN = (((1,), (0,)), ((), ()))
NT = (((1,), (1,)), ((), ()))
TN = (((0,), (0,)), ((), ()))


def call(kernel, out_shape, ins, outs, args, scratch=(), limit=20, flops=0, moved=0, name=None):
    return pl.pallas_call(
        kernel,
        out_shape=out_shape,
        in_specs=ins,
        out_specs=outs,
        scratch_shapes=list(scratch),
        compiler_params=pltpu.CompilerParams(vmem_limit_bytes=limit * MIB),
        cost_estimate=pl.CostEstimate(flops=flops, bytes_accessed=moved, transcendentals=0),
        name=name,
    )(*args)


def iota(shape, dim):
    return lax.broadcasted_iota(I32, shape, dim)


def as_bf16(flag):
    return flag.astype(F32).astype(BF16)


def dot1(a, b, dims):
    return lax.dot_general(a, b, dims, preferred_element_type=F32)


def split(x):
    hi = x.astype(BF16)
    return hi, (x - hi.astype(F32)).astype(BF16)


def dot3(a, b, dims):
    return dot1(a[0], b[0], dims) + (dot1(a[0], b[1], dims) + dot1(a[1], b[0], dims))


def row_to_col(row):
    return jnp.transpose(jnp.broadcast_to(row, (LANES, row.shape[1])))[:, 0:1]


def bucket_kernel(members, rows_dev, slots, own_ref, loc_ref, neg_ref, out_ref):
    devices = out_ref.shape[0]
    shift = rows_dev.bit_length() - 1

    def ranks(owner_row, count):
        hot = iota((devices, count), 0) == owner_row
        before = as_bf16(iota((count, count), 0) < iota((count, count), 1))
        seen = dot1(as_bf16(hot), before, NN)
        return hot, jnp.sum(jnp.where(hot, seen, 0.0), axis=0, keepdims=True).astype(I32)

    def table(hot, value, place):
        return dot1(jnp.where(hot, value, 0.0).astype(BF16), place, NT)

    def placed(lane_row, count):
        return as_bf16(iota((LANES, count), 0) == lane_row)

    tokens = own_ref.shape[0]
    own_col = jnp.broadcast_to(own_ref[...].astype(F32), (tokens, LANES))
    owner = jnp.transpose(own_col)[0:1].astype(I32)
    hot, rank = ranks(owner, tokens)
    place = placed(rank, tokens)
    local = loc_ref[...]
    high = table(hot, (local >> 6).astype(F32), place)
    low = table(hot, (local & 63).astype(F32), place)
    group = owner // members
    hot_member = (iota((devices, tokens), 0) & (members - 1)) == (owner & (members - 1))
    position = table(
        hot_member, (iota((1, tokens), 1) + 1).astype(F32), placed(group * slots + rank, tokens)
    )

    negatives = neg_ref.shape[1]
    ids = neg_ref[...]
    hot, rank = ranks(ids >> shift, negatives)
    place = placed(rank + slots, negatives)
    local = ids & (rows_dev - 1)
    high = high + table(hot, (local >> 6).astype(F32), place)
    low = low + table(hot, (local & 63).astype(F32), place)
    out_ref[:, 0:LANES] = high.astype(I32) * 64 + low.astype(I32)
    out_ref[:, LANES:] = position.astype(I32)


def gather_kernel(members, first, count, info, got, table, *outs):
    for d, out in enumerate(outs):
        source = (info[0] ^ d) * members

        def member(mr, carry, out=out, source=source):
            for k in range(count):
                row = got[source + mr, first + k]
                out[pl.ds(mr * count + k, 1), :] = table[pl.ds(row, 1), :]
            return carry

        lax.fori_loop(0, members, member, 0)


def score_kernel(members, info, neg_ref, *refs):
    encs = refs[:members]
    stats, prob_hi, prob_lo, pulled = refs[members:]
    tokens = encs[0].shape[0]
    neg = neg_ref[...]
    neg_t = split(jnp.transpose(neg))
    for e in range(members):
        lanes = pl.ds(pl.multiple_of((info[1] ^ e) * tokens, LANES), tokens)
        score = lax.dot_general(
            neg, encs[e][...], NT, precision=lax.Precision.HIGHEST, preferred_element_type=F32
        )
        top = jnp.max(score, axis=0, keepdims=True)
        prob = jnp.exp(score - top)
        stats[0:1, lanes] = top
        stats[1:2, lanes] = jnp.sum(prob, axis=0, keepdims=True)
        parts = split(prob)
        prob_hi[e] = parts[0]
        prob_lo[e] = parts[1]
        pulled[e] = dot3(neg_t, parts, NN)


def pick_kernel(members, slots, info, got, *refs):
    encs = refs[:members]
    outs = refs[members:]
    for e in range(members):
        mr = info[1] ^ e
        row = info[0] * members + mr
        enc = encs[e]
        for d, out in enumerate(outs):
            lane = LANES + (info[0] ^ d) * slots
            for k in range(slots):
                at = jnp.maximum(got[row, lane + k] - 1, 0)
                out[pl.ds(mr * slots + k, 1), :] = enc[pl.ds(at, 1), :]


def own_places(members, info, got):
    return got[pl.ds(pl.multiple_of(info[0] * members, members), members), LANES:]


def positive_kernel(members, groups, slots, tokens, info, got, stats, *refs):
    targets = refs[:groups]
    picked = refs[groups : 2 * groups]
    joined, own, row_t, column, place_rows = refs[2 * groups :]
    place_rows[...] = own_places(members, info, got)
    for e in range(members):
        mr = info[1] ^ e
        lanes = pl.ds(pl.multiple_of(mr * tokens, LANES), tokens)
        column[...] = row_to_col(place_rows[pl.ds(mr, 1), :])
        positive = jnp.zeros((1, tokens), F32)
        has = jnp.zeros((1, tokens), F32)
        rows, hots = [], []
        at = pl.ds(pl.multiple_of(mr * slots, slots), slots)
        for d in range(groups):
            place = column[pl.ds(pl.multiple_of((info[0] ^ d) * slots, slots), slots), :]
            hot = place == iota((slots, tokens), 1) + 1
            row = targets[d][at, :]
            value = jnp.sum(row * picked[d][at, :], axis=1, keepdims=True)
            positive += jnp.sum(jnp.where(hot, value, 0.0), axis=0, keepdims=True)
            has += jnp.sum(hot.astype(F32), axis=0, keepdims=True)
            rows.append(row)
            hots.append(hot.astype(F32))
        hot = jnp.concatenate(hots, axis=0).astype(BF16)
        high, low = split(jnp.concatenate(rows, axis=0))
        row_t[e] = dot1(high, hot, TN) + dot1(low, hot, TN)
        old = stats[0:1, lanes]
        top = jnp.where(has > 0, jnp.maximum(old, positive), old)
        joined[0:1, lanes] = top
        joined[1:2, lanes] = stats[1:2, lanes] * jnp.exp(old - top) + jnp.where(
            has > 0, jnp.exp(positive - top), 0.0
        )
        own[0:1, lanes] = positive
        own[1:2, lanes] = has


def join(first, second):
    top = jnp.maximum(first[0:1], second[0:1])
    total = first[1:2] * jnp.exp(first[0:1] - top) + second[1:2] * jnp.exp(second[0:1] - top)
    return top, total


def join_kernel(first, second, out):
    top, total = join(first[...], second[...])
    out[0:1, :] = top
    out[1:2, :] = total


def shares(info, e, tokens, final, stats, own):
    lanes = pl.ds(pl.multiple_of((info[1] ^ e) * tokens, LANES), tokens)
    top, total = final[0:1, lanes], final[1:2, lanes]
    scale = jnp.exp(stats[0:1, lanes] - top) / total
    extra = jnp.where(
        own[1:2, lanes] > 0, jnp.exp(own[0:1, lanes] - top) / total - 1.0, 0.0
    )
    return scale, extra


def pull_kernel(members, tokens, info, final, stats, own, pulled, row_t, *outs):
    for e in range(members):
        scale, extra = shares(info, e, tokens, final, stats, own)
        outs[e][...] = pulled[e] * scale + row_t[e] * extra


def grad_kernel(members, groups, slots, info, got, final, stats, own, prob_hi, prob_lo, *refs):
    encs = refs[:members]
    outs = refs[members : members + groups]
    total, coef, place_rows = refs[members + groups :]
    place_rows[...] = own_places(members, info, got)
    tokens, width = encs[0].shape
    for e in range(members):
        mr = info[1] ^ e
        scale, extra = shares(info, e, tokens, final, stats, own)
        enc = split(encs[e][...] * row_to_col(scale))
        part = dot3((prob_hi[e], prob_lo[e]), enc, NN)
        if e == 0:
            total[...] = part
        else:
            total[...] += part
        hot = place_rows[pl.ds(mr, 1), :] == iota((tokens, LANES), 0) + 1
        coef[pl.ds(mr, 1), :] = jnp.sum(
            jnp.where(hot, row_to_col(extra), 0.0), axis=0, keepdims=True
        )
    count = total.shape[0] // groups
    for d in range(groups):
        outs[d][0:count, :] = total[d * count : (d + 1) * count, :]
        outs[d][count:, 0:LANES] = coef[...]
        outs[d][count:, LANES:] = jnp.zeros((members, width - LANES), F32)


def scatter_kernel(members, groups, slots, count, info, got, *refs):
    grads = refs[:groups]
    picked = refs[groups : 2 * groups]
    out, column, rows = refs[2 * groups :]
    out[...] = jnp.zeros_like(out)
    for d in range(groups):
        source = (info[0] ^ d) * members
        grad = grads[d]
        negatives = members * count
        coef = grad[negatives:, 0:LANES]
        column[...] = jnp.transpose(jnp.concatenate([coef] * (LANES // members), axis=0))
        mine = column[pl.ds(pl.multiple_of(info[0] * slots, slots), slots), :]
        for mr in range(members):
            at = slice(mr * slots, (mr + 1) * slots)
            rows[at, :] = picked[d][at, :] * mine[:, mr : mr + 1]

        def member(mr, carry, source=source, grad=grad):
            for k in range(count):
                row = got[source + mr, slots + k]
                out[pl.ds(row, 1), :] += grad[pl.ds(mr * count + k, 1), :]
            for k in range(slots):
                row = got[source + mr, k]
                out[pl.ds(row, 1), :] += rows[pl.ds(mr * slots + k, 1), :]
            return carry

        lax.fori_loop(0, members, member, 0)


def add_kernel(*refs):
    total = refs[0][...]
    for ref in refs[1:-1]:
        total = total + ref[...]
    refs[-1][...] = total


def finish_kernel(valid, *refs):
    total = refs[0][...]
    for ref in refs[1:-1]:
        total = total + ref[...]
    refs[-1][...] = jnp.transpose(total) * row_to_col(valid[...].astype(F32))


def swap(value, axis, d):
    return lax.ppermute(value, axis, [(i, i ^ d) for i in range(lax.axis_size(axis))])


def shards(encoded, item_table, target_owner, target_local, negative_ids, valid):
    groups, members = lax.axis_size("group"), lax.axis_size("member")
    devices = groups * members
    tokens, width = encoded.shape
    rows_dev = item_table.shape[0]
    negatives = negative_ids.shape[0]
    slots = max(2, 4 * tokens // devices)
    count = negatives // devices
    near = max(1, members // 4)
    everyone = members * tokens
    shape = jax.ShapeDtypeStruct
    sds = lambda *s: shape(s, F32)

    info = jnp.stack([lax.axis_index("group"), lax.axis_index("member")]).astype(I32)
    masked = encoded * valid.astype(F32)[:, None]

    far = range(0, members, near)
    encs = [None] * members
    for z in far:
        encs[z] = swap(masked, "member", z) if z else masked
    for z in far:
        for x in range(1, near):
            encs[z ^ x] = swap(encs[z], "member", x)

    request = call(
        functools.partial(bucket_kernel, members, rows_dev, slots),
        shape((devices, 2 * LANES), I32),
        [VMEM] * 3,
        VMEM,
        (target_owner, target_local.reshape(1, -1), negative_ids.reshape(1, -1)),
        name="bucket",
    )
    got = lax.all_to_all(
        request, ("group", "member"), split_axis=0, concat_axis=0, tiled=True
    )

    negs = call(
        functools.partial(gather_kernel, members, slots, count),
        [sds(members * count, width)] * groups,
        [SMEM, SMEM, VMEM],
        [VMEM] * groups,
        (info, got, item_table),
        name="gather_negatives",
    )
    negs = [negs[0]] + [swap(negs[d], "group", d) for d in range(1, groups)]
    tgts = call(
        functools.partial(gather_kernel, members, 0, slots),
        [sds(members * slots, width)] * groups,
        [SMEM, SMEM, VMEM],
        [VMEM] * groups,
        (info, got, item_table),
        name="gather_targets",
    )
    tgts = [tgts[0]] + [swap(tgts[d], "group", d) for d in range(1, groups)]

    neg_all = jnp.concatenate(negs, axis=0)
    stats, prob_hi, prob_lo, pulled = call(
        functools.partial(score_kernel, members),
        [
            sds(2, everyone),
            shape((members, negatives, tokens), BF16),
            shape((members, negatives, tokens), BF16),
            sds(members, width, tokens),
        ],
        [SMEM] + [VMEM] * (1 + members),
        [VMEM] * 4,
        (info, neg_all, *encs),
        flops=18 * everyone * negatives * width,
        moved=8 * MIB,
        name="score",
    )
    picked = call(
        functools.partial(pick_kernel, members, slots),
        [sds(members * slots, width)] * groups,
        [SMEM, SMEM] + [VMEM] * members,
        [VMEM] * groups,
        (info, got, *encs),
        name="pick",
    )
    joined, own, row_t = call(
        functools.partial(positive_kernel, members, groups, slots, tokens),
        [sds(2, everyone), sds(2, everyone), sds(members, width, tokens)],
        [SMEM] + [VMEM] * (2 + 2 * groups),
        [VMEM] * 3,
        (info, got, stats, *tgts, *picked),
        scratch=[pltpu.VMEM((LANES, 1), I32), pltpu.VMEM((members, LANES), I32)],
        name="positive",
    )
    sent = [picked[0]] + [swap(picked[d], "group", d) for d in range(1, groups)]

    final = joined
    d = 1
    while d < members:
        final = call(
            join_kernel,
            sds(2, everyone),
            [VMEM] * 2,
            VMEM,
            (final, swap(final, "member", d)),
            name="join",
        )
        d *= 2

    pulls = call(
        functools.partial(pull_kernel, members, tokens),
        [sds(width, tokens)] * members,
        [SMEM] + [VMEM] * 5,
        [VMEM] * members,
        (info, final, stats, own, pulled, row_t),
        name="pull",
    )
    parts = []
    for z in reversed(far):
        arrived = [swap(pulls[z ^ x], "member", x) for x in range(1, near)]
        total = pulls[z]
        if arrived:
            total = call(
                add_kernel,
                sds(width, tokens),
                [VMEM] * (1 + len(arrived)),
                VMEM,
                (total, *arrived),
                name="add",
            )
        parts.append(swap(total, "member", z) if z else total)

    grads = call(
        functools.partial(grad_kernel, members, groups, slots),
        [sds(members * count + members, width)] * groups,
        [SMEM] + [VMEM] * (6 + members),
        [VMEM] * groups,
        (info, got, final, stats, own, prob_hi, prob_lo, *encs),
        scratch=[
            pltpu.VMEM((negatives, width), F32),
            pltpu.VMEM((members, LANES), F32),
            pltpu.VMEM((members, LANES), I32),
        ],
        flops=6 * everyone * negatives * width,
        moved=8 * MIB,
        name="grad",
    )
    grads = [grads[0]] + [swap(grads[d], "group", d) for d in range(1, groups)]
    table_grad = call(
        functools.partial(scatter_kernel, members, groups, slots, count),
        sds(rows_dev, width),
        [SMEM, SMEM] + [VMEM] * (2 * groups),
        VMEM,
        (info, got, *grads, *sent),
        scratch=[pltpu.VMEM((LANES, LANES), F32), pltpu.VMEM((members * slots, width), F32)],
        name="scatter",
    )
    encoded_grad = call(
        finish_kernel,
        sds(tokens, width),
        [VMEM] * (1 + len(parts)),
        VMEM,
        (valid.reshape(1, -1), *parts),
        name="finish",
    )
    return (encoded_grad, table_grad)


def solution(mesh):
    placed = (
        P(("group", "member"), None),
        P(("group", "member"), None),
        P(("group", "member"), None),
        P(("group", "member")),
        P(("group", "member")),
        P(("group", "member")),
    )
    return jax.shard_map(
        shards,
        mesh=mesh,
        in_specs=placed,
        out_specs=(P(("group", "member"), None), P(("group", "member"), None)),
        check_vma=False,
    )
```

time: 320 us -> 144 us (0.45)
  blocking collectives: 140 us -> 0 us
  local copies, waits for them, and re-layouts: 62.5 us -> 5.02 us
  Pallas kernels: 0 us -> 45.7 us
  starting transfers between devices: 5.67 us -> 33.1 us
  matrix products: 23.3 us -> 0 us
  other arithmetic: 22.4 us -> 1.84 us
  between operations: 14.3 us -> 0.85 us
  waiting for transfers between devices: 51.2 us -> 56.6 us
    all_gather x4 -> x0, blocking collectives: 125 us -> none  [the longest x2 61.2 us: merged(): everything = jax.tree.map(lambda part: lax.all_gather(part, axis), value)]
    pallas_call x0 -> x17, Pallas kernels: none -> 45.7 us  [call(): pl.pallas_call(kernel, out_shape=out_shape, in_specs=ins, out_specs=outs,...]
    ppermute x0 -> x29, waiting for transfers between devices: none -> 40.9 us  [swap(): lax.ppermute(value, axis, [(i, i ^ d) for i in range(lax.axis_size(axis))])]
    scatter x2 -> x0, local copies, waits for them, and re-layouts: 37.8 us -> none  [the longest x1 25.1 us: shards(): slot_source.at[owners_negative, rank_negative]]
    all_to_all x2 -> x1, waiting for transfers between devices: 45.9 us -> 15.7 us  [shards(): lax.all_to_all(request, ('group', 'member'), split_axis=0, concat_axis=0,...]
    ppermute x0 -> x29, starting transfers between devices: none -> 27.1 us  [swap(): lax.ppermute(value, axis, [(i, i ^ d) for i in range(lax.axis_size(axis))])]
    dot_general x3 -> x0, matrix products: 23.3 us -> none  [the longest x1 10.5 us: shards(): jnp.dot(prob, negative_rows, precision=lax.Precision.HIGHEST, preferred_e...]
    gather x5 -> x0, local copies, waits for them, and re-layouts: 23.2 us -> none  [the longest x1 6.83 us: shards(): found = item_table[asked]]
  transfers between devices with their start and end apart: 4 -> 30, of which waited for: 2 -> 17; matrix products, arithmetic and copies ran while one was open for 27% -> 1% of each run, Pallas kernels for 0% -> 29%
where the time goes in v1:
time: 144 us; the launch traced here: 143 us
  waiting for transfers between devices  56.6 us (39%)
  Pallas kernels  45.7 us (32%)
  starting transfers between devices  33.1 us (23%)
  local copies, waits for them, and re-layouts  5.02 us (3%)
  other arithmetic  1.84 us (1%)
    pallas_call x17, Pallas kernels, call(): pl.pallas_call(kernel, out_shape=out_shape, in_specs=ins, out_specs=outs,...  45.7 us
    ppermute x29, waiting for transfers between devices, swap(): lax.ppermute(value, axis, [(i, i ^ d) for i in range(lax.axis_size(axis))])  40.9 us
    ppermute x29, starting transfers between devices, swap(): lax.ppermute(value, axis, [(i, i ^ d) for i in range(lax.axis_size(axis))])  27.1 us
    all_to_all x1, waiting for transfers between devices, shards(): lax.all_to_all(request, ('group', 'member'), split_axis=0, concat_axis=0,...  15.7 us
    all_to_all x1, starting transfers between devices, shards(): lax.all_to_all(request, ('group', 'member'), split_axis=0, concat_axis=0,...  6.07 us
    unnamed x10, local copies, waits for them, and re-layouts  4.36 us
  transfers between devices with their start and end apart: 30, of which 17 were waited for; matrix products, arithmetic and copies ran while one was open for 1% of the time, Pallas kernels for 29%

profile of v1, /device:TPU:0, one launch (start us, length us, event | category | flops | bytes accessed | tf_op | source)
XLA Modules:
  0.0 143.1 jit_solution(837255468076130606)
XLA Ops:
  0.6 0.7 convert_element_type.3
  1.3 1.0 broadcast_multiply_fusion.refs_0_
  2.4 3.1 %collective-permute-start.4 = (f32[256,256]{1,0:T(8,128)S(1)}, f32[256,256]{1,0:T(8,128)S(1)}, u32[]{:S(2)}, u32[]{:S(2)}) collective-permute-start(f32[256,256]{1,0:T(8,128)S(1)} %broadcast_multiply_fusion.refs_0_), channel_id=1, source_target_pairs={{0,2},{1,3},{2,0},{3,1},{4,6},{5,7},{6,4},{7,5},{8,10},{9,11},{10,... | collective-permute-start | bytes 786440 | tf_op jit(solution)/shard_map/ppermute | solution.py:286
  5.5 2.6 %collective-permute-start.6 = (f32[256,256]{1,0:T(8,128)S(1)}, f32[256,256]{1,0:T(8,128)S(1)}, u32[]{:S(2)}, u32[]{:S(2)}) collective-permute-start(f32[256,256]{1,0:T(8,128)S(1)} %broadcast_multiply_fusion.refs_0_), channel_id=1, source_target_pairs={{0,4},{1,5},{2,6},{3,7},{4,0},{5,1},{6,2},{7,3},{8,12},{9,13},{10,... | collective-permute-start | bytes 786440 | tf_op jit(solution)/shard_map/ppermute | solution.py:286
  8.0 0.8 copy.9.own_ref
  9.5 0.7 copy-done.3
  10.2 0.7 bucket.1
  11.6 6.1 %all-to-all-start = ((s32[32,1,256]{2,1,0:T(1,128)}), s32[32,1,256]{2,1,0:T(1,128)S(1)}, u32[]{:S(2)}, u32[]{:S(2)}) async-start(s32[32,1,256]{2,1,0:T(1,128)} %copy.10), calls=%async_computation | async-start | bytes 65536 | tf_op jit(solution)/shard_map/all_to_all | solution.py:321
  17.7 15.7 %all-to-all-done = s32[32,1,256]{2,1,0:T(1,128)S(1)} async-done(((s32[32,1,256]{2,1,0:T(1,128)}), s32[32,1,256]{2,1,0:T(1,128)S(1)}, u32[]{:S(2)}, u32[]{:S(2)}) %all-to-all-start) | async-done | bytes 32800 | tf_op jit(solution)/shard_map/all_to_all | solution.py:321
  33.5 2.2 %copy-done = f32[4096,256]{1,0:T(8,128)S(1)} copy-done((f32[4096,256]{1,0:T(8,128)S(1)}, f32[4096,256]{1,0:T(8,128)}, u32[]{:S(2)}) %copy-start) | copy-done | bytes 4194328
  35.7 3.1 %gather_negatives.1 = (f32[128,256]{1,0:T(8,128)S(1)}, f32[128,256]{1,0:T(8,128)S(1)}, f32[128,256]{1,0:T(8,128)S(1)}, f32[128,256]{1,0:T(8,128)S(1)}) custom-call(s32[2]{0:T(128)S(1)} %pad_add_fusion.info, s32[32,256]{1,0:T(8,128)S(1)} %bitcast.9, f32[4096,256]{1,0:T(8,128)S(1)} %copy-done), custom_call_target="tpu_custom_call" | custom-call | tf_op jit(solution)/shard_map/gather_negatives/pallas_call | solution.py:24
  40.2 0.7 collective-permute-start.3
  40.9 1.3 collective-permute-start.5
  42.2 0.7 collective-permute-start.7
  42.9 1.3 collective-permute-start.9
  44.7 5.2 %gather_targets.1 = (f32[256,256]{1,0:T(8,128)S(1)}, f32[256,256]{1,0:T(8,128)S(1)}, f32[256,256]{1,0:T(8,128)S(1)}, f32[256,256]{1,0:T(8,128)S(1)}) custom-call(s32[2]{0:T(128)S(1)} %pad_add_fusion.info, s32[32,256]{1,0:T(8,128)S(1)} %bitcast.10, f32[4096,256]{1,0:T(8,128)S(1)} %copy-done), custom_call_target="tpu_custom_call" | custom-call | tf_op jit(solution)/shard_map/gather_targets/pallas_call | solution.py:24
  50.8 1.5 %collective-permute-start.11 = (f32[256,256]{1,0:T(8,128)S(1)}, f32[256,256]{1,0:T(8,128)S(1)}, u32[]{:S(2)}, u32[]{:S(2)}) collective-permute-start(f32[256,256]{1,0:T(8,128)S(1)} %get-tuple-element.40), channel_id=1, source_target_pairs={{0,16},{8,24},{16,0},{24,8},{1,17},{9,25},{17,1},{25,9},{2,18},{10... | collective-permute-start | bytes 786440 | tf_op jit(solution)/shard_map/ppermute | solution.py:286
  52.2 2.7 %collective-permute-done.5.refs_3_ = f32[256,256]{1,0:T(8,128)S(1)} collective-permute-done((f32[256,256]{1,0:T(8,128)S(1)}, f32[256,256]{1,0:T(8,128)S(1)}, u32[]{:S(2)}, u32[]{:S(2)}) %collective-permute-start.5) | collective-permute-done | bytes 262176 | tf_op jit(solution)/shard_map/ppermute | solution.py:286
  54.9 5.6 %collective-permute-done.7.refs_5_ = f32[256,256]{1,0:T(8,128)S(1)} collective-permute-done((f32[256,256]{1,0:T(8,128)S(1)}, f32[256,256]{1,0:T(8,128)S(1)}, u32[]{:S(2)}, u32[]{:S(2)}) %collective-permute-start.7) | collective-permute-done | bytes 262176 | tf_op jit(solution)/shard_map/ppermute | solution.py:286
  60.6 4.8 %collective-permute-done.9.refs_7_ = f32[256,256]{1,0:T(8,128)S(1)} collective-permute-done((f32[256,256]{1,0:T(8,128)S(1)}, f32[256,256]{1,0:T(8,128)S(1)}, u32[]{:S(2)}, u32[]{:S(2)}) %collective-permute-start.9) | collective-permute-done | bytes 262176 | tf_op jit(solution)/shard_map/ppermute | solution.py:286
  65.4 6.1 %pick.1 = (f32[256,256]{1,0:T(8,128)S(1)}, f32[256,256]{1,0:T(8,128)S(1)}, f32[256,256]{1,0:T(8,128)S(1)}, f32[256,256]{1,0:T(8,128)S(1)}) custom-call(s32[2]{0:T(128)S(1)} %pad_add_fusion.info, s32[32,256]{1,0:T(8,128)S(1)} %bitcast.11, f32[256,256]{1,0:T(8,128)S(1)} %broadcast_multiply_fusion.refs_0_, f32[256,256]{1,0:T(8,128)S(1)} %collective-permute-done.3.refs_1_, ...), custom_call_target="tpu_custom_call" | custom-call | tf_op jit(solution)/shard_map/pick/pallas_call | solution.py:24
  71.5 12.0 %score.1 = (f32[2,2048]{1,0:T(2,128)S(1)}, bf16[8,512,256]{2,1,0:T(8,128)(2,1)S(1)}, bf16[8,512,256]{2,1,0:T(8,128)(2,1)S(1)}, f32[8,256,256]{2,1,0:T(8,128)S(1)}) custom-call(s32[2]{0:T(128)S(1)} %pad_add_fusion.info, f32[512,256]{1,0:T(8,128)S(1)} %pad_maximum_fusion.neg_ref, f32[256,256]{1,0:T(8,128)S(1)} %broadcast_multiply_fusion.refs_0_, ...), custom_call_target="tpu_custom_call" | custom-call | flops 4831838208 | bytes 8388608 | tf_op jit(solution)/shard_map/score/pallas_call | solution.py:24
  83.6 1.9 %positive.1 = (f32[2,2048]{1,0:T(2,128)S(1)}, f32[2,2048]{1,0:T(2,128)S(1)}, f32[8,256,256]{2,1,0:T(8,128)S(1)}) custom-call(s32[2]{0:T(128)S(1)} %pad_add_fusion.info, s32[32,256]{1,0:T(8,128)S(1)} %bitcast.12, f32[2,2048]{1,0:T(2,128)S(1)} %get-tuple-element.37.stats, f32[256,256]{1,0:T(8,128)S(1)} %get-tuple-element.38.refs_0_, ...), custom_call_target="tpu_custom_call" | custom-call | tf_op jit(solution)/shard_map/positive/pallas_call | solution.py:24
  85.4 0.7 collective-permute-start.13
  86.2 3.1 %collective-permute-done.13.second = f32[2,2048]{1,0:T(2,128)S(1)} collective-permute-done((f32[2,2048]{1,0:T(2,128)S(1)}, f32[2,2048]{1,0:T(2,128)S(1)}, u32[]{:S(2)}, u32[]{:S(2)}) %collective-permute-start.13) | collective-permute-done | bytes 16416 | tf_op jit(solution)/shard_map/ppermute | solution.py:286
  89.3 0.8 collective-permute-start.14
  90.0 3.0 %collective-permute-done.14.second = f32[2,2048]{1,0:T(2,128)S(1)} collective-permute-done((f32[2,2048]{1,0:T(2,128)S(1)}, f32[2,2048]{1,0:T(2,128)S(1)}, u32[]{:S(2)}, u32[]{:S(2)}) %collective-permute-start.14) | collective-permute-done | bytes 16416 | tf_op jit(solution)/shard_map/ppermute | solution.py:286
  93.1 1.7 %collective-permute-start.15 = (f32[2,2048]{1,0:T(2,128)S(1)}, f32[2,2048]{1,0:T(2,128)S(1)}, u32[]{:S(2)}, u32[]{:S(2)}) collective-permute-start(f32[2,2048]{1,0:T(2,128)S(1)} %join.4.first), channel_id=1, source_target_pairs={{0,4},{1,5},{2,6},{3,7},{4,0},{5,1},{6,2},{7,3},{8,12},{9,13},{10,... | collective-permute-start | bytes 49160 | tf_op jit(solution)/shard_map/ppermute | solution.py:286
  94.8 3.0 %collective-permute-done.15.second = f32[2,2048]{1,0:T(2,128)S(1)} collective-permute-done((f32[2,2048]{1,0:T(2,128)S(1)}, f32[2,2048]{1,0:T(2,128)S(1)}, u32[]{:S(2)}, u32[]{:S(2)}) %collective-permute-start.15) | collective-permute-done | bytes 16416 | tf_op jit(solution)/shard_map/ppermute | solution.py:286
  97.8 0.8 pull.1
  98.7 0.9 collective-permute-start.20
  99.5 1.2 collective-permute-start.18
  100.7 0.8 collective-permute-start.16
  101.5 0.8 collective-permute-start.27
  102.3 2.6 %grad.1 = (f32[136,256]{1,0:T(8,128)S(1)}, f32[136,256]{1,0:T(8,128)S(1)}, f32[136,256]{1,0:T(8,128)S(1)}, f32[136,256]{1,0:T(8,128)S(1)}) custom-call(s32[2]{0:T(128)S(1)} %pad_add_fusion.info, s32[32,256]{1,0:T(8,128)S(1)} %bitcast.13, f32[2,2048]{1,0:T(2,128)S(1)} %join.5.final, f32[2,2048]{1,0:T(2,128)S(1)} %get-tuple-element.37.stats, ...), custom_call_target="tpu_custom_call" | custom-call | flops 1610612736 | bytes 8388608 | tf_op jit(solution)/shard_map/grad/pallas_call | solution.py:24
  105.0 3.0 %collective-permute-done.20.refs_1_ = f32[256,256]{1,0:T(8,128)S(1)} collective-permute-done((f32[256,256]{1,0:T(8,128)S(1)}, f32[256,256]{1,0:T(8,128)S(1)}, u32[]{:S(2)}, u32[]{:S(2)}) %collective-permute-start.20) | collective-permute-done | bytes 262176 | tf_op jit(solution)/shard_map/ppermute | solution.py:286
  108.0 3.3 %collective-permute-done.18.refs_1_ = f32[256,256]{1,0:T(8,128)S(1)} collective-permute-done((f32[256,256]{1,0:T(8,128)S(1)}, f32[256,256]{1,0:T(8,128)S(1)}, u32[]{:S(2)}, u32[]{:S(2)}) %collective-permute-start.18) | collective-permute-done | bytes 262176 | tf_op jit(solution)/shard_map/ppermute | solution.py:286
  111.2 0.7 collective-permute-start.24
  111.9 2.1 %collective-permute-done.16.refs_1_ = f32[256,256]{1,0:T(8,128)S(1)} collective-permute-done((f32[256,256]{1,0:T(8,128)S(1)}, f32[256,256]{1,0:T(8,128)S(1)}, u32[]{:S(2)}, u32[]{:S(2)}) %collective-permute-start.16) | collective-permute-done | bytes 262176 | tf_op jit(solution)/shard_map/ppermute | solution.py:286
  114.2 1.8 %collective-permute-start.28 = (f32[256,256]{1,0:T(8,128)S(1)}, f32[256,256]{1,0:T(8,128)S(1)}, u32[]{:S(2)}, u32[]{:S(2)}) collective-permute-start(f32[256,256]{1,0:T(8,128)S(1)} %get-tuple-element.45.refs_7_), channel_id=1, source_target_pairs={{0,24},{8,16},{16,8},{24,0},{1,25},{9,17},{17,9},{25,1},{2,26},{10... | collective-permute-start | bytes 786440 | tf_op jit(solution)/shard_map/ppermute | solution.py:286
  116.3 0.8 collective-permute-start.22
  117.1 3.0 %collective-permute-done.25.refs_3_ = f32[136,256]{1,0:T(8,128)S(1)} collective-permute-done((f32[136,256]{1,0:T(8,128)S(1)}, f32[136,256]{1,0:T(8,128)S(1)}, u32[]{:S(2)}, u32[]{:S(2)}) %collective-permute-start.25) | collective-permute-done | bytes 139296 | tf_op jit(solution)/shard_map/ppermute | solution.py:286
  120.1 0.7 collective-permute-start.21
  120.8 2.5 %collective-permute-start.19 = (f32[256,256]{1,0:T(8,128)S(1)}, f32[256,256]{1,0:T(8,128)S(1)}, u32[]{:S(2)}, u32[]{:S(2)}) collective-permute-start(f32[256,256]{1,0:T(8,128)S(1)} %add.7), channel_id=1, source_target_pairs={{0,4},{1,5},{2,6},{3,7},{4,0},{5,1},{6,2},{7,3},{8,12},{9,13},{10,... | collective-permute-start | bytes 786440 | tf_op jit(solution)/shard_map/ppermute | solution.py:286
  123.3 1.2 collective-permute-start.17
  124.9 12.1 %scatter.1 = f32[4096,256]{1,0:T(8,128)} custom-call(s32[2]{0:T(128)S(1)} %pad_add_fusion.info, s32[32,256]{1,0:T(8,128)S(1)} %bitcast.14, f32[136,256]{1,0:T(8,128)S(1)} %get-tuple-element.60.refs_0_, f32[136,256]{1,0:T(8,128)S(1)} %collective-permute-done.23.refs_1_, f32[136,256]{1,0:T(8,128)S(1)} %collective-permute-done.24.refs_2_, ...), custom_call_target="tpu_custom_call" | custom-call | tf_op jit(solution)/shard_map/scatter/pallas_call | solution.py:24
  137.1 5.1 %collective-permute-done.19.refs_1_ = f32[256,256]{1,0:T(8,128)S(1)} collective-permute-done((f32[256,256]{1,0:T(8,128)S(1)}, f32[256,256]{1,0:T(8,128)S(1)}, u32[]{:S(2)}, u32[]{:S(2)}) %collective-permute-start.19) | collective-permute-done | bytes 262176 | tf_op jit(solution)/shard_map/ppermute | solution.py:286
  142.2 1.0 finish.1
  (44 shorter events, 5.1 us)
Async XLA Ops:
  2.4 38.5 %collective-permute-start.4 = (f32[256,256]{1,0:T(8,128)S(1)}, f32[256,256]{1,0:T(8,128)S(1)}, u32[]{:S(2)}, u32[]{:S(2)}) collective-permute-start(f32[256,256]{1,0:T(8,128)S(1)} %broadcast_multiply_fusion.refs_0_), channel_id=1, source_target_pairs={{0,2},{1,3},{2,0},{3,1},{4,6},{5,7},{6,4},{7,5},{8,10},{9,11},{10,... | collective-permute-start | bytes 786440 | tf_op jit(solution)/shard_map/ppermute | solution.py:286
  5.5 36.7 %collective-permute-start.6 = (f32[256,256]{1,0:T(8,128)S(1)}, f32[256,256]{1,0:T(8,128)S(1)}, u32[]{:S(2)}, u32[]{:S(2)}) collective-permute-start(f32[256,256]{1,0:T(8,128)S(1)} %broadcast_multiply_fusion.refs_0_), channel_id=1, source_target_pairs={{0,4},{1,5},{2,6},{3,7},{4,0},{5,1},{6,2},{7,3},{8,12},{9,13},{10,... | collective-permute-start | bytes 786440 | tf_op jit(solution)/shard_map/ppermute | solution.py:286
  8.0 34.8 %collective-permute-start.8 = (f32[256,256]{1,0:T(8,128)S(1)}, f32[256,256]{1,0:T(8,128)S(1)}, u32[]{:S(2)}, u32[]{:S(2)}) collective-permute-start(f32[256,256]{1,0:T(8,128)S(1)} %broadcast_multiply_fusion.refs_0_), channel_id=1, source_target_pairs={{0,6},{1,7},{2,4},{3,5},{4,2},{5,3},{6,0},{7,1},{8,14},{9,15},{10,... | collective-permute-start | bytes 786440 | tf_op jit(solution)/shard_map/ppermute | solution.py:286
  8.9 0.7 copy-start.2
  9.5 0.7 copy-start.3
  11.6 21.9 %all-to-all-start = ((s32[32,1,256]{2,1,0:T(1,128)}), s32[32,1,256]{2,1,0:T(1,128)S(1)}, u32[]{:S(2)}, u32[]{:S(2)}) async-start(s32[32,1,256]{2,1,0:T(1,128)} %copy.10), calls=%async_computation | async-start | bytes 65536 | tf_op jit(solution)/shard_map/all_to_all | solution.py:321
  33.5 2.2 %copy-start = (f32[4096,256]{1,0:T(8,128)S(1)}, f32[4096,256]{1,0:T(8,128)}, u32[]{:S(2)}) copy-start(f32[4096,256]{1,0:T(8,128)} %table.3) | copy-start | bytes 12582916
  38.8 1.4 collective-permute-start
  38.9 5.8 %collective-permute-start.1 = (f32[128,256]{1,0:T(8,128)S(1)}, f32[128,256]{1,0:T(8,128)S(1)}, u32[]{:S(2)}, u32[]{:S(2)}) collective-permute-start(f32[128,256]{1,0:T(8,128)S(1)} %get-tuple-element.35), channel_id=1, source_target_pairs={{0,16},{8,24},{16,0},{24,8},{1,17},{9,25},{17,1},{25,9},{2,18},{10... | collective-permute-start | bytes 393224 | tf_op jit(solution)/shard_map/ppermute | solution.py:286
  40.2 10.6 %collective-permute-start.3 = (f32[256,256]{1,0:T(8,128)S(1)}, f32[256,256]{1,0:T(8,128)S(1)}, u32[]{:S(2)}, u32[]{:S(2)}) collective-permute-start(f32[256,256]{1,0:T(8,128)S(1)} %broadcast_multiply_fusion.refs_0_), channel_id=1, source_target_pairs={{0,1},{1,0},{2,3},{3,2},{4,5},{5,4},{6,7},{7,6},{8,9},{9,8},{10,11... | collective-permute-start | bytes 786440 | tf_op jit(solution)/shard_map/ppermute | solution.py:286
  40.9 14.1 %collective-permute-start.5 = (f32[256,256]{1,0:T(8,128)S(1)}, f32[256,256]{1,0:T(8,128)S(1)}, u32[]{:S(2)}, u32[]{:S(2)}) collective-permute-start(f32[256,256]{1,0:T(8,128)S(1)} %collective-permute-done.4.refs_2_), channel_id=1, source_target_pairs={{0,1},{1,0},{2,3},{3,2},{4,5},{5,4},{6,7},{7,6},{8,9},{9,8},{10,11... | collective-permute-start | bytes 786440 | tf_op jit(solution)/shard_map/ppermute | solution.py:286
  42.2 18.4 %collective-permute-start.7 = (f32[256,256]{1,0:T(8,128)S(1)}, f32[256,256]{1,0:T(8,128)S(1)}, u32[]{:S(2)}, u32[]{:S(2)}) collective-permute-start(f32[256,256]{1,0:T(8,128)S(1)} %collective-permute-done.6.refs_4_), channel_id=1, source_target_pairs={{0,1},{1,0},{2,3},{3,2},{4,5},{5,4},{6,7},{7,6},{8,9},{9,8},{10,11... | collective-permute-start | bytes 786440 | tf_op jit(solution)/shard_map/ppermute | solution.py:286
  42.9 22.5 %collective-permute-start.9 = (f32[256,256]{1,0:T(8,128)S(1)}, f32[256,256]{1,0:T(8,128)S(1)}, u32[]{:S(2)}, u32[]{:S(2)}) collective-permute-start(f32[256,256]{1,0:T(8,128)S(1)} %collective-permute-done.8.refs_6_), channel_id=1, source_target_pairs={{0,1},{1,0},{2,3},{3,2},{4,5},{5,4},{6,7},{7,6},{8,9},{9,8},{10,11... | collective-permute-start | bytes 786440 | tf_op jit(solution)/shard_map/ppermute | solution.py:286
  44.7 5.5 %collective-permute-start.2 = (f32[128,256]{1,0:T(8,128)S(1)}, f32[128,256]{1,0:T(8,128)S(1)}, u32[]{:S(2)}, u32[]{:S(2)}) collective-permute-start(f32[128,256]{1,0:T(8,128)S(1)} %get-tuple-element.36), channel_id=1, source_target_pairs={{0,24},{8,16},{16,8},{24,0},{1,25},{9,17},{17,9},{25,1},{2,26},{10... | collective-permute-start | bytes 393224 | tf_op jit(solution)/shard_map/ppermute | solution.py:286
  50.3 33.3 %collective-permute-start.10 = (f32[256,256]{1,0:T(8,128)S(1)}, f32[256,256]{1,0:T(8,128)S(1)}, u32[]{:S(2)}, u32[]{:S(2)}) collective-permute-start(f32[256,256]{1,0:T(8,128)S(1)} %get-tuple-element.39), channel_id=1, source_target_pairs={{0,8},{8,0},{16,24},{24,16},{1,9},{9,1},{17,25},{25,17},{2,10},{10... | collective-permute-start | bytes 786440 | tf_op jit(solution)/shard_map/ppermute | solution.py:286
  50.8 32.8 %collective-permute-start.11 = (f32[256,256]{1,0:T(8,128)S(1)}, f32[256,256]{1,0:T(8,128)S(1)}, u32[]{:S(2)}, u32[]{:S(2)}) collective-permute-start(f32[256,256]{1,0:T(8,128)S(1)} %get-tuple-element.40), channel_id=1, source_target_pairs={{0,16},{8,24},{16,0},{24,8},{1,17},{9,25},{17,1},{25,9},{2,18},{10... | collective-permute-start | bytes 786440 | tf_op jit(solution)/shard_map/ppermute | solution.py:286
  54.9 28.6 %collective-permute-start.12 = (f32[256,256]{1,0:T(8,128)S(1)}, f32[256,256]{1,0:T(8,128)S(1)}, u32[]{:S(2)}, u32[]{:S(2)}) collective-permute-start(f32[256,256]{1,0:T(8,128)S(1)} %get-tuple-element.41), channel_id=1, source_target_pairs={{0,24},{8,16},{16,8},{24,0},{1,25},{9,17},{17,9},{25,1},{2,26},{10... | collective-permute-start | bytes 786440 | tf_op jit(solution)/shard_map/ppermute | solution.py:286
  85.4 3.8 %collective-permute-start.13 = (f32[2,2048]{1,0:T(2,128)S(1)}, f32[2,2048]{1,0:T(2,128)S(1)}, u32[]{:S(2)}, u32[]{:S(2)}) collective-permute-start(f32[2,2048]{1,0:T(2,128)S(1)} %get-tuple-element.46.first), channel_id=1, source_target_pairs={{0,1},{1,0},{2,3},{3,2},{4,5},{5,4},{6,7},{7,6},{8,9},{9,8},{10,11... | collective-permute-start | bytes 49160 | tf_op jit(solution)/shard_map/ppermute | solution.py:286
  89.3 3.8 %collective-permute-start.14 = (f32[2,2048]{1,0:T(2,128)S(1)}, f32[2,2048]{1,0:T(2,128)S(1)}, u32[]{:S(2)}, u32[]{:S(2)}) collective-permute-start(f32[2,2048]{1,0:T(2,128)S(1)} %join.3.first), channel_id=1, source_target_pairs={{0,2},{1,3},{2,0},{3,1},{4,6},{5,7},{6,4},{7,5},{8,10},{9,11},{10,... | collective-permute-start | bytes 49160 | tf_op jit(solution)/shard_map/ppermute | solution.py:286
  93.1 4.7 %collective-permute-start.15 = (f32[2,2048]{1,0:T(2,128)S(1)}, f32[2,2048]{1,0:T(2,128)S(1)}, u32[]{:S(2)}, u32[]{:S(2)}) collective-permute-start(f32[2,2048]{1,0:T(2,128)S(1)} %join.4.first), channel_id=1, source_target_pairs={{0,4},{1,5},{2,6},{3,7},{4,0},{5,1},{6,2},{7,3},{8,12},{9,13},{10,... | collective-permute-start | bytes 49160 | tf_op jit(solution)/shard_map/ppermute | solution.py:286
  98.7 9.3 %collective-permute-start.20 = (f32[256,256]{1,0:T(8,128)S(1)}, f32[256,256]{1,0:T(8,128)S(1)}, u32[]{:S(2)}, u32[]{:S(2)}) collective-permute-start(f32[256,256]{1,0:T(8,128)S(1)} %get-tuple-element.55), channel_id=1, source_target_pairs={{0,1},{1,0},{2,3},{3,2},{4,5},{5,4},{6,7},{7,6},{8,9},{9,8},{10,11... | collective-permute-start | bytes 786440 | tf_op jit(solution)/shard_map/ppermute | solution.py:286
  99.5 11.7 %collective-permute-start.18 = (f32[256,256]{1,0:T(8,128)S(1)}, f32[256,256]{1,0:T(8,128)S(1)}, u32[]{:S(2)}, u32[]{:S(2)}) collective-permute-start(f32[256,256]{1,0:T(8,128)S(1)} %get-tuple-element.53), channel_id=1, source_target_pairs={{0,1},{1,0},{2,3},{3,2},{4,5},{5,4},{6,7},{7,6},{8,9},{9,8},{10,11... | collective-permute-start | bytes 786440 | tf_op jit(solution)/shard_map/ppermute | solution.py:286
  100.7 13.3 %collective-permute-start.16 = (f32[256,256]{1,0:T(8,128)S(1)}, f32[256,256]{1,0:T(8,128)S(1)}, u32[]{:S(2)}, u32[]{:S(2)}) collective-permute-start(f32[256,256]{1,0:T(8,128)S(1)} %get-tuple-element.51), channel_id=1, source_target_pairs={{0,1},{1,0},{2,3},{3,2},{4,5},{5,4},{6,7},{7,6},{8,9},{9,8},{10,11... | collective-permute-start | bytes 786440 | tf_op jit(solution)/shard_map/ppermute | solution.py:286
  101.5 19.3 %collective-permute-start.26 = (f32[256,256]{1,0:T(8,128)S(1)}, f32[256,256]{1,0:T(8,128)S(1)}, u32[]{:S(2)}, u32[]{:S(2)}) collective-permute-start(f32[256,256]{1,0:T(8,128)S(1)} %get-tuple-element.43.refs_5_), channel_id=1, source_target_pairs={{0,8},{8,0},{16,24},{24,16},{1,9},{9,1},{17,25},{25,17},{2,10},{10... | collective-permute-start | bytes 786440 | tf_op jit(solution)/shard_map/ppermute | solution.py:286
  101.5 21.8 %collective-permute-start.27 = (f32[256,256]{1,0:T(8,128)S(1)}, f32[256,256]{1,0:T(8,128)S(1)}, u32[]{:S(2)}, u32[]{:S(2)}) collective-permute-start(f32[256,256]{1,0:T(8,128)S(1)} %get-tuple-element.44.refs_6_), channel_id=1, source_target_pairs={{0,16},{8,24},{16,0},{24,8},{1,17},{9,25},{17,1},{25,9},{2,18},{10... | collective-permute-start | bytes 786440 | tf_op jit(solution)/shard_map/ppermute | solution.py:286
  108.0 6.2 %collective-permute-start.23 = (f32[136,256]{1,0:T(8,128)S(1)}, f32[136,256]{1,0:T(8,128)S(1)}, u32[]{:S(2)}, u32[]{:S(2)}) collective-permute-start(f32[136,256]{1,0:T(8,128)S(1)} %get-tuple-element.61), channel_id=1, source_target_pairs={{0,8},{8,0},{16,24},{24,16},{1,9},{9,1},{17,25},{25,17},{2,10},{10... | collective-permute-start | bytes 417800 | tf_op jit(solution)/shard_map/ppermute | solution.py:286
  111.2 5.1 %collective-permute-start.24 = (f32[136,256]{1,0:T(8,128)S(1)}, f32[136,256]{1,0:T(8,128)S(1)}, u32[]{:S(2)}, u32[]{:S(2)}) collective-permute-start(f32[136,256]{1,0:T(8,128)S(1)} %get-tuple-element.62), channel_id=1, source_target_pairs={{0,16},{8,24},{16,0},{24,8},{1,17},{9,25},{17,1},{25,9},{2,18},{10... | collective-permute-start | bytes 417800 | tf_op jit(solution)/shard_map/ppermute | solution.py:286
  114.0 6.0 %collective-permute-start.25 = (f32[136,256]{1,0:T(8,128)S(1)}, f32[136,256]{1,0:T(8,128)S(1)}, u32[]{:S(2)}, u32[]{:S(2)}) collective-permute-start(f32[136,256]{1,0:T(8,128)S(1)} %get-tuple-element.63), channel_id=1, source_target_pairs={{0,24},{8,16},{16,8},{24,0},{1,25},{9,17},{17,9},{25,1},{2,26},{10... | collective-permute-start | bytes 417800 | tf_op jit(solution)/shard_map/ppermute | solution.py:286
  114.2 10.7 %collective-permute-start.28 = (f32[256,256]{1,0:T(8,128)S(1)}, f32[256,256]{1,0:T(8,128)S(1)}, u32[]{:S(2)}, u32[]{:S(2)}) collective-permute-start(f32[256,256]{1,0:T(8,128)S(1)} %get-tuple-element.45.refs_7_), channel_id=1, source_target_pairs={{0,24},{8,16},{16,8},{24,0},{1,25},{9,17},{17,9},{25,1},{2,26},{10... | collective-permute-start | bytes 786440 | tf_op jit(solution)/shard_map/ppermute | solution.py:286
  116.3 20.8 %collective-permute-start.22 = (f32[256,256]{1,0:T(8,128)S(1)}, f32[256,256]{1,0:T(8,128)S(1)}, u32[]{:S(2)}, u32[]{:S(2)}) collective-permute-start(f32[256,256]{1,0:T(8,128)S(1)} %get-tuple-element.57), channel_id=1, source_target_pairs={{0,1},{1,0},{2,3},{3,2},{4,5},{5,4},{6,7},{7,6},{8,9},{9,8},{10,11... | collective-permute-start | bytes 786440 | tf_op jit(solution)/shard_map/ppermute | solution.py:286
  120.1 17.0 %collective-permute-start.21 = (f32[256,256]{1,0:T(8,128)S(1)}, f32[256,256]{1,0:T(8,128)S(1)}, u32[]{:S(2)}, u32[]{:S(2)}) collective-permute-start(f32[256,256]{1,0:T(8,128)S(1)} %add.8), channel_id=1, source_target_pairs={{0,2},{1,3},{2,0},{3,1},{4,6},{5,7},{6,4},{7,5},{8,10},{9,11},{10,... | collective-permute-start | bytes 786440 | tf_op jit(solution)/shard_map/ppermute | solution.py:286
  120.8 21.4 %collective-permute-start.19 = (f32[256,256]{1,0:T(8,128)S(1)}, f32[256,256]{1,0:T(8,128)S(1)}, u32[]{:S(2)}, u32[]{:S(2)}) collective-permute-start(f32[256,256]{1,0:T(8,128)S(1)} %add.7), channel_id=1, source_target_pairs={{0,4},{1,5},{2,6},{3,7},{4,0},{5,1},{6,2},{7,3},{8,12},{9,13},{10,... | collective-permute-start | bytes 786440 | tf_op jit(solution)/shard_map/ppermute | solution.py:286
  123.3 18.9 %collective-permute-start.17 = (f32[256,256]{1,0:T(8,128)S(1)}, f32[256,256]{1,0:T(8,128)S(1)}, u32[]{:S(2)}, u32[]{:S(2)}) collective-permute-start(f32[256,256]{1,0:T(8,128)S(1)} %add.6), channel_id=1, source_target_pairs={{0,6},{1,7},{2,4},{3,5},{4,2},{5,3},{6,0},{7,1},{8,14},{9,15},{10,... | collective-permute-start | bytes 786440 | tf_op jit(solution)/shard_map/ppermute | solution.py:286
  124.9 17.3 %copy-start.1 = (s32[256]{0:T(256)S(1)}, s32[256]{0:T(256)}, u32[]{:S(2)}) copy-start(s32[256]{0:T(256)} %param.11) | copy-start | bytes 3076

commit v2 on v1

v2 whole, which is shorter than its diff:
```python
import functools

import jax
import jax.numpy as jnp
from jax import lax
from jax.experimental import pallas as pl
from jax.experimental.pallas import tpu as pltpu
from jax.sharding import PartitionSpec as P

F32 = jnp.float32
BF16 = jnp.bfloat16
I32 = jnp.int32
LANES = 128
VMEM = pl.BlockSpec(memory_space=pltpu.VMEM)
ANY = pl.BlockSpec(memory_space=pl.ANY)
SMEM = pl.BlockSpec(memory_space=pltpu.SMEM)
MIB = 1 << 20
BATCH = 8

NN = (((1,), (0,)), ((), ()))
NT = (((1,), (1,)), ((), ()))
TN = (((0,), (0,)), ((), ()))


def call(kernel, out_shape, ins, outs, args, scratch=(), limit=10, flops=0, moved=0, name=None):
    return pl.pallas_call(
        kernel,
        out_shape=out_shape,
        in_specs=ins,
        out_specs=outs,
        scratch_shapes=list(scratch),
        compiler_params=pltpu.CompilerParams(vmem_limit_bytes=limit * MIB),
        cost_estimate=pl.CostEstimate(flops=flops, bytes_accessed=moved, transcendentals=0),
        name=name,
    )(*args)


def iota(shape, dim):
    return lax.broadcasted_iota(I32, shape, dim)


def as_bf16(flag):
    return flag.astype(F32).astype(BF16)


def dot1(a, b, dims):
    return lax.dot_general(a, b, dims, preferred_element_type=F32)


def split(x):
    hi = x.astype(BF16)
    return hi, (x - hi.astype(F32)).astype(BF16)


def dot3(a, b, dims):
    return dot1(a[0], b[0], dims) + (dot1(a[0], b[1], dims) + dot1(a[1], b[0], dims))


def row_to_col(row):
    return jnp.transpose(jnp.broadcast_to(row, (LANES, row.shape[1])))[:, 0:1]


def split3(x):
    hi = x.astype(BF16)
    rest = x - hi.astype(F32)
    mid = rest.astype(BF16)
    return hi, mid, (rest - mid.astype(F32)).astype(BF16)


def dot6(a, b, dims):
    small = dot1(a[2], b[0], dims) + dot1(a[1], b[1], dims) + dot1(a[0], b[2], dims)
    return (small + (dot1(a[1], b[0], dims) + dot1(a[0], b[1], dims))) + dot1(a[0], b[0], dims)


def copy_rows(source, row_of, target, base, count):
    for b in range(0, count, BATCH):
        rows = [source[pl.ds(row_of(b + k), 1), :] for k in range(BATCH)] if count % BATCH == 0 else None
        if rows is None:
            for k in range(count):
                target[pl.ds(base + k, 1), :] = source[pl.ds(row_of(k), 1), :]
            return
        target[pl.ds(pl.multiple_of(base + b, BATCH), BATCH), :] = jnp.concatenate(rows, axis=0)


def front_kernel(members, rows_dev, slots, tokens, negatives, info, ints, enc_ref, out_ref, masked_ref):
    devices = out_ref.shape[0]
    shift = rows_dev.bit_length() - 1
    owner = ints[:, 0:tokens]
    local = ints[:, tokens : 2 * tokens]
    valid = ints[:, 2 * tokens : 3 * tokens]
    ids = ints[:, 3 * tokens :]
    masked_ref[...] = enc_ref[...] * row_to_col(valid.astype(F32))

    def ranks(owner_row, count):
        hot = iota((devices, count), 0) == owner_row
        before = as_bf16(iota((count, count), 0) < iota((count, count), 1))
        seen = dot1(as_bf16(hot), before, NN)
        return hot, jnp.sum(jnp.where(hot, seen, 0.0), axis=0, keepdims=True).astype(I32)

    def table(hot, value, place):
        return dot1(jnp.where(hot, value, 0.0).astype(BF16), place, NT)

    def placed(lane_row, count):
        return as_bf16(iota((LANES, count), 0) == lane_row)

    hot, rank = ranks(owner, tokens)
    place = placed(rank, tokens)
    high = table(hot, (local >> 6).astype(F32), place)
    low = table(hot, (local & 63).astype(F32), place)
    group = owner >> (members.bit_length() - 1)
    hot_member = (iota((devices, tokens), 0) & (members - 1)) == (owner & (members - 1))
    position = table(
        hot_member, (iota((1, tokens), 1) + 1).astype(F32), placed(group * slots + rank, tokens)
    )

    hot, rank = ranks(ids >> shift, negatives)
    place = placed(rank + slots, negatives)
    local = ids & (rows_dev - 1)
    high = high + table(hot, (local >> 6).astype(F32), place)
    low = low + table(hot, (local & 63).astype(F32), place)
    out_ref[:, 0, 0:LANES] = high.astype(I32) * 64 + low.astype(I32)
    out_ref[:, 0, LANES:] = position.astype(I32)


def gather_kernel(members, groups, slots, count, info, got, table, *refs):
    for d, out in enumerate(refs[-groups:]):
        first = (info[0] ^ d) * members

        def member(mr, carry, out=out, first=first):
            asked = got.at[first + mr, 0]
            copy_rows(table, lambda k: asked[slots + k], out, mr * count, count)
            copy_rows(table, lambda k: asked[k], out, members * count + mr * slots, slots)
            return carry

        lax.fori_loop(0, members, member, 0)


def score_kernel(members, groups, negatives, info, *refs):
    rows, refs = refs[:groups], refs[groups:]
    encs = refs[:members]
    stats, prob_hi, prob_lo, pulled = refs[members:]
    tokens = encs[0].shape[0]
    neg = jnp.concatenate([row[0 : negatives // groups, :] for row in rows], axis=0)
    neg3 = split3(neg)
    neg_t = split(jnp.transpose(neg))
    for e in range(members):
        lanes = pl.ds(pl.multiple_of((info[1] ^ e) * tokens, LANES), tokens)
        score = dot6(neg3, split3(encs[e][...]), NT)
        top = jnp.max(score, axis=0, keepdims=True)
        prob = jnp.exp(score - top)
        stats[0:1, lanes] = top
        stats[1:2, lanes] = jnp.sum(prob, axis=0, keepdims=True)
        parts = split(prob)
        prob_hi[e] = parts[0]
        prob_lo[e] = parts[1]
        pulled[e] = dot3(neg_t, parts, NN)


def own_places(members, info, got):
    return got[pl.ds(info[0] * members, members), 0, LANES:]


def slot_hot(members, groups, slots, info, place_rows, column, mr, tokens):
    column[...] = row_to_col(place_rows[pl.ds(mr, 1), :])
    place = [
        column[pl.ds(pl.multiple_of((info[0] ^ d) * slots, slots), slots), :]
        for d in range(groups)
    ]
    return jnp.concatenate(place, axis=0) == iota((groups * slots, tokens), 1) + 1


def pick_kernel(members, groups, slots, info, got, *refs):
    encs = refs[:members]
    outs = refs[members : members + groups]
    place_rows, column = refs[members + groups :]
    place_rows[...] = own_places(members, info, got)
    for e in range(members):
        mr = info[1] ^ e
        tokens = encs[e].shape[0]
        hot = as_bf16(slot_hot(members, groups, slots, info, place_rows, column, mr, tokens))
        hi, mid, low = split3(encs[e][...])
        found = (dot1(hot, hi, NN) + dot1(hot, mid, NN)) + dot1(hot, low, NN)
        at = pl.ds(pl.multiple_of(mr * slots, slots), slots)
        for d in range(groups):
            outs[d][at, :] = found[d * slots : (d + 1) * slots]


def positive_kernel(members, groups, slots, tokens, info, got, stats, *refs):
    rows, picked = refs[:groups], refs[groups : 2 * groups]
    joined, own, row_t, place_rows, column = refs[2 * groups :]
    place_rows[...] = own_places(members, info, got)
    first = rows[0].shape[0] - members * slots
    for e in range(members):
        mr = info[1] ^ e
        lanes = pl.ds(pl.multiple_of(mr * tokens, LANES), tokens)
        at = pl.ds(pl.multiple_of(mr * slots, slots), slots)
        after = pl.ds(pl.multiple_of(first + mr * slots, slots), slots)
        hot = slot_hot(members, groups, slots, info, place_rows, column, mr, tokens)
        row = jnp.concatenate([r[after, :] for r in rows], axis=0)
        enc = jnp.concatenate([p[at, :] for p in picked], axis=0)
        value = jnp.sum(row * enc, axis=1, keepdims=True)
        positive = jnp.sum(jnp.where(hot, value, 0.0), axis=0, keepdims=True)
        has = jnp.sum(hot.astype(F32), axis=0, keepdims=True)
        high, low = split(row)
        row_t[e] = dot1(high, as_bf16(hot), TN) + dot1(low, as_bf16(hot), TN)
        old = stats[0:1, lanes]
        top = jnp.where(has > 0, jnp.maximum(old, positive), old)
        joined[0:1, lanes] = top
        joined[1:2, lanes] = stats[1:2, lanes] * jnp.exp(old - top) + jnp.where(
            has > 0, jnp.exp(positive - top), 0.0
        )
        own[0:1, lanes] = positive
        own[1:2, lanes] = has


def join(first, second):
    top = jnp.maximum(first[0:1], second[0:1])
    total = first[1:2] * jnp.exp(first[0:1] - top) + second[1:2] * jnp.exp(second[0:1] - top)
    return top, total


def join_kernel(first, second, *refs):
    out = refs[-1]
    top, total = join(first[...], second[...])
    out[0:1, :] = top
    out[1:2, :] = total


def shares(info, e, tokens, final, stats, own):
    lanes = pl.ds(pl.multiple_of((info[1] ^ e) * tokens, LANES), tokens)
    top, total = final[0:1, lanes], final[1:2, lanes]
    scale = jnp.exp(stats[0:1, lanes] - top) / total
    extra = jnp.where(
        own[1:2, lanes] > 0, jnp.exp(own[0:1, lanes] - top) / total - 1.0, 0.0
    )
    return scale, extra


def pull_kernel(members, tokens, info, final, stats, own, pulled, row_t, *outs):
    for e in range(members):
        scale, extra = shares(info, e, tokens, final, stats, own)
        outs[e][...] = pulled[e] * scale + row_t[e] * extra


def flat(table, lane, slots):
    return jnp.concatenate(
        [table[m : m + 1, lane : lane + slots] for m in range(table.shape[0])], axis=1
    )


def grad_kernel(members, groups, slots, info, got, final, stats, own, prob_hi, prob_lo, *refs):
    encs = refs[:members]
    out, total, coef, place_rows = refs[members:]
    place_rows[...] = own_places(members, info, got)
    tokens, width = encs[0].shape
    for e in range(members):
        mr = info[1] ^ e
        scale, extra = shares(info, e, tokens, final, stats, own)
        enc = split(encs[e][...] * row_to_col(scale))
        part = dot3((prob_hi[e], prob_lo[e]), enc, NN)
        if e == 0:
            total[...] = part
        else:
            total[...] += part
        hot = place_rows[pl.ds(mr, 1), :] == iota((tokens, LANES), 0) + 1
        coef[pl.ds(mr, 1), :] = jnp.sum(
            jnp.where(hot, row_to_col(extra), 0.0), axis=0, keepdims=True
        )
    count = total.shape[0] // groups
    for g in range(groups):
        out[info[0] ^ g, 0:count, :] = total[g * count : (g + 1) * count, :]
        line = flat(coef[...], g * slots, slots)
        out[g, count:, 0 : line.shape[1]] = jnp.broadcast_to(line, (8, line.shape[1]))


def equal_in_batch(ids):
    size = ids.shape[1]
    across = jnp.broadcast_to(ids.astype(F32), (size, size))
    same = (jnp.transpose(across) == across) & (
        (iota((size, size), 0) // BATCH) == (iota((size, size), 1) // BATCH)
    )
    return same.astype(F32)


def scatter_kernel(members, groups, slots, count, info, got_v, got, grads, *refs):
    picked = refs[:groups]
    out, negs, tgts = refs[groups:]
    out[...] = jnp.zeros_like(out)

    def add_rows(asked, first, source, base, number):
        for b in range(0, number, BATCH):
            rows = [asked[first + b + k] for k in range(BATCH)]
            new = [
                out[pl.ds(rows[k], 1), :] + source[pl.ds(base + b + k, 1), :]
                for k in range(BATCH)
            ]
            for k in range(BATCH):
                out[pl.ds(rows[k], 1), :] = new[k]

    for d in range(groups):
        g = info[0] ^ d
        asked = got_v[pl.ds(g * members, members), 0, 0:LANES]
        number = members * count
        same = as_bf16(equal_in_batch(flat(asked, slots, count)) > 0)
        high, low = split(grads[g, 0:number, :])
        negs[...] = dot1(same, high, NN) + dot1(same, low, NN)
        weight = equal_in_batch(flat(asked, 0, slots)) * grads[g, number : number + 1, 0 : members * slots]
        tgts[...] = dot3(split(weight), split(picked[d][...]), NN)
        merged = BATCH // count if count < BATCH else 1

        def member(step, carry, g=g, merged=merged):
            if merged == 1:
                add_rows(got.at[g * members + step, 0], slots, negs, step * count, count)
                add_rows(got.at[g * members + step, 0], 0, tgts, step * slots, slots)
                return carry
            first = g * members + step * merged
            rows = [
                got[first + k // count, 0, slots + k % count] for k in range(BATCH)
            ]
            new = [
                out[pl.ds(rows[k], 1), :] + negs[pl.ds(step * BATCH + k, 1), :]
                for k in range(BATCH)
            ]
            for k in range(BATCH):
                out[pl.ds(rows[k], 1), :] = new[k]
            for m in range(merged):
                add_rows(got.at[first + m, 0], 0, tgts, (step * merged + m) * slots, slots)
            return carry

        lax.fori_loop(0, members // merged, member, 0)


def add_kernel(*refs):
    total = refs[0][...]
    for ref in refs[1:-1]:
        total = total + ref[...]
    refs[-1][...] = total


def finish_kernel(valid, *refs):
    total = refs[0][...]
    for ref in refs[1:-1]:
        total = total + ref[...]
    refs[-1][...] = jnp.transpose(total) * row_to_col(valid[...].astype(F32))


def swap(value, axis, d):
    return lax.ppermute(value, axis, [(i, i ^ d) for i in range(lax.axis_size(axis))])


def shards(encoded, item_table, target_owner, target_local, negative_ids, valid):
    groups, members = lax.axis_size("group"), lax.axis_size("member")
    devices = groups * members
    tokens, width = encoded.shape
    rows_dev = item_table.shape[0]
    negatives = negative_ids.shape[0]
    slots = max(2, 4 * tokens // devices)
    count = negatives // devices
    near = max(1, members // 4)
    everyone = members * tokens
    shape = jax.ShapeDtypeStruct
    sds = lambda *s: shape(s, F32)

    info = jnp.stack([lax.axis_index("group"), lax.axis_index("member")]).astype(I32)
    ints = jnp.concatenate([target_owner.reshape(-1), target_local, valid, negative_ids])
    request, masked = call(
        functools.partial(front_kernel, members, rows_dev, slots, tokens, negatives),
        [shape((devices, 1, 2 * LANES), I32), sds(tokens, width)],
        [SMEM] + [VMEM] * 2,
        [VMEM] * 2,
        (info, ints.reshape(1, -1), encoded),
        name="front",
    )
    got = lax.all_to_all(
        request, ("group", "member"), split_axis=0, concat_axis=0, tiled=True
    )

    encs = [masked] + [None] * (members - 1)
    direct = [d for d in range(1, members) if d < 2 * near or d % near == 0]
    for d in direct:
        encs[d] = swap(masked, "member", d)
    for d in range(1, members):
        if d not in direct:
            encs[d] = swap(encs[d // near * near], "member", d % near)

    early = [encs[d] for d in direct]
    rows = call(
        functools.partial(gather_kernel, members, groups, slots, count),
        [sds(members * (count + slots), width)] * groups,
        [SMEM, SMEM, VMEM] + [ANY] * len(early),
        [VMEM] * groups,
        (info, got, item_table, *early),
        name="gather",
    )
    rows = [rows[0]] + [swap(rows[d], "group", d) for d in range(1, groups)]

    picked = call(
        functools.partial(pick_kernel, members, groups, slots),
        [sds(members * slots, width)] * groups,
        [SMEM] + [VMEM] * (1 + members),
        [VMEM] * groups,
        (info, got, *encs),
        scratch=[pltpu.VMEM((members, LANES), I32), pltpu.VMEM((LANES, 1), I32)],
        name="pick",
    )
    sent = [picked[0]] + [swap(picked[d], "group", d) for d in range(1, groups)]
    stats, prob_hi, prob_lo, pulled = call(
        functools.partial(score_kernel, members, groups, negatives),
        [
            sds(2, everyone),
            shape((members, negatives, tokens), BF16),
            shape((members, negatives, tokens), BF16),
            sds(members, width, tokens),
        ],
        [SMEM] + [VMEM] * (groups + members),
        [VMEM] * 4,
        (info, *rows, *encs),
        flops=18 * everyone * negatives * width,
        moved=8 * MIB,
        name="score",
    )
    joined, own, row_t = call(
        functools.partial(positive_kernel, members, groups, slots, tokens),
        [sds(2, everyone), sds(2, everyone), sds(members, width, tokens)],
        [SMEM] + [VMEM] * (2 + 2 * groups),
        [VMEM] * 3,
        (info, got, stats, *rows, *picked),
        scratch=[pltpu.VMEM((members, LANES), I32), pltpu.VMEM((LANES, 1), I32)],
        name="positive",
    )

    final = joined
    d = 1
    while d < members:
        late = sent[1:] if 2 * d == members else []
        final = call(
            join_kernel,
            sds(2, everyone),
            [VMEM] * 2 + [ANY] * len(late),
            VMEM,
            (final, swap(final, "member", d), *late),
            name="join",
        )
        d *= 2

    pulls = call(
        functools.partial(pull_kernel, members, tokens),
        [sds(width, tokens)] * members,
        [SMEM] + [VMEM] * 5,
        [VMEM] * members,
        (info, final, stats, own, pulled, row_t),
        name="pull",
    )
    parts = []
    for z in [*range(members - near, near, -near), 0]:
        arrived = [swap(pulls[z ^ x], "member", x) for x in range(1, near)]
        total = call(
            add_kernel,
            sds(width, tokens),
            [VMEM] * near,
            VMEM,
            (pulls[z], *arrived),
            name="add",
        )
        parts.append(swap(total, "member", z) if z else total)
    parts += [swap(pulls[d], "member", d) for d in range(near, 2 * near)]

    grads = call(
        functools.partial(grad_kernel, members, groups, slots),
        sds(groups, members * count + 8, width),
        [SMEM] + [VMEM] * (6 + members),
        VMEM,
        (info, got, final, stats, own, prob_hi, prob_lo, *encs),
        scratch=[
            pltpu.VMEM((negatives, width), F32),
            pltpu.VMEM((members, LANES), F32),
            pltpu.VMEM((members, LANES), I32),
        ],
        flops=6 * everyone * negatives * width,
        moved=8 * MIB,
        name="grad",
    )
    grads = lax.all_to_all(grads, "group", split_axis=0, concat_axis=0, tiled=True)
    table_grad = call(
        functools.partial(scatter_kernel, members, groups, slots, count),
        sds(rows_dev, width),
        [SMEM, VMEM, SMEM, VMEM] + [VMEM] * groups,
        VMEM,
        (info, got, got, grads, *sent),
        scratch=[
            pltpu.VMEM((members * count, width), F32),
            pltpu.VMEM((members * slots, width), F32),
        ],
        name="scatter",
    )
    encoded_grad = call(
        finish_kernel,
        sds(tokens, width),
        [VMEM] * (1 + len(parts)),
        VMEM,
        (valid.reshape(1, -1), *parts),
        name="finish",
    )
    return (encoded_grad, table_grad)


def solution(mesh):
    placed = (
        P(("group", "member"), None),
        P(("group", "member"), None),
        P(("group", "member"), None),
        P(("group", "member")),
        P(("group", "member")),
        P(("group", "member")),
    )
    return jax.shard_map(
        shards,
        mesh=mesh,
        in_specs=placed,
        out_specs=(P(("group", "member"), None), P(("group", "member"), None)),
        check_vma=False,
    )
```

time: 144 us -> 129 us (0.90)
  waiting for transfers between devices: 56.6 us -> 31.3 us
  blocking collectives: 0 us -> 22.4 us
  Pallas kernels: 45.7 us -> 38.8 us
  local copies, waits for them, and re-layouts: 5.02 us -> 3.14 us
  starting transfers between devices: 33.1 us -> 31.4 us
    all_to_all x0 -> x1, blocking collectives: none -> 22.4 us  [shards(): lax.all_to_all(request, ('group', 'member'), split_axis=0, concat_axis=0,...]
    all_to_all x1, waiting for transfers between devices: 15.7 us -> 0.23 us  [shards(): lax.all_to_all(grads, 'group', split_axis=0, concat_axis=0, tiled=True)]
    ppermute x29 -> x23, waiting for transfers between devices: 40.9 us -> 31.1 us  [swap(): lax.ppermute(value, axis, [(i, i ^ d) for i in range(lax.axis_size(axis))])]
    pallas_call x17 -> x15, Pallas kernels: 45.7 us -> 38.8 us  [call(): pl.pallas_call(kernel, out_shape=out_shape, in_specs=ins, out_specs=outs,...]
    all_to_all x1, starting transfers between devices: 6.07 us -> 3.65 us  [shards(): lax.all_to_all(grads, 'group', split_axis=0, concat_axis=0, tiled=True)]
    unnamed x10 -> x6, local copies, waits for them, and re-layouts: 4.36 us -> 3.14 us
    ppermute x29 -> x23, starting transfers between devices: 27.1 us -> 27.7 us  [swap(): lax.ppermute(value, axis, [(i, i ^ d) for i in range(lax.axis_size(axis))])]
  transfers between devices with their start and end apart: 30 -> 24, of which waited for: 17 -> 9; matrix products, arithmetic and copies ran while one was open for 1% -> 0% of each run, Pallas kernels for 29% -> 23%
where the time goes in v2:
time: 129 us
  Pallas kernels  38.8 us (30%)
  starting transfers between devices  31.4 us (24%)
  waiting for transfers between devices  31.3 us (24%)
  blocking collectives  22.4 us (17%)
  local copies, waits for them, and re-layouts  3.14 us (2%)
    pallas_call x15, Pallas kernels, call(): pl.pallas_call(kernel, out_shape=out_shape, in_specs=ins, out_specs=outs,...  38.8 us
    ppermute x23, waiting for transfers between devices, swap(): lax.ppermute(value, axis, [(i, i ^ d) for i in range(lax.axis_size(axis))])  31.1 us
    ppermute x23, starting transfers between devices, swap(): lax.ppermute(value, axis, [(i, i ^ d) for i in range(lax.axis_size(axis))])  27.7 us
    all_to_all x1, blocking collectives, shards(): lax.all_to_all(request, ('group', 'member'), split_axis=0, concat_axis=0,...  22.4 us
    all_to_all x1, starting transfers between devices, shards(): lax.all_to_all(grads, 'group', split_axis=0, concat_axis=0, tiled=True)  3.65 us
    unnamed x6, local copies, waits for them, and re-layouts  3.14 us
  transfers between devices with their start and end apart: 24, of which 9 were waited for; matrix products, arithmetic and copies ran while one was open for 0% of the time, Pallas kernels for 23%

profile of v2, /device:TPU:0, one launch (start us, length us, event | category | flops | bytes accessed | tf_op | source)
XLA Modules:
  0.0 128.8 jit_solution(6858933593645891200)
XLA Ops:
  0.6 0.7 pad_add_fusion
  1.4 0.1 pad_add_fusion.1.info
  1.5 0.9 copy-done.1
  2.4 1.2 front.1
  3.6 4.1 %collective-permute-start.3 = (f32[256,256]{1,0:T(8,128)S(1)}, f32[256,256]{1,0:T(8,128)S(1)}, u32[]{:S(2)}, u32[]{:S(2)}) collective-permute-start(f32[256,256]{1,0:T(8,128)S(1)} %get-tuple-element.28.refs_4_.refs_0_), channel_id=1, source_target_pairs={{0,4},{1,5},{2,6},{3,7},{4,0},{5,1},{6,2},{7,3},{8,12},{9,13},{10,... | collective-permute-start | bytes 786440 | tf_op jit(solution)/shard_map/ppermute | solution.py:348
  7.7 1.3 %collective-permute-start.4 = (f32[256,256]{1,0:T(8,128)S(1)}, f32[256,256]{1,0:T(8,128)S(1)}, u32[]{:S(2)}, u32[]{:S(2)}) collective-permute-start(f32[256,256]{1,0:T(8,128)S(1)} %get-tuple-element.28.refs_4_.refs_0_), channel_id=1, source_target_pairs={{0,6},{1,7},{2,4},{3,5},{4,2},{5,3},{6,0},{7,1},{8,14},{9,15},{10,... | collective-permute-start | bytes 786440 | tf_op jit(solution)/shard_map/ppermute | solution.py:348
  9.0 1.5 %collective-permute-start = (f32[256,256]{1,0:T(8,128)S(1)}, f32[256,256]{1,0:T(8,128)S(1)}, u32[]{:S(2)}, u32[]{:S(2)}) collective-permute-start(f32[256,256]{1,0:T(8,128)S(1)} %get-tuple-element.28.refs_4_.refs_0_), channel_id=1, source_target_pairs={{0,1},{1,0},{2,3},{3,2},{4,5},{5,4},{6,7},{7,6},{8,9},{9,8},{10,11... | collective-permute-start | bytes 786440 | tf_op jit(solution)/shard_map/ppermute | solution.py:348
  10.5 0.2 collective-permute-start.1
  10.8 1.8 %collective-permute-start.2 = (f32[256,256]{1,0:T(8,128)S(1)}, f32[256,256]{1,0:T(8,128)S(1)}, u32[]{:S(2)}, u32[]{:S(2)}) collective-permute-start(f32[256,256]{1,0:T(8,128)S(1)} %get-tuple-element.28.refs_4_.refs_0_), channel_id=1, source_target_pairs={{0,3},{1,2},{2,1},{3,0},{4,7},{5,6},{6,5},{7,4},{8,11},{9,10},{10,... | collective-permute-start | bytes 786440 | tf_op jit(solution)/shard_map/ppermute | solution.py:348
  12.5 22.4 %all_to_all.10.got.got_v = s32[32,1,256]{2,1,0:T(1,128)S(1)} all-to-all(s32[32,1,256]{2,1,0:T(1,128)S(1)} %get-tuple-element.27), channel_id=1, replica_groups=mesh['group'=4,'member'=8] {'group','member'}, dimensions={0} | all-to-all | bytes 65536 | tf_op jit(solution)/shard_map/all_to_all | solution.py:374
  35.0 0.0 copy-start
  35.0 2.2 %copy-done = f32[4096,256]{1,0:T(8,128)S(1)} copy-done((f32[4096,256]{1,0:T(8,128)S(1)}, f32[4096,256]{1,0:T(8,128)}, u32[]{:S(2)}) %copy-start) | copy-done | bytes 4194328
  37.2 4.5 %gather.1 = (f32[384,256]{1,0:T(8,128)S(1)}, f32[384,256]{1,0:T(8,128)S(1)}, f32[384,256]{1,0:T(8,128)S(1)}, f32[384,256]{1,0:T(8,128)S(1)}) custom-call(s32[2]{0:T(128)S(1)} %pad_add_fusion.1.info, s32[32,1,256]{2,1,0:T(1,128)S(1)} %all_to_all.10.got.got_v, f32[4096,256]{1,0:T(8,128)S(1)} %copy-done, ...), custom_call_target="tpu_custom_call" | custom-call | tf_op jit(solution)/shard_map/gather/pallas_call | solution.py:26
  41.7 0.2 collective-permute-start.5
  41.9 0.5 collective-permute-start.6
  42.4 1.2 collective-permute-start.7
  43.6 1.5 %collective-permute-start.8 = (f32[256,256]{1,0:T(8,128)S(1)}, f32[256,256]{1,0:T(8,128)S(1)}, u32[]{:S(2)}, u32[]{:S(2)}) collective-permute-start(f32[256,256]{1,0:T(8,128)S(1)} %collective-permute-done.3.refs_3_.refs_8_.refs_4_), channel_id=1, source_target_pairs={{0,1},{1,0},{2,3},{3,2},{4,5},{5,4},{6,7},{7,6},{8,9},{9,8},{10,11... | collective-permute-start | bytes 786440 | tf_op jit(solution)/shard_map/ppermute | solution.py:348
  45.1 0.5 collective-permute-start.9
  45.7 7.1 %collective-permute-done.8.refs_9_.refs_5_ = f32[256,256]{1,0:T(8,128)S(1)} collective-permute-done((f32[256,256]{1,0:T(8,128)S(1)}, f32[256,256]{1,0:T(8,128)S(1)}, u32[]{:S(2)}, u32[]{:S(2)}) %collective-permute-start.8) | collective-permute-done | bytes 262176 | tf_op jit(solution)/shard_map/ppermute | solution.py:348
  52.7 5.2 %collective-permute-done.9.refs_11_.refs_7_ = f32[256,256]{1,0:T(8,128)S(1)} collective-permute-done((f32[256,256]{1,0:T(8,128)S(1)}, f32[256,256]{1,0:T(8,128)S(1)}, u32[]{:S(2)}, u32[]{:S(2)}) %collective-permute-start.9) | collective-permute-done | bytes 262176 | tf_op jit(solution)/shard_map/ppermute | solution.py:348
  57.9 1.6 %pick.1 = (f32[256,256]{1,0:T(8,128)S(1)}, f32[256,256]{1,0:T(8,128)S(1)}, f32[256,256]{1,0:T(8,128)S(1)}, f32[256,256]{1,0:T(8,128)S(1)}) custom-call(s32[2]{0:T(128)S(1)} %pad_add_fusion.1.info, s32[32,1,256]{2,1,0:T(1,128)S(1)} %all_to_all.10.got.got_v, f32[256,256]{1,0:T(8,128)S(1)} %get-tuple-element.28.refs_4_.refs_0_, ...), custom_call_target="tpu_custom_call" | custom-call | tf_op jit(solution)/shard_map/pick/pallas_call | solution.py:26
  59.5 0.1 collective-permute-start.13
  59.6 0.5 collective-permute-start.14
  60.1 1.3 %collective-permute-start.15 = (f32[256,256]{1,0:T(8,128)S(1)}, f32[256,256]{1,0:T(8,128)S(1)}, u32[]{:S(2)}, u32[]{:S(2)}) collective-permute-start(f32[256,256]{1,0:T(8,128)S(1)} %get-tuple-element.37.refs_7_), channel_id=1, source_target_pairs={{0,24},{8,16},{16,8},{24,0},{1,25},{9,17},{17,9},{25,1},{2,26},{10... | collective-permute-start | bytes 786440 | tf_op jit(solution)/shard_map/ppermute | solution.py:348
  61.5 11.8 %score.1 = (f32[2,2048]{1,0:T(2,128)S(1)}, bf16[8,512,256]{2,1,0:T(8,128)(2,1)S(1)}, bf16[8,512,256]{2,1,0:T(8,128)(2,1)S(1)}, f32[8,256,256]{2,1,0:T(8,128)S(1)}) custom-call(s32[2]{0:T(128)S(1)} %pad_add_fusion.1.info, f32[384,256]{1,0:T(8,128)S(1)} %get-tuple-element.29.refs_0_, f32[384,256]{1,0:T(8,128)S(1)} %collective-permute-done.5.refs_1_, ...), custom_call_target="tpu_custom_call" | custom-call | flops 4831838208 | bytes 8388608 | tf_op jit(solution)/shard_map/score/pallas_call | solution.py:26
  73.2 1.9 %positive.1 = (f32[2,2048]{1,0:T(2,128)S(1)}, f32[2,2048]{1,0:T(2,128)S(1)}, f32[8,256,256]{2,1,0:T(8,128)S(1)}) custom-call(s32[2]{0:T(128)S(1)} %pad_add_fusion.1.info, s32[32,1,256]{2,1,0:T(1,128)S(1)} %all_to_all.10.got.got_v, f32[2,2048]{1,0:T(2,128)S(1)} %get-tuple-element.33.stats, f32[384,256]{1,0:T(8,128)S(1)} %get-tuple-element.29.refs_0_, ...), custom_call_target="tpu_custom_call" | custom-call | tf_op jit(solution)/shard_map/positive/pallas_call | solution.py:26
  75.1 1.5 %collective-permute-start.10 = (f32[2,2048]{1,0:T(2,128)S(1)}, f32[2,2048]{1,0:T(2,128)S(1)}, u32[]{:S(2)}, u32[]{:S(2)}) collective-permute-start(f32[2,2048]{1,0:T(2,128)S(1)} %get-tuple-element.38.first), channel_id=1, source_target_pairs={{0,1},{1,0},{2,3},{3,2},{4,5},{5,4},{6,7},{7,6},{8,9},{9,8},{10,11... | collective-permute-start | bytes 49160 | tf_op jit(solution)/shard_map/ppermute | solution.py:348
  76.7 2.3 %collective-permute-done.10.second = f32[2,2048]{1,0:T(2,128)S(1)} collective-permute-done((f32[2,2048]{1,0:T(2,128)S(1)}, f32[2,2048]{1,0:T(2,128)S(1)}, u32[]{:S(2)}, u32[]{:S(2)}) %collective-permute-start.10) | collective-permute-done | bytes 16416 | tf_op jit(solution)/shard_map/ppermute | solution.py:348
  79.0 0.1 collective-permute-start.11
  79.1 3.7 %collective-permute-done.11.second = f32[2,2048]{1,0:T(2,128)S(1)} collective-permute-done((f32[2,2048]{1,0:T(2,128)S(1)}, f32[2,2048]{1,0:T(2,128)S(1)}, u32[]{:S(2)}, u32[]{:S(2)}) %collective-permute-start.11) | collective-permute-done | bytes 16416 | tf_op jit(solution)/shard_map/ppermute | solution.py:348
  82.8 2.1 %collective-permute-start.12 = (f32[2,2048]{1,0:T(2,128)S(1)}, f32[2,2048]{1,0:T(2,128)S(1)}, u32[]{:S(2)}, u32[]{:S(2)}) collective-permute-start(f32[2,2048]{1,0:T(2,128)S(1)} %join.4.first), channel_id=1, source_target_pairs={{0,4},{1,5},{2,6},{3,7},{4,0},{5,1},{6,2},{7,3},{8,12},{9,13},{10,... | collective-permute-start | bytes 49160 | tf_op jit(solution)/shard_map/ppermute | solution.py:348
  84.9 2.6 %collective-permute-done.12.second = f32[2,2048]{1,0:T(2,128)S(1)} collective-permute-done((f32[2,2048]{1,0:T(2,128)S(1)}, f32[2,2048]{1,0:T(2,128)S(1)}, u32[]{:S(2)}, u32[]{:S(2)}) %collective-permute-start.12) | collective-permute-done | bytes 16416 | tf_op jit(solution)/shard_map/ppermute | solution.py:348
  87.5 1.6 %pull.1 = (f32[256,256]{1,0:T(8,128)S(1)}, f32[256,256]{1,0:T(8,128)}, f32[256,256]{1,0:T(8,128)}, f32[256,256]{1,0:T(8,128)}, f32[256,256]{1,0:T(8,128)S(1)}, /...) custom-call(s32[2]{0:T(128)S(1)} %pad_add_fusion.1.info, f32[2,2048]{1,0:T(2,128)S(1)} %join.5.final, ...), custom_call_target="tpu_custom_call" | custom-call | tf_op jit(solution)/shard_map/pull/pallas_call | solution.py:26
  89.2 1.5 %collective-permute-start.18 = (f32[256,256]{1,0:T(8,128)S(1)}, f32[256,256]{1,0:T(8,128)S(1)}, u32[]{:S(2)}, u32[]{:S(2)}) collective-permute-start(f32[256,256]{1,0:T(8,128)S(1)} %get-tuple-element.45), channel_id=1, source_target_pairs={{0,1},{1,0},{2,3},{3,2},{4,5},{5,4},{6,7},{7,6},{8,9},{9,8},{10,11... | collective-permute-start | bytes 786440 | tf_op jit(solution)/shard_map/ppermute | solution.py:348
  90.7 0.5 collective-permute-start.16
  91.2 3.4 %grad.1 = f32[4,136,256]{2,1,0:T(8,128)} custom-call(s32[2]{0:T(128)S(1)} %pad_add_fusion.1.info, s32[32,1,256]{2,1,0:T(1,128)S(1)} %all_to_all.10.got.got_v, f32[2,2048]{1,0:T(2,128)S(1)} %join.5.final, f32[2,2048]{1,0:T(2,128)S(1)} %get-tuple-element.33.stats, f32[2,2048]{1,0:T(2,128)S(1)} %get-tuple-element.39.own, ...), custom_call_target="tpu_custom_call" | custom-call | flops 1610612736 | bytes 8388608 | tf_op jit(solution)/shard_map/grad/pallas_call | solution.py:26
  94.6 3.7 %all-to-all-start.1 = ((f32[4,136,256]{2,1,0:T(8,128)}), f32[4,136,256]{2,1,0:T(8,128)S(1)}, u32[]{:S(2)}, u32[]{:S(2)}) async-start(f32[4,136,256]{2,1,0:T(8,128)} %grad.1), calls=%async_computation.1 | async-start | bytes 1114112 | tf_op jit(solution)/shard_map/all_to_all | solution.py:483
  98.3 1.5 %collective-permute-start.20 = (f32[256,256]{1,0:T(8,128)}, f32[256,256]{1,0:T(8,128)S(1)}, u32[]{:S(2)}, u32[]{:S(2)}) collective-permute-start(f32[256,256]{1,0:T(8,128)} %get-tuple-element.47), channel_id=1, source_target_pairs={{0,1},{1,0},{2,3},{3,2},{4,5},{5,4},{6,7},{7,6},{8,9},{9,8},{10,11... | collective-permute-start | bytes 786440 | tf_op jit(solution)/shard_map/ppermute | solution.py:348
  99.9 1.1 collective-permute-start.21
  100.9 1.0 collective-permute-start.22
  101.9 2.1 %collective-permute-start.19 = (f32[256,256]{1,0:T(8,128)S(1)}, f32[256,256]{1,0:T(8,128)S(1)}, u32[]{:S(2)}, u32[]{:S(2)}) collective-permute-start(f32[256,256]{1,0:T(8,128)S(1)} %add.12), channel_id=1, source_target_pairs={{0,4},{1,5},{2,6},{3,7},{4,0},{5,1},{6,2},{7,3},{8,12},{9,13},{10,... | collective-permute-start | bytes 786440 | tf_op jit(solution)/shard_map/ppermute | solution.py:348
  104.0 1.5 %collective-permute-start.17 = (f32[256,256]{1,0:T(8,128)S(1)}, f32[256,256]{1,0:T(8,128)S(1)}, u32[]{:S(2)}, u32[]{:S(2)}) collective-permute-start(f32[256,256]{1,0:T(8,128)S(1)} %add.11), channel_id=1, source_target_pairs={{0,6},{1,7},{2,4},{3,5},{4,2},{5,3},{6,0},{7,1},{8,14},{9,15},{10,... | collective-permute-start | bytes 786440 | tf_op jit(solution)/shard_map/ppermute | solution.py:348
  105.6 1.5 %collective-permute-done.20.refs_1_ = f32[256,256]{1,0:T(8,128)S(1)} collective-permute-done((f32[256,256]{1,0:T(8,128)}, f32[256,256]{1,0:T(8,128)S(1)}, u32[]{:S(2)}, u32[]{:S(2)}) %collective-permute-start.20) | collective-permute-done | bytes 262176 | tf_op jit(solution)/shard_map/ppermute | solution.py:348
  107.1 0.2 all-to-all-done.1.grads
  107.3 10.8 %scatter.1 = f32[4096,256]{1,0:T(8,128)} custom-call(s32[2]{0:T(128)S(1)} %pad_add_fusion.1.info, s32[32,1,256]{2,1,0:T(1,128)S(1)} %all_to_all.10.got.got_v, s32[32,1,256]{2,1,0:T(1,128)S(1)} %all_to_all.10.got.got_v, f32[4,136,256]{2,1,0:T(8,128)S(1)} %all-to-all-done.1.grads, f32[256,256]{1,0:T(8,128)S(1)} %get-tuple-element.34.refs_4_.refs_0_, ...), custom_call_target="tpu_custom_call" | custom-call | tf_op jit(solution)/shard_map/scatter/pallas_call | solution.py:26
  118.1 1.5 %collective-permute-done.22.refs_4_ = f32[256,256]{1,0:T(8,128)} collective-permute-done((f32[256,256]{1,0:T(8,128)}, f32[256,256]{1,0:T(8,128)}, u32[]{:S(2)}, u32[]{:S(2)}) %collective-permute-start.22) | collective-permute-done | bytes 262176 | tf_op jit(solution)/shard_map/ppermute | solution.py:348
  119.5 7.3 %collective-permute-done.17.refs_0_ = f32[256,256]{1,0:T(8,128)S(1)} collective-permute-done((f32[256,256]{1,0:T(8,128)S(1)}, f32[256,256]{1,0:T(8,128)S(1)}, u32[]{:S(2)}, u32[]{:S(2)}) %collective-permute-start.17) | collective-permute-done | bytes 262176 | tf_op jit(solution)/shard_map/ppermute | solution.py:348
  126.8 1.9 %finish.1 = f32[256,256]{1,0:T(8,128)} custom-call(s32[1,256]{1,0:T(1,128)S(1)} %bitcast.4, f32[256,256]{1,0:T(8,128)S(1)} %collective-permute-done.17.refs_0_, f32[256,256]{1,0:T(8,128)S(1)} %collective-permute-done.19.refs_1_, f32[256,256]{1,0:T(8,128)S(1)} %add.13.refs_2_, f32[256,256]{1,0:T(8,128)S(1)} %collective-permute-done.21.refs_3_, ...), custom_call_target="tpu_custom_call" | custom-call | tf_op jit(solution)/shard_map/finish/pallas_call | solution.py:26
  (25 shorter events, 0.2 us)
Async XLA Ops:
  1.5 1.0 copy-start.1
  3.6 31.4 %collective-permute-start.3 = (f32[256,256]{1,0:T(8,128)S(1)}, f32[256,256]{1,0:T(8,128)S(1)}, u32[]{:S(2)}, u32[]{:S(2)}) collective-permute-start(f32[256,256]{1,0:T(8,128)S(1)} %get-tuple-element.28.refs_4_.refs_0_), channel_id=1, source_target_pairs={{0,4},{1,5},{2,6},{3,7},{4,0},{5,1},{6,2},{7,3},{8,12},{9,13},{10,... | collective-permute-start | bytes 786440 | tf_op jit(solution)/shard_map/ppermute | solution.py:348
  7.7 27.3 %collective-permute-start.4 = (f32[256,256]{1,0:T(8,128)S(1)}, f32[256,256]{1,0:T(8,128)S(1)}, u32[]{:S(2)}, u32[]{:S(2)}) collective-permute-start(f32[256,256]{1,0:T(8,128)S(1)} %get-tuple-element.28.refs_4_.refs_0_), channel_id=1, source_target_pairs={{0,6},{1,7},{2,4},{3,5},{4,2},{5,3},{6,0},{7,1},{8,14},{9,15},{10,... | collective-permute-start | bytes 786440 | tf_op jit(solution)/shard_map/ppermute | solution.py:348
  9.0 25.9 %collective-permute-start = (f32[256,256]{1,0:T(8,128)S(1)}, f32[256,256]{1,0:T(8,128)S(1)}, u32[]{:S(2)}, u32[]{:S(2)}) collective-permute-start(f32[256,256]{1,0:T(8,128)S(1)} %get-tuple-element.28.refs_4_.refs_0_), channel_id=1, source_target_pairs={{0,1},{1,0},{2,3},{3,2},{4,5},{5,4},{6,7},{7,6},{8,9},{9,8},{10,11... | collective-permute-start | bytes 786440 | tf_op jit(solution)/shard_map/ppermute | solution.py:348
  10.5 24.4 %collective-permute-start.1 = (f32[256,256]{1,0:T(8,128)S(1)}, f32[256,256]{1,0:T(8,128)S(1)}, u32[]{:S(2)}, u32[]{:S(2)}) collective-permute-start(f32[256,256]{1,0:T(8,128)S(1)} %get-tuple-element.28.refs_4_.refs_0_), channel_id=1, source_target_pairs={{0,2},{1,3},{2,0},{3,1},{4,6},{5,7},{6,4},{7,5},{8,10},{9,11},{10,... | collective-permute-start | bytes 786440 | tf_op jit(solution)/shard_map/ppermute | solution.py:348
  10.8 24.2 %collective-permute-start.2 = (f32[256,256]{1,0:T(8,128)S(1)}, f32[256,256]{1,0:T(8,128)S(1)}, u32[]{:S(2)}, u32[]{:S(2)}) collective-permute-start(f32[256,256]{1,0:T(8,128)S(1)} %get-tuple-element.28.refs_4_.refs_0_), channel_id=1, source_target_pairs={{0,3},{1,2},{2,1},{3,0},{4,7},{5,6},{6,5},{7,4},{8,11},{9,10},{10,... | collective-permute-start | bytes 786440 | tf_op jit(solution)/shard_map/ppermute | solution.py:348
  35.0 2.2 %copy-start = (f32[4096,256]{1,0:T(8,128)S(1)}, f32[4096,256]{1,0:T(8,128)}, u32[]{:S(2)}) copy-start(f32[4096,256]{1,0:T(8,128)} %table.1) | copy-start | bytes 12582916
  41.7 18.4 %collective-permute-start.5 = (f32[384,256]{1,0:T(8,128)S(1)}, f32[384,256]{1,0:T(8,128)S(1)}, u32[]{:S(2)}, u32[]{:S(2)}) collective-permute-start(f32[384,256]{1,0:T(8,128)S(1)} %get-tuple-element.30), channel_id=1, source_target_pairs={{0,8},{8,0},{16,24},{24,16},{1,9},{9,1},{17,25},{25,17},{2,10},{10... | collective-permute-start | bytes 1179656 | tf_op jit(solution)/shard_map/ppermute | solution.py:348
  41.9 19.6 %collective-permute-start.6 = (f32[384,256]{1,0:T(8,128)S(1)}, f32[384,256]{1,0:T(8,128)S(1)}, u32[]{:S(2)}, u32[]{:S(2)}) collective-permute-start(f32[384,256]{1,0:T(8,128)S(1)} %get-tuple-element.31), channel_id=1, source_target_pairs={{0,16},{8,24},{16,0},{24,8},{1,17},{9,25},{17,1},{25,9},{2,18},{10... | collective-permute-start | bytes 1179656 | tf_op jit(solution)/shard_map/ppermute | solution.py:348
  42.4 19.1 %collective-permute-start.7 = (f32[384,256]{1,0:T(8,128)S(1)}, f32[384,256]{1,0:T(8,128)S(1)}, u32[]{:S(2)}, u32[]{:S(2)}) collective-permute-start(f32[384,256]{1,0:T(8,128)S(1)} %get-tuple-element.32), channel_id=1, source_target_pairs={{0,24},{8,16},{16,8},{24,0},{1,25},{9,17},{17,9},{25,1},{2,26},{10... | collective-permute-start | bytes 1179656 | tf_op jit(solution)/shard_map/ppermute | solution.py:348
  43.6 9.1 %collective-permute-start.8 = (f32[256,256]{1,0:T(8,128)S(1)}, f32[256,256]{1,0:T(8,128)S(1)}, u32[]{:S(2)}, u32[]{:S(2)}) collective-permute-start(f32[256,256]{1,0:T(8,128)S(1)} %collective-permute-done.3.refs_3_.refs_8_.refs_4_), channel_id=1, source_target_pairs={{0,1},{1,0},{2,3},{3,2},{4,5},{5,4},{6,7},{7,6},{8,9},{9,8},{10,11... | collective-permute-start | bytes 786440 | tf_op jit(solution)/shard_map/ppermute | solution.py:348
  45.1 12.8 %collective-permute-start.9 = (f32[256,256]{1,0:T(8,128)S(1)}, f32[256,256]{1,0:T(8,128)S(1)}, u32[]{:S(2)}, u32[]{:S(2)}) collective-permute-start(f32[256,256]{1,0:T(8,128)S(1)} %collective-permute-done.4.refs_4_.refs_10_.refs_6_), channel_id=1, source_target_pairs={{0,1},{1,0},{2,3},{3,2},{4,5},{5,4},{6,7},{7,6},{8,9},{9,8},{10,11... | collective-permute-start | bytes 786440 | tf_op jit(solution)/shard_map/ppermute | solution.py:348
  59.5 28.0 %collective-permute-start.13 = (f32[256,256]{1,0:T(8,128)S(1)}, f32[256,256]{1,0:T(8,128)S(1)}, u32[]{:S(2)}, u32[]{:S(2)}) collective-permute-start(f32[256,256]{1,0:T(8,128)S(1)} %get-tuple-element.35.refs_5_), channel_id=1, source_target_pairs={{0,8},{8,0},{16,24},{24,16},{1,9},{9,1},{17,25},{25,17},{2,10},{10... | collective-permute-start | bytes 786440 | tf_op jit(solution)/shard_map/ppermute | solution.py:348
  59.6 27.9 %collective-permute-start.14 = (f32[256,256]{1,0:T(8,128)S(1)}, f32[256,256]{1,0:T(8,128)S(1)}, u32[]{:S(2)}, u32[]{:S(2)}) collective-permute-start(f32[256,256]{1,0:T(8,128)S(1)} %get-tuple-element.36.refs_6_), channel_id=1, source_target_pairs={{0,16},{8,24},{16,0},{24,8},{1,17},{9,25},{17,1},{25,9},{2,18},{10... | collective-permute-start | bytes 786440 | tf_op jit(solution)/shard_map/ppermute | solution.py:348
  60.1 27.4 %collective-permute-start.15 = (f32[256,256]{1,0:T(8,128)S(1)}, f32[256,256]{1,0:T(8,128)S(1)}, u32[]{:S(2)}, u32[]{:S(2)}) collective-permute-start(f32[256,256]{1,0:T(8,128)S(1)} %get-tuple-element.37.refs_7_), channel_id=1, source_target_pairs={{0,24},{8,16},{16,8},{24,0},{1,25},{9,17},{17,9},{25,1},{2,26},{10... | collective-permute-start | bytes 786440 | tf_op jit(solution)/shard_map/ppermute | solution.py:348
  75.1 3.8 %collective-permute-start.10 = (f32[2,2048]{1,0:T(2,128)S(1)}, f32[2,2048]{1,0:T(2,128)S(1)}, u32[]{:S(2)}, u32[]{:S(2)}) collective-permute-start(f32[2,2048]{1,0:T(2,128)S(1)} %get-tuple-element.38.first), channel_id=1, source_target_pairs={{0,1},{1,0},{2,3},{3,2},{4,5},{5,4},{6,7},{7,6},{8,9},{9,8},{10,11... | collective-permute-start | bytes 49160 | tf_op jit(solution)/shard_map/ppermute | solution.py:348
  79.0 3.8 %collective-permute-start.11 = (f32[2,2048]{1,0:T(2,128)S(1)}, f32[2,2048]{1,0:T(2,128)S(1)}, u32[]{:S(2)}, u32[]{:S(2)}) collective-permute-start(f32[2,2048]{1,0:T(2,128)S(1)} %join.3.first), channel_id=1, source_target_pairs={{0,2},{1,3},{2,0},{3,1},{4,6},{5,7},{6,4},{7,5},{8,10},{9,11},{10,... | collective-permute-start | bytes 49160 | tf_op jit(solution)/shard_map/ppermute | solution.py:348
  82.8 4.7 %collective-permute-start.12 = (f32[2,2048]{1,0:T(2,128)S(1)}, f32[2,2048]{1,0:T(2,128)S(1)}, u32[]{:S(2)}, u32[]{:S(2)}) collective-permute-start(f32[2,2048]{1,0:T(2,128)S(1)} %join.4.first), channel_id=1, source_target_pairs={{0,4},{1,5},{2,6},{3,7},{4,0},{5,1},{6,2},{7,3},{8,12},{9,13},{10,... | collective-permute-start | bytes 49160 | tf_op jit(solution)/shard_map/ppermute | solution.py:348
  89.2 12.7 %collective-permute-start.18 = (f32[256,256]{1,0:T(8,128)S(1)}, f32[256,256]{1,0:T(8,128)S(1)}, u32[]{:S(2)}, u32[]{:S(2)}) collective-permute-start(f32[256,256]{1,0:T(8,128)S(1)} %get-tuple-element.45), channel_id=1, source_target_pairs={{0,1},{1,0},{2,3},{3,2},{4,5},{5,4},{6,7},{7,6},{8,9},{9,8},{10,11... | collective-permute-start | bytes 786440 | tf_op jit(solution)/shard_map/ppermute | solution.py:348
  90.7 13.3 %collective-permute-start.16 = (f32[256,256]{1,0:T(8,128)}, f32[256,256]{1,0:T(8,128)S(1)}, u32[]{:S(2)}, u32[]{:S(2)}) collective-permute-start(f32[256,256]{1,0:T(8,128)} %get-tuple-element.43), channel_id=1, source_target_pairs={{0,1},{1,0},{2,3},{3,2},{4,5},{5,4},{6,7},{7,6},{8,9},{9,8},{10,11... | collective-permute-start | bytes 786440 | tf_op jit(solution)/shard_map/ppermute | solution.py:348
  94.6 12.6 %all-to-all-start.1 = ((f32[4,136,256]{2,1,0:T(8,128)}), f32[4,136,256]{2,1,0:T(8,128)S(1)}, u32[]{:S(2)}, u32[]{:S(2)}) async-start(f32[4,136,256]{2,1,0:T(8,128)} %grad.1), calls=%async_computation.1 | async-start | bytes 1114112 | tf_op jit(solution)/shard_map/all_to_all | solution.py:483
  98.3 8.7 %collective-permute-start.20 = (f32[256,256]{1,0:T(8,128)}, f32[256,256]{1,0:T(8,128)S(1)}, u32[]{:S(2)}, u32[]{:S(2)}) collective-permute-start(f32[256,256]{1,0:T(8,128)} %get-tuple-element.47), channel_id=1, source_target_pairs={{0,1},{1,0},{2,3},{3,2},{4,5},{5,4},{6,7},{7,6},{8,9},{9,8},{10,11... | collective-permute-start | bytes 786440 | tf_op jit(solution)/shard_map/ppermute | solution.py:348
  99.9 18.2 %collective-permute-start.21 = (f32[256,256]{1,0:T(8,128)}, f32[256,256]{1,0:T(8,128)S(1)}, u32[]{:S(2)}, u32[]{:S(2)}) collective-permute-start(f32[256,256]{1,0:T(8,128)} %get-tuple-element.48), channel_id=1, source_target_pairs={{0,2},{1,3},{2,0},{3,1},{4,6},{5,7},{6,4},{7,5},{8,10},{9,11},{10,... | collective-permute-start | bytes 786440 | tf_op jit(solution)/shard_map/ppermute | solution.py:348
  100.9 18.6 %collective-permute-start.22 = (f32[256,256]{1,0:T(8,128)}, f32[256,256]{1,0:T(8,128)}, u32[]{:S(2)}, u32[]{:S(2)}) collective-permute-start(f32[256,256]{1,0:T(8,128)} %get-tuple-element.49), channel_id=1, source_target_pairs={{0,3},{1,2},{2,1},{3,0},{4,7},{5,6},{6,5},{7,4},{8,11},{9,10},{10,... | collective-permute-start | bytes 786440 | tf_op jit(solution)/shard_map/ppermute | solution.py:348
  101.9 17.6 %collective-permute-start.19 = (f32[256,256]{1,0:T(8,128)S(1)}, f32[256,256]{1,0:T(8,128)S(1)}, u32[]{:S(2)}, u32[]{:S(2)}) collective-permute-start(f32[256,256]{1,0:T(8,128)S(1)} %add.12), channel_id=1, source_target_pairs={{0,4},{1,5},{2,6},{3,7},{4,0},{5,1},{6,2},{7,3},{8,12},{9,13},{10,... | collective-permute-start | bytes 786440 | tf_op jit(solution)/shard_map/ppermute | solution.py:348
  104.0 22.8 %collective-permute-start.17 = (f32[256,256]{1,0:T(8,128)S(1)}, f32[256,256]{1,0:T(8,128)S(1)}, u32[]{:S(2)}, u32[]{:S(2)}) collective-permute-start(f32[256,256]{1,0:T(8,128)S(1)} %add.11), channel_id=1, source_target_pairs={{0,6},{1,7},{2,4},{3,5},{4,2},{5,3},{6,0},{7,1},{8,14},{9,15},{10,... | collective-permute-start | bytes 786440 | tf_op jit(solution)/shard_map/ppermute | solution.py:348
  107.0 19.8 %copy-start.2 = (s32[256]{0:T(256)S(1)}, s32[256]{0:T(256)}, u32[]{:S(2)}) copy-start(s32[256]{0:T(256)} %param.11) | copy-start | bytes 3076

commit v3 on v2

--- a/solution.py
+++ b/solution.py
@@ -122,38 +122,36 @@
     out_ref[:, 0, LANES:] = position.astype(I32)
 
 
-def gather_kernel(members, groups, slots, count, info, got, table, *refs):
+def gather_kernel(members, groups, part, count, info, got, table, *refs):
     for d, out in enumerate(refs[-groups:]):
         first = (info[0] ^ d) * members
 
         def member(mr, carry, out=out, first=first):
             asked = got.at[first + mr, 0]
-            copy_rows(table, lambda k: asked[slots + k], out, mr * count, count)
-            copy_rows(table, lambda k: asked[k], out, members * count + mr * slots, slots)
+            copy_rows(table, lambda k: asked[part + k], out, mr * count, count)
             return carry
 
         lax.fori_loop(0, members, member, 0)
 
 
-def score_kernel(members, groups, negatives, info, *refs):
+def score_kernel(blocks, groups, info, *refs):
     rows, refs = refs[:groups], refs[groups:]
-    encs = refs[:members]
-    stats, prob_hi, prob_lo, pulled = refs[members:]
+    encs, refs = refs[: len(blocks)], refs[len(blocks) :]
+    stats, prob_hi, prob_lo = refs[-3:]
+    if len(refs) > 3:
+        stats[...] = refs[0][...]
     tokens = encs[0].shape[0]
-    neg = jnp.concatenate([row[0 : negatives // groups, :] for row in rows], axis=0)
-    neg3 = split3(neg)
-    neg_t = split(jnp.transpose(neg))
-    for e in range(members):
+    neg = split3(jnp.concatenate([row[...] for row in rows], axis=0))
+    for i, e in enumerate(blocks):
         lanes = pl.ds(pl.multiple_of((info[1] ^ e) * tokens, LANES), tokens)
-        score = dot6(neg3, split3(encs[e][...]), NT)
+        score = dot6(neg, split3(encs[i][...]), NT)
         top = jnp.max(score, axis=0, keepdims=True)
         prob = jnp.exp(score - top)
         stats[0:1, lanes] = top
         stats[1:2, lanes] = jnp.sum(prob, axis=0, keepdims=True)
         parts = split(prob)
-        prob_hi[e] = parts[0]
-        prob_lo[e] = parts[1]
-        pulled[e] = dot3(neg_t, parts, NN)
+        prob_hi[i] = parts[0]
+        prob_lo[i] = parts[1]
 
 
 def own_places(members, info, got):
@@ -187,22 +185,18 @@
 
 def positive_kernel(members, groups, slots, tokens, info, got, stats, *refs):
     rows, picked = refs[:groups], refs[groups : 2 * groups]
-    joined, own, row_t, place_rows, column = refs[2 * groups :]
+    joined, own, place_rows, column = refs[2 * groups :]
     place_rows[...] = own_places(members, info, got)
-    first = rows[0].shape[0] - members * slots
     for e in range(members):
         mr = info[1] ^ e
         lanes = pl.ds(pl.multiple_of(mr * tokens, LANES), tokens)
         at = pl.ds(pl.multiple_of(mr * slots, slots), slots)
-        after = pl.ds(pl.multiple_of(first + mr * slots, slots), slots)
         hot = slot_hot(members, groups, slots, info, place_rows, column, mr, tokens)
-        row = jnp.concatenate([r[after, :] for r in rows], axis=0)
+        row = jnp.concatenate([r[at, :] for r in rows], axis=0)
         enc = jnp.concatenate([p[at, :] for p in picked], axis=0)
         value = jnp.sum(row * enc, axis=1, keepdims=True)
         positive = jnp.sum(jnp.where(hot, value, 0.0), axis=0, keepdims=True)
         has = jnp.sum(hot.astype(F32), axis=0, keepdims=True)
-        high, low = split(row)
-        row_t[e] = dot1(high, as_bf16(hot), TN) + dot1(low, as_bf16(hot), TN)
         old = stats[0:1, lanes]
         top = jnp.where(has > 0, jnp.maximum(old, positive), old)
         joined[0:1, lanes] = top
@@ -213,6 +207,24 @@
         own[1:2, lanes] = has
 
 
+def pulled_kernel(members, groups, slots, halves, info, got, *refs):
+    negs, refs = refs[:groups], refs[groups:]
+    rows, refs = refs[:groups], refs[groups:]
+    probs, (pulled, row_t, place_rows, column) = refs[:-4], refs[-4:]
+    place_rows[...] = own_places(members, info, got)
+    neg = jnp.concatenate([row[...] for row in negs], axis=0)
+    neg_t = split(jnp.transpose(neg))
+    tokens = pulled.shape[2]
+    for h, blocks in enumerate(halves):
+        for i, e in enumerate(blocks):
+            mr = info[1] ^ e
+            pulled[e] = dot3(neg_t, (probs[2 * h][i], probs[2 * h + 1][i]), NN)
+            at = pl.ds(pl.multiple_of(mr * slots, slots), slots)
+            hot = slot_hot(members, groups, slots, info, place_rows, column, mr, tokens)
+            high, low = split(jnp.concatenate([r[at, :] for r in rows], axis=0))
+            row_t[e] = dot1(high, as_bf16(hot), TN) + dot1(low, as_bf16(hot), TN)
+
+
 def join(first, second):
     top = jnp.maximum(first[0:1], second[0:1])
     total = first[1:2] * jnp.exp(first[0:1] - top) + second[1:2] * jnp.exp(second[0:1] - top)
@@ -248,17 +260,18 @@
     )
 
 
-def grad_kernel(members, groups, slots, info, got, final, stats, own, prob_hi, prob_lo, *refs):
+def grad_kernel(members, groups, slots, halves, info, got, final, stats, own, *refs):
+    probs, refs = refs[: 2 * len(halves)], refs[2 * len(halves) :]
     encs = refs[:members]
     out, total, coef, place_rows = refs[members:]
     place_rows[...] = own_places(members, info, got)
     tokens, width = encs[0].shape
-    for e in range(members):
+    for h, i, e in [(h, i, e) for h, blocks in enumerate(halves) for i, e in enumerate(blocks)]:
         mr = info[1] ^ e
         scale, extra = shares(info, e, tokens, final, stats, own)
         enc = split(encs[e][...] * row_to_col(scale))
-        part = dot3((prob_hi[e], prob_lo[e]), enc, NN)
-        if e == 0:
+        part = dot3((probs[2 * h][i], probs[2 * h + 1][i]), enc, NN)
+        if h == 0 and i == 0:
             total[...] = part
         else:
             total[...] += part
@@ -376,24 +389,44 @@
     )
 
     encs = [masked] + [None] * (members - 1)
-    direct = [d for d in range(1, members) if d < 2 * near or d % near == 0]
-    for d in direct:
-        encs[d] = swap(masked, "member", d)
-    for d in range(1, members):
-        if d not in direct:
-            encs[d] = swap(encs[d // near * near], "member", d % near)
-
-    early = [encs[d] for d in direct]
-    rows = call(
-        functools.partial(gather_kernel, members, groups, slots, count),
-        [sds(members * (count + slots), width)] * groups,
-        [SMEM, SMEM, VMEM] + [ANY] * len(early),
+    for z in range(near, members, near):
+        known = 2 * near if z == 3 * near else 0
+        encs[z] = swap(encs[known], "member", z ^ known)
+    for z in range(0, members, near):
+        for x in range(1, near):
+            encs[z ^ x] = swap(encs[z], "member", x)
+    halves = [[d for d in range(members) if (d < near) or d in (near, 2 * near)], []]
+    halves[1] = [d for d in range(members) if d not in halves[0]]
+
+    early = [encs[d] for d in halves[0] if d]
+    gather = lambda part, many, deps, name: call(
+        functools.partial(gather_kernel, members, groups, part, many),
+        [sds(members * many, width)] * groups,
+        [SMEM, SMEM, VMEM] + [ANY] * len(deps),
         [VMEM] * groups,
-        (info, got, item_table, *early),
-        name="gather",
-    )
+        (info, got, item_table, *deps),
+        name=name,
+    )
+    negs = gather(slots, count, early, "gather_negatives")
+    negs = [negs[0]] + [swap(negs[d], "group", d) for d in range(1, groups)]
+    rows = gather(0, slots, [], "gather_targets")
     rows = [rows[0]] + [swap(rows[d], "group", d) for d in range(1, groups)]
 
+    stats, probs = [], []
+    for blocks in halves:
+        many = len(blocks)
+        *stats, hi, lo = call(
+            functools.partial(score_kernel, blocks, groups),
+            [sds(2, everyone)] + [shape((many, negatives, tokens), BF16)] * 2,
+            [SMEM] + [VMEM] * (groups + many + len(stats)),
+            [VMEM] * 3,
+            (info, *negs, *[encs[e] for e in blocks], *stats),
+            flops=12 * many * tokens * negatives * width,
+            moved=MIB,
+            name="score",
+        )
+        probs += [hi, lo]
+    stats = stats[0]
     picked = call(
         functools.partial(pick_kernel, members, groups, slots),
         [sds(members * slots, width)] * groups,
@@ -404,29 +437,25 @@
         name="pick",
     )
     sent = [picked[0]] + [swap(picked[d], "group", d) for d in range(1, groups)]
-    stats, prob_hi, prob_lo, pulled = call(
-        functools.partial(score_kernel, members, groups, negatives),
-        [
-            sds(2, everyone),
-            shape((members, negatives, tokens), BF16),
-            shape((members, negatives, tokens), BF16),
-            sds(members, width, tokens),
-        ],
-        [SMEM] + [VMEM] * (groups + members),
-        [VMEM] * 4,
-        (info, *rows, *encs),
-        flops=18 * everyone * negatives * width,
-        moved=8 * MIB,
-        name="score",
-    )
-    joined, own, row_t = call(
+    joined, own = call(
         functools.partial(positive_kernel, members, groups, slots, tokens),
-        [sds(2, everyone), sds(2, everyone), sds(members, width, tokens)],
+        [sds(2, everyone)] * 2,
         [SMEM] + [VMEM] * (2 + 2 * groups),
-        [VMEM] * 3,
+        [VMEM] * 2,
         (info, got, stats, *rows, *picked),
         scratch=[pltpu.VMEM((members, LANES), I32), pltpu.VMEM((LANES, 1), I32)],
         name="positive",
+    )
+    pulled, row_t = call(
+        functools.partial(pulled_kernel, members, groups, slots, halves),
+        [sds(members, width, tokens)] * 2,
+        [SMEM] + [VMEM] * (1 + 2 * groups + len(probs)),
+        [VMEM] * 2,
+        (info, got, *negs, *rows, *probs),
+        scratch=[pltpu.VMEM((members, LANES), I32), pltpu.VMEM((LANES, 1), I32)],
+        flops=6 * everyone * negatives * width,
+        moved=MIB,
+        name="pulled",
     )
 
     final = joined
@@ -451,26 +480,27 @@
         (info, final, stats, own, pulled, row_t),
         name="pull",
     )
-    parts = []
-    for z in [*range(members - near, near, -near), 0]:
+    def added(*terms):
+        if len(terms) == 1:
+            return terms[0]
+        return call(
+            add_kernel, sds(width, tokens), [VMEM] * len(terms), VMEM, terms, name="add"
+        )
+
+    sums = {}
+    for z in [*range(members - near, 0, -near), 0]:
         arrived = [swap(pulls[z ^ x], "member", x) for x in range(1, near)]
-        total = call(
-            add_kernel,
-            sds(width, tokens),
-            [VMEM] * near,
-            VMEM,
-            (pulls[z], *arrived),
-            name="add",
-        )
-        parts.append(swap(total, "member", z) if z else total)
-    parts += [swap(pulls[d], "member", d) for d in range(near, 2 * near)]
+        if z == 2 * near and 3 * near in sums:
+            arrived.append(swap(sums.pop(3 * near), "member", near))
+        sums[z] = added(pulls[z], *arrived)
+    parts = [swap(total, "member", z) if z else total for z, total in sums.items()]
 
     grads = call(
-        functools.partial(grad_kernel, members, groups, slots),
+        functools.partial(grad_kernel, members, groups, slots, halves),
         sds(groups, members * count + 8, width),
-        [SMEM] + [VMEM] * (6 + members),
+        [SMEM] + [VMEM] * (4 + len(probs) + members),
         VMEM,
-        (info, got, final, stats, own, prob_hi, prob_lo, *encs),
+        (info, got, final, stats, own, *probs, *encs),
         scratch=[
             pltpu.VMEM((negatives, width), F32),
             pltpu.VMEM((members, LANES), F32),

time: 129 us -> 115 us (0.89)
  blocking collectives: 22.4 us -> 0 us
  starting transfers between devices: 31.4 us -> 35.9 us
  waiting for transfers between devices: 31.3 us -> 34.3 us
    all_to_all x1 -> x0, blocking collectives: 22.4 us -> none  [shards(): lax.all_to_all(request, ('group', 'member'), split_axis=0, concat_axis=0,...]
    all_to_all x0 -> x1, starting transfers between devices: none -> 5.63 us  [shards(): lax.all_to_all(request, ('group', 'member'), split_axis=0, concat_axis=0,...]
    all_to_all x0 -> x1, waiting for transfers between devices: none -> 5.36 us  [shards(): lax.all_to_all(request, ('group', 'member'), split_axis=0, concat_axis=0,...]
    ppermute x23 -> x26, waiting for transfers between devices: 31.1 us -> 28.7 us  [swap(): lax.ppermute(value, axis, [(i, i ^ d) for i in range(lax.axis_size(axis))])]
    ppermute x23 -> x26, starting transfers between devices: 27.7 us -> 26.7 us  [swap(): lax.ppermute(value, axis, [(i, i ^ d) for i in range(lax.axis_size(axis))])]
    unnamed x6 -> x12, local copies, waits for them, and re-layouts: 3.14 us -> 4.1 us
    pallas_call x15 -> x19, Pallas kernels: 38.8 us -> 39 us  [call(): pl.pallas_call(kernel, out_shape=out_shape, in_specs=ins, out_specs=outs,...]
  transfers between devices with their start and end apart: 24 -> 28, of which waited for: 9 -> 11; matrix products, arithmetic and copies ran while one was open for 0% -> 0% of each run, Pallas kernels for 23% -> 30%
where the time goes in v3:
time: 115 us
  Pallas kernels  39 us (34%)
  starting transfers between devices  35.9 us (31%)
  waiting for transfers between devices  34.3 us (30%)
  local copies, waits for them, and re-layouts  4.1 us (4%)
    pallas_call x19, Pallas kernels, call(): pl.pallas_call(kernel, out_shape=out_shape, in_specs=ins, out_specs=outs,...  39 us
    ppermute x26, waiting for transfers between devices, swap(): lax.ppermute(value, axis, [(i, i ^ d) for i in range(lax.axis_size(axis))])  28.7 us
    ppermute x26, starting transfers between devices, swap(): lax.ppermute(value, axis, [(i, i ^ d) for i in range(lax.axis_size(axis))])  26.7 us
    all_to_all x1, starting transfers between devices, shards(): lax.all_to_all(request, ('group', 'member'), split_axis=0, concat_axis=0,...  5.63 us
    all_to_all x1, waiting for transfers between devices, shards(): lax.all_to_all(request, ('group', 'member'), split_axis=0, concat_axis=0,...  5.36 us
    unnamed x12, local copies, waits for them, and re-layouts  4.1 us
    all_to_all x1, starting transfers between devices, shards(): lax.all_to_all(grads, 'group', split_axis=0, concat_axis=0, tiled=True)  3.65 us
  transfers between devices with their start and end apart: 28, of which 11 were waited for; matrix products, arithmetic and copies ran while one was open for 0% of the time, Pallas kernels for 30%

profile of v3, /device:TPU:0, one launch (start us, length us, event | category | flops | bytes accessed | tf_op | source)
XLA Modules:
  0.0 115.0 jit_solution(11213450100193377555)
XLA Ops:
  0.6 0.7 pad_add_fusion
  1.5 0.9 copy-done.1
  2.4 1.8 %front.1 = (s32[32,1,256]{2,1,0:T(1,128)}, f32[256,256]{1,0:T(8,128)S(1)}) custom-call(s32[2]{0:T(128)S(1)} %pad_add_fusion.1.info, s32[1,1280]{1,0:T(1,128)S(1)} %reshape.15.ints, f32[256,256]{1,0:T(8,128)S(1)} %copy-done.1), custom_call_target="tpu_custom_call" | custom-call | tf_op jit(solution)/shard_map/front/pallas_call | solution.py:26
  4.2 4.0 %collective-permute-start.2 = (f32[256,256]{1,0:T(8,128)S(1)}, f32[256,256]{1,0:T(8,128)S(1)}, u32[]{:S(2)}, u32[]{:S(2)}) collective-permute-start(f32[256,256]{1,0:T(8,128)S(1)} %get-tuple-element.35.refs_4_.refs_0_), channel_id=1, source_target_pairs={{0,4},{1,5},{2,6},{3,7},{4,0},{5,1},{6,2},{7,3},{8,12},{9,13},{10,... | collective-permute-start | bytes 786440 | tf_op jit(solution)/shard_map/ppermute | solution.py:361
  8.2 1.6 %collective-permute-start.1 = (f32[256,256]{1,0:T(8,128)S(1)}, f32[256,256]{1,0:T(8,128)S(1)}, u32[]{:S(2)}, u32[]{:S(2)}) collective-permute-start(f32[256,256]{1,0:T(8,128)S(1)} %get-tuple-element.35.refs_4_.refs_0_), channel_id=1, source_target_pairs={{0,2},{1,3},{2,0},{3,1},{4,6},{5,7},{6,4},{7,5},{8,10},{9,11},{10,... | collective-permute-start | bytes 786440 | tf_op jit(solution)/shard_map/ppermute | solution.py:361
  9.8 1.5 %collective-permute-start = (f32[256,256]{1,0:T(8,128)S(1)}, f32[256,256]{1,0:T(8,128)S(1)}, u32[]{:S(2)}, u32[]{:S(2)}) collective-permute-start(f32[256,256]{1,0:T(8,128)S(1)} %get-tuple-element.35.refs_4_.refs_0_), channel_id=1, source_target_pairs={{0,1},{1,0},{2,3},{3,2},{4,5},{5,4},{6,7},{7,6},{8,9},{9,8},{10,11... | collective-permute-start | bytes 786440 | tf_op jit(solution)/shard_map/ppermute | solution.py:361
  11.3 9.0 %collective-permute-done.2.refs_2_.refs_7_.refs_4_.refs_8_ = f32[256,256]{1,0:T(8,128)S(1)} collective-permute-done((f32[256,256]{1,0:T(8,128)S(1)}, f32[256,256]{1,0:T(8,128)S(1)}, u32[]{:S(2)}, u32[]{:S(2)}) %collective-permute-start.2) | collective-permute-done | bytes 262176 | tf_op jit(solution)/shard_map/ppermute | solution.py:361
  20.9 5.6 %all-to-all-start = ((s32[32,1,256]{2,1,0:T(1,128)}), s32[32,1,256]{2,1,0:T(1,128)S(1)}, u32[]{:S(2)}, u32[]{:S(2)}) async-start(s32[32,1,256]{2,1,0:T(1,128)} %get-tuple-element.34), calls=%async_computation | async-start | bytes 65536 | tf_op jit(solution)/shard_map/all_to_all | solution.py:387
  26.5 1.8 %collective-permute-start.7 = (f32[256,256]{1,0:T(8,128)S(1)}, f32[256,256]{1,0:T(8,128)S(1)}, u32[]{:S(2)}, u32[]{:S(2)}) collective-permute-start(f32[256,256]{1,0:T(8,128)S(1)} %collective-permute-done.2.refs_2_.refs_7_.refs_4_.refs_8_), channel_id=1, source_target_pairs={{0,1},{1,0},{2,3},{3,2},{4,5},{5,4},{6,7},{7,6},{8,9},{9,8},{10,11... | collective-permute-start | bytes 786440 | tf_op jit(solution)/shard_map/ppermute | solution.py:361
  28.3 5.4 %all-to-all-done.got.got_v = s32[32,1,256]{2,1,0:T(1,128)S(1)} async-done(((s32[32,1,256]{2,1,0:T(1,128)}), s32[32,1,256]{2,1,0:T(1,128)S(1)}, u32[]{:S(2)}, u32[]{:S(2)}) %all-to-all-start) | async-done | bytes 32800 | tf_op jit(solution)/shard_map/all_to_all | solution.py:387
  33.7 2.2 %copy-done = f32[4096,256]{1,0:T(8,128)S(1)} copy-done((f32[4096,256]{1,0:T(8,128)S(1)}, f32[4096,256]{1,0:T(8,128)}, u32[]{:S(2)}) %copy-start) | copy-done | bytes 4194328
  35.9 2.3 %gather_negatives.1 = (f32[128,256]{1,0:T(8,128)S(1)}, f32[128,256]{1,0:T(8,128)S(1)}, f32[128,256]{1,0:T(8,128)S(1)}, f32[128,256]{1,0:T(8,128)S(1)}) custom-call(s32[2]{0:T(128)S(1)} %pad_add_fusion.1.info, s32[32,1,256]{2,1,0:T(1,128)S(1)} %all-to-all-done.got.got_v, f32[4096,256]{1,0:T(8,128)S(1)} %copy-done, ...), custom_call_target="tpu_custom_call" | custom-call | tf_op jit(solution)/shard_map/gather_negatives/pallas_call | solution.py:26
  39.0 1.2 %collective-permute-start.5 = (f32[128,256]{1,0:T(8,128)S(1)}, f32[128,256]{1,0:T(8,128)S(1)}, u32[]{:S(2)}, u32[]{:S(2)}) collective-permute-start(f32[128,256]{1,0:T(8,128)S(1)} %get-tuple-element.39), channel_id=1, source_target_pairs={{0,24},{8,16},{16,8},{24,0},{1,25},{9,17},{17,9},{25,1},{2,26},{10... | collective-permute-start | bytes 393224 | tf_op jit(solution)/shard_map/ppermute | solution.py:361
  40.2 0.6 collective-permute-start.6
  40.8 1.4 %collective-permute-start.9 = (f32[256,256]{1,0:T(8,128)S(1)}, f32[256,256]{1,0:T(8,128)S(1)}, u32[]{:S(2)}, u32[]{:S(2)}) collective-permute-start(f32[256,256]{1,0:T(8,128)S(1)} %collective-permute-done.8.refs_6_.refs_10_), channel_id=1, source_target_pairs={{0,1},{1,0},{2,3},{3,2},{4,5},{5,4},{6,7},{7,6},{8,9},{9,8},{10,11... | collective-permute-start | bytes 786440 | tf_op jit(solution)/shard_map/ppermute | solution.py:361
  42.2 3.3 %gather_targets.1 = (f32[256,256]{1,0:T(8,128)S(1)}, f32[256,256]{1,0:T(8,128)S(1)}, f32[256,256]{1,0:T(8,128)S(1)}, f32[256,256]{1,0:T(8,128)S(1)}) custom-call(s32[2]{0:T(128)S(1)} %pad_add_fusion.1.info, s32[32,1,256]{2,1,0:T(1,128)S(1)} %all-to-all-done.got.got_v, f32[4096,256]{1,0:T(8,128)S(1)} %copy-done), custom_call_target="tpu_custom_call" | custom-call | tf_op jit(solution)/shard_map/gather_targets/pallas_call | solution.py:26
  45.6 1.0 collective-permute-done.5.refs_3_
  47.2 1.3 %collective-permute-start.12 = (f32[256,256]{1,0:T(8,128)S(1)}, f32[256,256]{1,0:T(8,128)S(1)}, u32[]{:S(2)}, u32[]{:S(2)}) collective-permute-start(f32[256,256]{1,0:T(8,128)S(1)} %get-tuple-element.45), channel_id=1, source_target_pairs={{0,24},{8,16},{16,8},{24,0},{1,25},{9,17},{17,9},{25,1},{2,26},{10... | collective-permute-start | bytes 786440 | tf_op jit(solution)/shard_map/ppermute | solution.py:361
  48.5 3.1 %score.2 = (f32[2,2048]{1,0:T(2,128)S(1)}, bf16[4,512,256]{2,1,0:T(8,128)(2,1)S(1)}, bf16[4,512,256]{2,1,0:T(8,128)(2,1)S(1)}) custom-call(s32[2]{0:T(128)S(1)} %pad_add_fusion.1.info, f32[128,256]{1,0:T(8,128)S(1)} %get-tuple-element.36.refs_0_, f32[128,256]{1,0:T(8,128)S(1)} %collective-permute-done.3.refs_1_, ...), custom_call_target="tpu_custom_call" | custom-call | flops 1610612736 | bytes 1048576 | tf_op jit(solution)/shard_map/score/pallas_call | solution.py:26
  51.6 2.8 %collective-permute-done.9.refs_7_.refs_11_ = f32[256,256]{1,0:T(8,128)S(1)} collective-permute-done((f32[256,256]{1,0:T(8,128)S(1)}, f32[256,256]{1,0:T(8,128)S(1)}, u32[]{:S(2)}, u32[]{:S(2)}) %collective-permute-start.9) | collective-permute-done | bytes 262176 | tf_op jit(solution)/shard_map/ppermute | solution.py:361
  54.4 1.6 %pick.1 = (f32[256,256]{1,0:T(8,128)S(1)}, f32[256,256]{1,0:T(8,128)S(1)}, f32[256,256]{1,0:T(8,128)S(1)}, f32[256,256]{1,0:T(8,128)S(1)}) custom-call(s32[2]{0:T(128)S(1)} %pad_add_fusion.1.info, s32[32,1,256]{2,1,0:T(1,128)S(1)} %all-to-all-done.got.got_v, f32[256,256]{1,0:T(8,128)S(1)} %get-tuple-element.35.refs_4_.refs_0_, ...), custom_call_target="tpu_custom_call" | custom-call | tf_op jit(solution)/shard_map/pick/pallas_call | solution.py:26
  56.1 0.7 collective-permute-start.17
  56.7 1.2 %collective-permute-start.18 = (f32[256,256]{1,0:T(8,128)S(1)}, f32[256,256]{1,0:T(8,128)S(1)}, u32[]{:S(2)}, u32[]{:S(2)}) collective-permute-start(f32[256,256]{1,0:T(8,128)S(1)} %get-tuple-element.49.refs_7_), channel_id=1, source_target_pairs={{0,24},{8,16},{16,8},{24,0},{1,25},{9,17},{17,9},{25,1},{2,26},{10... | collective-permute-start | bytes 786440 | tf_op jit(solution)/shard_map/ppermute | solution.py:361
  57.9 3.1 %score.3 = (f32[2,2048]{1,0:T(2,128)S(1)}, bf16[4,512,256]{2,1,0:T(8,128)(2,1)S(1)}, bf16[4,512,256]{2,1,0:T(8,128)(2,1)S(1)}) custom-call(s32[2]{0:T(128)S(1)} %pad_add_fusion.1.info, f32[128,256]{1,0:T(8,128)S(1)} %get-tuple-element.36.refs_0_, f32[128,256]{1,0:T(8,128)S(1)} %collective-permute-done.3.refs_1_, ...), custom_call_target="tpu_custom_call" | custom-call | flops 1610612736 | bytes 1048576 | tf_op jit(solution)/shard_map/score/pallas_call | solution.py:26
  61.0 1.2 %positive.1 = (f32[2,2048]{1,0:T(2,128)S(1)}, f32[2,2048]{1,0:T(2,128)S(1)}) custom-call(s32[2]{0:T(128)S(1)} %pad_add_fusion.1.info, s32[32,1,256]{2,1,0:T(1,128)S(1)} %all-to-all-done.got.got_v, f32[2,2048]{1,0:T(2,128)S(1)} %get-tuple-element.41.stats, f32[256,256]{1,0:T(8,128)S(1)} %get-tuple-element.42.refs_0_.refs_4_, ...), custom_call_target="tpu_custom_call" | custom-call | tf_op jit(solution)/shard_map/positive/pallas_call | solution.py:26
  62.2 0.8 collective-permute-start.13
  63.0 3.0 %collective-permute-done.13.second = f32[2,2048]{1,0:T(2,128)S(1)} collective-permute-done((f32[2,2048]{1,0:T(2,128)S(1)}, f32[2,2048]{1,0:T(2,128)S(1)}, u32[]{:S(2)}, u32[]{:S(2)}) %collective-permute-start.13) | collective-permute-done | bytes 16416 | tf_op jit(solution)/shard_map/ppermute | solution.py:361
  66.6 3.2 %collective-permute-done.14.second = f32[2,2048]{1,0:T(2,128)S(1)} collective-permute-done((f32[2,2048]{1,0:T(2,128)S(1)}, f32[2,2048]{1,0:T(2,128)S(1)}, u32[]{:S(2)}, u32[]{:S(2)}) %collective-permute-start.14) | collective-permute-done | bytes 16416 | tf_op jit(solution)/shard_map/ppermute | solution.py:361
  69.9 0.8 collective-permute-start.15
  70.7 3.1 %pulled.1 = (f32[8,256,256]{2,1,0:T(8,128)S(1)}, f32[8,256,256]{2,1,0:T(8,128)S(1)}) custom-call(s32[2]{0:T(128)S(1)} %pad_add_fusion.1.info, s32[32,1,256]{2,1,0:T(1,128)S(1)} %all-to-all-done.got.got_v, f32[128,256]{1,0:T(8,128)S(1)} %get-tuple-element.36.refs_0_, f32[128,256]{1,0:T(8,128)S(1)} %collective-permute-done.3.refs_1_, ...), custom_call_target="tpu_custom_call" | custom-call | flops 1610612736 | bytes 1048576 | tf_op jit(solution)/shard_map/pulled/pallas_call | solution.py:26
  73.8 0.9 collective-permute-done.15.second
  74.7 1.5 %pull.1 = (f32[256,256]{1,0:T(8,128)S(1)}, f32[256,256]{1,0:T(8,128)S(1)}, f32[256,256]{1,0:T(8,128)S(1)}, f32[256,256]{1,0:T(8,128)}, f32[256,256]{1,0:T(8,128)...) custom-call(s32[2]{0:T(128)S(1)} %pad_add_fusion.1.info, f32[2,2048]{1,0:T(2,128)S(1)} %join.5.final, ...), custom_call_target="tpu_custom_call" | custom-call | tf_op jit(solution)/shard_map/pull/pallas_call | solution.py:26
  76.3 0.7 collective-permute-start.20
  77.0 1.3 %collective-permute-start.19 = (f32[256,256]{1,0:T(8,128)}, f32[256,256]{1,0:T(8,128)}, u32[]{:S(2)}, u32[]{:S(2)}) collective-permute-start(f32[256,256]{1,0:T(8,128)} %get-tuple-element.59), channel_id=1, source_target_pairs={{0,1},{1,0},{2,3},{3,2},{4,5},{5,4},{6,7},{7,6},{8,9},{9,8},{10,11... | collective-permute-start | bytes 786440 | tf_op jit(solution)/shard_map/ppermute | solution.py:361
  78.3 0.7 collective-permute-start.23
  79.1 6.5 %collective-permute-done.20.refs_1_ = f32[256,256]{1,0:T(8,128)S(1)} collective-permute-done((f32[256,256]{1,0:T(8,128)S(1)}, f32[256,256]{1,0:T(8,128)S(1)}, u32[]{:S(2)}, u32[]{:S(2)}) %collective-permute-start.20) | collective-permute-done | bytes 262176 | tf_op jit(solution)/shard_map/ppermute | solution.py:361
  86.0 3.4 %grad.1 = f32[4,136,256]{2,1,0:T(8,128)} custom-call(s32[2]{0:T(128)S(1)} %pad_add_fusion.1.info, s32[32,1,256]{2,1,0:T(1,128)S(1)} %all-to-all-done.got.got_v, f32[2,2048]{1,0:T(2,128)S(1)} %join.5.final, f32[2,2048]{1,0:T(2,128)S(1)} %get-tuple-element.41.stats, f32[2,2048]{1,0:T(2,128)S(1)} %get-tuple-element.51.own, ...), custom_call_target="tpu_custom_call" | custom-call | flops 1610612736 | bytes 8388608 | tf_op jit(solution)/shard_map/grad/pallas_call | solution.py:26
  89.5 3.7 %all-to-all-start.1 = ((f32[4,136,256]{2,1,0:T(8,128)}), f32[4,136,256]{2,1,0:T(8,128)S(1)}, u32[]{:S(2)}, u32[]{:S(2)}) async-start(f32[4,136,256]{2,1,0:T(8,128)} %grad.1), calls=%async_computation.1 | async-start | bytes 1114112 | tf_op jit(solution)/shard_map/all_to_all | solution.py:513
  93.1 0.8 collective-permute-start.25
  94.0 1.0 add.14
  95.0 1.7 %collective-permute-start.24 = (f32[256,256]{1,0:T(8,128)S(1)}, f32[256,256]{1,0:T(8,128)S(1)}, u32[]{:S(2)}, u32[]{:S(2)}) collective-permute-start(f32[256,256]{1,0:T(8,128)S(1)} %add.14), channel_id=1, source_target_pairs={{0,2},{1,3},{2,0},{3,1},{4,6},{5,7},{6,4},{7,5},{8,10},{9,11},{10,... | collective-permute-start | bytes 786440 | tf_op jit(solution)/shard_map/ppermute | solution.py:361
  96.7 0.9 copy-done.3
  97.6 1.8 %add.13 = f32[256,256]{1,0:T(8,128)} custom-call(f32[256,256]{1,0:T(8,128)S(1)} %copy-done.3, f32[256,256]{1,0:T(8,128)} %collective-permute-done.19.refs_1_, f32[256,256]{1,0:T(8,128)} %collective-permute-done.21.refs_2_), custom_call_target="tpu_custom_call" | custom-call | tf_op jit(solution)/shard_map/add/pallas_call | solution.py:26
  99.4 1.3 %collective-permute-start.22 = (f32[256,256]{1,0:T(8,128)}, f32[256,256]{1,0:T(8,128)S(1)}, u32[]{:S(2)}, u32[]{:S(2)}) collective-permute-start(f32[256,256]{1,0:T(8,128)} %add.13), channel_id=1, source_target_pairs={{0,4},{1,5},{2,6},{3,7},{4,0},{5,1},{6,2},{7,3},{8,12},{9,13},{10,... | collective-permute-start | bytes 786440 | tf_op jit(solution)/shard_map/ppermute | solution.py:361
  100.7 1.2 %collective-permute-done.25.refs_1_ = f32[256,256]{1,0:T(8,128)S(1)} collective-permute-done((f32[256,256]{1,0:T(8,128)}, f32[256,256]{1,0:T(8,128)S(1)}, u32[]{:S(2)}, u32[]{:S(2)}) %collective-permute-start.25) | collective-permute-done | bytes 262176 | tf_op jit(solution)/shard_map/ppermute | solution.py:361
  102.1 10.8 %scatter.1 = f32[4096,256]{1,0:T(8,128)} custom-call(s32[2]{0:T(128)S(1)} %pad_add_fusion.1.info, s32[32,1,256]{2,1,0:T(1,128)S(1)} %all-to-all-done.got.got_v, s32[32,1,256]{2,1,0:T(1,128)S(1)} %all-to-all-done.got.got_v, f32[4,136,256]{2,1,0:T(8,128)S(1)} %all-to-all-done.1.grads, f32[256,256]{1,0:T(8,128)S(1)} %get-tuple-element.46.refs_4_.refs_0_, ...), custom_call_target="tpu_custom_call" | custom-call | tf_op jit(solution)/shard_map/scatter/pallas_call | solution.py:26
  112.9 1.1 collective-permute-done.22.refs_0_
  114.0 1.0 finish.1
  (42 shorter events, 3.7 us)
Async XLA Ops:
  1.5 1.0 copy-start.1
  4.2 16.1 %collective-permute-start.2 = (f32[256,256]{1,0:T(8,128)S(1)}, f32[256,256]{1,0:T(8,128)S(1)}, u32[]{:S(2)}, u32[]{:S(2)}) collective-permute-start(f32[256,256]{1,0:T(8,128)S(1)} %get-tuple-element.35.refs_4_.refs_0_), channel_id=1, source_target_pairs={{0,4},{1,5},{2,6},{3,7},{4,0},{5,1},{6,2},{7,3},{8,12},{9,13},{10,... | collective-permute-start | bytes 786440 | tf_op jit(solution)/shard_map/ppermute | solution.py:361
  8.2 25.5 %collective-permute-start.1 = (f32[256,256]{1,0:T(8,128)S(1)}, f32[256,256]{1,0:T(8,128)S(1)}, u32[]{:S(2)}, u32[]{:S(2)}) collective-permute-start(f32[256,256]{1,0:T(8,128)S(1)} %get-tuple-element.35.refs_4_.refs_0_), channel_id=1, source_target_pairs={{0,2},{1,3},{2,0},{3,1},{4,6},{5,7},{6,4},{7,5},{8,10},{9,11},{10,... | collective-permute-start | bytes 786440 | tf_op jit(solution)/shard_map/ppermute | solution.py:361
  9.8 23.9 %collective-permute-start = (f32[256,256]{1,0:T(8,128)S(1)}, f32[256,256]{1,0:T(8,128)S(1)}, u32[]{:S(2)}, u32[]{:S(2)}) collective-permute-start(f32[256,256]{1,0:T(8,128)S(1)} %get-tuple-element.35.refs_4_.refs_0_), channel_id=1, source_target_pairs={{0,1},{1,0},{2,3},{3,2},{4,5},{5,4},{6,7},{7,6},{8,9},{9,8},{10,11... | collective-permute-start | bytes 786440 | tf_op jit(solution)/shard_map/ppermute | solution.py:361
  20.3 20.6 %collective-permute-start.8 = (f32[256,256]{1,0:T(8,128)S(1)}, f32[256,256]{1,0:T(8,128)S(1)}, u32[]{:S(2)}, u32[]{:S(2)}) collective-permute-start(f32[256,256]{1,0:T(8,128)S(1)} %collective-permute-done.2.refs_2_.refs_7_.refs_4_.refs_8_), channel_id=1, source_target_pairs={{0,2},{1,3},{2,0},{3,1},{4,6},{5,7},{6,4},{7,5},{8,10},{9,11},{10,... | collective-permute-start | bytes 786440 | tf_op jit(solution)/shard_map/ppermute | solution.py:361
  20.9 12.8 %all-to-all-start = ((s32[32,1,256]{2,1,0:T(1,128)}), s32[32,1,256]{2,1,0:T(1,128)S(1)}, u32[]{:S(2)}, u32[]{:S(2)}) async-start(s32[32,1,256]{2,1,0:T(1,128)} %get-tuple-element.34), calls=%async_computation | async-start | bytes 65536 | tf_op jit(solution)/shard_map/all_to_all | solution.py:387
  26.5 20.7 %collective-permute-start.7 = (f32[256,256]{1,0:T(8,128)S(1)}, f32[256,256]{1,0:T(8,128)S(1)}, u32[]{:S(2)}, u32[]{:S(2)}) collective-permute-start(f32[256,256]{1,0:T(8,128)S(1)} %collective-permute-done.2.refs_2_.refs_7_.refs_4_.refs_8_), channel_id=1, source_target_pairs={{0,1},{1,0},{2,3},{3,2},{4,5},{5,4},{6,7},{7,6},{8,9},{9,8},{10,11... | collective-permute-start | bytes 786440 | tf_op jit(solution)/shard_map/ppermute | solution.py:361
  33.7 2.2 %copy-start = (f32[4096,256]{1,0:T(8,128)S(1)}, f32[4096,256]{1,0:T(8,128)}, u32[]{:S(2)}) copy-start(f32[4096,256]{1,0:T(8,128)} %table.3) | copy-start | bytes 12582916
  38.2 2.0 %collective-permute-start.3 = (f32[128,256]{1,0:T(8,128)S(1)}, f32[128,256]{1,0:T(8,128)S(1)}, u32[]{:S(2)}, u32[]{:S(2)}) collective-permute-start(f32[128,256]{1,0:T(8,128)S(1)} %get-tuple-element.37), channel_id=1, source_target_pairs={{0,8},{8,0},{16,24},{24,16},{1,9},{9,1},{17,25},{25,17},{2,10},{10... | collective-permute-start | bytes 393224 | tf_op jit(solution)/shard_map/ppermute | solution.py:361
  38.4 7.1 %collective-permute-start.4 = (f32[128,256]{1,0:T(8,128)S(1)}, f32[128,256]{1,0:T(8,128)S(1)}, u32[]{:S(2)}, u32[]{:S(2)}) collective-permute-start(f32[128,256]{1,0:T(8,128)S(1)} %get-tuple-element.38), channel_id=1, source_target_pairs={{0,16},{8,24},{16,0},{24,8},{1,17},{9,25},{17,1},{25,9},{2,18},{10... | collective-permute-start | bytes 393224 | tf_op jit(solution)/shard_map/ppermute | solution.py:361
  39.0 7.6 %collective-permute-start.5 = (f32[128,256]{1,0:T(8,128)S(1)}, f32[128,256]{1,0:T(8,128)S(1)}, u32[]{:S(2)}, u32[]{:S(2)}) collective-permute-start(f32[128,256]{1,0:T(8,128)S(1)} %get-tuple-element.39), channel_id=1, source_target_pairs={{0,24},{8,16},{16,8},{24,0},{1,25},{9,17},{17,9},{25,1},{2,26},{10... | collective-permute-start | bytes 393224 | tf_op jit(solution)/shard_map/ppermute | solution.py:361
  40.2 11.4 %collective-permute-start.6 = (f32[256,256]{1,0:T(8,128)S(1)}, f32[256,256]{1,0:T(8,128)S(1)}, u32[]{:S(2)}, u32[]{:S(2)}) collective-permute-start(f32[256,256]{1,0:T(8,128)S(1)} %collective-permute-done.1.refs_1_.refs_6_.refs_2_), channel_id=1, source_target_pairs={{0,1},{1,0},{2,3},{3,2},{4,5},{5,4},{6,7},{7,6},{8,9},{9,8},{10,11... | collective-permute-start | bytes 786440 | tf_op jit(solution)/shard_map/ppermute | solution.py:361
  40.8 13.5 %collective-permute-start.9 = (f32[256,256]{1,0:T(8,128)S(1)}, f32[256,256]{1,0:T(8,128)S(1)}, u32[]{:S(2)}, u32[]{:S(2)}) collective-permute-start(f32[256,256]{1,0:T(8,128)S(1)} %collective-permute-done.8.refs_6_.refs_10_), channel_id=1, source_target_pairs={{0,1},{1,0},{2,3},{3,2},{4,5},{5,4},{6,7},{7,6},{8,9},{9,8},{10,11... | collective-permute-start | bytes 786440 | tf_op jit(solution)/shard_map/ppermute | solution.py:361
  45.5 11.2 %collective-permute-start.10 = (f32[256,256]{1,0:T(8,128)S(1)}, f32[256,256]{1,0:T(8,128)S(1)}, u32[]{:S(2)}, u32[]{:S(2)}) collective-permute-start(f32[256,256]{1,0:T(8,128)S(1)} %get-tuple-element.43), channel_id=1, source_target_pairs={{0,8},{8,0},{16,24},{24,16},{1,9},{9,1},{17,25},{25,17},{2,10},{10... | collective-permute-start | bytes 786440 | tf_op jit(solution)/shard_map/ppermute | solution.py:361
  46.6 14.5 %collective-permute-start.11 = (f32[256,256]{1,0:T(8,128)S(1)}, f32[256,256]{1,0:T(8,128)S(1)}, u32[]{:S(2)}, u32[]{:S(2)}) collective-permute-start(f32[256,256]{1,0:T(8,128)S(1)} %get-tuple-element.44), channel_id=1, source_target_pairs={{0,16},{8,24},{16,0},{24,8},{1,17},{9,25},{17,1},{25,9},{2,18},{10... | collective-permute-start | bytes 786440 | tf_op jit(solution)/shard_map/ppermute | solution.py:361
  47.2 13.8 %collective-permute-start.12 = (f32[256,256]{1,0:T(8,128)S(1)}, f32[256,256]{1,0:T(8,128)S(1)}, u32[]{:S(2)}, u32[]{:S(2)}) collective-permute-start(f32[256,256]{1,0:T(8,128)S(1)} %get-tuple-element.45), channel_id=1, source_target_pairs={{0,24},{8,16},{16,8},{24,0},{1,25},{9,17},{17,9},{25,1},{2,26},{10... | collective-permute-start | bytes 786440 | tf_op jit(solution)/shard_map/ppermute | solution.py:361
  56.0 18.7 %collective-permute-start.16 = (f32[256,256]{1,0:T(8,128)S(1)}, f32[256,256]{1,0:T(8,128)S(1)}, u32[]{:S(2)}, u32[]{:S(2)}) collective-permute-start(f32[256,256]{1,0:T(8,128)S(1)} %get-tuple-element.47.refs_5_), channel_id=1, source_target_pairs={{0,8},{8,0},{16,24},{24,16},{1,9},{9,1},{17,25},{25,17},{2,10},{10... | collective-permute-start | bytes 786440 | tf_op jit(solution)/shard_map/ppermute | solution.py:361
  56.1 18.6 %collective-permute-start.17 = (f32[256,256]{1,0:T(8,128)S(1)}, f32[256,256]{1,0:T(8,128)S(1)}, u32[]{:S(2)}, u32[]{:S(2)}) collective-permute-start(f32[256,256]{1,0:T(8,128)S(1)} %get-tuple-element.48.refs_6_), channel_id=1, source_target_pairs={{0,16},{8,24},{16,0},{24,8},{1,17},{9,25},{17,1},{25,9},{2,18},{10... | collective-permute-start | bytes 786440 | tf_op jit(solution)/shard_map/ppermute | solution.py:361
  56.7 18.0 %collective-permute-start.18 = (f32[256,256]{1,0:T(8,128)S(1)}, f32[256,256]{1,0:T(8,128)S(1)}, u32[]{:S(2)}, u32[]{:S(2)}) collective-permute-start(f32[256,256]{1,0:T(8,128)S(1)} %get-tuple-element.49.refs_7_), channel_id=1, source_target_pairs={{0,24},{8,16},{16,8},{24,0},{1,25},{9,17},{17,9},{25,1},{2,26},{10... | collective-permute-start | bytes 786440 | tf_op jit(solution)/shard_map/ppermute | solution.py:361
  62.2 3.8 %collective-permute-start.13 = (f32[2,2048]{1,0:T(2,128)S(1)}, f32[2,2048]{1,0:T(2,128)S(1)}, u32[]{:S(2)}, u32[]{:S(2)}) collective-permute-start(f32[2,2048]{1,0:T(2,128)S(1)} %get-tuple-element.50.first), channel_id=1, source_target_pairs={{0,1},{1,0},{2,3},{3,2},{4,5},{5,4},{6,7},{7,6},{8,9},{9,8},{10,11... | collective-permute-start | bytes 49160 | tf_op jit(solution)/shard_map/ppermute | solution.py:361
  66.1 3.8 %collective-permute-start.14 = (f32[2,2048]{1,0:T(2,128)S(1)}, f32[2,2048]{1,0:T(2,128)S(1)}, u32[]{:S(2)}, u32[]{:S(2)}) collective-permute-start(f32[2,2048]{1,0:T(2,128)S(1)} %join.3.first), channel_id=1, source_target_pairs={{0,2},{1,3},{2,0},{3,1},{4,6},{5,7},{6,4},{7,5},{8,10},{9,11},{10,... | collective-permute-start | bytes 49160 | tf_op jit(solution)/shard_map/ppermute | solution.py:361
  69.9 4.8 %collective-permute-start.15 = (f32[2,2048]{1,0:T(2,128)S(1)}, f32[2,2048]{1,0:T(2,128)S(1)}, u32[]{:S(2)}, u32[]{:S(2)}) collective-permute-start(f32[2,2048]{1,0:T(2,128)S(1)} %join.4.first), channel_id=1, source_target_pairs={{0,4},{1,5},{2,6},{3,7},{4,0},{5,1},{6,2},{7,3},{8,12},{9,13},{10,... | collective-permute-start | bytes 49160 | tf_op jit(solution)/shard_map/ppermute | solution.py:361
  76.3 9.3 %copy-start.5 = (f32[256,256]{1,0:T(8,128)}, f32[256,256]{1,0:T(8,128)S(1)}, u32[]{:S(2)}) copy-start(f32[256,256]{1,0:T(8,128)S(1)} %get-tuple-element.65) | copy-start | bytes 786436
  76.3 9.8 %copy-start.2 = (f32[256,256]{1,0:T(8,128)}, f32[256,256]{1,0:T(8,128)S(1)}, u32[]{:S(2)}) copy-start(f32[256,256]{1,0:T(8,128)S(1)} %get-tuple-element.58.refs_0_) | copy-start | bytes 786436
  76.3 9.2 %collective-permute-start.20 = (f32[256,256]{1,0:T(8,128)S(1)}, f32[256,256]{1,0:T(8,128)S(1)}, u32[]{:S(2)}, u32[]{:S(2)}) collective-permute-start(f32[256,256]{1,0:T(8,128)S(1)} %get-tuple-element.61), channel_id=1, source_target_pairs={{0,1},{1,0},{2,3},{3,2},{4,5},{5,4},{6,7},{7,6},{8,9},{9,8},{10,11... | collective-permute-start | bytes 786440 | tf_op jit(solution)/shard_map/ppermute | solution.py:361
  77.0 19.6 %collective-permute-start.19 = (f32[256,256]{1,0:T(8,128)}, f32[256,256]{1,0:T(8,128)}, u32[]{:S(2)}, u32[]{:S(2)}) collective-permute-start(f32[256,256]{1,0:T(8,128)} %get-tuple-element.59), channel_id=1, source_target_pairs={{0,1},{1,0},{2,3},{3,2},{4,5},{5,4},{6,7},{7,6},{8,9},{9,8},{10,11... | collective-permute-start | bytes 786440 | tf_op jit(solution)/shard_map/ppermute | solution.py:361
  78.3 15.7 %collective-permute-start.23 = (f32[256,256]{1,0:T(8,128)}, f32[256,256]{1,0:T(8,128)}, u32[]{:S(2)}, u32[]{:S(2)}) collective-permute-start(f32[256,256]{1,0:T(8,128)} %get-tuple-element.63), channel_id=1, source_target_pairs={{0,1},{1,0},{2,3},{3,2},{4,5},{5,4},{6,7},{7,6},{8,9},{9,8},{10,11... | collective-permute-start | bytes 786440 | tf_op jit(solution)/shard_map/ppermute | solution.py:361
  85.6 11.1 %collective-permute-start.21 = (f32[256,256]{1,0:T(8,128)S(1)}, f32[256,256]{1,0:T(8,128)}, u32[]{:S(2)}, u32[]{:S(2)}) collective-permute-start(f32[256,256]{1,0:T(8,128)S(1)} %add.12), channel_id=1, source_target_pairs={{0,2},{1,3},{2,0},{3,1},{4,6},{5,7},{6,4},{7,5},{8,10},{9,11},{10,... | collective-permute-start | bytes 786440 | tf_op jit(solution)/shard_map/ppermute | solution.py:361
  89.5 12.6 %all-to-all-start.1 = ((f32[4,136,256]{2,1,0:T(8,128)}), f32[4,136,256]{2,1,0:T(8,128)S(1)}, u32[]{:S(2)}, u32[]{:S(2)}) async-start(f32[4,136,256]{2,1,0:T(8,128)} %grad.1), calls=%async_computation.1 | async-start | bytes 1114112 | tf_op jit(solution)/shard_map/all_to_all | solution.py:513
  93.1 8.7 %collective-permute-start.25 = (f32[256,256]{1,0:T(8,128)}, f32[256,256]{1,0:T(8,128)S(1)}, u32[]{:S(2)}, u32[]{:S(2)}) collective-permute-start(f32[256,256]{1,0:T(8,128)} %copy-done.5), channel_id=1, source_target_pairs={{0,1},{1,0},{2,3},{3,2},{4,5},{5,4},{6,7},{7,6},{8,9},{9,8},{10,11... | collective-permute-start | bytes 786440 | tf_op jit(solution)/shard_map/ppermute | solution.py:361
  94.0 20.1 %copy-start.4 = (s32[256]{0:T(256)S(1)}, s32[256]{0:T(256)}, u32[]{:S(2)}) copy-start(s32[256]{0:T(256)} %param.11) | copy-start | bytes 3076
  95.0 17.9 %collective-permute-start.24 = (f32[256,256]{1,0:T(8,128)S(1)}, f32[256,256]{1,0:T(8,128)S(1)}, u32[]{:S(2)}, u32[]{:S(2)}) collective-permute-start(f32[256,256]{1,0:T(8,128)S(1)} %add.14), channel_id=1, source_target_pairs={{0,2},{1,3},{2,0},{3,1},{4,6},{5,7},{6,4},{7,5},{8,10},{9,11},{10,... | collective-permute-start | bytes 786440 | tf_op jit(solution)/shard_map/ppermute | solution.py:361
  96.7 1.0 copy-start.3
  99.4 14.6 %collective-permute-start.22 = (f32[256,256]{1,0:T(8,128)}, f32[256,256]{1,0:T(8,128)S(1)}, u32[]{:S(2)}, u32[]{:S(2)}) collective-permute-start(f32[256,256]{1,0:T(8,128)} %add.13), channel_id=1, source_target_pairs={{0,4},{1,5},{2,6},{3,7},{4,0},{5,1},{6,2},{7,3},{8,12},{9,13},{10,... | collective-permute-start | bytes 786440 | tf_op jit(solution)/shard_map/ppermute | solution.py:361

commit v4 on v3

--- a/solution.py
+++ b/solution.py
@@ -248,10 +248,10 @@
     return scale, extra
 
 
-def pull_kernel(members, tokens, info, final, stats, own, pulled, row_t, *outs):
-    for e in range(members):
+def pull_kernel(blocks, tokens, info, final, stats, own, pulled, row_t, *refs):
+    for e, out in zip(blocks, refs[-len(blocks) :]):
         scale, extra = shares(info, e, tokens, final, stats, own)
-        outs[e][...] = pulled[e] * scale + row_t[e] * extra
+        out[...] = pulled[e] * scale + row_t[e] * extra
 
 
 def flat(table, lane, slots):
@@ -263,7 +263,8 @@
 def grad_kernel(members, groups, slots, halves, info, got, final, stats, own, *refs):
     probs, refs = refs[: 2 * len(halves)], refs[2 * len(halves) :]
     encs = refs[:members]
-    out, total, coef, place_rows = refs[members:]
+    outs = refs[members : members + groups]
+    total, coef, place_rows = refs[members + groups :]
     place_rows[...] = own_places(members, info, got)
     tokens, width = encs[0].shape
     for h, i, e in [(h, i, e) for h, blocks in enumerate(halves) for i, e in enumerate(blocks)]:
@@ -280,10 +281,13 @@
             jnp.where(hot, row_to_col(extra), 0.0), axis=0, keepdims=True
         )
     count = total.shape[0] // groups
-    for g in range(groups):
-        out[info[0] ^ g, 0:count, :] = total[g * count : (g + 1) * count, :]
-        line = flat(coef[...], g * slots, slots)
-        out[g, count:, 0 : line.shape[1]] = jnp.broadcast_to(line, (8, line.shape[1]))
+    lines = [flat(coef[...], g * slots, slots) for g in range(groups)]
+    for d, out in enumerate(outs):
+        out[0:count, :] = total[d * count : (d + 1) * count, :]
+        line = lines[0]
+        for g in range(1, groups):
+            line = jnp.where((info[0] ^ d) == g, lines[g], line)
+        out[count:, 0 : line.shape[1]] = jnp.broadcast_to(line, (8, line.shape[1]))
 
 
 def equal_in_batch(ids):
@@ -295,9 +299,9 @@
     return same.astype(F32)
 
 
-def scatter_kernel(members, groups, slots, count, info, got_v, got, grads, *refs):
-    picked = refs[:groups]
-    out, negs, tgts = refs[groups:]
+def scatter_kernel(members, groups, slots, count, info, got_v, got, *refs):
+    grads, picked = refs[:groups], refs[groups : 2 * groups]
+    out, negs, tgts = refs[2 * groups :]
     out[...] = jnp.zeros_like(out)
 
     def add_rows(asked, first, source, base, number):
@@ -315,9 +319,10 @@
         asked = got_v[pl.ds(g * members, members), 0, 0:LANES]
         number = members * count
         same = as_bf16(equal_in_batch(flat(asked, slots, count)) > 0)
-        high, low = split(grads[g, 0:number, :])
+        high, low = split(grads[d][0:number, :])
         negs[...] = dot1(same, high, NN) + dot1(same, low, NN)
-        weight = equal_in_batch(flat(asked, 0, slots)) * grads[g, number : number + 1, 0 : members * slots]
+        weight = equal_in_batch(flat(asked, 0, slots))
+        weight = weight * grads[d][number : number + 1, 0 : members * slots]
         tgts[...] = dot3(split(weight), split(picked[d][...]), NN)
         merged = BATCH // count if count < BATCH else 1
 
@@ -343,9 +348,9 @@
         lax.fori_loop(0, members // merged, member, 0)
 
 
-def add_kernel(*refs):
+def add_kernel(terms, *refs):
     total = refs[0][...]
-    for ref in refs[1:-1]:
+    for ref in refs[1:terms]:
         total = total + ref[...]
     refs[-1][...] = total
 
@@ -389,12 +394,13 @@
     )
 
     encs = [masked] + [None] * (members - 1)
-    for z in range(near, members, near):
-        known = 2 * near if z == 3 * near else 0
-        encs[z] = swap(encs[known], "member", z ^ known)
+    for z in (near, 2 * near):
+        encs[z] = swap(masked, "member", z)
+    onward, got = lax.optimization_barrier((encs[2 * near], got))
+    encs[3 * near] = swap(onward, "member", near)
     for z in range(0, members, near):
         for x in range(1, near):
-            encs[z ^ x] = swap(encs[z], "member", x)
+            encs[z ^ x] = swap(onward if z == 2 * near else encs[z], "member", x)
     halves = [[d for d in range(members) if (d < near) or d in (near, 2 * near)], []]
     halves[1] = [d for d in range(members) if d not in halves[0]]
 
@@ -472,34 +478,11 @@
         )
         d *= 2
 
-    pulls = call(
-        functools.partial(pull_kernel, members, tokens),
-        [sds(width, tokens)] * members,
-        [SMEM] + [VMEM] * 5,
-        [VMEM] * members,
-        (info, final, stats, own, pulled, row_t),
-        name="pull",
-    )
-    def added(*terms):
-        if len(terms) == 1:
-            return terms[0]
-        return call(
-            add_kernel, sds(width, tokens), [VMEM] * len(terms), VMEM, terms, name="add"
-        )
-
-    sums = {}
-    for z in [*range(members - near, 0, -near), 0]:
-        arrived = [swap(pulls[z ^ x], "member", x) for x in range(1, near)]
-        if z == 2 * near and 3 * near in sums:
-            arrived.append(swap(sums.pop(3 * near), "member", near))
-        sums[z] = added(pulls[z], *arrived)
-    parts = [swap(total, "member", z) if z else total for z, total in sums.items()]
-
     grads = call(
         functools.partial(grad_kernel, members, groups, slots, halves),
-        sds(groups, members * count + 8, width),
+        [sds(members * count + 8, width)] * groups,
         [SMEM] + [VMEM] * (4 + len(probs) + members),
-        VMEM,
+        [VMEM] * groups,
         (info, got, final, stats, own, *probs, *encs),
         scratch=[
             pltpu.VMEM((negatives, width), F32),
@@ -510,13 +493,47 @@
         moved=8 * MIB,
         name="grad",
     )
-    grads = lax.all_to_all(grads, "group", split_axis=0, concat_axis=0, tiled=True)
+    def added(terms, deps):
+        return call(
+            functools.partial(add_kernel, len(terms)),
+            sds(width, tokens),
+            [VMEM] * len(terms) + [ANY] * len(deps),
+            VMEM,
+            (*terms, *deps),
+            name="add",
+        )
+
+    graded = [grads[0]]
+    grads = graded + [swap(grads[d], "group", d) for d in range(1, groups)]
+    def scaled(first, many, deps):
+        blocks = list(range(first, first + many))
+        return call(
+            functools.partial(pull_kernel, blocks, tokens),
+            [sds(width, tokens)] * many,
+            [SMEM] + [VMEM] * 5 + [ANY] * len(deps),
+            [VMEM] * many,
+            (info, final, stats, own, pulled, row_t, *deps),
+            name="pull",
+        )
+
+    def beside(blocks):
+        return [swap(blocks[x], "member", x) for x in range(1, near)]
+
+    farthest = scaled(3 * near, near, [])
+    arrived = beside(farthest)
+    far = scaled(2 * near, near, arrived)
+    total = added([farthest[0], *arrived], graded)
+    total = added([far[0], *beside(far), swap(total, "member", near)], grads[1:])
+    close = scaled(0, 2 * near, [total])
+    parts = [swap(total, "member", 2 * near), close[0]]
+    parts += [swap(close[d], "member", d) for d in range(1, 2 * near)]
+
     table_grad = call(
         functools.partial(scatter_kernel, members, groups, slots, count),
         sds(rows_dev, width),
-        [SMEM, VMEM, SMEM, VMEM] + [VMEM] * groups,
+        [SMEM, VMEM, SMEM] + [VMEM] * (2 * groups),
         VMEM,
-        (info, got, got, grads, *sent),
+        (info, got, got, *grads, *sent),
         scratch=[
             pltpu.VMEM((members * count, width), F32),
             pltpu.VMEM((members * slots, width), F32),

time: 115 us -> 108 us (0.939)
  blocking collectives: 0 us -> 12.2 us
  waiting for transfers between devices: 34.3 us -> 23.3 us
  starting transfers between devices: 35.9 us -> 32 us
  Pallas kernels: 39 us -> 35.2 us
    all_to_all x0 -> x1, blocking collectives: none -> 12.2 us  [shards(): lax.all_to_all(request, ('group', 'member'), split_axis=0, concat_axis=0,...]
    all_to_all x2 -> x0, starting transfers between devices: 9.28 us -> none  [the longest x1 5.63 us: shards(): lax.all_to_all(request, ('group', 'member'), split_axis=0, concat_axis=0,...]
    all_to_all x2 -> x0, waiting for transfers between devices: 5.59 us -> none  [the longest x1 5.36 us: shards(): lax.all_to_all(request, ('group', 'member'), split_axis=0, concat_axis=0,...]
    ppermute x26 -> x29, starting transfers between devices: 26.7 us -> 32 us  [swap(): lax.ppermute(value, axis, [(i, i ^ d) for i in range(lax.axis_size(axis))])]
    ppermute x26 -> x29, waiting for transfers between devices: 28.7 us -> 23.3 us  [swap(): lax.ppermute(value, axis, [(i, i ^ d) for i in range(lax.axis_size(axis))])]
    pallas_call x19, Pallas kernels: 39 us -> 35.2 us  [call(): pl.pallas_call(kernel, out_shape=out_shape, in_specs=ins, out_specs=outs,...]
    unnamed x12 -> x6, local copies, waits for them, and re-layouts: 4.1 us -> 3.14 us
  transfers between devices with their start and end apart: 28 -> 29, of which waited for: 11 -> 8; matrix products, arithmetic and copies ran while one was open for 0% -> 0% of each run, Pallas kernels for 30% -> 29%
where the time goes in v4:
time: 108 us
  Pallas kernels  35.2 us (33%)
  starting transfers between devices  32 us (30%)
  waiting for transfers between devices  23.3 us (22%)
  blocking collectives  12.2 us (11%)
  local copies, waits for them, and re-layouts  3.15 us (3%)
    pallas_call x19, Pallas kernels, call(): pl.pallas_call(kernel, out_shape=out_shape, in_specs=ins, out_specs=outs,...  35.2 us
    ppermute x29, starting transfers between devices, swap(): lax.ppermute(value, axis, [(i, i ^ d) for i in range(lax.axis_size(axis))])  32 us
    ppermute x29, waiting for transfers between devices, swap(): lax.ppermute(value, axis, [(i, i ^ d) for i in range(lax.axis_size(axis))])  23.3 us
    all_to_all x1, blocking collectives, shards(): lax.all_to_all(request, ('group', 'member'), split_axis=0, concat_axis=0,...  12.2 us
    unnamed x6, local copies, waits for them, and re-layouts  3.14 us
  transfers between devices with their start and end apart: 29, of which 8 were waited for; matrix products, arithmetic and copies ran while one was open for 0% of the time, Pallas kernels for 29%

profile of v4, /device:TPU:0, one launch (start us, length us, event | category | flops | bytes accessed | tf_op | source)
XLA Modules:
  0.0 107.5 jit_solution(12486862921613119583)
XLA Ops:
  0.6 0.7 pad_add_fusion
  1.5 0.9 copy-done.1
  2.4 1.2 %front.1 = (s32[32,1,256]{2,1,0:T(1,128)S(1)}, f32[256,256]{1,0:T(8,128)S(1)}) custom-call(s32[2]{0:T(128)S(1)} %pad_add_fusion.1.info, s32[1,1280]{1,0:T(1,128)S(1)} %reshape.15.ints, f32[256,256]{1,0:T(8,128)S(1)} %copy-done.1), custom_call_target="tpu_custom_call" | custom-call | tf_op jit(solution)/shard_map/front/pallas_call | solution.py:26
  3.6 4.1 %collective-permute-start = (f32[256,256]{1,0:T(8,128)S(1)}, f32[256,256]{1,0:T(8,128)S(1)}, u32[]{:S(2)}, u32[]{:S(2)}) collective-permute-start(f32[256,256]{1,0:T(8,128)S(1)} %get-tuple-element.40.refs_4_.refs_0_), channel_id=1, source_target_pairs={{0,4},{1,5},{2,6},{3,7},{4,0},{5,1},{6,2},{7,3},{8,12},{9,13},{10,... | collective-permute-start | bytes 786440 | tf_op jit(solution)/shard_map/ppermute | solution.py:366
  7.7 1.6 %collective-permute-start.2 = (f32[256,256]{1,0:T(8,128)S(1)}, f32[256,256]{1,0:T(8,128)S(1)}, u32[]{:S(2)}, u32[]{:S(2)}) collective-permute-start(f32[256,256]{1,0:T(8,128)S(1)} %get-tuple-element.40.refs_4_.refs_0_), channel_id=1, source_target_pairs={{0,2},{1,3},{2,0},{3,1},{4,6},{5,7},{6,4},{7,5},{8,10},{9,11},{10,... | collective-permute-start | bytes 786440 | tf_op jit(solution)/shard_map/ppermute | solution.py:366
  9.3 1.5 %collective-permute-start.1 = (f32[256,256]{1,0:T(8,128)S(1)}, f32[256,256]{1,0:T(8,128)S(1)}, u32[]{:S(2)}, u32[]{:S(2)}) collective-permute-start(f32[256,256]{1,0:T(8,128)S(1)} %get-tuple-element.40.refs_4_.refs_0_), channel_id=1, source_target_pairs={{0,1},{1,0},{2,3},{3,2},{4,5},{5,4},{6,7},{7,6},{8,9},{9,8},{10,11... | collective-permute-start | bytes 786440 | tf_op jit(solution)/shard_map/ppermute | solution.py:366
  10.8 12.2 %all_to_all.5.got.got_v = s32[32,1,256]{2,1,0:T(1,128)S(1)} all-to-all(s32[32,1,256]{2,1,0:T(1,128)S(1)} %get-tuple-element.41), channel_id=1, replica_groups=mesh['group'=4,'member'=8] {'group','member'}, dimensions={0} | all-to-all | bytes 65536 | tf_op jit(solution)/shard_map/all_to_all | solution.py:392
  23.0 0.7 collective-permute-start.8
  23.7 0.7 collective-permute-start.6
  24.3 2.2 %copy-done = f32[4096,256]{1,0:T(8,128)S(1)} copy-done((f32[4096,256]{1,0:T(8,128)S(1)}, f32[4096,256]{1,0:T(8,128)}, u32[]{:S(2)}) %copy-start) | copy-done | bytes 4194328
  26.5 2.3 %gather_negatives.1 = (f32[128,256]{1,0:T(8,128)S(1)}, f32[128,256]{1,0:T(8,128)S(1)}, f32[128,256]{1,0:T(8,128)S(1)}, f32[128,256]{1,0:T(8,128)S(1)}) custom-call(s32[2]{0:T(128)S(1)} %pad_add_fusion.1.info, s32[32,1,256]{2,1,0:T(1,128)S(1)} %all_to_all.5.got.got_v, f32[4096,256]{1,0:T(8,128)S(1)} %copy-done, ...), custom_call_target="tpu_custom_call" | custom-call | tf_op jit(solution)/shard_map/gather_negatives/pallas_call | solution.py:26
  28.9 0.6 collective-permute-start.4
  29.6 1.2 %collective-permute-start.5 = (f32[128,256]{1,0:T(8,128)S(1)}, f32[128,256]{1,0:T(8,128)S(1)}, u32[]{:S(2)}, u32[]{:S(2)}) collective-permute-start(f32[128,256]{1,0:T(8,128)S(1)} %get-tuple-element.46), channel_id=1, source_target_pairs={{0,24},{8,16},{16,8},{24,0},{1,25},{9,17},{17,9},{25,1},{2,26},{10... | collective-permute-start | bytes 393224 | tf_op jit(solution)/shard_map/ppermute | solution.py:366
  30.8 1.4 %collective-permute-start.7 = (f32[256,256]{1,0:T(8,128)S(1)}, f32[256,256]{1,0:T(8,128)S(1)}, u32[]{:S(2)}, u32[]{:S(2)}) collective-permute-start(f32[256,256]{1,0:T(8,128)S(1)} %collective-permute-done.refs_2_.refs_7_.refs_4_.refs_8_), channel_id=1, source_target_pairs={{0,1},{1,0},{2,3},{3,2},{4,5},{5,4},{6,7},{7,6},{8,9},{9,8},{10,11... | collective-permute-start | bytes 786440 | tf_op jit(solution)/shard_map/ppermute | solution.py:366
  32.1 0.7 collective-permute-start.9
  32.8 3.3 %gather_targets.1 = (f32[256,256]{1,0:T(8,128)S(1)}, f32[256,256]{1,0:T(8,128)S(1)}, f32[256,256]{1,0:T(8,128)S(1)}, f32[256,256]{1,0:T(8,128)S(1)}) custom-call(s32[2]{0:T(128)S(1)} %pad_add_fusion.1.info, s32[32,1,256]{2,1,0:T(1,128)S(1)} %all_to_all.5.got.got_v, f32[4096,256]{1,0:T(8,128)S(1)} %copy-done), custom_call_target="tpu_custom_call" | custom-call | tf_op jit(solution)/shard_map/gather_targets/pallas_call | solution.py:26
  36.2 1.0 collective-permute-done.5.refs_3_
  37.8 1.3 %collective-permute-start.12 = (f32[256,256]{1,0:T(8,128)S(1)}, f32[256,256]{1,0:T(8,128)S(1)}, u32[]{:S(2)}, u32[]{:S(2)}) collective-permute-start(f32[256,256]{1,0:T(8,128)S(1)} %get-tuple-element.53), channel_id=1, source_target_pairs={{0,24},{8,16},{16,8},{24,0},{1,25},{9,17},{17,9},{25,1},{2,26},{10... | collective-permute-start | bytes 786440 | tf_op jit(solution)/shard_map/ppermute | solution.py:366
  39.1 3.1 %score.2 = (f32[2,2048]{1,0:T(2,128)S(1)}, bf16[4,512,256]{2,1,0:T(8,128)(2,1)S(1)}, bf16[4,512,256]{2,1,0:T(8,128)(2,1)S(1)}) custom-call(s32[2]{0:T(128)S(1)} %pad_add_fusion.1.info, f32[128,256]{1,0:T(8,128)S(1)} %get-tuple-element.43.refs_0_, f32[128,256]{1,0:T(8,128)S(1)} %collective-permute-done.3.refs_1_, ...), custom_call_target="tpu_custom_call" | custom-call | flops 1610612736 | bytes 1048576 | tf_op jit(solution)/shard_map/score/pallas_call | solution.py:26
  42.2 2.8 %collective-permute-done.9.refs_7_.refs_11_ = f32[256,256]{1,0:T(8,128)S(1)} collective-permute-done((f32[256,256]{1,0:T(8,128)S(1)}, f32[256,256]{1,0:T(8,128)S(1)}, u32[]{:S(2)}, u32[]{:S(2)}) %collective-permute-start.9) | collective-permute-done | bytes 262176 | tf_op jit(solution)/shard_map/ppermute | solution.py:366
  45.0 1.6 %pick.1 = (f32[256,256]{1,0:T(8,128)S(1)}, f32[256,256]{1,0:T(8,128)S(1)}, f32[256,256]{1,0:T(8,128)S(1)}, f32[256,256]{1,0:T(8,128)S(1)}) custom-call(s32[2]{0:T(128)S(1)} %pad_add_fusion.1.info, s32[32,1,256]{2,1,0:T(1,128)S(1)} %all_to_all.5.got.got_v, f32[256,256]{1,0:T(8,128)S(1)} %get-tuple-element.40.refs_4_.refs_0_, ...), custom_call_target="tpu_custom_call" | custom-call | tf_op jit(solution)/shard_map/pick/pallas_call | solution.py:26
  46.7 0.6 collective-permute-start.17
  47.3 1.2 %collective-permute-start.18 = (f32[256,256]{1,0:T(8,128)S(1)}, f32[256,256]{1,0:T(8,128)S(1)}, u32[]{:S(2)}, u32[]{:S(2)}) collective-permute-start(f32[256,256]{1,0:T(8,128)S(1)} %get-tuple-element.57.refs_7_), channel_id=1, source_target_pairs={{0,24},{8,16},{16,8},{24,0},{1,25},{9,17},{17,9},{25,1},{2,26},{10... | collective-permute-start | bytes 786440 | tf_op jit(solution)/shard_map/ppermute | solution.py:366
  48.5 3.1 %score.3 = (f32[2,2048]{1,0:T(2,128)S(1)}, bf16[4,512,256]{2,1,0:T(8,128)(2,1)S(1)}, bf16[4,512,256]{2,1,0:T(8,128)(2,1)S(1)}) custom-call(s32[2]{0:T(128)S(1)} %pad_add_fusion.1.info, f32[128,256]{1,0:T(8,128)S(1)} %get-tuple-element.43.refs_0_, f32[128,256]{1,0:T(8,128)S(1)} %collective-permute-done.3.refs_1_, ...), custom_call_target="tpu_custom_call" | custom-call | flops 1610612736 | bytes 1048576 | tf_op jit(solution)/shard_map/score/pallas_call | solution.py:26
  51.6 1.2 %positive.1 = (f32[2,2048]{1,0:T(2,128)S(1)}, f32[2,2048]{1,0:T(2,128)S(1)}) custom-call(s32[2]{0:T(128)S(1)} %pad_add_fusion.1.info, s32[32,1,256]{2,1,0:T(1,128)S(1)} %all_to_all.5.got.got_v, f32[2,2048]{1,0:T(2,128)S(1)} %get-tuple-element.49.stats, f32[256,256]{1,0:T(8,128)S(1)} %get-tuple-element.50.refs_0_.refs_4_, ...), custom_call_target="tpu_custom_call" | custom-call | tf_op jit(solution)/shard_map/positive/pallas_call | solution.py:26
  52.8 1.4 %collective-permute-start.13 = (f32[2,2048]{1,0:T(2,128)S(1)}, f32[2,2048]{1,0:T(2,128)S(1)}, u32[]{:S(2)}, u32[]{:S(2)}) collective-permute-start(f32[2,2048]{1,0:T(2,128)S(1)} %get-tuple-element.58.first), channel_id=1, source_target_pairs={{0,1},{1,0},{2,3},{3,2},{4,5},{5,4},{6,7},{7,6},{8,9},{9,8},{10,11... | collective-permute-start | bytes 49160 | tf_op jit(solution)/shard_map/ppermute | solution.py:366
  54.2 2.4 %collective-permute-done.13.second = f32[2,2048]{1,0:T(2,128)S(1)} collective-permute-done((f32[2,2048]{1,0:T(2,128)S(1)}, f32[2,2048]{1,0:T(2,128)S(1)}, u32[]{:S(2)}, u32[]{:S(2)}) %collective-permute-start.13) | collective-permute-done | bytes 16416 | tf_op jit(solution)/shard_map/ppermute | solution.py:366
  56.6 1.4 %collective-permute-start.14 = (f32[2,2048]{1,0:T(2,128)S(1)}, f32[2,2048]{1,0:T(2,128)S(1)}, u32[]{:S(2)}, u32[]{:S(2)}) collective-permute-start(f32[2,2048]{1,0:T(2,128)S(1)} %join.3.first), channel_id=1, source_target_pairs={{0,2},{1,3},{2,0},{3,1},{4,6},{5,7},{6,4},{7,5},{8,10},{9,11},{10,... | collective-permute-start | bytes 49160 | tf_op jit(solution)/shard_map/ppermute | solution.py:366
  58.0 2.4 %collective-permute-done.14.second = f32[2,2048]{1,0:T(2,128)S(1)} collective-permute-done((f32[2,2048]{1,0:T(2,128)S(1)}, f32[2,2048]{1,0:T(2,128)S(1)}, u32[]{:S(2)}, u32[]{:S(2)}) %collective-permute-start.14) | collective-permute-done | bytes 16416 | tf_op jit(solution)/shard_map/ppermute | solution.py:366
  60.5 2.6 %collective-permute-start.15 = (f32[2,2048]{1,0:T(2,128)S(1)}, f32[2,2048]{1,0:T(2,128)S(1)}, u32[]{:S(2)}, u32[]{:S(2)}) collective-permute-start(f32[2,2048]{1,0:T(2,128)S(1)} %join.4.first), channel_id=1, source_target_pairs={{0,4},{1,5},{2,6},{3,7},{4,0},{5,1},{6,2},{7,3},{8,12},{9,13},{10,... | collective-permute-start | bytes 49160 | tf_op jit(solution)/shard_map/ppermute | solution.py:366
  63.0 3.1 %pulled.1 = (f32[8,256,256]{2,1,0:T(8,128)S(1)}, f32[8,256,256]{2,1,0:T(8,128)S(1)}) custom-call(s32[2]{0:T(128)S(1)} %pad_add_fusion.1.info, s32[32,1,256]{2,1,0:T(1,128)S(1)} %all_to_all.5.got.got_v, f32[128,256]{1,0:T(8,128)S(1)} %get-tuple-element.43.refs_0_, f32[128,256]{1,0:T(8,128)S(1)} %collective-permute-done.3.refs_1_, ...), custom_call_target="tpu_custom_call" | custom-call | flops 1610612736 | bytes 1048576 | tf_op jit(solution)/shard_map/pulled/pallas_call | solution.py:26
  66.2 0.6 pull.3
  66.8 1.4 %collective-permute-start.19 = (f32[256,256]{1,0:T(8,128)S(1)}, f32[256,256]{1,0:T(8,128)S(1)}, u32[]{:S(2)}, u32[]{:S(2)}) collective-permute-start(f32[256,256]{1,0:T(8,128)S(1)} %get-tuple-element.66), channel_id=1, source_target_pairs={{0,1},{1,0},{2,3},{3,2},{4,5},{5,4},{6,7},{7,6},{8,9},{9,8},{10,11... | collective-permute-start | bytes 786440 | tf_op jit(solution)/shard_map/ppermute | solution.py:366
  68.3 2.6 %grad.1 = (f32[136,256]{1,0:T(8,128)S(1)}, f32[136,256]{1,0:T(8,128)S(1)}, f32[136,256]{1,0:T(8,128)S(1)}, f32[136,256]{1,0:T(8,128)S(1)}) custom-call(s32[2]{0:T(128)S(1)} %pad_add_fusion.1.info, s32[32,1,256]{2,1,0:T(1,128)S(1)} %all_to_all.5.got.got_v, f32[2,2048]{1,0:T(2,128)S(1)} %join.5.final, f32[2,2048]{1,0:T(2,128)S(1)} %get-tuple-element.49.stats, ...), custom_call_target="tpu_custom_call" | custom-call | flops 1610612736 | bytes 8388608 | tf_op jit(solution)/shard_map/grad/pallas_call | solution.py:26
  70.9 2.6 %collective-permute-done.19.refs_0_.refs_1_ = f32[256,256]{1,0:T(8,128)S(1)} collective-permute-done((f32[256,256]{1,0:T(8,128)S(1)}, f32[256,256]{1,0:T(8,128)S(1)}, u32[]{:S(2)}, u32[]{:S(2)}) %collective-permute-start.19) | collective-permute-done | bytes 262176 | tf_op jit(solution)/shard_map/ppermute | solution.py:366
  74.1 1.4 %collective-permute-start.20 = (f32[256,256]{1,0:T(8,128)S(1)}, f32[256,256]{1,0:T(8,128)S(1)}, u32[]{:S(2)}, u32[]{:S(2)}) collective-permute-start(f32[256,256]{1,0:T(8,128)S(1)} %get-tuple-element.68), channel_id=1, source_target_pairs={{0,1},{1,0},{2,3},{3,2},{4,5},{5,4},{6,7},{7,6},{8,9},{9,8},{10,11... | collective-permute-start | bytes 786440 | tf_op jit(solution)/shard_map/ppermute | solution.py:366
  75.6 0.7 collective-permute-start.21
  76.8 1.3 %collective-permute-start.24 = (f32[136,256]{1,0:T(8,128)S(1)}, f32[136,256]{1,0:T(8,128)S(1)}, u32[]{:S(2)}, u32[]{:S(2)}) collective-permute-start(f32[136,256]{1,0:T(8,128)S(1)} %get-tuple-element.73), channel_id=1, source_target_pairs={{0,24},{8,16},{16,8},{24,0},{1,25},{9,17},{17,9},{25,1},{2,26},{10... | collective-permute-start | bytes 417800 | tf_op jit(solution)/shard_map/ppermute | solution.py:366
  78.1 4.6 %collective-permute-done.23.refs_4_.refs_2_ = f32[136,256]{1,0:T(8,128)S(1)} collective-permute-done((f32[136,256]{1,0:T(8,128)S(1)}, f32[136,256]{1,0:T(8,128)S(1)}, u32[]{:S(2)}, u32[]{:S(2)}) %collective-permute-start.23) | collective-permute-done | bytes 139296 | tf_op jit(solution)/shard_map/ppermute | solution.py:366
  82.7 2.2 %collective-permute-done.24.refs_5_.refs_3_ = f32[136,256]{1,0:T(8,128)S(1)} collective-permute-done((f32[136,256]{1,0:T(8,128)S(1)}, f32[136,256]{1,0:T(8,128)S(1)}, u32[]{:S(2)}, u32[]{:S(2)}) %collective-permute-start.24) | collective-permute-done | bytes 139296 | tf_op jit(solution)/shard_map/ppermute | solution.py:366
  85.0 0.7 pull.5
  85.7 0.7 collective-permute-start.26
  86.4 1.5 %collective-permute-start.27 = (f32[256,256]{1,0:T(8,128)S(1)}, f32[256,256]{1,0:T(8,128)S(1)}, u32[]{:S(2)}, u32[]{:S(2)}) collective-permute-start(f32[256,256]{1,0:T(8,128)S(1)} %get-tuple-element.76), channel_id=1, source_target_pairs={{0,2},{1,3},{2,0},{3,1},{4,6},{5,7},{6,4},{7,5},{8,10},{9,11},{10,... | collective-permute-start | bytes 786440 | tf_op jit(solution)/shard_map/ppermute | solution.py:366
  87.8 1.4 %collective-permute-start.28 = (f32[256,256]{1,0:T(8,128)S(1)}, f32[256,256]{1,0:T(8,128)S(1)}, u32[]{:S(2)}, u32[]{:S(2)}) collective-permute-start(f32[256,256]{1,0:T(8,128)S(1)} %get-tuple-element.77), channel_id=1, source_target_pairs={{0,3},{1,2},{2,1},{3,0},{4,7},{5,6},{6,5},{7,4},{8,11},{9,10},{10,... | collective-permute-start | bytes 786440 | tf_op jit(solution)/shard_map/ppermute | solution.py:366
  89.2 1.3 %collective-permute-start.25 = (f32[256,256]{1,0:T(8,128)S(1)}, f32[256,256]{1,0:T(8,128)S(1)}, u32[]{:S(2)}, u32[]{:S(2)}) collective-permute-start(f32[256,256]{1,0:T(8,128)S(1)} %add.11.refs_0_), channel_id=1, source_target_pairs={{0,4},{1,5},{2,6},{3,7},{4,0},{5,1},{6,2},{7,3},{8,12},{9,13},{10,... | collective-permute-start | bytes 786440 | tf_op jit(solution)/shard_map/ppermute | solution.py:366
  90.5 10.7 %scatter.1 = f32[4096,256]{1,0:T(8,128)} custom-call(s32[2]{0:T(128)S(1)} %pad_add_fusion.1.info, s32[32,1,256]{2,1,0:T(1,128)S(1)} %all_to_all.5.got.got_v, s32[32,1,256]{2,1,0:T(1,128)S(1)} %all_to_all.5.got.got_v, f32[136,256]{1,0:T(8,128)S(1)} %get-tuple-element.70.refs_2_.refs_0_, f32[136,256]{1,0:T(8,128)S(1)} %collective-permute-done.22.refs_3_.refs_1_, ...), custom_call_target="tpu_custom_call" | custom-call | tf_op jit(solution)/shard_map/scatter/pallas_call | solution.py:26
  101.3 5.3 %collective-permute-done.28.refs_4_ = f32[256,256]{1,0:T(8,128)S(1)} collective-permute-done((f32[256,256]{1,0:T(8,128)S(1)}, f32[256,256]{1,0:T(8,128)S(1)}, u32[]{:S(2)}, u32[]{:S(2)}) %collective-permute-start.28) | collective-permute-done | bytes 262176 | tf_op jit(solution)/shard_map/ppermute | solution.py:366
  106.6 1.0 finish.1
  (39 shorter events, 2.2 us)
Async XLA Ops:
  1.5 1.0 copy-start.1
  3.6 19.4 %collective-permute-start = (f32[256,256]{1,0:T(8,128)S(1)}, f32[256,256]{1,0:T(8,128)S(1)}, u32[]{:S(2)}, u32[]{:S(2)}) collective-permute-start(f32[256,256]{1,0:T(8,128)S(1)} %get-tuple-element.40.refs_4_.refs_0_), channel_id=1, source_target_pairs={{0,4},{1,5},{2,6},{3,7},{4,0},{5,1},{6,2},{7,3},{8,12},{9,13},{10,... | collective-permute-start | bytes 786440 | tf_op jit(solution)/shard_map/ppermute | solution.py:366
  7.7 16.0 %collective-permute-start.2 = (f32[256,256]{1,0:T(8,128)S(1)}, f32[256,256]{1,0:T(8,128)S(1)}, u32[]{:S(2)}, u32[]{:S(2)}) collective-permute-start(f32[256,256]{1,0:T(8,128)S(1)} %get-tuple-element.40.refs_4_.refs_0_), channel_id=1, source_target_pairs={{0,2},{1,3},{2,0},{3,1},{4,6},{5,7},{6,4},{7,5},{8,10},{9,11},{10,... | collective-permute-start | bytes 786440 | tf_op jit(solution)/shard_map/ppermute | solution.py:366
  9.3 15.1 %collective-permute-start.1 = (f32[256,256]{1,0:T(8,128)S(1)}, f32[256,256]{1,0:T(8,128)S(1)}, u32[]{:S(2)}, u32[]{:S(2)}) collective-permute-start(f32[256,256]{1,0:T(8,128)S(1)} %get-tuple-element.40.refs_4_.refs_0_), channel_id=1, source_target_pairs={{0,1},{1,0},{2,3},{3,2},{4,5},{5,4},{6,7},{7,6},{8,9},{9,8},{10,11... | collective-permute-start | bytes 786440 | tf_op jit(solution)/shard_map/ppermute | solution.py:366
  23.0 9.2 %collective-permute-start.8 = (f32[256,256]{1,0:T(8,128)S(1)}, f32[256,256]{1,0:T(8,128)S(1)}, u32[]{:S(2)}, u32[]{:S(2)}) collective-permute-start(f32[256,256]{1,0:T(8,128)S(1)} %collective-permute-done.refs_2_.refs_7_.refs_4_.refs_8_), channel_id=1, source_target_pairs={{0,2},{1,3},{2,0},{3,1},{4,6},{5,7},{6,4},{7,5},{8,10},{9,11},{10,... | collective-permute-start | bytes 786440 | tf_op jit(solution)/shard_map/ppermute | solution.py:366
  23.7 14.1 %collective-permute-start.6 = (f32[256,256]{1,0:T(8,128)S(1)}, f32[256,256]{1,0:T(8,128)S(1)}, u32[]{:S(2)}, u32[]{:S(2)}) collective-permute-start(f32[256,256]{1,0:T(8,128)S(1)} %collective-permute-done.2.refs_1_.refs_6_.refs_2_), channel_id=1, source_target_pairs={{0,1},{1,0},{2,3},{3,2},{4,5},{5,4},{6,7},{7,6},{8,9},{9,8},{10,11... | collective-permute-start | bytes 786440 | tf_op jit(solution)/shard_map/ppermute | solution.py:366
  24.3 2.2 %copy-start = (f32[4096,256]{1,0:T(8,128)S(1)}, f32[4096,256]{1,0:T(8,128)}, u32[]{:S(2)}) copy-start(f32[4096,256]{1,0:T(8,128)} %table.3) | copy-start | bytes 12582916
  28.8 1.9 %collective-permute-start.3 = (f32[128,256]{1,0:T(8,128)S(1)}, f32[128,256]{1,0:T(8,128)S(1)}, u32[]{:S(2)}, u32[]{:S(2)}) collective-permute-start(f32[128,256]{1,0:T(8,128)S(1)} %get-tuple-element.44), channel_id=1, source_target_pairs={{0,8},{8,0},{16,24},{24,16},{1,9},{9,1},{17,25},{25,17},{2,10},{10... | collective-permute-start | bytes 393224 | tf_op jit(solution)/shard_map/ppermute | solution.py:366
  28.9 7.2 %collective-permute-start.4 = (f32[128,256]{1,0:T(8,128)S(1)}, f32[128,256]{1,0:T(8,128)S(1)}, u32[]{:S(2)}, u32[]{:S(2)}) collective-permute-start(f32[128,256]{1,0:T(8,128)S(1)} %get-tuple-element.45), channel_id=1, source_target_pairs={{0,16},{8,24},{16,0},{24,8},{1,17},{9,25},{17,1},{25,9},{2,18},{10... | collective-permute-start | bytes 393224 | tf_op jit(solution)/shard_map/ppermute | solution.py:366
  29.6 7.6 %collective-permute-start.5 = (f32[128,256]{1,0:T(8,128)S(1)}, f32[128,256]{1,0:T(8,128)S(1)}, u32[]{:S(2)}, u32[]{:S(2)}) collective-permute-start(f32[128,256]{1,0:T(8,128)S(1)} %get-tuple-element.46), channel_id=1, source_target_pairs={{0,24},{8,16},{16,8},{24,0},{1,25},{9,17},{17,9},{25,1},{2,26},{10... | collective-permute-start | bytes 393224 | tf_op jit(solution)/shard_map/ppermute | solution.py:366
  30.8 11.4 %collective-permute-start.7 = (f32[256,256]{1,0:T(8,128)S(1)}, f32[256,256]{1,0:T(8,128)S(1)}, u32[]{:S(2)}, u32[]{:S(2)}) collective-permute-start(f32[256,256]{1,0:T(8,128)S(1)} %collective-permute-done.refs_2_.refs_7_.refs_4_.refs_8_), channel_id=1, source_target_pairs={{0,1},{1,0},{2,3},{3,2},{4,5},{5,4},{6,7},{7,6},{8,9},{9,8},{10,11... | collective-permute-start | bytes 786440 | tf_op jit(solution)/shard_map/ppermute | solution.py:366
  32.1 12.8 %collective-permute-start.9 = (f32[256,256]{1,0:T(8,128)S(1)}, f32[256,256]{1,0:T(8,128)S(1)}, u32[]{:S(2)}, u32[]{:S(2)}) collective-permute-start(f32[256,256]{1,0:T(8,128)S(1)} %collective-permute-done.8.refs_6_.refs_10_), channel_id=1, source_target_pairs={{0,1},{1,0},{2,3},{3,2},{4,5},{5,4},{6,7},{7,6},{8,9},{9,8},{10,11... | collective-permute-start | bytes 786440 | tf_op jit(solution)/shard_map/ppermute | solution.py:366
  36.1 11.2 %collective-permute-start.10 = (f32[256,256]{1,0:T(8,128)S(1)}, f32[256,256]{1,0:T(8,128)S(1)}, u32[]{:S(2)}, u32[]{:S(2)}) collective-permute-start(f32[256,256]{1,0:T(8,128)S(1)} %get-tuple-element.51), channel_id=1, source_target_pairs={{0,8},{8,0},{16,24},{24,16},{1,9},{9,1},{17,25},{25,17},{2,10},{10... | collective-permute-start | bytes 786440 | tf_op jit(solution)/shard_map/ppermute | solution.py:366
  37.2 14.4 %collective-permute-start.11 = (f32[256,256]{1,0:T(8,128)S(1)}, f32[256,256]{1,0:T(8,128)S(1)}, u32[]{:S(2)}, u32[]{:S(2)}) collective-permute-start(f32[256,256]{1,0:T(8,128)S(1)} %get-tuple-element.52), channel_id=1, source_target_pairs={{0,16},{8,24},{16,0},{24,8},{1,17},{9,25},{17,1},{25,9},{2,18},{10... | collective-permute-start | bytes 786440 | tf_op jit(solution)/shard_map/ppermute | solution.py:366
  37.8 13.8 %collective-permute-start.12 = (f32[256,256]{1,0:T(8,128)S(1)}, f32[256,256]{1,0:T(8,128)S(1)}, u32[]{:S(2)}, u32[]{:S(2)}) collective-permute-start(f32[256,256]{1,0:T(8,128)S(1)} %get-tuple-element.53), channel_id=1, source_target_pairs={{0,24},{8,16},{16,8},{24,0},{1,25},{9,17},{17,9},{25,1},{2,26},{10... | collective-permute-start | bytes 786440 | tf_op jit(solution)/shard_map/ppermute | solution.py:366
  46.6 19.6 %collective-permute-start.16 = (f32[256,256]{1,0:T(8,128)S(1)}, f32[256,256]{1,0:T(8,128)S(1)}, u32[]{:S(2)}, u32[]{:S(2)}) collective-permute-start(f32[256,256]{1,0:T(8,128)S(1)} %get-tuple-element.55.refs_5_), channel_id=1, source_target_pairs={{0,8},{8,0},{16,24},{24,16},{1,9},{9,1},{17,25},{25,17},{2,10},{10... | collective-permute-start | bytes 786440 | tf_op jit(solution)/shard_map/ppermute | solution.py:366
  46.7 19.5 %collective-permute-start.17 = (f32[256,256]{1,0:T(8,128)S(1)}, f32[256,256]{1,0:T(8,128)S(1)}, u32[]{:S(2)}, u32[]{:S(2)}) collective-permute-start(f32[256,256]{1,0:T(8,128)S(1)} %get-tuple-element.56.refs_6_), channel_id=1, source_target_pairs={{0,16},{8,24},{16,0},{24,8},{1,17},{9,25},{17,1},{25,9},{2,18},{10... | collective-permute-start | bytes 786440 | tf_op jit(solution)/shard_map/ppermute | solution.py:366
  47.3 18.9 %collective-permute-start.18 = (f32[256,256]{1,0:T(8,128)S(1)}, f32[256,256]{1,0:T(8,128)S(1)}, u32[]{:S(2)}, u32[]{:S(2)}) collective-permute-start(f32[256,256]{1,0:T(8,128)S(1)} %get-tuple-element.57.refs_7_), channel_id=1, source_target_pairs={{0,24},{8,16},{16,8},{24,0},{1,25},{9,17},{17,9},{25,1},{2,26},{10... | collective-permute-start | bytes 786440 | tf_op jit(solution)/shard_map/ppermute | solution.py:366
  52.8 3.8 %collective-permute-start.13 = (f32[2,2048]{1,0:T(2,128)S(1)}, f32[2,2048]{1,0:T(2,128)S(1)}, u32[]{:S(2)}, u32[]{:S(2)}) collective-permute-start(f32[2,2048]{1,0:T(2,128)S(1)} %get-tuple-element.58.first), channel_id=1, source_target_pairs={{0,1},{1,0},{2,3},{3,2},{4,5},{5,4},{6,7},{7,6},{8,9},{9,8},{10,11... | collective-permute-start | bytes 49160 | tf_op jit(solution)/shard_map/ppermute | solution.py:366
  56.6 3.8 %collective-permute-start.14 = (f32[2,2048]{1,0:T(2,128)S(1)}, f32[2,2048]{1,0:T(2,128)S(1)}, u32[]{:S(2)}, u32[]{:S(2)}) collective-permute-start(f32[2,2048]{1,0:T(2,128)S(1)} %join.3.first), channel_id=1, source_target_pairs={{0,2},{1,3},{2,0},{3,1},{4,6},{5,7},{6,4},{7,5},{8,10},{9,11},{10,... | collective-permute-start | bytes 49160 | tf_op jit(solution)/shard_map/ppermute | solution.py:366
  60.5 5.7 %collective-permute-start.15 = (f32[2,2048]{1,0:T(2,128)S(1)}, f32[2,2048]{1,0:T(2,128)S(1)}, u32[]{:S(2)}, u32[]{:S(2)}) collective-permute-start(f32[2,2048]{1,0:T(2,128)S(1)} %join.4.first), channel_id=1, source_target_pairs={{0,4},{1,5},{2,6},{3,7},{4,0},{5,1},{6,2},{7,3},{8,12},{9,13},{10,... | collective-permute-start | bytes 49160 | tf_op jit(solution)/shard_map/ppermute | solution.py:366
  66.8 6.6 %collective-permute-start.19 = (f32[256,256]{1,0:T(8,128)S(1)}, f32[256,256]{1,0:T(8,128)S(1)}, u32[]{:S(2)}, u32[]{:S(2)}) collective-permute-start(f32[256,256]{1,0:T(8,128)S(1)} %get-tuple-element.66), channel_id=1, source_target_pairs={{0,1},{1,0},{2,3},{3,2},{4,5},{5,4},{6,7},{7,6},{8,9},{9,8},{10,11... | collective-permute-start | bytes 786440 | tf_op jit(solution)/shard_map/ppermute | solution.py:366
  74.1 10.8 %collective-permute-start.20 = (f32[256,256]{1,0:T(8,128)S(1)}, f32[256,256]{1,0:T(8,128)S(1)}, u32[]{:S(2)}, u32[]{:S(2)}) collective-permute-start(f32[256,256]{1,0:T(8,128)S(1)} %get-tuple-element.68), channel_id=1, source_target_pairs={{0,1},{1,0},{2,3},{3,2},{4,5},{5,4},{6,7},{7,6},{8,9},{9,8},{10,11... | collective-permute-start | bytes 786440 | tf_op jit(solution)/shard_map/ppermute | solution.py:366
  75.6 9.3 %collective-permute-start.21 = (f32[256,256]{1,0:T(8,128)S(1)}, f32[256,256]{1,0:T(8,128)S(1)}, u32[]{:S(2)}, u32[]{:S(2)}) collective-permute-start(f32[256,256]{1,0:T(8,128)S(1)} %add.10), channel_id=1, source_target_pairs={{0,2},{1,3},{2,0},{3,1},{4,6},{5,7},{6,4},{7,5},{8,10},{9,11},{10,... | collective-permute-start | bytes 786440 | tf_op jit(solution)/shard_map/ppermute | solution.py:366
  76.2 1.9 %collective-permute-start.22 = (f32[136,256]{1,0:T(8,128)S(1)}, f32[136,256]{1,0:T(8,128)S(1)}, u32[]{:S(2)}, u32[]{:S(2)}) collective-permute-start(f32[136,256]{1,0:T(8,128)S(1)} %get-tuple-element.71), channel_id=1, source_target_pairs={{0,8},{8,0},{16,24},{24,16},{1,9},{9,1},{17,25},{25,17},{2,10},{10... | collective-permute-start | bytes 417800 | tf_op jit(solution)/shard_map/ppermute | solution.py:366
  76.2 6.5 %collective-permute-start.23 = (f32[136,256]{1,0:T(8,128)S(1)}, f32[136,256]{1,0:T(8,128)S(1)}, u32[]{:S(2)}, u32[]{:S(2)}) collective-permute-start(f32[136,256]{1,0:T(8,128)S(1)} %get-tuple-element.72), channel_id=1, source_target_pairs={{0,16},{8,24},{16,0},{24,8},{1,17},{9,25},{17,1},{25,9},{2,18},{10... | collective-permute-start | bytes 417800 | tf_op jit(solution)/shard_map/ppermute | solution.py:366
  76.8 8.1 %collective-permute-start.24 = (f32[136,256]{1,0:T(8,128)S(1)}, f32[136,256]{1,0:T(8,128)S(1)}, u32[]{:S(2)}, u32[]{:S(2)}) collective-permute-start(f32[136,256]{1,0:T(8,128)S(1)} %get-tuple-element.73), channel_id=1, source_target_pairs={{0,24},{8,16},{16,8},{24,0},{1,25},{9,17},{17,9},{25,1},{2,26},{10... | collective-permute-start | bytes 417800 | tf_op jit(solution)/shard_map/ppermute | solution.py:366
  85.0 21.6 %copy-start.2 = (s32[256]{0:T(256)S(1)}, s32[256]{0:T(256)}, u32[]{:S(2)}) copy-start(s32[256]{0:T(256)} %param.11) | copy-start | bytes 3076
  85.7 15.6 %collective-permute-start.26 = (f32[256,256]{1,0:T(8,128)S(1)}, f32[256,256]{1,0:T(8,128)S(1)}, u32[]{:S(2)}, u32[]{:S(2)}) collective-permute-start(f32[256,256]{1,0:T(8,128)S(1)} %get-tuple-element.75), channel_id=1, source_target_pairs={{0,1},{1,0},{2,3},{3,2},{4,5},{5,4},{6,7},{7,6},{8,9},{9,8},{10,11... | collective-permute-start | bytes 786440 | tf_op jit(solution)/shard_map/ppermute | solution.py:366
  86.4 14.9 %collective-permute-start.27 = (f32[256,256]{1,0:T(8,128)S(1)}, f32[256,256]{1,0:T(8,128)S(1)}, u32[]{:S(2)}, u32[]{:S(2)}) collective-permute-start(f32[256,256]{1,0:T(8,128)S(1)} %get-tuple-element.76), channel_id=1, source_target_pairs={{0,2},{1,3},{2,0},{3,1},{4,6},{5,7},{6,4},{7,5},{8,10},{9,11},{10,... | collective-permute-start | bytes 786440 | tf_op jit(solution)/shard_map/ppermute | solution.py:366
  87.8 18.7 %collective-permute-start.28 = (f32[256,256]{1,0:T(8,128)S(1)}, f32[256,256]{1,0:T(8,128)S(1)}, u32[]{:S(2)}, u32[]{:S(2)}) collective-permute-start(f32[256,256]{1,0:T(8,128)S(1)} %get-tuple-element.77), channel_id=1, source_target_pairs={{0,3},{1,2},{2,1},{3,0},{4,7},{5,6},{6,5},{7,4},{8,11},{9,10},{10,... | collective-permute-start | bytes 786440 | tf_op jit(solution)/shard_map/ppermute | solution.py:366
  89.2 17.4 %collective-permute-start.25 = (f32[256,256]{1,0:T(8,128)S(1)}, f32[256,256]{1,0:T(8,128)S(1)}, u32[]{:S(2)}, u32[]{:S(2)}) collective-permute-start(f32[256,256]{1,0:T(8,128)S(1)} %add.11.refs_0_), channel_id=1, source_target_pairs={{0,4},{1,5},{2,6},{3,7},{4,0},{5,1},{6,2},{7,3},{8,12},{9,13},{10,... | collective-permute-start | bytes 786440 | tf_op jit(solution)/shard_map/ppermute | solution.py:366

commit v5 on v4

--- a/solution.py
+++ b/solution.py
@@ -119,7 +119,10 @@
     high = high + table(hot, (local >> 6).astype(F32), place)
     low = low + table(hot, (local & 63).astype(F32), place)
     out_ref[:, 0, 0:LANES] = high.astype(I32) * 64 + low.astype(I32)
-    out_ref[:, 0, LANES:] = position.astype(I32)
+    out_ref[:, 0, LANES : 2 * LANES] = position.astype(I32)
+    if out_ref.shape[2] > 2 * LANES:
+        rest = out_ref.shape[2] - 2 * LANES
+        out_ref[:, 0, 2 * LANES :] = jnp.zeros((devices, rest), I32)
 
 
 def gather_kernel(members, groups, part, count, info, got, table, *refs):
@@ -155,7 +158,7 @@
 
 
 def own_places(members, info, got):
-    return got[pl.ds(info[0] * members, members), 0, LANES:]
+    return got[pl.ds(info[0] * members, members), 0, LANES : 2 * LANES]
 
 
 def slot_hot(members, groups, slots, info, place_rows, column, mr, tokens):
@@ -207,22 +210,21 @@
         own[1:2, lanes] = has
 
 
-def pulled_kernel(members, groups, slots, halves, info, got, *refs):
+def pulled_kernel(members, groups, slots, blocks, info, got, *refs):
     negs, refs = refs[:groups], refs[groups:]
     rows, refs = refs[:groups], refs[groups:]
-    probs, (pulled, row_t, place_rows, column) = refs[:-4], refs[-4:]
+    prob_hi, prob_lo, pulled, row_t, place_rows, column = refs
     place_rows[...] = own_places(members, info, got)
     neg = jnp.concatenate([row[...] for row in negs], axis=0)
     neg_t = split(jnp.transpose(neg))
     tokens = pulled.shape[2]
-    for h, blocks in enumerate(halves):
-        for i, e in enumerate(blocks):
-            mr = info[1] ^ e
-            pulled[e] = dot3(neg_t, (probs[2 * h][i], probs[2 * h + 1][i]), NN)
-            at = pl.ds(pl.multiple_of(mr * slots, slots), slots)
-            hot = slot_hot(members, groups, slots, info, place_rows, column, mr, tokens)
-            high, low = split(jnp.concatenate([r[at, :] for r in rows], axis=0))
-            row_t[e] = dot1(high, as_bf16(hot), TN) + dot1(low, as_bf16(hot), TN)
+    for i, e in enumerate(blocks):
+        mr = info[1] ^ e
+        pulled[i] = dot3(neg_t, (prob_hi[i], prob_lo[i]), NN)
+        at = pl.ds(pl.multiple_of(mr * slots, slots), slots)
+        hot = slot_hot(members, groups, slots, info, place_rows, column, mr, tokens)
+        high, low = split(jnp.concatenate([r[at, :] for r in rows], axis=0))
+        row_t[i] = dot1(high, as_bf16(hot), TN) + dot1(low, as_bf16(hot), TN)
 
 
 def join(first, second):
@@ -248,10 +250,12 @@
     return scale, extra
 
 
-def pull_kernel(blocks, tokens, info, final, stats, own, pulled, row_t, *refs):
+def pull_kernel(halves, blocks, tokens, info, final, stats, own, *refs):
     for e, out in zip(blocks, refs[-len(blocks) :]):
+        h = 0 if e in halves[0] else 1
+        pulled, row_t = (ref[halves[h].index(e)] for ref in refs[2 * h : 2 * h + 2])
         scale, extra = shares(info, e, tokens, final, stats, own)
-        out[...] = pulled[e] * scale + row_t[e] * extra
+        out[...] = pulled * scale + row_t * extra
 
 
 def flat(table, lane, slots):
@@ -263,8 +267,7 @@
 def grad_kernel(members, groups, slots, halves, info, got, final, stats, own, *refs):
     probs, refs = refs[: 2 * len(halves)], refs[2 * len(halves) :]
     encs = refs[:members]
-    outs = refs[members : members + groups]
-    total, coef, place_rows = refs[members + groups :]
+    *outs, total, coef, place_rows = refs[-groups - 3 :]
     place_rows[...] = own_places(members, info, got)
     tokens, width = encs[0].shape
     for h, i, e in [(h, i, e) for h, blocks in enumerate(halves) for i, e in enumerate(blocks)]:
@@ -383,7 +386,7 @@
     ints = jnp.concatenate([target_owner.reshape(-1), target_local, valid, negative_ids])
     request, masked = call(
         functools.partial(front_kernel, members, rows_dev, slots, tokens, negatives),
-        [shape((devices, 1, 2 * LANES), I32), sds(tokens, width)],
+        [shape((devices, 1, max(2 * LANES, (1 << 15) // devices)), I32), sds(tokens, width)],
         [SMEM] + [VMEM] * 2,
         [VMEM] * 2,
         (info, ints.reshape(1, -1), encoded),
@@ -452,22 +455,25 @@
         scratch=[pltpu.VMEM((members, LANES), I32), pltpu.VMEM((LANES, 1), I32)],
         name="positive",
     )
-    pulled, row_t = call(
-        functools.partial(pulled_kernel, members, groups, slots, halves),
-        [sds(members, width, tokens)] * 2,
-        [SMEM] + [VMEM] * (1 + 2 * groups + len(probs)),
-        [VMEM] * 2,
-        (info, got, *negs, *rows, *probs),
-        scratch=[pltpu.VMEM((members, LANES), I32), pltpu.VMEM((LANES, 1), I32)],
-        flops=6 * everyone * negatives * width,
-        moved=MIB,
-        name="pulled",
-    )
+    pulled = []
+    for h, blocks in enumerate(halves):
+        pulled += call(
+            functools.partial(pulled_kernel, members, groups, slots, blocks),
+            [sds(len(blocks), width, tokens)] * 2,
+            [SMEM] + [VMEM] * (3 + 2 * groups),
+            [VMEM] * 2,
+            (info, got, *negs, *rows, *probs[2 * h : 2 * h + 2]),
+            scratch=[pltpu.VMEM((members, LANES), I32), pltpu.VMEM((LANES, 1), I32)],
+            flops=6 * len(blocks) * tokens * negatives * width,
+            moved=MIB,
+            name="pulled",
+        )
 
     final = joined
-    d = 1
+    d, hops = 1, 0
     while d < members:
-        late = sent[1:] if 2 * d == members else []
+        late = pulled[2 * hops : 2 * hops + 2]
+        hops += 1
         final = call(
             join_kernel,
             sds(2, everyone),
@@ -481,9 +487,9 @@
     grads = call(
         functools.partial(grad_kernel, members, groups, slots, halves),
         [sds(members * count + 8, width)] * groups,
-        [SMEM] + [VMEM] * (4 + len(probs) + members),
+        [SMEM] + [VMEM] * (4 + len(probs) + members) + [ANY] * (groups - 1),
         [VMEM] * groups,
-        (info, got, final, stats, own, *probs, *encs),
+        (info, got, final, stats, own, *probs, *encs, *sent[1:]),
         scratch=[
             pltpu.VMEM((negatives, width), F32),
             pltpu.VMEM((members, LANES), F32),
@@ -505,28 +511,30 @@
 
     graded = [grads[0]]
     grads = graded + [swap(grads[d], "group", d) for d in range(1, groups)]
-    def scaled(first, many, deps):
-        blocks = list(range(first, first + many))
+    def scaled(blocks, deps):
         return call(
-            functools.partial(pull_kernel, blocks, tokens),
-            [sds(width, tokens)] * many,
-            [SMEM] + [VMEM] * 5 + [ANY] * len(deps),
-            [VMEM] * many,
-            (info, final, stats, own, pulled, row_t, *deps),
+            functools.partial(pull_kernel, halves, blocks, tokens),
+            [sds(width, tokens)] * len(blocks),
+            [SMEM] + [VMEM] * 7 + [ANY] * len(deps),
+            [VMEM] * len(blocks),
+            (info, final, stats, own, *pulled, *deps),
             name="pull",
         )
 
     def beside(blocks):
-        return [swap(blocks[x], "member", x) for x in range(1, near)]
-
-    farthest = scaled(3 * near, near, [])
-    arrived = beside(farthest)
-    far = scaled(2 * near, near, arrived)
-    total = added([farthest[0], *arrived], graded)
-    total = added([far[0], *beside(far), swap(total, "member", near)], grads[1:])
-    close = scaled(0, 2 * near, [total])
-    parts = [swap(total, "member", 2 * near), close[0]]
-    parts += [swap(close[d], "member", d) for d in range(1, 2 * near)]
+        return [swap(block, "member", x) for x, block in enumerate(blocks, 1)]
+
+    along = list(range(near))
+    farthest, *rest, nearest = scaled([3 * near + x for x in along] + [near], [])
+    arrived = beside(rest)
+    nearest = swap(nearest, "member", near)
+    far, *others = scaled([2 * near + x for x in along], [*arrived, nearest, *graded])
+    total = swap(added([farthest, *arrived], graded), "member", near)
+    half = added([far, *beside(others)], grads[1:])
+    close = [*along[1:], *[near + x for x in along[1:]]]
+    kept, *sends = scaled([0, *close], [half])
+    parts = [swap(block, "member", d) for d, block in zip(close, sends)]
+    parts += [nearest, kept, swap(added([half, total], []), "member", 2 * near)]
 
     table_grad = call(
         functools.partial(scatter_kernel, members, groups, slots, count),

time: 108 us -> 111 us (1.028)
  blocking collectives: 12.2 us -> 0 us
  Pallas kernels: 35.2 us -> 41.6 us
  starting transfers between devices: 32 us -> 36.6 us
  waiting for transfers between devices: 23.3 us -> 27.5 us
    all_to_all x1 -> x0, blocking collectives: 12.2 us -> none  [shards(): lax.all_to_all(request, ('group', 'member'), split_axis=0, concat_axis=0,...]
    all_to_all x0 -> x1, waiting for transfers between devices: none -> 8.98 us  [shards(): lax.all_to_all(request, ('group', 'member'), split_axis=0, concat_axis=0,...]
    pallas_call x19 -> x21, Pallas kernels: 35.2 us -> 41.6 us  [call(): pl.pallas_call(kernel, out_shape=out_shape, in_specs=ins, out_specs=outs,...]
    ppermute x29, waiting for transfers between devices: 23.3 us -> 18.5 us  [swap(): lax.ppermute(value, axis, [(i, i ^ d) for i in range(lax.axis_size(axis))])]
    all_to_all x0 -> x1, starting transfers between devices: none -> 3.82 us  [shards(): lax.all_to_all(request, ('group', 'member'), split_axis=0, concat_axis=0,...]
  transfers between devices with their start and end apart: 29 -> 30, of which waited for: 8 -> 12; matrix products, arithmetic and copies ran while one was open for 0% -> 0% of each run, Pallas kernels for 29% -> 35%
where the time goes in v5:
time: 111 us; the launch traced here: 110 us
  Pallas kernels  41.6 us (37%)
  starting transfers between devices  36.6 us (33%)
  waiting for transfers between devices  27.5 us (25%)
  local copies, waits for them, and re-layouts  3.15 us (3%)
    pallas_call x21, Pallas kernels, call(): pl.pallas_call(kernel, out_shape=out_shape, in_specs=ins, out_specs=outs,...  41.6 us
    ppermute x29, starting transfers between devices, swap(): lax.ppermute(value, axis, [(i, i ^ d) for i in range(lax.axis_size(axis))])  32.7 us
    ppermute x29, waiting for transfers between devices, swap(): lax.ppermute(value, axis, [(i, i ^ d) for i in range(lax.axis_size(axis))])  18.5 us
    all_to_all x1, waiting for transfers between devices, shards(): lax.all_to_all(request, ('group', 'member'), split_axis=0, concat_axis=0,...  8.98 us
    all_to_all x1, starting transfers between devices, shards(): lax.all_to_all(request, ('group', 'member'), split_axis=0, concat_axis=0,...  3.82 us
    unnamed x6, local copies, waits for them, and re-layouts  3.15 us
  transfers between devices with their start and end apart: 30, of which 12 were waited for; matrix products, arithmetic and copies ran while one was open for 0% of the time, Pallas kernels for 35%

profile of v5, /device:TPU:0, one launch (start us, length us, event | category | flops | bytes accessed | tf_op | source)
XLA Modules:
  0.0 110.5 jit_solution(3556847861245182868)
XLA Ops:
  0.6 0.7 pad_add_fusion
  1.5 0.9 copy-done.1
  2.4 1.8 %front.1 = (s32[32,1,1024]{2,1,0:T(1,128)}, f32[256,256]{1,0:T(8,128)S(1)}) custom-call(s32[2]{0:T(128)S(1)} %pad_add_fusion.1.info, s32[1,1280]{1,0:T(1,128)S(1)} %reshape.15.ints, f32[256,256]{1,0:T(8,128)S(1)} %copy-done.1), custom_call_target="tpu_custom_call" | custom-call | tf_op jit(solution)/shard_map/front/pallas_call | solution.py:26
  4.2 4.0 %collective-permute-start = (f32[256,256]{1,0:T(8,128)S(1)}, f32[256,256]{1,0:T(8,128)S(1)}, u32[]{:S(2)}, u32[]{:S(2)}) collective-permute-start(f32[256,256]{1,0:T(8,128)S(1)} %get-tuple-element.42.refs_4_.refs_0_), channel_id=1, source_target_pairs={{0,4},{1,5},{2,6},{3,7},{4,0},{5,1},{6,2},{7,3},{8,12},{9,13},{10,... | collective-permute-start | bytes 786440 | tf_op jit(solution)/shard_map/ppermute | solution.py:369
  8.3 3.8 %all-to-all-start = ((s32[32,1,1024]{2,1,0:T(1,128)}), s32[32,1,1024]{2,1,0:T(1,128)S(1)}, u32[]{:S(2)}, u32[]{:S(2)}) async-start(s32[32,1,1024]{2,1,0:T(1,128)} %get-tuple-element.43), calls=%async_computation | async-start | bytes 262144 | tf_op jit(solution)/shard_map/all_to_all | solution.py:395
  12.1 1.8 %collective-permute-start.2 = (f32[256,256]{1,0:T(8,128)S(1)}, f32[256,256]{1,0:T(8,128)S(1)}, u32[]{:S(2)}, u32[]{:S(2)}) collective-permute-start(f32[256,256]{1,0:T(8,128)S(1)} %get-tuple-element.42.refs_4_.refs_0_), channel_id=1, source_target_pairs={{0,2},{1,3},{2,0},{3,1},{4,6},{5,7},{6,4},{7,5},{8,10},{9,11},{10,... | collective-permute-start | bytes 786440 | tf_op jit(solution)/shard_map/ppermute | solution.py:369
  13.9 1.5 %collective-permute-start.1 = (f32[256,256]{1,0:T(8,128)S(1)}, f32[256,256]{1,0:T(8,128)S(1)}, u32[]{:S(2)}, u32[]{:S(2)}) collective-permute-start(f32[256,256]{1,0:T(8,128)S(1)} %get-tuple-element.42.refs_4_.refs_0_), channel_id=1, source_target_pairs={{0,1},{1,0},{2,3},{3,2},{4,5},{5,4},{6,7},{7,6},{8,9},{9,8},{10,11... | collective-permute-start | bytes 786440 | tf_op jit(solution)/shard_map/ppermute | solution.py:369
  15.4 9.0 %all-to-all-done.got.got_v = s32[32,1,1024]{2,1,0:T(1,128)S(1)} async-done(((s32[32,1,1024]{2,1,0:T(1,128)}), s32[32,1,1024]{2,1,0:T(1,128)S(1)}, u32[]{:S(2)}, u32[]{:S(2)}) %all-to-all-start) | async-done | bytes 131104 | tf_op jit(solution)/shard_map/all_to_all | solution.py:395
  24.4 1.1 collective-permute-start.8
  25.8 1.3 %collective-permute-done.2.refs_1_.refs_6_.refs_2_ = f32[256,256]{1,0:T(8,128)S(1)} collective-permute-done((f32[256,256]{1,0:T(8,128)S(1)}, f32[256,256]{1,0:T(8,128)S(1)}, u32[]{:S(2)}, u32[]{:S(2)}) %collective-permute-start.2) | collective-permute-done | bytes 262176 | tf_op jit(solution)/shard_map/ppermute | solution.py:369
  27.1 2.2 %copy-done = f32[4096,256]{1,0:T(8,128)S(1)} copy-done((f32[4096,256]{1,0:T(8,128)S(1)}, f32[4096,256]{1,0:T(8,128)}, u32[]{:S(2)}) %copy-start) | copy-done | bytes 4194328
  29.3 3.9 %gather_negatives.1 = (f32[128,256]{1,0:T(8,128)S(1)}, f32[128,256]{1,0:T(8,128)S(1)}, f32[128,256]{1,0:T(8,128)S(1)}, f32[128,256]{1,0:T(8,128)S(1)}) custom-call(s32[2]{0:T(128)S(1)} %pad_add_fusion.1.info, s32[32,1,1024]{2,1,0:T(1,128)S(1)} %all-to-all-done.got.got_v, f32[4096,256]{1,0:T(8,128)S(1)} %copy-done, ...), custom_call_target="tpu_custom_call" | custom-call | tf_op jit(solution)/shard_map/gather_negatives/pallas_call | solution.py:26
  33.3 2.1 %collective-permute-start.4 = (f32[128,256]{1,0:T(8,128)S(1)}, f32[128,256]{1,0:T(8,128)S(1)}, u32[]{:S(2)}, u32[]{:S(2)}) collective-permute-start(f32[128,256]{1,0:T(8,128)S(1)} %get-tuple-element.47), channel_id=1, source_target_pairs={{0,16},{8,24},{16,0},{24,8},{1,17},{9,25},{17,1},{25,9},{2,18},{10... | collective-permute-start | bytes 393224 | tf_op jit(solution)/shard_map/ppermute | solution.py:369
  35.5 1.7 %collective-permute-start.6 = (f32[256,256]{1,0:T(8,128)S(1)}, f32[256,256]{1,0:T(8,128)S(1)}, u32[]{:S(2)}, u32[]{:S(2)}) collective-permute-start(f32[256,256]{1,0:T(8,128)S(1)} %collective-permute-done.2.refs_1_.refs_6_.refs_2_), channel_id=1, source_target_pairs={{0,1},{1,0},{2,3},{3,2},{4,5},{5,4},{6,7},{7,6},{8,9},{9,8},{10,11... | collective-permute-start | bytes 786440 | tf_op jit(solution)/shard_map/ppermute | solution.py:369
  37.1 0.4 collective-permute-start.9
  37.5 4.9 %gather_targets.1 = (f32[256,256]{1,0:T(8,128)S(1)}, f32[256,256]{1,0:T(8,128)S(1)}, f32[256,256]{1,0:T(8,128)S(1)}, f32[256,256]{1,0:T(8,128)S(1)}) custom-call(s32[2]{0:T(128)S(1)} %pad_add_fusion.1.info, s32[32,1,1024]{2,1,0:T(1,128)S(1)} %all-to-all-done.got.got_v, f32[4096,256]{1,0:T(8,128)S(1)} %copy-done), custom_call_target="tpu_custom_call" | custom-call | tf_op jit(solution)/shard_map/gather_targets/pallas_call | solution.py:26
  42.5 1.8 %collective-permute-start.11 = (f32[256,256]{1,0:T(8,128)S(1)}, f32[256,256]{1,0:T(8,128)S(1)}, u32[]{:S(2)}, u32[]{:S(2)}) collective-permute-start(f32[256,256]{1,0:T(8,128)S(1)} %get-tuple-element.54), channel_id=1, source_target_pairs={{0,16},{8,24},{16,0},{24,8},{1,17},{9,25},{17,1},{25,9},{2,18},{10... | collective-permute-start | bytes 786440 | tf_op jit(solution)/shard_map/ppermute | solution.py:369
  44.4 3.1 %score.2 = (f32[2,2048]{1,0:T(2,128)S(1)}, bf16[4,512,256]{2,1,0:T(8,128)(2,1)S(1)}, bf16[4,512,256]{2,1,0:T(8,128)(2,1)S(1)}) custom-call(s32[2]{0:T(128)S(1)} %pad_add_fusion.1.info, f32[128,256]{1,0:T(8,128)S(1)} %get-tuple-element.45.refs_0_, f32[128,256]{1,0:T(8,128)S(1)} %collective-permute-done.3.refs_1_, ...), custom_call_target="tpu_custom_call" | custom-call | flops 1610612736 | bytes 1048576 | tf_op jit(solution)/shard_map/score/pallas_call | solution.py:26
  47.5 2.1 %collective-permute-done.9.refs_7_.refs_11_ = f32[256,256]{1,0:T(8,128)S(1)} collective-permute-done((f32[256,256]{1,0:T(8,128)S(1)}, f32[256,256]{1,0:T(8,128)S(1)}, u32[]{:S(2)}, u32[]{:S(2)}) %collective-permute-start.9) | collective-permute-done | bytes 262176 | tf_op jit(solution)/shard_map/ppermute | solution.py:369
  49.6 1.6 %pick.1 = (f32[256,256]{1,0:T(8,128)S(1)}, f32[256,256]{1,0:T(8,128)S(1)}, f32[256,256]{1,0:T(8,128)S(1)}, f32[256,256]{1,0:T(8,128)S(1)}) custom-call(s32[2]{0:T(128)S(1)} %pad_add_fusion.1.info, s32[32,1,1024]{2,1,0:T(1,128)S(1)} %all-to-all-done.got.got_v, f32[256,256]{1,0:T(8,128)S(1)} %get-tuple-element.42.refs_4_.refs_0_, ...), custom_call_target="tpu_custom_call" | custom-call | tf_op jit(solution)/shard_map/pick/pallas_call | solution.py:26
  51.3 1.9 %collective-permute-start.19 = (f32[256,256]{1,0:T(8,128)S(1)}, f32[256,256]{1,0:T(8,128)S(1)}, u32[]{:S(2)}, u32[]{:S(2)}) collective-permute-start(f32[256,256]{1,0:T(8,128)S(1)} %get-tuple-element.58.refs_6_), channel_id=1, source_target_pairs={{0,16},{8,24},{16,0},{24,8},{1,17},{9,25},{17,1},{25,9},{2,18},{10... | collective-permute-start | bytes 786440 | tf_op jit(solution)/shard_map/ppermute | solution.py:369
  53.1 3.1 %score.3 = (f32[2,2048]{1,0:T(2,128)S(1)}, bf16[4,512,256]{2,1,0:T(8,128)(2,1)S(1)}, bf16[4,512,256]{2,1,0:T(8,128)(2,1)S(1)}) custom-call(s32[2]{0:T(128)S(1)} %pad_add_fusion.1.info, f32[128,256]{1,0:T(8,128)S(1)} %get-tuple-element.45.refs_0_, f32[128,256]{1,0:T(8,128)S(1)} %collective-permute-done.3.refs_1_, ...), custom_call_target="tpu_custom_call" | custom-call | flops 1610612736 | bytes 1048576 | tf_op jit(solution)/shard_map/score/pallas_call | solution.py:26
  56.5 1.2 %positive.1 = (f32[2,2048]{1,0:T(2,128)S(1)}, f32[2,2048]{1,0:T(2,128)S(1)}) custom-call(s32[2]{0:T(128)S(1)} %pad_add_fusion.1.info, s32[32,1,1024]{2,1,0:T(1,128)S(1)} %all-to-all-done.got.got_v, f32[2,2048]{1,0:T(2,128)S(1)} %get-tuple-element.51.stats, f32[256,256]{1,0:T(8,128)S(1)} %get-tuple-element.52.refs_0_.refs_4_, ...), custom_call_target="tpu_custom_call" | custom-call | tf_op jit(solution)/shard_map/positive/pallas_call | solution.py:26
  57.8 1.6 %collective-permute-start.13 = (f32[2,2048]{1,0:T(2,128)S(1)}, f32[2,2048]{1,0:T(2,128)S(1)}, u32[]{:S(2)}, u32[]{:S(2)}) collective-permute-start(f32[2,2048]{1,0:T(2,128)S(1)} %get-tuple-element.60.first), channel_id=1, source_target_pairs={{0,1},{1,0},{2,3},{3,2},{4,5},{5,4},{6,7},{7,6},{8,9},{9,8},{10,11... | collective-permute-start | bytes 49160 | tf_op jit(solution)/shard_map/ppermute | solution.py:369
  59.3 2.0 %pulled.2 = (f32[4,256,256]{2,1,0:T(8,128)S(1)}, f32[4,256,256]{2,1,0:T(8,128)S(1)}) custom-call(s32[2]{0:T(128)S(1)} %pad_add_fusion.1.info, s32[32,1,1024]{2,1,0:T(1,128)S(1)} %all-to-all-done.got.got_v, f32[128,256]{1,0:T(8,128)S(1)} %get-tuple-element.45.refs_0_, f32[128,256]{1,0:T(8,128)S(1)} %collective-permute-done.3.refs_1_, ...), custom_call_target="tpu_custom_call" | custom-call | flops 805306368 | bytes 1048576 | tf_op jit(solution)/shard_map/pulled/pallas_call | solution.py:26
  61.7 2.0 %pulled.3 = (f32[4,256,256]{2,1,0:T(8,128)S(1)}, f32[4,256,256]{2,1,0:T(8,128)S(1)}) custom-call(s32[2]{0:T(128)S(1)} %pad_add_fusion.1.info, s32[32,1,1024]{2,1,0:T(1,128)S(1)} %all-to-all-done.got.got_v, f32[128,256]{1,0:T(8,128)S(1)} %get-tuple-element.45.refs_0_, f32[128,256]{1,0:T(8,128)S(1)} %collective-permute-done.3.refs_1_, ...), custom_call_target="tpu_custom_call" | custom-call | flops 805306368 | bytes 1048576 | tf_op jit(solution)/shard_map/pulled/pallas_call | solution.py:26
  63.6 1.7 %collective-permute-done.14.second = f32[2,2048]{1,0:T(2,128)S(1)} collective-permute-done((f32[2,2048]{1,0:T(2,128)S(1)}, f32[2,2048]{1,0:T(2,128)S(1)}, u32[]{:S(2)}, u32[]{:S(2)}) %collective-permute-start.14) | collective-permute-done | bytes 16416 | tf_op jit(solution)/shard_map/ppermute | solution.py:369
  65.4 2.5 %collective-permute-start.15 = (f32[2,2048]{1,0:T(2,128)S(1)}, f32[2,2048]{1,0:T(2,128)S(1)}, u32[]{:S(2)}, u32[]{:S(2)}) collective-permute-start(f32[2,2048]{1,0:T(2,128)S(1)} %join.4.first), channel_id=1, source_target_pairs={{0,4},{1,5},{2,6},{3,7},{4,0},{5,1},{6,2},{7,3},{8,12},{9,13},{10,... | collective-permute-start | bytes 49160 | tf_op jit(solution)/shard_map/ppermute | solution.py:369
  67.9 2.2 %collective-permute-done.15.second = f32[2,2048]{1,0:T(2,128)S(1)} collective-permute-done((f32[2,2048]{1,0:T(2,128)S(1)}, f32[2,2048]{1,0:T(2,128)S(1)}, u32[]{:S(2)}, u32[]{:S(2)}) %collective-permute-start.15) | collective-permute-done | bytes 16416 | tf_op jit(solution)/shard_map/ppermute | solution.py:369
  70.1 0.7 pull.3
  70.8 1.6 %collective-permute-start.16 = (f32[256,256]{1,0:T(8,128)S(1)}, f32[256,256]{1,0:T(8,128)S(1)}, u32[]{:S(2)}, u32[]{:S(2)}) collective-permute-start(f32[256,256]{1,0:T(8,128)S(1)} %get-tuple-element.70), channel_id=1, source_target_pairs={{0,1},{1,0},{2,3},{3,2},{4,5},{5,4},{6,7},{7,6},{8,9},{9,8},{10,11... | collective-permute-start | bytes 786440 | tf_op jit(solution)/shard_map/ppermute | solution.py:369
  72.3 1.2 %collective-permute-start.17 = (f32[256,256]{1,0:T(8,128)S(1)}, f32[256,256]{1,0:T(8,128)S(1)}, u32[]{:S(2)}, u32[]{:S(2)}) collective-permute-start(f32[256,256]{1,0:T(8,128)S(1)} %get-tuple-element.71), channel_id=1, source_target_pairs={{0,2},{1,3},{2,0},{3,1},{4,6},{5,7},{6,4},{7,5},{8,10},{9,11},{10,... | collective-permute-start | bytes 786440 | tf_op jit(solution)/shard_map/ppermute | solution.py:369
  73.6 2.7 %grad.1 = (f32[136,256]{1,0:T(8,128)S(1)}, f32[136,256]{1,0:T(8,128)S(1)}, f32[136,256]{1,0:T(8,128)S(1)}, f32[136,256]{1,0:T(8,128)S(1)}) custom-call(s32[2]{0:T(128)S(1)} %pad_add_fusion.1.info, s32[32,1,1024]{2,1,0:T(1,128)S(1)} %all-to-all-done.got.got_v, f32[2,2048]{1,0:T(2,128)S(1)} %join.5.final, f32[2,2048]{1,0:T(2,128)S(1)} %get-tuple-element.51.stats, ...), custom_call_target="tpu_custom_call" | custom-call | flops 1610612736 | bytes 8388608 | tf_op jit(solution)/shard_map/grad/pallas_call | solution.py:26
  76.2 1.4 %collective-permute-done.16.refs_4_.refs_1_ = f32[256,256]{1,0:T(8,128)S(1)} collective-permute-done((f32[256,256]{1,0:T(8,128)S(1)}, f32[256,256]{1,0:T(8,128)S(1)}, u32[]{:S(2)}, u32[]{:S(2)}) %collective-permute-start.16) | collective-permute-done | bytes 262176 | tf_op jit(solution)/shard_map/ppermute | solution.py:369
  77.6 1.1 %collective-permute-done.17.refs_5_.refs_2_ = f32[256,256]{1,0:T(8,128)S(1)} collective-permute-done((f32[256,256]{1,0:T(8,128)S(1)}, f32[256,256]{1,0:T(8,128)S(1)}, u32[]{:S(2)}, u32[]{:S(2)}) %collective-permute-start.17) | collective-permute-done | bytes 262176 | tf_op jit(solution)/shard_map/ppermute | solution.py:369
  78.7 0.6 pull.4
  79.3 0.7 collective-permute-start.21
  80.1 1.2 %collective-permute-start.27 = (f32[256,256]{1,0:T(8,128)S(1)}, f32[256,256]{1,0:T(8,128)S(1)}, u32[]{:S(2)}, u32[]{:S(2)}) collective-permute-start(f32[256,256]{1,0:T(8,128)S(1)} %add.12), channel_id=1, source_target_pairs={{0,2},{1,3},{2,0},{3,1},{4,6},{5,7},{6,4},{7,5},{8,10},{9,11},{10,... | collective-permute-start | bytes 786440 | tf_op jit(solution)/shard_map/ppermute | solution.py:369
  81.3 1.5 %collective-permute-start.23 = (f32[136,256]{1,0:T(8,128)S(1)}, f32[136,256]{1,0:T(8,128)S(1)}, u32[]{:S(2)}, u32[]{:S(2)}) collective-permute-start(f32[136,256]{1,0:T(8,128)S(1)} %get-tuple-element.76), channel_id=1, source_target_pairs={{0,16},{8,24},{16,0},{24,8},{1,17},{9,25},{17,1},{25,9},{2,18},{10... | collective-permute-start | bytes 417800 | tf_op jit(solution)/shard_map/ppermute | solution.py:369
  83.2 4.6 %collective-permute-done.23.refs_3_.refs_2_ = f32[136,256]{1,0:T(8,128)S(1)} collective-permute-done((f32[136,256]{1,0:T(8,128)S(1)}, f32[136,256]{1,0:T(8,128)S(1)}, u32[]{:S(2)}, u32[]{:S(2)}) %collective-permute-start.23) | collective-permute-done | bytes 139296 | tf_op jit(solution)/shard_map/ppermute | solution.py:369
  87.8 2.2 %collective-permute-done.24.refs_4_.refs_3_ = f32[136,256]{1,0:T(8,128)S(1)} collective-permute-done((f32[136,256]{1,0:T(8,128)S(1)}, f32[136,256]{1,0:T(8,128)S(1)}, u32[]{:S(2)}, u32[]{:S(2)}) %collective-permute-start.24) | collective-permute-done | bytes 139296 | tf_op jit(solution)/shard_map/ppermute | solution.py:369
  90.0 0.7 pull.5
  90.8 3.0 %collective-permute-start.28 = (f32[256,256]{1,0:T(8,128)S(1)}, f32[256,256]{1,0:T(8,128)S(1)}, u32[]{:S(2)}, u32[]{:S(2)}) collective-permute-start(f32[256,256]{1,0:T(8,128)S(1)} %add.13), channel_id=1, source_target_pairs={{0,4},{1,5},{2,6},{3,7},{4,0},{5,1},{6,2},{7,3},{8,12},{9,13},{10,... | collective-permute-start | bytes 786440 | tf_op jit(solution)/shard_map/ppermute | solution.py:369
  93.8 1.4 %collective-permute-start.25 = (f32[256,256]{1,0:T(8,128)S(1)}, f32[256,256]{1,0:T(8,128)S(1)}, u32[]{:S(2)}, u32[]{:S(2)}) collective-permute-start(f32[256,256]{1,0:T(8,128)S(1)} %get-tuple-element.78), channel_id=1, source_target_pairs={{0,1},{1,0},{2,3},{3,2},{4,5},{5,4},{6,7},{7,6},{8,9},{9,8},{10,11... | collective-permute-start | bytes 786440 | tf_op jit(solution)/shard_map/ppermute | solution.py:369
  95.2 0.6 collective-permute-start.26
  95.8 12.3 %scatter.1 = f32[4096,256]{1,0:T(8,128)} custom-call(s32[2]{0:T(128)S(1)} %pad_add_fusion.1.info, s32[32,1,1024]{2,1,0:T(1,128)S(1)} %all-to-all-done.got.got_v, s32[32,1,1024]{2,1,0:T(1,128)S(1)} %all-to-all-done.got.got_v, f32[136,256]{1,0:T(8,128)S(1)} %get-tuple-element.72.refs_6_.refs_2_.refs_0_, ...), custom_call_target="tpu_custom_call" | custom-call | tf_op jit(solution)/shard_map/scatter/pallas_call | solution.py:26
  108.1 1.4 %collective-permute-done.26.refs_1_ = f32[256,256]{1,0:T(8,128)S(1)} collective-permute-done((f32[256,256]{1,0:T(8,128)S(1)}, f32[256,256]{1,0:T(8,128)S(1)}, u32[]{:S(2)}, u32[]{:S(2)}) %collective-permute-start.26) | collective-permute-done | bytes 262176 | tf_op jit(solution)/shard_map/ppermute | solution.py:369
  109.5 1.0 finish.1
  (42 shorter events, 2.1 us)
Async XLA Ops:
  1.5 1.0 copy-start.1
  4.2 20.2 %collective-permute-start = (f32[256,256]{1,0:T(8,128)S(1)}, f32[256,256]{1,0:T(8,128)S(1)}, u32[]{:S(2)}, u32[]{:S(2)}) collective-permute-start(f32[256,256]{1,0:T(8,128)S(1)} %get-tuple-element.42.refs_4_.refs_0_), channel_id=1, source_target_pairs={{0,4},{1,5},{2,6},{3,7},{4,0},{5,1},{6,2},{7,3},{8,12},{9,13},{10,... | collective-permute-start | bytes 786440 | tf_op jit(solution)/shard_map/ppermute | solution.py:369
  8.3 16.1 %all-to-all-start = ((s32[32,1,1024]{2,1,0:T(1,128)}), s32[32,1,1024]{2,1,0:T(1,128)S(1)}, u32[]{:S(2)}, u32[]{:S(2)}) async-start(s32[32,1,1024]{2,1,0:T(1,128)} %get-tuple-element.43), calls=%async_computation | async-start | bytes 262144 | tf_op jit(solution)/shard_map/all_to_all | solution.py:395
  12.1 15.0 %collective-permute-start.2 = (f32[256,256]{1,0:T(8,128)S(1)}, f32[256,256]{1,0:T(8,128)S(1)}, u32[]{:S(2)}, u32[]{:S(2)}) collective-permute-start(f32[256,256]{1,0:T(8,128)S(1)} %get-tuple-element.42.refs_4_.refs_0_), channel_id=1, source_target_pairs={{0,2},{1,3},{2,0},{3,1},{4,6},{5,7},{6,4},{7,5},{8,10},{9,11},{10,... | collective-permute-start | bytes 786440 | tf_op jit(solution)/shard_map/ppermute | solution.py:369
  13.9 13.2 %collective-permute-start.1 = (f32[256,256]{1,0:T(8,128)S(1)}, f32[256,256]{1,0:T(8,128)S(1)}, u32[]{:S(2)}, u32[]{:S(2)}) collective-permute-start(f32[256,256]{1,0:T(8,128)S(1)} %get-tuple-element.42.refs_4_.refs_0_), channel_id=1, source_target_pairs={{0,1},{1,0},{2,3},{3,2},{4,5},{5,4},{6,7},{7,6},{8,9},{9,8},{10,11... | collective-permute-start | bytes 786440 | tf_op jit(solution)/shard_map/ppermute | solution.py:369
  24.4 12.8 %collective-permute-start.8 = (f32[256,256]{1,0:T(8,128)S(1)}, f32[256,256]{1,0:T(8,128)S(1)}, u32[]{:S(2)}, u32[]{:S(2)}) collective-permute-start(f32[256,256]{1,0:T(8,128)S(1)} %collective-permute-done.refs_2_.refs_7_.refs_4_.refs_8_), channel_id=1, source_target_pairs={{0,2},{1,3},{2,0},{3,1},{4,6},{5,7},{6,4},{7,5},{8,10},{9,11},{10,... | collective-permute-start | bytes 786440 | tf_op jit(solution)/shard_map/ppermute | solution.py:369
  25.5 18.8 %collective-permute-start.7 = (f32[256,256]{1,0:T(8,128)S(1)}, f32[256,256]{1,0:T(8,128)S(1)}, u32[]{:S(2)}, u32[]{:S(2)}) collective-permute-start(f32[256,256]{1,0:T(8,128)S(1)} %collective-permute-done.refs_2_.refs_7_.refs_4_.refs_8_), channel_id=1, source_target_pairs={{0,1},{1,0},{2,3},{3,2},{4,5},{5,4},{6,7},{7,6},{8,9},{9,8},{10,11... | collective-permute-start | bytes 786440 | tf_op jit(solution)/shard_map/ppermute | solution.py:369
  27.1 2.2 %copy-start = (f32[4096,256]{1,0:T(8,128)S(1)}, f32[4096,256]{1,0:T(8,128)}, u32[]{:S(2)}) copy-start(f32[4096,256]{1,0:T(8,128)} %table.3) | copy-start | bytes 12582916
  33.3 2.2 %collective-permute-start.3 = (f32[128,256]{1,0:T(8,128)S(1)}, f32[128,256]{1,0:T(8,128)S(1)}, u32[]{:S(2)}, u32[]{:S(2)}) collective-permute-start(f32[128,256]{1,0:T(8,128)S(1)} %get-tuple-element.46), channel_id=1, source_target_pairs={{0,8},{8,0},{16,24},{24,16},{1,9},{9,1},{17,25},{25,17},{2,10},{10... | collective-permute-start | bytes 393224 | tf_op jit(solution)/shard_map/ppermute | solution.py:369
  33.3 9.1 %collective-permute-start.4 = (f32[128,256]{1,0:T(8,128)S(1)}, f32[128,256]{1,0:T(8,128)S(1)}, u32[]{:S(2)}, u32[]{:S(2)}) collective-permute-start(f32[128,256]{1,0:T(8,128)S(1)} %get-tuple-element.47), channel_id=1, source_target_pairs={{0,16},{8,24},{16,0},{24,8},{1,17},{9,25},{17,1},{25,9},{2,18},{10... | collective-permute-start | bytes 393224 | tf_op jit(solution)/shard_map/ppermute | solution.py:369
  35.4 7.1 %collective-permute-start.5 = (f32[128,256]{1,0:T(8,128)S(1)}, f32[128,256]{1,0:T(8,128)S(1)}, u32[]{:S(2)}, u32[]{:S(2)}) collective-permute-start(f32[128,256]{1,0:T(8,128)S(1)} %get-tuple-element.48), channel_id=1, source_target_pairs={{0,24},{8,16},{16,8},{24,0},{1,25},{9,17},{17,9},{25,1},{2,26},{10... | collective-permute-start | bytes 393224 | tf_op jit(solution)/shard_map/ppermute | solution.py:369
  35.5 12.0 %collective-permute-start.6 = (f32[256,256]{1,0:T(8,128)S(1)}, f32[256,256]{1,0:T(8,128)S(1)}, u32[]{:S(2)}, u32[]{:S(2)}) collective-permute-start(f32[256,256]{1,0:T(8,128)S(1)} %collective-permute-done.2.refs_1_.refs_6_.refs_2_), channel_id=1, source_target_pairs={{0,1},{1,0},{2,3},{3,2},{4,5},{5,4},{6,7},{7,6},{8,9},{9,8},{10,11... | collective-permute-start | bytes 786440 | tf_op jit(solution)/shard_map/ppermute | solution.py:369
  37.1 12.4 %collective-permute-start.9 = (f32[256,256]{1,0:T(8,128)S(1)}, f32[256,256]{1,0:T(8,128)S(1)}, u32[]{:S(2)}, u32[]{:S(2)}) collective-permute-start(f32[256,256]{1,0:T(8,128)S(1)} %collective-permute-done.8.refs_6_.refs_10_), channel_id=1, source_target_pairs={{0,1},{1,0},{2,3},{3,2},{4,5},{5,4},{6,7},{7,6},{8,9},{9,8},{10,11... | collective-permute-start | bytes 786440 | tf_op jit(solution)/shard_map/ppermute | solution.py:369
  42.4 13.8 %collective-permute-start.10 = (f32[256,256]{1,0:T(8,128)S(1)}, f32[256,256]{1,0:T(8,128)S(1)}, u32[]{:S(2)}, u32[]{:S(2)}) collective-permute-start(f32[256,256]{1,0:T(8,128)S(1)} %get-tuple-element.53), channel_id=1, source_target_pairs={{0,8},{8,0},{16,24},{24,16},{1,9},{9,1},{17,25},{25,17},{2,10},{10... | collective-permute-start | bytes 786440 | tf_op jit(solution)/shard_map/ppermute | solution.py:369
  42.5 13.8 %collective-permute-start.11 = (f32[256,256]{1,0:T(8,128)S(1)}, f32[256,256]{1,0:T(8,128)S(1)}, u32[]{:S(2)}, u32[]{:S(2)}) collective-permute-start(f32[256,256]{1,0:T(8,128)S(1)} %get-tuple-element.54), channel_id=1, source_target_pairs={{0,16},{8,24},{16,0},{24,8},{1,17},{9,25},{17,1},{25,9},{2,18},{10... | collective-permute-start | bytes 786440 | tf_op jit(solution)/shard_map/ppermute | solution.py:369
  44.3 12.2 %collective-permute-start.12 = (f32[256,256]{1,0:T(8,128)S(1)}, f32[256,256]{1,0:T(8,128)S(1)}, u32[]{:S(2)}, u32[]{:S(2)}) collective-permute-start(f32[256,256]{1,0:T(8,128)S(1)} %get-tuple-element.55), channel_id=1, source_target_pairs={{0,24},{8,16},{16,8},{24,0},{1,25},{9,17},{17,9},{25,1},{2,26},{10... | collective-permute-start | bytes 786440 | tf_op jit(solution)/shard_map/ppermute | solution.py:369
  51.2 22.4 %collective-permute-start.18 = (f32[256,256]{1,0:T(8,128)S(1)}, f32[256,256]{1,0:T(8,128)S(1)}, u32[]{:S(2)}, u32[]{:S(2)}) collective-permute-start(f32[256,256]{1,0:T(8,128)S(1)} %get-tuple-element.57.refs_5_), channel_id=1, source_target_pairs={{0,8},{8,0},{16,24},{24,16},{1,9},{9,1},{17,25},{25,17},{2,10},{10... | collective-permute-start | bytes 786440 | tf_op jit(solution)/shard_map/ppermute | solution.py:369
  51.3 22.3 %collective-permute-start.19 = (f32[256,256]{1,0:T(8,128)S(1)}, f32[256,256]{1,0:T(8,128)S(1)}, u32[]{:S(2)}, u32[]{:S(2)}) collective-permute-start(f32[256,256]{1,0:T(8,128)S(1)} %get-tuple-element.58.refs_6_), channel_id=1, source_target_pairs={{0,16},{8,24},{16,0},{24,8},{1,17},{9,25},{17,1},{25,9},{2,18},{10... | collective-permute-start | bytes 786440 | tf_op jit(solution)/shard_map/ppermute | solution.py:369
  56.2 17.3 %collective-permute-start.20 = (f32[256,256]{1,0:T(8,128)S(1)}, f32[256,256]{1,0:T(8,128)S(1)}, u32[]{:S(2)}, u32[]{:S(2)}) collective-permute-start(f32[256,256]{1,0:T(8,128)S(1)} %get-tuple-element.59.refs_7_), channel_id=1, source_target_pairs={{0,24},{8,16},{16,8},{24,0},{1,25},{9,17},{17,9},{25,1},{2,26},{10... | collective-permute-start | bytes 786440 | tf_op jit(solution)/shard_map/ppermute | solution.py:369
  57.8 3.8 %collective-permute-start.13 = (f32[2,2048]{1,0:T(2,128)S(1)}, f32[2,2048]{1,0:T(2,128)S(1)}, u32[]{:S(2)}, u32[]{:S(2)}) collective-permute-start(f32[2,2048]{1,0:T(2,128)S(1)} %get-tuple-element.60.first), channel_id=1, source_target_pairs={{0,1},{1,0},{2,3},{3,2},{4,5},{5,4},{6,7},{7,6},{8,9},{9,8},{10,11... | collective-permute-start | bytes 49160 | tf_op jit(solution)/shard_map/ppermute | solution.py:369
  61.6 3.8 %collective-permute-start.14 = (f32[2,2048]{1,0:T(2,128)S(1)}, f32[2,2048]{1,0:T(2,128)S(1)}, u32[]{:S(2)}, u32[]{:S(2)}) collective-permute-start(f32[2,2048]{1,0:T(2,128)S(1)} %join.3.first), channel_id=1, source_target_pairs={{0,2},{1,3},{2,0},{3,1},{4,6},{5,7},{6,4},{7,5},{8,10},{9,11},{10,... | collective-permute-start | bytes 49160 | tf_op jit(solution)/shard_map/ppermute | solution.py:369
  65.4 4.7 %collective-permute-start.15 = (f32[2,2048]{1,0:T(2,128)S(1)}, f32[2,2048]{1,0:T(2,128)S(1)}, u32[]{:S(2)}, u32[]{:S(2)}) collective-permute-start(f32[2,2048]{1,0:T(2,128)S(1)} %join.4.first), channel_id=1, source_target_pairs={{0,4},{1,5},{2,6},{3,7},{4,0},{5,1},{6,2},{7,3},{8,12},{9,13},{10,... | collective-permute-start | bytes 49160 | tf_op jit(solution)/shard_map/ppermute | solution.py:369
  70.8 6.8 %collective-permute-start.16 = (f32[256,256]{1,0:T(8,128)S(1)}, f32[256,256]{1,0:T(8,128)S(1)}, u32[]{:S(2)}, u32[]{:S(2)}) collective-permute-start(f32[256,256]{1,0:T(8,128)S(1)} %get-tuple-element.70), channel_id=1, source_target_pairs={{0,1},{1,0},{2,3},{3,2},{4,5},{5,4},{6,7},{7,6},{8,9},{9,8},{10,11... | collective-permute-start | bytes 786440 | tf_op jit(solution)/shard_map/ppermute | solution.py:369
  72.3 6.4 %collective-permute-start.17 = (f32[256,256]{1,0:T(8,128)S(1)}, f32[256,256]{1,0:T(8,128)S(1)}, u32[]{:S(2)}, u32[]{:S(2)}) collective-permute-start(f32[256,256]{1,0:T(8,128)S(1)} %get-tuple-element.71), channel_id=1, source_target_pairs={{0,2},{1,3},{2,0},{3,1},{4,6},{5,7},{6,4},{7,5},{8,10},{9,11},{10,... | collective-permute-start | bytes 786440 | tf_op jit(solution)/shard_map/ppermute | solution.py:369
  79.3 10.7 %collective-permute-start.21 = (f32[256,256]{1,0:T(8,128)S(1)}, f32[256,256]{1,0:T(8,128)S(1)}, u32[]{:S(2)}, u32[]{:S(2)}) collective-permute-start(f32[256,256]{1,0:T(8,128)S(1)} %get-tuple-element.74), channel_id=1, source_target_pairs={{0,1},{1,0},{2,3},{3,2},{4,5},{5,4},{6,7},{7,6},{8,9},{9,8},{10,11... | collective-permute-start | bytes 786440 | tf_op jit(solution)/shard_map/ppermute | solution.py:369
  80.1 10.7 %collective-permute-start.27 = (f32[256,256]{1,0:T(8,128)S(1)}, f32[256,256]{1,0:T(8,128)S(1)}, u32[]{:S(2)}, u32[]{:S(2)}) collective-permute-start(f32[256,256]{1,0:T(8,128)S(1)} %add.12), channel_id=1, source_target_pairs={{0,2},{1,3},{2,0},{3,1},{4,6},{5,7},{6,4},{7,5},{8,10},{9,11},{10,... | collective-permute-start | bytes 786440 | tf_op jit(solution)/shard_map/ppermute | solution.py:369
  81.3 1.9 %collective-permute-start.22 = (f32[136,256]{1,0:T(8,128)S(1)}, f32[136,256]{1,0:T(8,128)S(1)}, u32[]{:S(2)}, u32[]{:S(2)}) collective-permute-start(f32[136,256]{1,0:T(8,128)S(1)} %get-tuple-element.75), channel_id=1, source_target_pairs={{0,8},{8,0},{16,24},{24,16},{1,9},{9,1},{17,25},{25,17},{2,10},{10... | collective-permute-start | bytes 417800 | tf_op jit(solution)/shard_map/ppermute | solution.py:369
  81.3 6.5 %collective-permute-start.23 = (f32[136,256]{1,0:T(8,128)S(1)}, f32[136,256]{1,0:T(8,128)S(1)}, u32[]{:S(2)}, u32[]{:S(2)}) collective-permute-start(f32[136,256]{1,0:T(8,128)S(1)} %get-tuple-element.76), channel_id=1, source_target_pairs={{0,16},{8,24},{16,0},{24,8},{1,17},{9,25},{17,1},{25,9},{2,18},{10... | collective-permute-start | bytes 417800 | tf_op jit(solution)/shard_map/ppermute | solution.py:369
  82.8 7.2 %collective-permute-start.24 = (f32[136,256]{1,0:T(8,128)S(1)}, f32[136,256]{1,0:T(8,128)S(1)}, u32[]{:S(2)}, u32[]{:S(2)}) collective-permute-start(f32[136,256]{1,0:T(8,128)S(1)} %get-tuple-element.77), channel_id=1, source_target_pairs={{0,24},{8,16},{16,8},{24,0},{1,25},{9,17},{17,9},{25,1},{2,26},{10... | collective-permute-start | bytes 417800 | tf_op jit(solution)/shard_map/ppermute | solution.py:369
  90.7 18.8 %copy-start.2 = (s32[256]{0:T(256)S(1)}, s32[256]{0:T(256)}, u32[]{:S(2)}) copy-start(s32[256]{0:T(256)} %param.11) | copy-start | bytes 3076
  90.8 17.3 %collective-permute-start.28 = (f32[256,256]{1,0:T(8,128)S(1)}, f32[256,256]{1,0:T(8,128)S(1)}, u32[]{:S(2)}, u32[]{:S(2)}) collective-permute-start(f32[256,256]{1,0:T(8,128)S(1)} %add.13), channel_id=1, source_target_pairs={{0,4},{1,5},{2,6},{3,7},{4,0},{5,1},{6,2},{7,3},{8,12},{9,13},{10,... | collective-permute-start | bytes 786440 | tf_op jit(solution)/shard_map/ppermute | solution.py:369
  93.8 14.4 %collective-permute-start.25 = (f32[256,256]{1,0:T(8,128)S(1)}, f32[256,256]{1,0:T(8,128)S(1)}, u32[]{:S(2)}, u32[]{:S(2)}) collective-permute-start(f32[256,256]{1,0:T(8,128)S(1)} %get-tuple-element.78), channel_id=1, source_target_pairs={{0,1},{1,0},{2,3},{3,2},{4,5},{5,4},{6,7},{7,6},{8,9},{9,8},{10,11... | collective-permute-start | bytes 786440 | tf_op jit(solution)/shard_map/ppermute | solution.py:369
  95.2 14.3 %collective-permute-start.26 = (f32[256,256]{1,0:T(8,128)S(1)}, f32[256,256]{1,0:T(8,128)S(1)}, u32[]{:S(2)}, u32[]{:S(2)}) collective-permute-start(f32[256,256]{1,0:T(8,128)S(1)} %get-tuple-element.79), channel_id=1, source_target_pairs={{0,3},{1,2},{2,1},{3,0},{4,7},{5,6},{6,5},{7,4},{8,11},{9,10},{10,... | collective-permute-start | bytes 786440 | tf_op jit(solution)/shard_map/ppermute | solution.py:369

commit v6 on v5

--- a/solution.py
+++ b/solution.py
@@ -120,9 +120,6 @@
     low = low + table(hot, (local & 63).astype(F32), place)
     out_ref[:, 0, 0:LANES] = high.astype(I32) * 64 + low.astype(I32)
     out_ref[:, 0, LANES : 2 * LANES] = position.astype(I32)
-    if out_ref.shape[2] > 2 * LANES:
-        rest = out_ref.shape[2] - 2 * LANES
-        out_ref[:, 0, 2 * LANES :] = jnp.zeros((devices, rest), I32)
 
 
 def gather_kernel(members, groups, part, count, info, got, table, *refs):
@@ -302,10 +299,11 @@
     return same.astype(F32)
 
 
-def scatter_kernel(members, groups, slots, count, info, got_v, got, *refs):
-    grads, picked = refs[:groups], refs[groups : 2 * groups]
-    out, negs, tgts = refs[2 * groups :]
-    out[...] = jnp.zeros_like(out)
+def scatter_kernel(members, groups, own, slots, count, info, got_v, got, *refs):
+    size = len(own)
+    grads, picked = refs[:size], refs[size : 2 * size]
+    out, negs, tgts = refs[-3:]
+    out[...] = refs[2 * size][...] if own[0] else jnp.zeros_like(out)
 
     def add_rows(asked, first, source, base, number):
         for b in range(0, number, BATCH):
@@ -317,16 +315,16 @@
             for k in range(BATCH):
                 out[pl.ds(rows[k], 1), :] = new[k]
 
-    for d in range(groups):
+    for i, d in enumerate(own):
         g = info[0] ^ d
         asked = got_v[pl.ds(g * members, members), 0, 0:LANES]
         number = members * count
         same = as_bf16(equal_in_batch(flat(asked, slots, count)) > 0)
-        high, low = split(grads[d][0:number, :])
+        high, low = split(grads[i][0:number, :])
         negs[...] = dot1(same, high, NN) + dot1(same, low, NN)
         weight = equal_in_batch(flat(asked, 0, slots))
-        weight = weight * grads[d][number : number + 1, 0 : members * slots]
-        tgts[...] = dot3(split(weight), split(picked[d][...]), NN)
+        weight = weight * grads[i][number : number + 1, 0 : members * slots]
+        tgts[...] = dot3(split(weight), split(picked[i][...]), NN)
         merged = BATCH // count if count < BATCH else 1
 
         def member(step, carry, g=g, merged=merged):
@@ -386,7 +384,7 @@
     ints = jnp.concatenate([target_owner.reshape(-1), target_local, valid, negative_ids])
     request, masked = call(
         functools.partial(front_kernel, members, rows_dev, slots, tokens, negatives),
-        [shape((devices, 1, max(2 * LANES, (1 << 15) // devices)), I32), sds(tokens, width)],
+        [shape((devices, 1, 2 * LANES), I32), sds(tokens, width)],
         [SMEM] + [VMEM] * 2,
         [VMEM] * 2,
         (info, ints.reshape(1, -1), encoded),
@@ -525,29 +523,34 @@
         return [swap(block, "member", x) for x, block in enumerate(blocks, 1)]
 
     along = list(range(near))
+    def scatter(own, base, deps, flops):
+        return call(
+            functools.partial(scatter_kernel, members, groups, own, slots, count),
+            sds(rows_dev, width),
+            [SMEM, VMEM, SMEM] + [VMEM] * (2 * len(own) + len(base)) + [ANY] * len(deps),
+            VMEM,
+            (info, got, got, *[grads[d] for d in own], *[sent[d] for d in own], *base, *deps),
+            scratch=[
+                pltpu.VMEM((members * count, width), F32),
+                pltpu.VMEM((members * slots, width), F32),
+            ],
+            flops=flops,
+            name="scatter",
+        )
+
+    table_own = scatter([0], [], grads[1:], 1 << 33)
     farthest, *rest, nearest = scaled([3 * near + x for x in along] + [near], [])
     arrived = beside(rest)
     nearest = swap(nearest, "member", near)
     far, *others = scaled([2 * near + x for x in along], [*arrived, nearest, *graded])
     total = swap(added([farthest, *arrived], graded), "member", near)
-    half = added([far, *beside(others)], grads[1:])
+    half = added([far, *beside(others)], [table_own])
     close = [*along[1:], *[near + x for x in along[1:]]]
     kept, *sends = scaled([0, *close], [half])
     parts = [swap(block, "member", d) for d, block in zip(close, sends)]
     parts += [nearest, kept, swap(added([half, total], []), "member", 2 * near)]
 
-    table_grad = call(
-        functools.partial(scatter_kernel, members, groups, slots, count),
-        sds(rows_dev, width),
-        [SMEM, VMEM, SMEM] + [VMEM] * (2 * groups),
-        VMEM,
-        (info, got, got, *grads, *sent),
-        scratch=[
-            pltpu.VMEM((members * count, width), F32),
-            pltpu.VMEM((members * slots, width), F32),
-        ],
-        name="scatter",
-    )
+    table_grad = scatter(list(range(1, groups)), [table_own], [], 0)
     encoded_grad = call(
         finish_kernel,
         sds(tokens, width),

time: 111 us -> 102 us (0.919)
  waiting for transfers between devices: 27.5 us -> 14.4 us
  blocking collectives: 0 us -> 12.2 us
  Pallas kernels: 41.6 us -> 37.5 us
  starting transfers between devices: 36.6 us -> 33.2 us
    all_to_all x0 -> x1, blocking collectives: none -> 12.2 us  [shards(): lax.all_to_all(request, ('group', 'member'), split_axis=0, concat_axis=0,...]
    all_to_all x1 -> x0, waiting for transfers between devices: 8.98 us -> none  [shards(): lax.all_to_all(request, ('group', 'member'), split_axis=0, concat_axis=0,...]
    pallas_call x21 -> x22, Pallas kernels: 41.6 us -> 37.5 us  [call(): pl.pallas_call(kernel, out_shape=out_shape, in_specs=ins, out_specs=outs,...]
    ppermute x29, waiting for transfers between devices: 18.5 us -> 14.4 us  [swap(): lax.ppermute(value, axis, [(i, i ^ d) for i in range(lax.axis_size(axis))])]
    all_to_all x1 -> x0, starting transfers between devices: 3.82 us -> none  [shards(): lax.all_to_all(request, ('group', 'member'), split_axis=0, concat_axis=0,...]
  transfers between devices with their start and end apart: 30 -> 29, of which waited for: 12 -> 9; matrix products, arithmetic and copies ran while one was open for 0% -> 0% of each run, Pallas kernels for 35% -> 35%
where the time goes in v6:
time: 102 us
  Pallas kernels  37.5 us (37%)
  starting transfers between devices  33.2 us (33%)
  waiting for transfers between devices  14.4 us (14%)
  blocking collectives  12.2 us (12%)
  local copies, waits for them, and re-layouts  3.15 us (3%)
    pallas_call x22, Pallas kernels, call(): pl.pallas_call(kernel, out_shape=out_shape, in_specs=ins, out_specs=outs,...  37.5 us
    ppermute x29, starting transfers between devices, swap(): lax.ppermute(value, axis, [(i, i ^ d) for i in range(lax.axis_size(axis))])  33.2 us
    ppermute x29, waiting for transfers between devices, swap(): lax.ppermute(value, axis, [(i, i ^ d) for i in range(lax.axis_size(axis))])  14.4 us
    all_to_all x1, blocking collectives, shards(): lax.all_to_all(request, ('group', 'member'), split_axis=0, concat_axis=0,...  12.2 us
    unnamed x6, local copies, waits for them, and re-layouts  3.14 us
  transfers between devices with their start and end apart: 29, of which 9 were waited for; matrix products, arithmetic and copies ran while one was open for 0% of the time, Pallas kernels for 35%

profile of v6, /device:TPU:0, one launch (start us, length us, event | category | flops | bytes accessed | tf_op | source)
XLA Modules:
  0.0 102.1 jit_solution(1255770746180908619)
XLA Ops:
  0.6 0.7 pad_add_fusion
  1.5 0.9 copy-done.1
  2.4 1.2 %front.1 = (s32[32,1,256]{2,1,0:T(1,128)S(1)}, f32[256,256]{1,0:T(8,128)S(1)}) custom-call(s32[2]{0:T(128)S(1)} %pad_add_fusion.1.info, s32[1,1280]{1,0:T(1,128)S(1)} %reshape.15.ints, f32[256,256]{1,0:T(8,128)S(1)} %copy-done.1), custom_call_target="tpu_custom_call" | custom-call | tf_op jit(solution)/shard_map/front/pallas_call | solution.py:26
  3.6 4.1 %collective-permute-start = (f32[256,256]{1,0:T(8,128)S(1)}, f32[256,256]{1,0:T(8,128)S(1)}, u32[]{:S(2)}, u32[]{:S(2)}) collective-permute-start(f32[256,256]{1,0:T(8,128)S(1)} %get-tuple-element.42.refs_4_.refs_0_), channel_id=1, source_target_pairs={{0,4},{1,5},{2,6},{3,7},{4,0},{5,1},{6,2},{7,3},{8,12},{9,13},{10,... | collective-permute-start | bytes 786440 | tf_op jit(solution)/shard_map/ppermute | solution.py:367
  7.7 1.6 %collective-permute-start.2 = (f32[256,256]{1,0:T(8,128)S(1)}, f32[256,256]{1,0:T(8,128)S(1)}, u32[]{:S(2)}, u32[]{:S(2)}) collective-permute-start(f32[256,256]{1,0:T(8,128)S(1)} %get-tuple-element.42.refs_4_.refs_0_), channel_id=1, source_target_pairs={{0,2},{1,3},{2,0},{3,1},{4,6},{5,7},{6,4},{7,5},{8,10},{9,11},{10,... | collective-permute-start | bytes 786440 | tf_op jit(solution)/shard_map/ppermute | solution.py:367
  9.3 1.5 %collective-permute-start.1 = (f32[256,256]{1,0:T(8,128)S(1)}, f32[256,256]{1,0:T(8,128)S(1)}, u32[]{:S(2)}, u32[]{:S(2)}) collective-permute-start(f32[256,256]{1,0:T(8,128)S(1)} %get-tuple-element.42.refs_4_.refs_0_), channel_id=1, source_target_pairs={{0,1},{1,0},{2,3},{3,2},{4,5},{5,4},{6,7},{7,6},{8,9},{9,8},{10,11... | collective-permute-start | bytes 786440 | tf_op jit(solution)/shard_map/ppermute | solution.py:367
  10.8 12.2 %all_to_all.5.got.got_v = s32[32,1,256]{2,1,0:T(1,128)S(1)} all-to-all(s32[32,1,256]{2,1,0:T(1,128)S(1)} %get-tuple-element.43), channel_id=1, replica_groups=mesh['group'=4,'member'=8] {'group','member'}, dimensions={0} | all-to-all | bytes 65536 | tf_op jit(solution)/shard_map/all_to_all | solution.py:393
  22.9 0.7 collective-permute-start.8
  23.7 0.7 collective-permute-start.6
  24.3 2.2 %copy-done = f32[4096,256]{1,0:T(8,128)S(1)} copy-done((f32[4096,256]{1,0:T(8,128)S(1)}, f32[4096,256]{1,0:T(8,128)}, u32[]{:S(2)}) %copy-start) | copy-done | bytes 4194328
  26.5 2.3 %gather_negatives.1 = (f32[128,256]{1,0:T(8,128)S(1)}, f32[128,256]{1,0:T(8,128)S(1)}, f32[128,256]{1,0:T(8,128)S(1)}, f32[128,256]{1,0:T(8,128)S(1)}) custom-call(s32[2]{0:T(128)S(1)} %pad_add_fusion.1.info, s32[32,1,256]{2,1,0:T(1,128)S(1)} %all_to_all.5.got.got_v, f32[4096,256]{1,0:T(8,128)S(1)} %copy-done, ...), custom_call_target="tpu_custom_call" | custom-call | tf_op jit(solution)/shard_map/gather_negatives/pallas_call | solution.py:26
  29.6 1.2 %collective-permute-start.5 = (f32[128,256]{1,0:T(8,128)S(1)}, f32[128,256]{1,0:T(8,128)S(1)}, u32[]{:S(2)}, u32[]{:S(2)}) collective-permute-start(f32[128,256]{1,0:T(8,128)S(1)} %get-tuple-element.48), channel_id=1, source_target_pairs={{0,24},{8,16},{16,8},{24,0},{1,25},{9,17},{17,9},{25,1},{2,26},{10... | collective-permute-start | bytes 393224 | tf_op jit(solution)/shard_map/ppermute | solution.py:367
  30.8 1.4 %collective-permute-start.7 = (f32[256,256]{1,0:T(8,128)S(1)}, f32[256,256]{1,0:T(8,128)S(1)}, u32[]{:S(2)}, u32[]{:S(2)}) collective-permute-start(f32[256,256]{1,0:T(8,128)S(1)} %collective-permute-done.refs_2_.refs_7_.refs_4_.refs_8_), channel_id=1, source_target_pairs={{0,1},{1,0},{2,3},{3,2},{4,5},{5,4},{6,7},{7,6},{8,9},{9,8},{10,11... | collective-permute-start | bytes 786440 | tf_op jit(solution)/shard_map/ppermute | solution.py:367
  32.1 0.7 collective-permute-start.9
  32.8 3.3 %gather_targets.1 = (f32[256,256]{1,0:T(8,128)S(1)}, f32[256,256]{1,0:T(8,128)S(1)}, f32[256,256]{1,0:T(8,128)S(1)}, f32[256,256]{1,0:T(8,128)S(1)}) custom-call(s32[2]{0:T(128)S(1)} %pad_add_fusion.1.info, s32[32,1,256]{2,1,0:T(1,128)S(1)} %all_to_all.5.got.got_v, f32[4096,256]{1,0:T(8,128)S(1)} %copy-done), custom_call_target="tpu_custom_call" | custom-call | tf_op jit(solution)/shard_map/gather_targets/pallas_call | solution.py:26
  36.2 1.0 collective-permute-done.5.refs_3_
  37.8 1.3 %collective-permute-start.12 = (f32[256,256]{1,0:T(8,128)S(1)}, f32[256,256]{1,0:T(8,128)S(1)}, u32[]{:S(2)}, u32[]{:S(2)}) collective-permute-start(f32[256,256]{1,0:T(8,128)S(1)} %get-tuple-element.55), channel_id=1, source_target_pairs={{0,24},{8,16},{16,8},{24,0},{1,25},{9,17},{17,9},{25,1},{2,26},{10... | collective-permute-start | bytes 786440 | tf_op jit(solution)/shard_map/ppermute | solution.py:367
  39.1 3.1 %score.2 = (f32[2,2048]{1,0:T(2,128)S(1)}, bf16[4,512,256]{2,1,0:T(8,128)(2,1)S(1)}, bf16[4,512,256]{2,1,0:T(8,128)(2,1)S(1)}) custom-call(s32[2]{0:T(128)S(1)} %pad_add_fusion.1.info, f32[128,256]{1,0:T(8,128)S(1)} %get-tuple-element.45.refs_0_, f32[128,256]{1,0:T(8,128)S(1)} %collective-permute-done.3.refs_1_, ...), custom_call_target="tpu_custom_call" | custom-call | flops 1610612736 | bytes 1048576 | tf_op jit(solution)/shard_map/score/pallas_call | solution.py:26
  42.2 2.8 %collective-permute-done.9.refs_7_.refs_11_ = f32[256,256]{1,0:T(8,128)S(1)} collective-permute-done((f32[256,256]{1,0:T(8,128)S(1)}, f32[256,256]{1,0:T(8,128)S(1)}, u32[]{:S(2)}, u32[]{:S(2)}) %collective-permute-start.9) | collective-permute-done | bytes 262176 | tf_op jit(solution)/shard_map/ppermute | solution.py:367
  45.0 1.6 %pick.1 = (f32[256,256]{1,0:T(8,128)S(1)}, f32[256,256]{1,0:T(8,128)S(1)}, f32[256,256]{1,0:T(8,128)S(1)}, f32[256,256]{1,0:T(8,128)S(1)}) custom-call(s32[2]{0:T(128)S(1)} %pad_add_fusion.1.info, s32[32,1,256]{2,1,0:T(1,128)S(1)} %all_to_all.5.got.got_v, f32[256,256]{1,0:T(8,128)S(1)} %get-tuple-element.42.refs_4_.refs_0_, ...), custom_call_target="tpu_custom_call" | custom-call | tf_op jit(solution)/shard_map/pick/pallas_call | solution.py:26
  47.3 1.2 %collective-permute-start.20 = (f32[256,256]{1,0:T(8,128)S(1)}, f32[256,256]{1,0:T(8,128)S(1)}, u32[]{:S(2)}, u32[]{:S(2)}) collective-permute-start(f32[256,256]{1,0:T(8,128)S(1)} %get-tuple-element.59.refs_7_), channel_id=1, source_target_pairs={{0,24},{8,16},{16,8},{24,0},{1,25},{9,17},{17,9},{25,1},{2,26},{10... | collective-permute-start | bytes 786440 | tf_op jit(solution)/shard_map/ppermute | solution.py:367
  48.5 3.1 %score.3 = (f32[2,2048]{1,0:T(2,128)S(1)}, bf16[4,512,256]{2,1,0:T(8,128)(2,1)S(1)}, bf16[4,512,256]{2,1,0:T(8,128)(2,1)S(1)}) custom-call(s32[2]{0:T(128)S(1)} %pad_add_fusion.1.info, f32[128,256]{1,0:T(8,128)S(1)} %get-tuple-element.45.refs_0_, f32[128,256]{1,0:T(8,128)S(1)} %collective-permute-done.3.refs_1_, ...), custom_call_target="tpu_custom_call" | custom-call | flops 1610612736 | bytes 1048576 | tf_op jit(solution)/shard_map/score/pallas_call | solution.py:26
  51.6 1.2 %positive.1 = (f32[2,2048]{1,0:T(2,128)S(1)}, f32[2,2048]{1,0:T(2,128)S(1)}) custom-call(s32[2]{0:T(128)S(1)} %pad_add_fusion.1.info, s32[32,1,256]{2,1,0:T(1,128)S(1)} %all_to_all.5.got.got_v, f32[2,2048]{1,0:T(2,128)S(1)} %get-tuple-element.51.stats, f32[256,256]{1,0:T(8,128)S(1)} %get-tuple-element.52.refs_0_.refs_4_, ...), custom_call_target="tpu_custom_call" | custom-call | tf_op jit(solution)/shard_map/positive/pallas_call | solution.py:26
  52.8 1.4 %collective-permute-start.13 = (f32[2,2048]{1,0:T(2,128)S(1)}, f32[2,2048]{1,0:T(2,128)S(1)}, u32[]{:S(2)}, u32[]{:S(2)}) collective-permute-start(f32[2,2048]{1,0:T(2,128)S(1)} %get-tuple-element.60.first), channel_id=1, source_target_pairs={{0,1},{1,0},{2,3},{3,2},{4,5},{5,4},{6,7},{7,6},{8,9},{9,8},{10,11... | collective-permute-start | bytes 49160 | tf_op jit(solution)/shard_map/ppermute | solution.py:367
  54.2 2.0 %pulled.2 = (f32[4,256,256]{2,1,0:T(8,128)S(1)}, f32[4,256,256]{2,1,0:T(8,128)S(1)}) custom-call(s32[2]{0:T(128)S(1)} %pad_add_fusion.1.info, s32[32,1,256]{2,1,0:T(1,128)S(1)} %all_to_all.5.got.got_v, f32[128,256]{1,0:T(8,128)S(1)} %get-tuple-element.45.refs_0_, f32[128,256]{1,0:T(8,128)S(1)} %collective-permute-done.3.refs_1_, ...), custom_call_target="tpu_custom_call" | custom-call | flops 805306368 | bytes 1048576 | tf_op jit(solution)/shard_map/pulled/pallas_call | solution.py:26
  56.6 1.4 %collective-permute-start.14 = (f32[2,2048]{1,0:T(2,128)S(1)}, f32[2,2048]{1,0:T(2,128)S(1)}, u32[]{:S(2)}, u32[]{:S(2)}) collective-permute-start(f32[2,2048]{1,0:T(2,128)S(1)} %join.3.first), channel_id=1, source_target_pairs={{0,2},{1,3},{2,0},{3,1},{4,6},{5,7},{6,4},{7,5},{8,10},{9,11},{10,... | collective-permute-start | bytes 49160 | tf_op jit(solution)/shard_map/ppermute | solution.py:367
  58.0 2.0 %pulled.3 = (f32[4,256,256]{2,1,0:T(8,128)S(1)}, f32[4,256,256]{2,1,0:T(8,128)S(1)}) custom-call(s32[2]{0:T(128)S(1)} %pad_add_fusion.1.info, s32[32,1,256]{2,1,0:T(1,128)S(1)} %all_to_all.5.got.got_v, f32[128,256]{1,0:T(8,128)S(1)} %get-tuple-element.45.refs_0_, f32[128,256]{1,0:T(8,128)S(1)} %collective-permute-done.3.refs_1_, ...), custom_call_target="tpu_custom_call" | custom-call | flops 805306368 | bytes 1048576 | tf_op jit(solution)/shard_map/pulled/pallas_call | solution.py:26
  60.5 2.6 %collective-permute-start.15 = (f32[2,2048]{1,0:T(2,128)S(1)}, f32[2,2048]{1,0:T(2,128)S(1)}, u32[]{:S(2)}, u32[]{:S(2)}) collective-permute-start(f32[2,2048]{1,0:T(2,128)S(1)} %join.4.first), channel_id=1, source_target_pairs={{0,4},{1,5},{2,6},{3,7},{4,0},{5,1},{6,2},{7,3},{8,12},{9,13},{10,... | collective-permute-start | bytes 49160 | tf_op jit(solution)/shard_map/ppermute | solution.py:367
  63.0 2.1 %collective-permute-done.15.second = f32[2,2048]{1,0:T(2,128)S(1)} collective-permute-done((f32[2,2048]{1,0:T(2,128)S(1)}, f32[2,2048]{1,0:T(2,128)S(1)}, u32[]{:S(2)}, u32[]{:S(2)}) %collective-permute-start.15) | collective-permute-done | bytes 16416 | tf_op jit(solution)/shard_map/ppermute | solution.py:367
  65.2 0.7 pull.3
  65.9 1.4 %collective-permute-start.16 = (f32[256,256]{1,0:T(8,128)S(1)}, f32[256,256]{1,0:T(8,128)S(1)}, u32[]{:S(2)}, u32[]{:S(2)}) collective-permute-start(f32[256,256]{1,0:T(8,128)S(1)} %get-tuple-element.70), channel_id=1, source_target_pairs={{0,1},{1,0},{2,3},{3,2},{4,5},{5,4},{6,7},{7,6},{8,9},{9,8},{10,11... | collective-permute-start | bytes 786440 | tf_op jit(solution)/shard_map/ppermute | solution.py:367
  67.3 1.3 %collective-permute-start.17 = (f32[256,256]{1,0:T(8,128)S(1)}, f32[256,256]{1,0:T(8,128)S(1)}, u32[]{:S(2)}, u32[]{:S(2)}) collective-permute-start(f32[256,256]{1,0:T(8,128)S(1)} %get-tuple-element.71), channel_id=1, source_target_pairs={{0,2},{1,3},{2,0},{3,1},{4,6},{5,7},{6,4},{7,5},{8,10},{9,11},{10,... | collective-permute-start | bytes 786440 | tf_op jit(solution)/shard_map/ppermute | solution.py:367
  68.6 2.6 %grad.1 = (f32[136,256]{1,0:T(8,128)S(1)}, f32[136,256]{1,0:T(8,128)S(1)}, f32[136,256]{1,0:T(8,128)S(1)}, f32[136,256]{1,0:T(8,128)S(1)}) custom-call(s32[2]{0:T(128)S(1)} %pad_add_fusion.1.info, s32[32,1,256]{2,1,0:T(1,128)S(1)} %all_to_all.5.got.got_v, f32[2,2048]{1,0:T(2,128)S(1)} %join.5.final, f32[2,2048]{1,0:T(2,128)S(1)} %get-tuple-element.51.stats, ...), custom_call_target="tpu_custom_call" | custom-call | flops 1610612736 | bytes 8388608 | tf_op jit(solution)/shard_map/grad/pallas_call | solution.py:26
  71.3 0.7 collective-permute-start.23
  72.1 1.1 %collective-permute-start.24 = (f32[136,256]{1,0:T(8,128)S(1)}, f32[136,256]{1,0:T(8,128)S(1)}, u32[]{:S(2)}, u32[]{:S(2)}) collective-permute-start(f32[136,256]{1,0:T(8,128)S(1)} %get-tuple-element.77), channel_id=1, source_target_pairs={{0,24},{8,16},{16,8},{24,0},{1,25},{9,17},{17,9},{25,1},{2,26},{10... | collective-permute-start | bytes 417800 | tf_op jit(solution)/shard_map/ppermute | solution.py:367
  73.2 0.8 collective-permute-start.27
  74.7 1.1 %collective-permute-start.21 = (f32[256,256]{1,0:T(8,128)S(1)}, f32[256,256]{1,0:T(8,128)S(1)}, u32[]{:S(2)}, u32[]{:S(2)}) collective-permute-start(f32[256,256]{1,0:T(8,128)S(1)} %get-tuple-element.74), channel_id=1, source_target_pairs={{0,1},{1,0},{2,3},{3,2},{4,5},{5,4},{6,7},{7,6},{8,9},{9,8},{10,11... | collective-permute-start | bytes 786440 | tf_op jit(solution)/shard_map/ppermute | solution.py:367
  75.8 2.1 %collective-permute-done.23.refs_3_.refs_1_ = f32[136,256]{1,0:T(8,128)S(1)} collective-permute-done((f32[136,256]{1,0:T(8,128)S(1)}, f32[136,256]{1,0:T(8,128)S(1)}, u32[]{:S(2)}, u32[]{:S(2)}) %collective-permute-start.23) | collective-permute-done | bytes 139296 | tf_op jit(solution)/shard_map/ppermute | solution.py:367
  77.9 2.1 %collective-permute-done.24.refs_4_.refs_2_ = f32[136,256]{1,0:T(8,128)S(1)} collective-permute-done((f32[136,256]{1,0:T(8,128)S(1)}, f32[136,256]{1,0:T(8,128)S(1)}, u32[]{:S(2)}, u32[]{:S(2)}) %collective-permute-start.24) | collective-permute-done | bytes 139296 | tf_op jit(solution)/shard_map/ppermute | solution.py:367
  80.0 3.3 %scatter.2.refs_2_.refs_6_ = f32[4096,256]{1,0:T(8,128)S(1)} custom-call(s32[2]{0:T(128)S(1)} %pad_add_fusion.1.info, s32[32,1,256]{2,1,0:T(1,128)S(1)} %all_to_all.5.got.got_v, s32[32,1,256]{2,1,0:T(1,128)S(1)} %all_to_all.5.got.got_v, f32[136,256]{1,0:T(8,128)S(1)} %get-tuple-element.72.refs_6_.refs_0_.refs_2_, ...), custom_call_target="tpu_custom_call" | custom-call | flops 8589934592 | tf_op jit(solution)/shard_map/scatter/pallas_call | solution.py:26
  83.3 0.7 pull.5
  84.0 0.7 collective-permute-start.25
  84.7 1.8 %collective-permute-start.26 = (f32[256,256]{1,0:T(8,128)S(1)}, f32[256,256]{1,0:T(8,128)S(1)}, u32[]{:S(2)}, u32[]{:S(2)}) collective-permute-start(f32[256,256]{1,0:T(8,128)S(1)} %get-tuple-element.79), channel_id=1, source_target_pairs={{0,3},{1,2},{2,1},{3,0},{4,7},{5,6},{6,5},{7,4},{8,11},{9,10},{10,... | collective-permute-start | bytes 786440 | tf_op jit(solution)/shard_map/ppermute | solution.py:367
  86.6 2.3 %collective-permute-start.28 = (f32[256,256]{1,0:T(8,128)S(1)}, f32[256,256]{1,0:T(8,128)S(1)}, u32[]{:S(2)}, u32[]{:S(2)}) collective-permute-start(f32[256,256]{1,0:T(8,128)S(1)} %add.13), channel_id=1, source_target_pairs={{0,4},{1,5},{2,6},{3,7},{4,0},{5,1},{6,2},{7,3},{8,12},{9,13},{10,... | collective-permute-start | bytes 786440 | tf_op jit(solution)/shard_map/ppermute | solution.py:367
  88.9 8.8 %scatter.3 = f32[4096,256]{1,0:T(8,128)} custom-call(s32[2]{0:T(128)S(1)} %pad_add_fusion.1.info, s32[32,1,256]{2,1,0:T(1,128)S(1)} %all_to_all.5.got.got_v, s32[32,1,256]{2,1,0:T(1,128)S(1)} %all_to_all.5.got.got_v, f32[136,256]{1,0:T(8,128)S(1)} %collective-permute-done.22.refs_2_.refs_0_, f32[136,256]{1,0:T(8,128)S(1)} %collective-permute-done.23.refs_3_.refs_1_, ...), custom_call_target="tpu_custom_call" | custom-call | tf_op jit(solution)/shard_map/scatter/pallas_call | solution.py:26
  97.7 2.0 %collective-permute-done.26.refs_1_ = f32[256,256]{1,0:T(8,128)S(1)} collective-permute-done((f32[256,256]{1,0:T(8,128)S(1)}, f32[256,256]{1,0:T(8,128)S(1)}, u32[]{:S(2)}, u32[]{:S(2)}) %collective-permute-start.26) | collective-permute-done | bytes 262176 | tf_op jit(solution)/shard_map/ppermute | solution.py:367
  99.7 1.5 %collective-permute-done.28.refs_4_ = f32[256,256]{1,0:T(8,128)S(1)} collective-permute-done((f32[256,256]{1,0:T(8,128)S(1)}, f32[256,256]{1,0:T(8,128)S(1)}, u32[]{:S(2)}, u32[]{:S(2)}) %collective-permute-start.28) | collective-permute-done | bytes 262176 | tf_op jit(solution)/shard_map/ppermute | solution.py:367
  101.1 1.0 finish.1
  (42 shorter events, 3.9 us)
Async XLA Ops:
  1.5 1.0 copy-start.1
  3.6 19.4 %collective-permute-start = (f32[256,256]{1,0:T(8,128)S(1)}, f32[256,256]{1,0:T(8,128)S(1)}, u32[]{:S(2)}, u32[]{:S(2)}) collective-permute-start(f32[256,256]{1,0:T(8,128)S(1)} %get-tuple-element.42.refs_4_.refs_0_), channel_id=1, source_target_pairs={{0,4},{1,5},{2,6},{3,7},{4,0},{5,1},{6,2},{7,3},{8,12},{9,13},{10,... | collective-permute-start | bytes 786440 | tf_op jit(solution)/shard_map/ppermute | solution.py:367
  7.7 16.0 %collective-permute-start.2 = (f32[256,256]{1,0:T(8,128)S(1)}, f32[256,256]{1,0:T(8,128)S(1)}, u32[]{:S(2)}, u32[]{:S(2)}) collective-permute-start(f32[256,256]{1,0:T(8,128)S(1)} %get-tuple-element.42.refs_4_.refs_0_), channel_id=1, source_target_pairs={{0,2},{1,3},{2,0},{3,1},{4,6},{5,7},{6,4},{7,5},{8,10},{9,11},{10,... | collective-permute-start | bytes 786440 | tf_op jit(solution)/shard_map/ppermute | solution.py:367
  9.3 15.1 %collective-permute-start.1 = (f32[256,256]{1,0:T(8,128)S(1)}, f32[256,256]{1,0:T(8,128)S(1)}, u32[]{:S(2)}, u32[]{:S(2)}) collective-permute-start(f32[256,256]{1,0:T(8,128)S(1)} %get-tuple-element.42.refs_4_.refs_0_), channel_id=1, source_target_pairs={{0,1},{1,0},{2,3},{3,2},{4,5},{5,4},{6,7},{7,6},{8,9},{9,8},{10,11... | collective-permute-start | bytes 786440 | tf_op jit(solution)/shard_map/ppermute | solution.py:367
  22.9 9.2 %collective-permute-start.8 = (f32[256,256]{1,0:T(8,128)S(1)}, f32[256,256]{1,0:T(8,128)S(1)}, u32[]{:S(2)}, u32[]{:S(2)}) collective-permute-start(f32[256,256]{1,0:T(8,128)S(1)} %collective-permute-done.refs_2_.refs_7_.refs_4_.refs_8_), channel_id=1, source_target_pairs={{0,2},{1,3},{2,0},{3,1},{4,6},{5,7},{6,4},{7,5},{8,10},{9,11},{10,... | collective-permute-start | bytes 786440 | tf_op jit(solution)/shard_map/ppermute | solution.py:367
  23.7 14.1 %collective-permute-start.6 = (f32[256,256]{1,0:T(8,128)S(1)}, f32[256,256]{1,0:T(8,128)S(1)}, u32[]{:S(2)}, u32[]{:S(2)}) collective-permute-start(f32[256,256]{1,0:T(8,128)S(1)} %collective-permute-done.2.refs_1_.refs_6_.refs_2_), channel_id=1, source_target_pairs={{0,1},{1,0},{2,3},{3,2},{4,5},{5,4},{6,7},{7,6},{8,9},{9,8},{10,11... | collective-permute-start | bytes 786440 | tf_op jit(solution)/shard_map/ppermute | solution.py:367
  24.3 2.2 %copy-start = (f32[4096,256]{1,0:T(8,128)S(1)}, f32[4096,256]{1,0:T(8,128)}, u32[]{:S(2)}) copy-start(f32[4096,256]{1,0:T(8,128)} %table.3) | copy-start | bytes 12582916
  28.8 1.9 %collective-permute-start.3 = (f32[128,256]{1,0:T(8,128)S(1)}, f32[128,256]{1,0:T(8,128)S(1)}, u32[]{:S(2)}, u32[]{:S(2)}) collective-permute-start(f32[128,256]{1,0:T(8,128)S(1)} %get-tuple-element.46), channel_id=1, source_target_pairs={{0,8},{8,0},{16,24},{24,16},{1,9},{9,1},{17,25},{25,17},{2,10},{10... | collective-permute-start | bytes 393224 | tf_op jit(solution)/shard_map/ppermute | solution.py:367
  28.9 7.2 %collective-permute-start.4 = (f32[128,256]{1,0:T(8,128)S(1)}, f32[128,256]{1,0:T(8,128)S(1)}, u32[]{:S(2)}, u32[]{:S(2)}) collective-permute-start(f32[128,256]{1,0:T(8,128)S(1)} %get-tuple-element.47), channel_id=1, source_target_pairs={{0,16},{8,24},{16,0},{24,8},{1,17},{9,25},{17,1},{25,9},{2,18},{10... | collective-permute-start | bytes 393224 | tf_op jit(solution)/shard_map/ppermute | solution.py:367
  29.6 7.6 %collective-permute-start.5 = (f32[128,256]{1,0:T(8,128)S(1)}, f32[128,256]{1,0:T(8,128)S(1)}, u32[]{:S(2)}, u32[]{:S(2)}) collective-permute-start(f32[128,256]{1,0:T(8,128)S(1)} %get-tuple-element.48), channel_id=1, source_target_pairs={{0,24},{8,16},{16,8},{24,0},{1,25},{9,17},{17,9},{25,1},{2,26},{10... | collective-permute-start | bytes 393224 | tf_op jit(solution)/shard_map/ppermute | solution.py:367
  30.8 11.4 %collective-permute-start.7 = (f32[256,256]{1,0:T(8,128)S(1)}, f32[256,256]{1,0:T(8,128)S(1)}, u32[]{:S(2)}, u32[]{:S(2)}) collective-permute-start(f32[256,256]{1,0:T(8,128)S(1)} %collective-permute-done.refs_2_.refs_7_.refs_4_.refs_8_), channel_id=1, source_target_pairs={{0,1},{1,0},{2,3},{3,2},{4,5},{5,4},{6,7},{7,6},{8,9},{9,8},{10,11... | collective-permute-start | bytes 786440 | tf_op jit(solution)/shard_map/ppermute | solution.py:367
  32.1 12.8 %collective-permute-start.9 = (f32[256,256]{1,0:T(8,128)S(1)}, f32[256,256]{1,0:T(8,128)S(1)}, u32[]{:S(2)}, u32[]{:S(2)}) collective-permute-start(f32[256,256]{1,0:T(8,128)S(1)} %collective-permute-done.8.refs_6_.refs_10_), channel_id=1, source_target_pairs={{0,1},{1,0},{2,3},{3,2},{4,5},{5,4},{6,7},{7,6},{8,9},{9,8},{10,11... | collective-permute-start | bytes 786440 | tf_op jit(solution)/shard_map/ppermute | solution.py:367
  36.1 11.2 %collective-permute-start.10 = (f32[256,256]{1,0:T(8,128)S(1)}, f32[256,256]{1,0:T(8,128)S(1)}, u32[]{:S(2)}, u32[]{:S(2)}) collective-permute-start(f32[256,256]{1,0:T(8,128)S(1)} %get-tuple-element.53), channel_id=1, source_target_pairs={{0,8},{8,0},{16,24},{24,16},{1,9},{9,1},{17,25},{25,17},{2,10},{10... | collective-permute-start | bytes 786440 | tf_op jit(solution)/shard_map/ppermute | solution.py:367
  37.2 14.4 %collective-permute-start.11 = (f32[256,256]{1,0:T(8,128)S(1)}, f32[256,256]{1,0:T(8,128)S(1)}, u32[]{:S(2)}, u32[]{:S(2)}) collective-permute-start(f32[256,256]{1,0:T(8,128)S(1)} %get-tuple-element.54), channel_id=1, source_target_pairs={{0,16},{8,24},{16,0},{24,8},{1,17},{9,25},{17,1},{25,9},{2,18},{10... | collective-permute-start | bytes 786440 | tf_op jit(solution)/shard_map/ppermute | solution.py:367
  37.8 13.8 %collective-permute-start.12 = (f32[256,256]{1,0:T(8,128)S(1)}, f32[256,256]{1,0:T(8,128)S(1)}, u32[]{:S(2)}, u32[]{:S(2)}) collective-permute-start(f32[256,256]{1,0:T(8,128)S(1)} %get-tuple-element.55), channel_id=1, source_target_pairs={{0,24},{8,16},{16,8},{24,0},{1,25},{9,17},{17,9},{25,1},{2,26},{10... | collective-permute-start | bytes 786440 | tf_op jit(solution)/shard_map/ppermute | solution.py:367
  46.6 22.0 %collective-permute-start.18 = (f32[256,256]{1,0:T(8,128)S(1)}, f32[256,256]{1,0:T(8,128)S(1)}, u32[]{:S(2)}, u32[]{:S(2)}) collective-permute-start(f32[256,256]{1,0:T(8,128)S(1)} %get-tuple-element.57.refs_5_), channel_id=1, source_target_pairs={{0,8},{8,0},{16,24},{24,16},{1,9},{9,1},{17,25},{25,17},{2,10},{10... | collective-permute-start | bytes 786440 | tf_op jit(solution)/shard_map/ppermute | solution.py:367
  46.6 22.0 %collective-permute-start.19 = (f32[256,256]{1,0:T(8,128)S(1)}, f32[256,256]{1,0:T(8,128)S(1)}, u32[]{:S(2)}, u32[]{:S(2)}) collective-permute-start(f32[256,256]{1,0:T(8,128)S(1)} %get-tuple-element.58.refs_6_), channel_id=1, source_target_pairs={{0,16},{8,24},{16,0},{24,8},{1,17},{9,25},{17,1},{25,9},{2,18},{10... | collective-permute-start | bytes 786440 | tf_op jit(solution)/shard_map/ppermute | solution.py:367
  47.3 21.3 %collective-permute-start.20 = (f32[256,256]{1,0:T(8,128)S(1)}, f32[256,256]{1,0:T(8,128)S(1)}, u32[]{:S(2)}, u32[]{:S(2)}) collective-permute-start(f32[256,256]{1,0:T(8,128)S(1)} %get-tuple-element.59.refs_7_), channel_id=1, source_target_pairs={{0,24},{8,16},{16,8},{24,0},{1,25},{9,17},{17,9},{25,1},{2,26},{10... | collective-permute-start | bytes 786440 | tf_op jit(solution)/shard_map/ppermute | solution.py:367
  52.8 3.8 %collective-permute-start.13 = (f32[2,2048]{1,0:T(2,128)S(1)}, f32[2,2048]{1,0:T(2,128)S(1)}, u32[]{:S(2)}, u32[]{:S(2)}) collective-permute-start(f32[2,2048]{1,0:T(2,128)S(1)} %get-tuple-element.60.first), channel_id=1, source_target_pairs={{0,1},{1,0},{2,3},{3,2},{4,5},{5,4},{6,7},{7,6},{8,9},{9,8},{10,11... | collective-permute-start | bytes 49160 | tf_op jit(solution)/shard_map/ppermute | solution.py:367
  56.6 3.8 %collective-permute-start.14 = (f32[2,2048]{1,0:T(2,128)S(1)}, f32[2,2048]{1,0:T(2,128)S(1)}, u32[]{:S(2)}, u32[]{:S(2)}) collective-permute-start(f32[2,2048]{1,0:T(2,128)S(1)} %join.3.first), channel_id=1, source_target_pairs={{0,2},{1,3},{2,0},{3,1},{4,6},{5,7},{6,4},{7,5},{8,10},{9,11},{10,... | collective-permute-start | bytes 49160 | tf_op jit(solution)/shard_map/ppermute | solution.py:367
  60.5 4.7 %collective-permute-start.15 = (f32[2,2048]{1,0:T(2,128)S(1)}, f32[2,2048]{1,0:T(2,128)S(1)}, u32[]{:S(2)}, u32[]{:S(2)}) collective-permute-start(f32[2,2048]{1,0:T(2,128)S(1)} %join.4.first), channel_id=1, source_target_pairs={{0,4},{1,5},{2,6},{3,7},{4,0},{5,1},{6,2},{7,3},{8,12},{9,13},{10,... | collective-permute-start | bytes 49160 | tf_op jit(solution)/shard_map/ppermute | solution.py:367
  65.9 7.4 %collective-permute-start.16 = (f32[256,256]{1,0:T(8,128)S(1)}, f32[256,256]{1,0:T(8,128)S(1)}, u32[]{:S(2)}, u32[]{:S(2)}) collective-permute-start(f32[256,256]{1,0:T(8,128)S(1)} %get-tuple-element.70), channel_id=1, source_target_pairs={{0,1},{1,0},{2,3},{3,2},{4,5},{5,4},{6,7},{7,6},{8,9},{9,8},{10,11... | collective-permute-start | bytes 786440 | tf_op jit(solution)/shard_map/ppermute | solution.py:367
  67.3 6.7 %collective-permute-start.17 = (f32[256,256]{1,0:T(8,128)S(1)}, f32[256,256]{1,0:T(8,128)S(1)}, u32[]{:S(2)}, u32[]{:S(2)}) collective-permute-start(f32[256,256]{1,0:T(8,128)S(1)} %get-tuple-element.71), channel_id=1, source_target_pairs={{0,2},{1,3},{2,0},{3,1},{4,6},{5,7},{6,4},{7,5},{8,10},{9,11},{10,... | collective-permute-start | bytes 786440 | tf_op jit(solution)/shard_map/ppermute | solution.py:367
  71.3 4.5 %collective-permute-start.22 = (f32[136,256]{1,0:T(8,128)S(1)}, f32[136,256]{1,0:T(8,128)S(1)}, u32[]{:S(2)}, u32[]{:S(2)}) collective-permute-start(f32[136,256]{1,0:T(8,128)S(1)} %get-tuple-element.75), channel_id=1, source_target_pairs={{0,8},{8,0},{16,24},{24,16},{1,9},{9,1},{17,25},{25,17},{2,10},{10... | collective-permute-start | bytes 417800 | tf_op jit(solution)/shard_map/ppermute | solution.py:367
  71.3 6.5 %collective-permute-start.23 = (f32[136,256]{1,0:T(8,128)S(1)}, f32[136,256]{1,0:T(8,128)S(1)}, u32[]{:S(2)}, u32[]{:S(2)}) collective-permute-start(f32[136,256]{1,0:T(8,128)S(1)} %get-tuple-element.76), channel_id=1, source_target_pairs={{0,16},{8,24},{16,0},{24,8},{1,17},{9,25},{17,1},{25,9},{2,18},{10... | collective-permute-start | bytes 417800 | tf_op jit(solution)/shard_map/ppermute | solution.py:367
  72.1 7.9 %collective-permute-start.24 = (f32[136,256]{1,0:T(8,128)S(1)}, f32[136,256]{1,0:T(8,128)S(1)}, u32[]{:S(2)}, u32[]{:S(2)}) collective-permute-start(f32[136,256]{1,0:T(8,128)S(1)} %get-tuple-element.77), channel_id=1, source_target_pairs={{0,24},{8,16},{16,8},{24,0},{1,25},{9,17},{17,9},{25,1},{2,26},{10... | collective-permute-start | bytes 417800 | tf_op jit(solution)/shard_map/ppermute | solution.py:367
  73.2 13.3 %collective-permute-start.27 = (f32[256,256]{1,0:T(8,128)S(1)}, f32[256,256]{1,0:T(8,128)S(1)}, u32[]{:S(2)}, u32[]{:S(2)}) collective-permute-start(f32[256,256]{1,0:T(8,128)S(1)} %add.12), channel_id=1, source_target_pairs={{0,2},{1,3},{2,0},{3,1},{4,6},{5,7},{6,4},{7,5},{8,10},{9,11},{10,... | collective-permute-start | bytes 786440 | tf_op jit(solution)/shard_map/ppermute | solution.py:367
  74.7 8.6 %collective-permute-start.21 = (f32[256,256]{1,0:T(8,128)S(1)}, f32[256,256]{1,0:T(8,128)S(1)}, u32[]{:S(2)}, u32[]{:S(2)}) collective-permute-start(f32[256,256]{1,0:T(8,128)S(1)} %get-tuple-element.74), channel_id=1, source_target_pairs={{0,1},{1,0},{2,3},{3,2},{4,5},{5,4},{6,7},{7,6},{8,9},{9,8},{10,11... | collective-permute-start | bytes 786440 | tf_op jit(solution)/shard_map/ppermute | solution.py:367
  84.0 13.7 %collective-permute-start.25 = (f32[256,256]{1,0:T(8,128)S(1)}, f32[256,256]{1,0:T(8,128)S(1)}, u32[]{:S(2)}, u32[]{:S(2)}) collective-permute-start(f32[256,256]{1,0:T(8,128)S(1)} %get-tuple-element.78), channel_id=1, source_target_pairs={{0,1},{1,0},{2,3},{3,2},{4,5},{5,4},{6,7},{7,6},{8,9},{9,8},{10,11... | collective-permute-start | bytes 786440 | tf_op jit(solution)/shard_map/ppermute | solution.py:367
  84.7 14.9 %collective-permute-start.26 = (f32[256,256]{1,0:T(8,128)S(1)}, f32[256,256]{1,0:T(8,128)S(1)}, u32[]{:S(2)}, u32[]{:S(2)}) collective-permute-start(f32[256,256]{1,0:T(8,128)S(1)} %get-tuple-element.79), channel_id=1, source_target_pairs={{0,3},{1,2},{2,1},{3,0},{4,7},{5,6},{6,5},{7,4},{8,11},{9,10},{10,... | collective-permute-start | bytes 786440 | tf_op jit(solution)/shard_map/ppermute | solution.py:367
  86.6 14.6 %copy-start.2 = (s32[256]{0:T(256)S(1)}, s32[256]{0:T(256)}, u32[]{:S(2)}) copy-start(s32[256]{0:T(256)} %param.11) | copy-start | bytes 3076
  86.6 14.6 %collective-permute-start.28 = (f32[256,256]{1,0:T(8,128)S(1)}, f32[256,256]{1,0:T(8,128)S(1)}, u32[]{:S(2)}, u32[]{:S(2)}) collective-permute-start(f32[256,256]{1,0:T(8,128)S(1)} %add.13), channel_id=1, source_target_pairs={{0,4},{1,5},{2,6},{3,7},{4,0},{5,1},{6,2},{7,3},{8,12},{9,13},{10,... | collective-permute-start | bytes 786440 | tf_op jit(solution)/shard_map/ppermute | solution.py:367

commit v7 on v6

--- a/solution.py
+++ b/solution.py
@@ -399,7 +399,7 @@
         encs[z] = swap(masked, "member", z)
     onward, got = lax.optimization_barrier((encs[2 * near], got))
     encs[3 * near] = swap(onward, "member", near)
-    for z in range(0, members, near):
+    for z in (0, 2 * near, 3 * near):
         for x in range(1, near):
             encs[z ^ x] = swap(onward if z == 2 * near else encs[z], "member", x)
     halves = [[d for d in range(members) if (d < near) or d in (near, 2 * near)], []]
@@ -415,8 +415,10 @@
         name=name,
     )
     negs = gather(slots, count, early, "gather_negatives")
+    for x in range(1, near):
+        encs[near + x] = swap(lax.optimization_barrier((encs[x], negs[0]))[0], "member", near)
     negs = [negs[0]] + [swap(negs[d], "group", d) for d in range(1, groups)]
-    rows = gather(0, slots, [], "gather_targets")
+    rows = gather(0, slots, [encs[2 * near + x] for x in range(1, near)], "gather_targets")
     rows = [rows[0]] + [swap(rows[d], "group", d) for d in range(1, groups)]
 
     stats, probs = [], []
@@ -497,13 +499,14 @@
         moved=8 * MIB,
         name="grad",
     )
-    def added(terms, deps):
+    def added(terms, deps, flops=0):
         return call(
             functools.partial(add_kernel, len(terms)),
             sds(width, tokens),
             [VMEM] * len(terms) + [ANY] * len(deps),
             VMEM,
             (*terms, *deps),
+            flops=flops,
             name="add",
         )
 
@@ -538,17 +541,19 @@
             name="scatter",
         )
 
-    table_own = scatter([0], [], grads[1:], 1 << 33)
     farthest, *rest, nearest = scaled([3 * near + x for x in along] + [near], [])
     arrived = beside(rest)
     nearest = swap(nearest, "member", near)
     far, *others = scaled([2 * near + x for x in along], [*arrived, nearest, *graded])
-    total = swap(added([farthest, *arrived], graded), "member", near)
-    half = added([far, *beside(others)], [table_own])
+    total = added([farthest, *arrived], graded)
+    table_own = scatter([0], [], [total], 1 << 33)
+    total = swap(total, "member", near)
+    far = added([far], [table_own, *grads[1:]])
+    half = added([far, *beside(others), total], [])
     close = [*along[1:], *[near + x for x in along[1:]]]
     kept, *sends = scaled([0, *close], [half])
     parts = [swap(block, "member", d) for d, block in zip(close, sends)]
-    parts += [nearest, kept, swap(added([half, total], []), "member", 2 * near)]
+    parts.append(added([nearest, kept, swap(half, "member", 2 * near)], []))
 
     table_grad = scatter(list(range(1, groups)), [table_own], [], 0)
     encoded_grad = call(

time: 102 us -> 100 us (0.980)
  blocking collectives: 12.2 us -> 0 us
  starting transfers between devices: 33.2 us -> 39.6 us
  waiting for transfers between devices: 14.4 us -> 17.3 us
    all_to_all x1 -> x0, blocking collectives: 12.2 us -> none  [shards(): lax.all_to_all(request, ('group', 'member'), split_axis=0, concat_axis=0,...]
    all_to_all x0 -> x1, waiting for transfers between devices: none -> 7.36 us  [shards(): lax.all_to_all(request, ('group', 'member'), split_axis=0, concat_axis=0,...]
    ppermute x29, waiting for transfers between devices: 14.4 us -> 9.93 us  [swap(): lax.ppermute(value, axis, [(i, i ^ d) for i in range(lax.axis_size(axis))])]
    all_to_all x0 -> x1, starting transfers between devices: none -> 3.82 us  [shards(): lax.all_to_all(request, ('group', 'member'), split_axis=0, concat_axis=0,...]
    ppermute x29, starting transfers between devices: 33.2 us -> 35.7 us  [swap(): lax.ppermute(value, axis, [(i, i ^ d) for i in range(lax.axis_size(axis))])]
    pallas_call x22 -> x23, Pallas kernels: 37.5 us -> 38.2 us  [call(): pl.pallas_call(kernel, out_shape=out_shape, in_specs=ins, out_specs=outs,...]
  transfers between devices with their start and end apart: 29 -> 30, of which waited for: 9 -> 9; matrix products, arithmetic and copies ran while one was open for 0% -> 0% of each run, Pallas kernels for 35% -> 35%
where the time goes in v7:
time: 100 us; the launch traced here: 99.9 us
  starting transfers between devices  39.6 us (40%)
  Pallas kernels  38.2 us (38%)
  waiting for transfers between devices  17.3 us (17%)
  local copies, waits for them, and re-layouts  3.15 us (3%)
    pallas_call x23, Pallas kernels, call(): pl.pallas_call(kernel, out_shape=out_shape, in_specs=ins, out_specs=outs,...  38.2 us
    ppermute x29, starting transfers between devices, swap(): lax.ppermute(value, axis, [(i, i ^ d) for i in range(lax.axis_size(axis))])  35.7 us
    ppermute x29, waiting for transfers between devices, swap(): lax.ppermute(value, axis, [(i, i ^ d) for i in range(lax.axis_size(axis))])  9.93 us
    all_to_all x1, waiting for transfers between devices, shards(): lax.all_to_all(request, ('group', 'member'), split_axis=0, concat_axis=0,...  7.36 us
    all_to_all x1, starting transfers between devices, shards(): lax.all_to_all(request, ('group', 'member'), split_axis=0, concat_axis=0,...  3.82 us
    unnamed x6, local copies, waits for them, and re-layouts  3.14 us
  transfers between devices with their start and end apart: 30, of which 9 were waited for; matrix products, arithmetic and copies ran while one was open for 0% of the time, Pallas kernels for 35%

profile of v7, /device:TPU:0, one launch (start us, length us, event | category | flops | bytes accessed | tf_op | source)
XLA Modules:
  0.0 99.9 jit_solution(11232642703924766161)
XLA Ops:
  0.6 0.7 pad_add_fusion
  1.5 0.9 copy-done.1
  2.4 1.8 %front.1 = (s32[32,1,256]{2,1,0:T(1,128)}, f32[256,256]{1,0:T(8,128)S(1)}) custom-call(s32[2]{0:T(128)S(1)} %pad_add_fusion.1.info, s32[1,1280]{1,0:T(1,128)S(1)} %reshape.15.ints, f32[256,256]{1,0:T(8,128)S(1)} %copy-done.1), custom_call_target="tpu_custom_call" | custom-call | tf_op jit(solution)/shard_map/front/pallas_call | solution.py:26
  4.2 4.0 %collective-permute-start = (f32[256,256]{1,0:T(8,128)S(1)}, f32[256,256]{1,0:T(8,128)S(1)}, u32[]{:S(2)}, u32[]{:S(2)}) collective-permute-start(f32[256,256]{1,0:T(8,128)S(1)} %get-tuple-element.43.refs_4_.refs_0_), channel_id=1, source_target_pairs={{0,4},{1,5},{2,6},{3,7},{4,0},{5,1},{6,2},{7,3},{8,12},{9,13},{10,... | collective-permute-start | bytes 786440 | tf_op jit(solution)/shard_map/ppermute | solution.py:367
  8.2 3.8 %all-to-all-start = ((s32[32,1,256]{2,1,0:T(1,128)}), s32[32,1,256]{2,1,0:T(1,128)S(1)}, u32[]{:S(2)}, u32[]{:S(2)}) async-start(s32[32,1,256]{2,1,0:T(1,128)} %get-tuple-element.44), calls=%async_computation | async-start | bytes 65536 | tf_op jit(solution)/shard_map/all_to_all | solution.py:393
  12.1 1.8 %collective-permute-start.1 = (f32[256,256]{1,0:T(8,128)S(1)}, f32[256,256]{1,0:T(8,128)S(1)}, u32[]{:S(2)}, u32[]{:S(2)}) collective-permute-start(f32[256,256]{1,0:T(8,128)S(1)} %get-tuple-element.43.refs_4_.refs_0_), channel_id=1, source_target_pairs={{0,1},{1,0},{2,3},{3,2},{4,5},{5,4},{6,7},{7,6},{8,9},{9,8},{10,11... | collective-permute-start | bytes 786440 | tf_op jit(solution)/shard_map/ppermute | solution.py:367
  13.9 1.5 %collective-permute-start.2 = (f32[256,256]{1,0:T(8,128)S(1)}, f32[256,256]{1,0:T(8,128)S(1)}, u32[]{:S(2)}, u32[]{:S(2)}) collective-permute-start(f32[256,256]{1,0:T(8,128)S(1)} %get-tuple-element.43.refs_4_.refs_0_), channel_id=1, source_target_pairs={{0,2},{1,3},{2,0},{3,1},{4,6},{5,7},{6,4},{7,5},{8,10},{9,11},{10,... | collective-permute-start | bytes 786440 | tf_op jit(solution)/shard_map/ppermute | solution.py:367
  15.4 7.4 %all-to-all-done.got.got_v = s32[32,1,256]{2,1,0:T(1,128)S(1)} async-done(((s32[32,1,256]{2,1,0:T(1,128)}), s32[32,1,256]{2,1,0:T(1,128)S(1)}, u32[]{:S(2)}, u32[]{:S(2)}) %all-to-all-start) | async-done | bytes 32800 | tf_op jit(solution)/shard_map/all_to_all | solution.py:393
  22.7 0.6 collective-permute-start.7
  23.9 2.3 %collective-permute-done.2.refs_1_.refs_6_.refs_2_ = f32[256,256]{1,0:T(8,128)S(1)} collective-permute-done((f32[256,256]{1,0:T(8,128)S(1)}, f32[256,256]{1,0:T(8,128)S(1)}, u32[]{:S(2)}, u32[]{:S(2)}) %collective-permute-start.2) | collective-permute-done | bytes 262176 | tf_op jit(solution)/shard_map/ppermute | solution.py:367
  26.3 2.2 %copy-done = f32[4096,256]{1,0:T(8,128)S(1)} copy-done((f32[4096,256]{1,0:T(8,128)S(1)}, f32[4096,256]{1,0:T(8,128)}, u32[]{:S(2)}) %copy-start) | copy-done | bytes 4194328
  28.4 2.3 %gather_negatives.1 = (f32[128,256]{1,0:T(8,128)S(1)}, f32[128,256]{1,0:T(8,128)S(1)}, f32[128,256]{1,0:T(8,128)S(1)}, f32[128,256]{1,0:T(8,128)S(1)}) custom-call(s32[2]{0:T(128)S(1)} %pad_add_fusion.1.info, s32[32,1,256]{2,1,0:T(1,128)S(1)} %all-to-all-done.got.got_v, f32[4096,256]{1,0:T(8,128)S(1)} %copy-done, ...), custom_call_target="tpu_custom_call" | custom-call | tf_op jit(solution)/shard_map/gather_negatives/pallas_call | solution.py:26
  30.8 1.6 %collective-permute-start.4 = (f32[128,256]{1,0:T(8,128)S(1)}, f32[128,256]{1,0:T(8,128)S(1)}, u32[]{:S(2)}, u32[]{:S(2)}) collective-permute-start(f32[128,256]{1,0:T(8,128)S(1)} %get-tuple-element.48), channel_id=1, source_target_pairs={{0,16},{8,24},{16,0},{24,8},{1,17},{9,25},{17,1},{25,9},{2,18},{10... | collective-permute-start | bytes 393224 | tf_op jit(solution)/shard_map/ppermute | solution.py:367
  32.7 1.4 %collective-permute-start.9 = (f32[256,256]{1,0:T(8,128)S(1)}, f32[256,256]{1,0:T(8,128)S(1)}, u32[]{:S(2)}, u32[]{:S(2)}) collective-permute-start(f32[256,256]{1,0:T(8,128)S(1)} %collective-permute-done.8.refs_6_.refs_10_), channel_id=1, source_target_pairs={{0,1},{1,0},{2,3},{3,2},{4,5},{5,4},{6,7},{7,6},{8,9},{9,8},{10,11... | collective-permute-start | bytes 786440 | tf_op jit(solution)/shard_map/ppermute | solution.py:367
  34.1 3.3 %gather_targets.1 = (f32[256,256]{1,0:T(8,128)S(1)}, f32[256,256]{1,0:T(8,128)S(1)}, f32[256,256]{1,0:T(8,128)S(1)}, f32[256,256]{1,0:T(8,128)S(1)}) custom-call(s32[2]{0:T(128)S(1)} %pad_add_fusion.1.info, s32[32,1,256]{2,1,0:T(1,128)S(1)} %all-to-all-done.got.got_v, f32[4096,256]{1,0:T(8,128)S(1)} %copy-done, ...), custom_call_target="tpu_custom_call" | custom-call | tf_op jit(solution)/shard_map/gather_targets/pallas_call | solution.py:26
  37.5 1.8 %collective-permute-start.11 = (f32[256,256]{1,0:T(8,128)S(1)}, f32[256,256]{1,0:T(8,128)S(1)}, u32[]{:S(2)}, u32[]{:S(2)}) collective-permute-start(f32[256,256]{1,0:T(8,128)S(1)} %get-tuple-element.56), channel_id=1, source_target_pairs={{0,16},{8,24},{16,0},{24,8},{1,17},{9,25},{17,1},{25,9},{2,18},{10... | collective-permute-start | bytes 786440 | tf_op jit(solution)/shard_map/ppermute | solution.py:367
  39.3 1.6 %collective-permute-start.12 = (f32[256,256]{1,0:T(8,128)S(1)}, f32[256,256]{1,0:T(8,128)S(1)}, u32[]{:S(2)}, u32[]{:S(2)}) collective-permute-start(f32[256,256]{1,0:T(8,128)S(1)} %get-tuple-element.57), channel_id=1, source_target_pairs={{0,24},{8,16},{16,8},{24,0},{1,25},{9,17},{17,9},{25,1},{2,26},{10... | collective-permute-start | bytes 786440 | tf_op jit(solution)/shard_map/ppermute | solution.py:367
  40.8 3.1 %score.2 = (f32[2,2048]{1,0:T(2,128)S(1)}, bf16[4,512,256]{2,1,0:T(8,128)(2,1)S(1)}, bf16[4,512,256]{2,1,0:T(8,128)(2,1)S(1)}) custom-call(s32[2]{0:T(128)S(1)} %pad_add_fusion.1.info, f32[128,256]{1,0:T(8,128)S(1)} %get-tuple-element.46.refs_0_, f32[128,256]{1,0:T(8,128)S(1)} %collective-permute-done.3.refs_1_, ...), custom_call_target="tpu_custom_call" | custom-call | flops 1610612736 | bytes 1048576 | tf_op jit(solution)/shard_map/score/pallas_call | solution.py:26
  43.9 1.6 %pick.1 = (f32[256,256]{1,0:T(8,128)S(1)}, f32[256,256]{1,0:T(8,128)S(1)}, f32[256,256]{1,0:T(8,128)S(1)}, f32[256,256]{1,0:T(8,128)S(1)}) custom-call(s32[2]{0:T(128)S(1)} %pad_add_fusion.1.info, s32[32,1,256]{2,1,0:T(1,128)S(1)} %all-to-all-done.got.got_v, f32[256,256]{1,0:T(8,128)S(1)} %get-tuple-element.43.refs_4_.refs_0_, ...), custom_call_target="tpu_custom_call" | custom-call | tf_op jit(solution)/shard_map/pick/pallas_call | solution.py:26
  46.2 3.1 %score.3 = (f32[2,2048]{1,0:T(2,128)S(1)}, bf16[4,512,256]{2,1,0:T(8,128)(2,1)S(1)}, bf16[4,512,256]{2,1,0:T(8,128)(2,1)S(1)}) custom-call(s32[2]{0:T(128)S(1)} %pad_add_fusion.1.info, f32[128,256]{1,0:T(8,128)S(1)} %get-tuple-element.46.refs_0_, f32[128,256]{1,0:T(8,128)S(1)} %collective-permute-done.3.refs_1_, ...), custom_call_target="tpu_custom_call" | custom-call | flops 1610612736 | bytes 1048576 | tf_op jit(solution)/shard_map/score/pallas_call | solution.py:26
  49.2 1.4 %collective-permute-start.20 = (f32[256,256]{1,0:T(8,128)S(1)}, f32[256,256]{1,0:T(8,128)S(1)}, u32[]{:S(2)}, u32[]{:S(2)}) collective-permute-start(f32[256,256]{1,0:T(8,128)S(1)} %get-tuple-element.61.refs_7_), channel_id=1, source_target_pairs={{0,24},{8,16},{16,8},{24,0},{1,25},{9,17},{17,9},{25,1},{2,26},{10... | collective-permute-start | bytes 786440 | tf_op jit(solution)/shard_map/ppermute | solution.py:367
  50.6 0.9 collective-permute-done.12.refs_3_.refs_7_
  51.5 1.2 %positive.1 = (f32[2,2048]{1,0:T(2,128)S(1)}, f32[2,2048]{1,0:T(2,128)S(1)}) custom-call(s32[2]{0:T(128)S(1)} %pad_add_fusion.1.info, s32[32,1,256]{2,1,0:T(1,128)S(1)} %all-to-all-done.got.got_v, f32[2,2048]{1,0:T(2,128)S(1)} %get-tuple-element.53.stats, f32[256,256]{1,0:T(8,128)S(1)} %get-tuple-element.54.refs_0_.refs_4_, ...), custom_call_target="tpu_custom_call" | custom-call | tf_op jit(solution)/shard_map/positive/pallas_call | solution.py:26
  52.7 1.1 %collective-permute-start.13 = (f32[2,2048]{1,0:T(2,128)S(1)}, f32[2,2048]{1,0:T(2,128)S(1)}, u32[]{:S(2)}, u32[]{:S(2)}) collective-permute-start(f32[2,2048]{1,0:T(2,128)S(1)} %get-tuple-element.62.first), channel_id=1, source_target_pairs={{0,1},{1,0},{2,3},{3,2},{4,5},{5,4},{6,7},{7,6},{8,9},{9,8},{10,11... | collective-permute-start | bytes 49160 | tf_op jit(solution)/shard_map/ppermute | solution.py:367
  53.8 2.0 %pulled.2 = (f32[4,256,256]{2,1,0:T(8,128)S(1)}, f32[4,256,256]{2,1,0:T(8,128)S(1)}) custom-call(s32[2]{0:T(128)S(1)} %pad_add_fusion.1.info, s32[32,1,256]{2,1,0:T(1,128)S(1)} %all-to-all-done.got.got_v, f32[128,256]{1,0:T(8,128)S(1)} %get-tuple-element.46.refs_0_, f32[128,256]{1,0:T(8,128)S(1)} %collective-permute-done.3.refs_1_, ...), custom_call_target="tpu_custom_call" | custom-call | flops 805306368 | bytes 1048576 | tf_op jit(solution)/shard_map/pulled/pallas_call | solution.py:26
  55.8 0.7 collective-permute-done.13.second
  56.5 2.0 %collective-permute-start.14 = (f32[2,2048]{1,0:T(2,128)S(1)}, f32[2,2048]{1,0:T(2,128)S(1)}, u32[]{:S(2)}, u32[]{:S(2)}) collective-permute-start(f32[2,2048]{1,0:T(2,128)S(1)} %join.3.first), channel_id=1, source_target_pairs={{0,2},{1,3},{2,0},{3,1},{4,6},{5,7},{6,4},{7,5},{8,10},{9,11},{10,... | collective-permute-start | bytes 49160 | tf_op jit(solution)/shard_map/ppermute | solution.py:367
  58.6 2.0 %pulled.3 = (f32[4,256,256]{2,1,0:T(8,128)S(1)}, f32[4,256,256]{2,1,0:T(8,128)S(1)}) custom-call(s32[2]{0:T(128)S(1)} %pad_add_fusion.1.info, s32[32,1,256]{2,1,0:T(1,128)S(1)} %all-to-all-done.got.got_v, f32[128,256]{1,0:T(8,128)S(1)} %get-tuple-element.46.refs_0_, f32[128,256]{1,0:T(8,128)S(1)} %collective-permute-done.3.refs_1_, ...), custom_call_target="tpu_custom_call" | custom-call | flops 805306368 | bytes 1048576 | tf_op jit(solution)/shard_map/pulled/pallas_call | solution.py:26
  60.6 4.0 %collective-permute-start.15 = (f32[2,2048]{1,0:T(2,128)S(1)}, f32[2,2048]{1,0:T(2,128)S(1)}, u32[]{:S(2)}, u32[]{:S(2)}) collective-permute-start(f32[2,2048]{1,0:T(2,128)S(1)} %join.4.first), channel_id=1, source_target_pairs={{0,4},{1,5},{2,6},{3,7},{4,0},{5,1},{6,2},{7,3},{8,12},{9,13},{10,... | collective-permute-start | bytes 49160 | tf_op jit(solution)/shard_map/ppermute | solution.py:367
  64.6 1.7 %collective-permute-done.15.second = f32[2,2048]{1,0:T(2,128)S(1)} collective-permute-done((f32[2,2048]{1,0:T(2,128)S(1)}, f32[2,2048]{1,0:T(2,128)S(1)}, u32[]{:S(2)}, u32[]{:S(2)}) %collective-permute-start.15) | collective-permute-done | bytes 16416 | tf_op jit(solution)/shard_map/ppermute | solution.py:367
  66.4 0.7 pull.3
  67.0 0.6 collective-permute-start.16
  67.6 0.7 collective-permute-start.17
  68.4 2.7 %grad.1 = (f32[136,256]{1,0:T(8,128)S(1)}, f32[136,256]{1,0:T(8,128)S(1)}, f32[136,256]{1,0:T(8,128)S(1)}, f32[136,256]{1,0:T(8,128)S(1)}) custom-call(s32[2]{0:T(128)S(1)} %pad_add_fusion.1.info, s32[32,1,256]{2,1,0:T(1,128)S(1)} %all-to-all-done.got.got_v, f32[2,2048]{1,0:T(2,128)S(1)} %join.5.final, f32[2,2048]{1,0:T(2,128)S(1)} %get-tuple-element.53.stats, ...), custom_call_target="tpu_custom_call" | custom-call | flops 1610612736 | bytes 8388608 | tf_op jit(solution)/shard_map/grad/pallas_call | solution.py:26
  71.1 1.6 %collective-permute-start.22 = (f32[136,256]{1,0:T(8,128)S(1)}, f32[136,256]{1,0:T(8,128)S(1)}, u32[]{:S(2)}, u32[]{:S(2)}) collective-permute-start(f32[136,256]{1,0:T(8,128)S(1)} %get-tuple-element.78), channel_id=1, source_target_pairs={{0,16},{8,24},{16,0},{24,8},{1,17},{9,25},{17,1},{25,9},{2,18},{10... | collective-permute-start | bytes 417800 | tf_op jit(solution)/shard_map/ppermute | solution.py:367
  73.5 0.6 collective-permute-done.17.refs_5_.refs_0_
  74.1 0.6 pull.4
  74.7 1.5 %collective-permute-start.24 = (f32[256,256]{1,0:T(8,128)S(1)}, f32[256,256]{1,0:T(8,128)S(1)}, u32[]{:S(2)}, u32[]{:S(2)}) collective-permute-start(f32[256,256]{1,0:T(8,128)S(1)} %get-tuple-element.80), channel_id=1, source_target_pairs={{0,1},{1,0},{2,3},{3,2},{4,5},{5,4},{6,7},{7,6},{8,9},{9,8},{10,11... | collective-permute-start | bytes 786440 | tf_op jit(solution)/shard_map/ppermute | solution.py:367
  76.2 0.8 collective-permute-start.25
  77.0 3.3 %scatter.2.refs_1_.refs_6_ = f32[4096,256]{1,0:T(8,128)S(1)} custom-call(s32[2]{0:T(128)S(1)} %pad_add_fusion.1.info, s32[32,1,256]{2,1,0:T(1,128)S(1)} %all-to-all-done.got.got_v, s32[32,1,256]{2,1,0:T(1,128)S(1)} %all-to-all-done.got.got_v, f32[136,256]{1,0:T(8,128)S(1)} %get-tuple-element.74.refs_6_.refs_2_.refs_0_, ...), custom_call_target="tpu_custom_call" | custom-call | flops 8589934592 | tf_op jit(solution)/shard_map/scatter/pallas_call | solution.py:26
  80.4 1.9 %collective-permute-done.24.refs_1_ = f32[256,256]{1,0:T(8,128)S(1)} collective-permute-done((f32[256,256]{1,0:T(8,128)S(1)}, f32[256,256]{1,0:T(8,128)S(1)}, u32[]{:S(2)}, u32[]{:S(2)}) %collective-permute-start.24) | collective-permute-done | bytes 262176 | tf_op jit(solution)/shard_map/ppermute | solution.py:367
  82.2 1.3 %collective-permute-done.25.refs_2_ = f32[256,256]{1,0:T(8,128)S(1)} collective-permute-done((f32[256,256]{1,0:T(8,128)S(1)}, f32[256,256]{1,0:T(8,128)S(1)}, u32[]{:S(2)}, u32[]{:S(2)}) %collective-permute-start.25) | collective-permute-done | bytes 262176 | tf_op jit(solution)/shard_map/ppermute | solution.py:367
  83.6 0.7 pull.5
  84.3 2.5 %collective-permute-start.28 = (f32[256,256]{1,0:T(8,128)S(1)}, f32[256,256]{1,0:T(8,128)S(1)}, u32[]{:S(2)}, u32[]{:S(2)}) collective-permute-start(f32[256,256]{1,0:T(8,128)S(1)} %add.14.refs_4_), channel_id=1, source_target_pairs={{0,4},{1,5},{2,6},{3,7},{4,0},{5,1},{6,2},{7,3},{8,12},{9,13},{10,... | collective-permute-start | bytes 786440 | tf_op jit(solution)/shard_map/ppermute | solution.py:367
  86.8 0.8 collective-permute-start.26
  87.6 2.4 %collective-permute-start.27 = (f32[256,256]{1,0:T(8,128)S(1)}, f32[256,256]{1,0:T(8,128)S(1)}, u32[]{:S(2)}, u32[]{:S(2)}) collective-permute-start(f32[256,256]{1,0:T(8,128)S(1)} %get-tuple-element.82), channel_id=1, source_target_pairs={{0,3},{1,2},{2,1},{3,0},{4,7},{5,6},{6,5},{7,4},{8,11},{9,10},{10,... | collective-permute-start | bytes 786440 | tf_op jit(solution)/shard_map/ppermute | solution.py:367
  90.0 8.8 %scatter.3 = f32[4096,256]{1,0:T(8,128)} custom-call(s32[2]{0:T(128)S(1)} %pad_add_fusion.1.info, s32[32,1,256]{2,1,0:T(1,128)S(1)} %all-to-all-done.got.got_v, s32[32,1,256]{2,1,0:T(1,128)S(1)} %all-to-all-done.got.got_v, f32[136,256]{1,0:T(8,128)S(1)} %collective-permute-done.21.refs_2_.refs_0_, f32[136,256]{1,0:T(8,128)S(1)} %collective-permute-done.22.refs_3_.refs_1_, ...), custom_call_target="tpu_custom_call" | custom-call | tf_op jit(solution)/shard_map/scatter/pallas_call | solution.py:26
  98.9 1.0 finish.1
  (44 shorter events, 2.7 us)
Async XLA Ops:
  1.5 1.0 copy-start.1
  4.2 18.5 %collective-permute-start = (f32[256,256]{1,0:T(8,128)S(1)}, f32[256,256]{1,0:T(8,128)S(1)}, u32[]{:S(2)}, u32[]{:S(2)}) collective-permute-start(f32[256,256]{1,0:T(8,128)S(1)} %get-tuple-element.43.refs_4_.refs_0_), channel_id=1, source_target_pairs={{0,4},{1,5},{2,6},{3,7},{4,0},{5,1},{6,2},{7,3},{8,12},{9,13},{10,... | collective-permute-start | bytes 786440 | tf_op jit(solution)/shard_map/ppermute | solution.py:367
  8.2 14.5 %all-to-all-start = ((s32[32,1,256]{2,1,0:T(1,128)}), s32[32,1,256]{2,1,0:T(1,128)S(1)}, u32[]{:S(2)}, u32[]{:S(2)}) async-start(s32[32,1,256]{2,1,0:T(1,128)} %get-tuple-element.44), calls=%async_computation | async-start | bytes 65536 | tf_op jit(solution)/shard_map/all_to_all | solution.py:393
  12.1 11.9 %collective-permute-start.1 = (f32[256,256]{1,0:T(8,128)S(1)}, f32[256,256]{1,0:T(8,128)S(1)}, u32[]{:S(2)}, u32[]{:S(2)}) collective-permute-start(f32[256,256]{1,0:T(8,128)S(1)} %get-tuple-element.43.refs_4_.refs_0_), channel_id=1, source_target_pairs={{0,1},{1,0},{2,3},{3,2},{4,5},{5,4},{6,7},{7,6},{8,9},{9,8},{10,11... | collective-permute-start | bytes 786440 | tf_op jit(solution)/shard_map/ppermute | solution.py:367
  13.9 12.4 %collective-permute-start.2 = (f32[256,256]{1,0:T(8,128)S(1)}, f32[256,256]{1,0:T(8,128)S(1)}, u32[]{:S(2)}, u32[]{:S(2)}) collective-permute-start(f32[256,256]{1,0:T(8,128)S(1)} %get-tuple-element.43.refs_4_.refs_0_), channel_id=1, source_target_pairs={{0,2},{1,3},{2,0},{3,1},{4,6},{5,7},{6,4},{7,5},{8,10},{9,11},{10,... | collective-permute-start | bytes 786440 | tf_op jit(solution)/shard_map/ppermute | solution.py:367
  22.7 10.0 %collective-permute-start.7 = (f32[256,256]{1,0:T(8,128)S(1)}, f32[256,256]{1,0:T(8,128)S(1)}, u32[]{:S(2)}, u32[]{:S(2)}) collective-permute-start(f32[256,256]{1,0:T(8,128)S(1)} %collective-permute-done.refs_2_.refs_7_.refs_4_.refs_8_), channel_id=1, source_target_pairs={{0,1},{1,0},{2,3},{3,2},{4,5},{5,4},{6,7},{7,6},{8,9},{9,8},{10,11... | collective-permute-start | bytes 786440 | tf_op jit(solution)/shard_map/ppermute | solution.py:367
  23.4 9.3 %collective-permute-start.8 = (f32[256,256]{1,0:T(8,128)S(1)}, f32[256,256]{1,0:T(8,128)S(1)}, u32[]{:S(2)}, u32[]{:S(2)}) collective-permute-start(f32[256,256]{1,0:T(8,128)S(1)} %collective-permute-done.refs_2_.refs_7_.refs_4_.refs_8_), channel_id=1, source_target_pairs={{0,2},{1,3},{2,0},{3,1},{4,6},{5,7},{6,4},{7,5},{8,10},{9,11},{10,... | collective-permute-start | bytes 786440 | tf_op jit(solution)/shard_map/ppermute | solution.py:367
  26.2 2.2 %copy-start = (f32[4096,256]{1,0:T(8,128)S(1)}, f32[4096,256]{1,0:T(8,128)}, u32[]{:S(2)}) copy-start(f32[4096,256]{1,0:T(8,128)} %table.3) | copy-start | bytes 12582916
  30.8 6.6 %collective-permute-start.3 = (f32[128,256]{1,0:T(8,128)S(1)}, f32[128,256]{1,0:T(8,128)S(1)}, u32[]{:S(2)}, u32[]{:S(2)}) collective-permute-start(f32[128,256]{1,0:T(8,128)S(1)} %get-tuple-element.47), channel_id=1, source_target_pairs={{0,8},{8,0},{16,24},{24,16},{1,9},{9,1},{17,25},{25,17},{2,10},{10... | collective-permute-start | bytes 393224 | tf_op jit(solution)/shard_map/ppermute | solution.py:367
  30.8 6.6 %collective-permute-start.4 = (f32[128,256]{1,0:T(8,128)S(1)}, f32[128,256]{1,0:T(8,128)S(1)}, u32[]{:S(2)}, u32[]{:S(2)}) collective-permute-start(f32[128,256]{1,0:T(8,128)S(1)} %get-tuple-element.48), channel_id=1, source_target_pairs={{0,16},{8,24},{16,0},{24,8},{1,17},{9,25},{17,1},{25,9},{2,18},{10... | collective-permute-start | bytes 393224 | tf_op jit(solution)/shard_map/ppermute | solution.py:367
  32.5 6.8 %collective-permute-start.5 = (f32[128,256]{1,0:T(8,128)S(1)}, f32[128,256]{1,0:T(8,128)S(1)}, u32[]{:S(2)}, u32[]{:S(2)}) collective-permute-start(f32[128,256]{1,0:T(8,128)S(1)} %get-tuple-element.49), channel_id=1, source_target_pairs={{0,24},{8,16},{16,8},{24,0},{1,25},{9,17},{17,9},{25,1},{2,26},{10... | collective-permute-start | bytes 393224 | tf_op jit(solution)/shard_map/ppermute | solution.py:367
  32.7 11.2 %collective-permute-start.6 = (f32[256,256]{1,0:T(8,128)S(1)}, f32[256,256]{1,0:T(8,128)S(1)}, u32[]{:S(2)}, u32[]{:S(2)}) collective-permute-start(f32[256,256]{1,0:T(8,128)S(1)} %collective-permute-done.1.refs_0_.refs_5_.refs_1_), channel_id=1, source_target_pairs={{0,2},{1,3},{2,0},{3,1},{4,6},{5,7},{6,4},{7,5},{8,10},{9,11},{10,... | collective-permute-start | bytes 786440 | tf_op jit(solution)/shard_map/ppermute | solution.py:367
  32.7 11.2 %collective-permute-start.9 = (f32[256,256]{1,0:T(8,128)S(1)}, f32[256,256]{1,0:T(8,128)S(1)}, u32[]{:S(2)}, u32[]{:S(2)}) collective-permute-start(f32[256,256]{1,0:T(8,128)S(1)} %collective-permute-done.8.refs_6_.refs_10_), channel_id=1, source_target_pairs={{0,1},{1,0},{2,3},{3,2},{4,5},{5,4},{6,7},{7,6},{8,9},{9,8},{10,11... | collective-permute-start | bytes 786440 | tf_op jit(solution)/shard_map/ppermute | solution.py:367
  37.4 11.9 %collective-permute-start.10 = (f32[256,256]{1,0:T(8,128)S(1)}, f32[256,256]{1,0:T(8,128)S(1)}, u32[]{:S(2)}, u32[]{:S(2)}) collective-permute-start(f32[256,256]{1,0:T(8,128)S(1)} %get-tuple-element.55), channel_id=1, source_target_pairs={{0,8},{8,0},{16,24},{24,16},{1,9},{9,1},{17,25},{25,17},{2,10},{10... | collective-permute-start | bytes 786440 | tf_op jit(solution)/shard_map/ppermute | solution.py:367
  37.5 13.2 %collective-permute-start.11 = (f32[256,256]{1,0:T(8,128)S(1)}, f32[256,256]{1,0:T(8,128)S(1)}, u32[]{:S(2)}, u32[]{:S(2)}) collective-permute-start(f32[256,256]{1,0:T(8,128)S(1)} %get-tuple-element.56), channel_id=1, source_target_pairs={{0,16},{8,24},{16,0},{24,8},{1,17},{9,25},{17,1},{25,9},{2,18},{10... | collective-permute-start | bytes 786440 | tf_op jit(solution)/shard_map/ppermute | solution.py:367
  39.3 12.2 %collective-permute-start.12 = (f32[256,256]{1,0:T(8,128)S(1)}, f32[256,256]{1,0:T(8,128)S(1)}, u32[]{:S(2)}, u32[]{:S(2)}) collective-permute-start(f32[256,256]{1,0:T(8,128)S(1)} %get-tuple-element.57), channel_id=1, source_target_pairs={{0,24},{8,16},{16,8},{24,0},{1,25},{9,17},{17,9},{25,1},{2,26},{10... | collective-permute-start | bytes 786440 | tf_op jit(solution)/shard_map/ppermute | solution.py:367
  45.5 22.8 %collective-permute-start.18 = (f32[256,256]{1,0:T(8,128)S(1)}, f32[256,256]{1,0:T(8,128)S(1)}, u32[]{:S(2)}, u32[]{:S(2)}) collective-permute-start(f32[256,256]{1,0:T(8,128)S(1)} %get-tuple-element.59.refs_5_), channel_id=1, source_target_pairs={{0,8},{8,0},{16,24},{24,16},{1,9},{9,1},{17,25},{25,17},{2,10},{10... | collective-permute-start | bytes 786440 | tf_op jit(solution)/shard_map/ppermute | solution.py:367
  45.6 22.7 %collective-permute-start.19 = (f32[256,256]{1,0:T(8,128)S(1)}, f32[256,256]{1,0:T(8,128)S(1)}, u32[]{:S(2)}, u32[]{:S(2)}) collective-permute-start(f32[256,256]{1,0:T(8,128)S(1)} %get-tuple-element.60.refs_6_), channel_id=1, source_target_pairs={{0,16},{8,24},{16,0},{24,8},{1,17},{9,25},{17,1},{25,9},{2,18},{10... | collective-permute-start | bytes 786440 | tf_op jit(solution)/shard_map/ppermute | solution.py:367
  49.2 19.1 %collective-permute-start.20 = (f32[256,256]{1,0:T(8,128)S(1)}, f32[256,256]{1,0:T(8,128)S(1)}, u32[]{:S(2)}, u32[]{:S(2)}) collective-permute-start(f32[256,256]{1,0:T(8,128)S(1)} %get-tuple-element.61.refs_7_), channel_id=1, source_target_pairs={{0,24},{8,16},{16,8},{24,0},{1,25},{9,17},{17,9},{25,1},{2,26},{10... | collective-permute-start | bytes 786440 | tf_op jit(solution)/shard_map/ppermute | solution.py:367
  52.7 3.8 %collective-permute-start.13 = (f32[2,2048]{1,0:T(2,128)S(1)}, f32[2,2048]{1,0:T(2,128)S(1)}, u32[]{:S(2)}, u32[]{:S(2)}) collective-permute-start(f32[2,2048]{1,0:T(2,128)S(1)} %get-tuple-element.62.first), channel_id=1, source_target_pairs={{0,1},{1,0},{2,3},{3,2},{4,5},{5,4},{6,7},{7,6},{8,9},{9,8},{10,11... | collective-permute-start | bytes 49160 | tf_op jit(solution)/shard_map/ppermute | solution.py:367
  56.5 4.0 %collective-permute-start.14 = (f32[2,2048]{1,0:T(2,128)S(1)}, f32[2,2048]{1,0:T(2,128)S(1)}, u32[]{:S(2)}, u32[]{:S(2)}) collective-permute-start(f32[2,2048]{1,0:T(2,128)S(1)} %join.3.first), channel_id=1, source_target_pairs={{0,2},{1,3},{2,0},{3,1},{4,6},{5,7},{6,4},{7,5},{8,10},{9,11},{10,... | collective-permute-start | bytes 49160 | tf_op jit(solution)/shard_map/ppermute | solution.py:367
  60.6 5.8 %collective-permute-start.15 = (f32[2,2048]{1,0:T(2,128)S(1)}, f32[2,2048]{1,0:T(2,128)S(1)}, u32[]{:S(2)}, u32[]{:S(2)}) collective-permute-start(f32[2,2048]{1,0:T(2,128)S(1)} %join.4.first), channel_id=1, source_target_pairs={{0,4},{1,5},{2,6},{3,7},{4,0},{5,1},{6,2},{7,3},{8,12},{9,13},{10,... | collective-permute-start | bytes 49160 | tf_op jit(solution)/shard_map/ppermute | solution.py:367
  67.0 6.4 %collective-permute-start.16 = (f32[256,256]{1,0:T(8,128)S(1)}, f32[256,256]{1,0:T(8,128)S(1)}, u32[]{:S(2)}, u32[]{:S(2)}) collective-permute-start(f32[256,256]{1,0:T(8,128)S(1)} %get-tuple-element.72), channel_id=1, source_target_pairs={{0,1},{1,0},{2,3},{3,2},{4,5},{5,4},{6,7},{7,6},{8,9},{9,8},{10,11... | collective-permute-start | bytes 786440 | tf_op jit(solution)/shard_map/ppermute | solution.py:367
  67.6 6.4 %collective-permute-start.17 = (f32[256,256]{1,0:T(8,128)S(1)}, f32[256,256]{1,0:T(8,128)S(1)}, u32[]{:S(2)}, u32[]{:S(2)}) collective-permute-start(f32[256,256]{1,0:T(8,128)S(1)} %get-tuple-element.73), channel_id=1, source_target_pairs={{0,2},{1,3},{2,0},{3,1},{4,6},{5,7},{6,4},{7,5},{8,10},{9,11},{10,... | collective-permute-start | bytes 786440 | tf_op jit(solution)/shard_map/ppermute | solution.py:367
  71.0 9.3 %collective-permute-start.21 = (f32[136,256]{1,0:T(8,128)S(1)}, f32[136,256]{1,0:T(8,128)S(1)}, u32[]{:S(2)}, u32[]{:S(2)}) collective-permute-start(f32[136,256]{1,0:T(8,128)S(1)} %get-tuple-element.77), channel_id=1, source_target_pairs={{0,8},{8,0},{16,24},{24,16},{1,9},{9,1},{17,25},{25,17},{2,10},{10... | collective-permute-start | bytes 417800 | tf_op jit(solution)/shard_map/ppermute | solution.py:367
  71.1 9.2 %collective-permute-start.22 = (f32[136,256]{1,0:T(8,128)S(1)}, f32[136,256]{1,0:T(8,128)S(1)}, u32[]{:S(2)}, u32[]{:S(2)}) collective-permute-start(f32[136,256]{1,0:T(8,128)S(1)} %get-tuple-element.78), channel_id=1, source_target_pairs={{0,16},{8,24},{16,0},{24,8},{1,17},{9,25},{17,1},{25,9},{2,18},{10... | collective-permute-start | bytes 417800 | tf_op jit(solution)/shard_map/ppermute | solution.py:367
  72.7 7.6 %collective-permute-start.23 = (f32[136,256]{1,0:T(8,128)S(1)}, f32[136,256]{1,0:T(8,128)S(1)}, u32[]{:S(2)}, u32[]{:S(2)}) collective-permute-start(f32[136,256]{1,0:T(8,128)S(1)} %get-tuple-element.79), channel_id=1, source_target_pairs={{0,24},{8,16},{16,8},{24,0},{1,25},{9,17},{17,9},{25,1},{2,26},{10... | collective-permute-start | bytes 417800 | tf_op jit(solution)/shard_map/ppermute | solution.py:367
  74.7 7.6 %collective-permute-start.24 = (f32[256,256]{1,0:T(8,128)S(1)}, f32[256,256]{1,0:T(8,128)S(1)}, u32[]{:S(2)}, u32[]{:S(2)}) collective-permute-start(f32[256,256]{1,0:T(8,128)S(1)} %get-tuple-element.80), channel_id=1, source_target_pairs={{0,1},{1,0},{2,3},{3,2},{4,5},{5,4},{6,7},{7,6},{8,9},{9,8},{10,11... | collective-permute-start | bytes 786440 | tf_op jit(solution)/shard_map/ppermute | solution.py:367
  76.2 7.3 %collective-permute-start.25 = (f32[256,256]{1,0:T(8,128)S(1)}, f32[256,256]{1,0:T(8,128)S(1)}, u32[]{:S(2)}, u32[]{:S(2)}) collective-permute-start(f32[256,256]{1,0:T(8,128)S(1)} %add.12.refs_2_), channel_id=1, source_target_pairs={{0,2},{1,3},{2,0},{3,1},{4,6},{5,7},{6,4},{7,5},{8,10},{9,11},{10,... | collective-permute-start | bytes 786440 | tf_op jit(solution)/shard_map/ppermute | solution.py:367
  84.3 14.6 %collective-permute-start.28 = (f32[256,256]{1,0:T(8,128)S(1)}, f32[256,256]{1,0:T(8,128)S(1)}, u32[]{:S(2)}, u32[]{:S(2)}) collective-permute-start(f32[256,256]{1,0:T(8,128)S(1)} %add.14.refs_4_), channel_id=1, source_target_pairs={{0,4},{1,5},{2,6},{3,7},{4,0},{5,1},{6,2},{7,3},{8,12},{9,13},{10,... | collective-permute-start | bytes 786440 | tf_op jit(solution)/shard_map/ppermute | solution.py:367
  86.8 12.1 %collective-permute-start.26 = (f32[256,256]{1,0:T(8,128)S(1)}, f32[256,256]{1,0:T(8,128)S(1)}, u32[]{:S(2)}, u32[]{:S(2)}) collective-permute-start(f32[256,256]{1,0:T(8,128)S(1)} %get-tuple-element.81), channel_id=1, source_target_pairs={{0,1},{1,0},{2,3},{3,2},{4,5},{5,4},{6,7},{7,6},{8,9},{9,8},{10,11... | collective-permute-start | bytes 786440 | tf_op jit(solution)/shard_map/ppermute | solution.py:367
  87.6 11.3 %copy-start.2 = (s32[256]{0:T(256)S(1)}, s32[256]{0:T(256)}, u32[]{:S(2)}) copy-start(s32[256]{0:T(256)} %param.11) | copy-start | bytes 3076
  87.6 11.3 %collective-permute-start.27 = (f32[256,256]{1,0:T(8,128)S(1)}, f32[256,256]{1,0:T(8,128)S(1)}, u32[]{:S(2)}, u32[]{:S(2)}) collective-permute-start(f32[256,256]{1,0:T(8,128)S(1)} %get-tuple-element.82), channel_id=1, source_target_pairs={{0,3},{1,2},{2,1},{3,0},{4,7},{5,6},{6,5},{7,4},{8,11},{9,10},{10,... | collective-permute-start | bytes 786440 | tf_op jit(solution)/shard_map/ppermute | solution.py:367

commit v8 on v7

--- a/solution.py
+++ b/solution.py
@@ -405,7 +405,7 @@
     halves = [[d for d in range(members) if (d < near) or d in (near, 2 * near)], []]
     halves[1] = [d for d in range(members) if d not in halves[0]]
 
-    early = [encs[d] for d in halves[0] if d]
+    early = [encs[d] for d in halves[0] if d and d != near]
     gather = lambda part, many, deps, name: call(
         functools.partial(gather_kernel, members, groups, part, many),
         [sds(members * many, width)] * groups,
@@ -418,7 +418,7 @@
     for x in range(1, near):
         encs[near + x] = swap(lax.optimization_barrier((encs[x], negs[0]))[0], "member", near)
     negs = [negs[0]] + [swap(negs[d], "group", d) for d in range(1, groups)]
-    rows = gather(0, slots, [encs[2 * near + x] for x in range(1, near)], "gather_targets")
+    rows = gather(0, slots, [encs[near], *encs[2 * near + 1 : 3 * near]], "gather_targets")
     rows = [rows[0]] + [swap(rows[d], "group", d) for d in range(1, groups)]
 
     stats, probs = [], []
@@ -541,21 +541,25 @@
             name="scatter",
         )
 
+    def after(blocks, done):
+        return [lax.optimization_barrier((block, done))[0] for block in blocks]
+
+    close = [*along[1:], *[near + x for x in along[1:]]]
     farthest, *rest, nearest = scaled([3 * near + x for x in along] + [near], [])
     arrived = beside(rest)
     nearest = swap(nearest, "member", near)
-    far, *others = scaled([2 * near + x for x in along], [*arrived, nearest, *graded])
-    total = added([farthest, *arrived], graded)
-    table_own = scatter([0], [], [total], 1 << 33)
-    total = swap(total, "member", near)
-    far = added([far], [table_own, *grads[1:]])
-    half = added([far, *beside(others), total], [])
-    close = [*along[1:], *[near + x for x in along[1:]]]
-    kept, *sends = scaled([0, *close], [half])
-    parts = [swap(block, "member", d) for d, block in zip(close, sends)]
+    kept, far, *others = scaled([0, *[2 * near + x for x in along], *close], graded)
+    others, sends = others[: near - 1], others[near - 1 :]
+    total = added([farthest, *arrived], [*graded, nearest])
+    others = after(others, total)
+    early_groups = list(range(2))
+    table_own = scatter(early_groups, [], [total], 1 << 33)
+    far = added([far], [table_own, *grads[2:]])
+    half = added([far, swap(total, "member", near), *beside(others)], [])
+    parts = [swap(b, "member", d) for d, b in zip(close, after(sends, half))]
     parts.append(added([nearest, kept, swap(half, "member", 2 * near)], []))
 
-    table_grad = scatter(list(range(1, groups)), [table_own], [], 0)
+    table_grad = scatter(list(range(2, groups)), [table_own], [], 0)
     encoded_grad = call(
         finish_kernel,
         sds(tokens, width),

time: 100 us -> 102 us (1.020)
  waiting for transfers between devices: 17.3 us -> 22.8 us
  starting transfers between devices: 39.6 us -> 36.1 us
    ppermute x29, waiting for transfers between devices: 9.93 us -> 14.6 us  [swap(): lax.ppermute(value, axis, [(i, i ^ d) for i in range(lax.axis_size(axis))])]
    ppermute x29, starting transfers between devices: 35.7 us -> 33.2 us  [swap(): lax.ppermute(value, axis, [(i, i ^ d) for i in range(lax.axis_size(axis))])]
    pallas_call x23 -> x22, Pallas kernels: 38.2 us -> 37.6 us  [call(): pl.pallas_call(kernel, out_shape=out_shape, in_specs=ins, out_specs=outs,...]
  transfers between devices with their start and end apart: 30 -> 30, of which waited for: 9 -> 9; matrix products, arithmetic and copies ran while one was open for 0% -> 0% of each run, Pallas kernels for 35% -> 34%
where the time goes in v8:
time: 102 us; the launch traced here: 101 us
  Pallas kernels  37.6 us (37%)
  starting transfers between devices  36.1 us (35%)
  waiting for transfers between devices  22.8 us (22%)
  local copies, waits for them, and re-layouts  3.15 us (3%)
    pallas_call x22, Pallas kernels, call(): pl.pallas_call(kernel, out_shape=out_shape, in_specs=ins, out_specs=outs,...  37.6 us
    ppermute x29, starting transfers between devices, swap(): lax.ppermute(value, axis, [(i, i ^ d) for i in range(lax.axis_size(axis))])  33.2 us
    ppermute x29, waiting for transfers between devices, swap(): lax.ppermute(value, axis, [(i, i ^ d) for i in range(lax.axis_size(axis))])  14.6 us
    all_to_all x1, waiting for transfers between devices, shards(): lax.all_to_all(request, ('group', 'member'), split_axis=0, concat_axis=0,...  8.26 us
    unnamed x6, local copies, waits for them, and re-layouts  3.14 us
    all_to_all x1, starting transfers between devices, shards(): lax.all_to_all(request, ('group', 'member'), split_axis=0, concat_axis=0,...  2.9 us
  transfers between devices with their start and end apart: 30, of which 9 were waited for; matrix products, arithmetic and copies ran while one was open for 0% of the time, Pallas kernels for 34%

profile of v8, /device:TPU:0, one launch (start us, length us, event | category | flops | bytes accessed | tf_op | source)
XLA Modules:
  0.0 101.3 jit_solution(10159017303227492646)
XLA Ops:
  0.6 0.7 pad_add_fusion
  1.5 0.9 copy-done.1
  2.4 1.8 %front.1 = (s32[32,1,256]{2,1,0:T(1,128)}, f32[256,256]{1,0:T(8,128)S(1)}) custom-call(s32[2]{0:T(128)S(1)} %pad_add_fusion.1.info, s32[1,1280]{1,0:T(1,128)S(1)} %reshape.15.ints, f32[256,256]{1,0:T(8,128)S(1)} %copy-done.1), custom_call_target="tpu_custom_call" | custom-call | tf_op jit(solution)/shard_map/front/pallas_call | solution.py:26
  4.2 4.0 %collective-permute-start = (f32[256,256]{1,0:T(8,128)S(1)}, f32[256,256]{1,0:T(8,128)S(1)}, u32[]{:S(2)}, u32[]{:S(2)}) collective-permute-start(f32[256,256]{1,0:T(8,128)S(1)} %get-tuple-element.46.refs_4_.refs_0_), channel_id=1, source_target_pairs={{0,4},{1,5},{2,6},{3,7},{4,0},{5,1},{6,2},{7,3},{8,12},{9,13},{10,... | collective-permute-start | bytes 786440 | tf_op jit(solution)/shard_map/ppermute | solution.py:367
  8.2 1.5 %collective-permute-start.1 = (f32[256,256]{1,0:T(8,128)S(1)}, f32[256,256]{1,0:T(8,128)S(1)}, u32[]{:S(2)}, u32[]{:S(2)}) collective-permute-start(f32[256,256]{1,0:T(8,128)S(1)} %get-tuple-element.46.refs_4_.refs_0_), channel_id=1, source_target_pairs={{0,1},{1,0},{2,3},{3,2},{4,5},{5,4},{6,7},{7,6},{8,9},{9,8},{10,11... | collective-permute-start | bytes 786440 | tf_op jit(solution)/shard_map/ppermute | solution.py:367
  9.7 2.9 %all-to-all-start = ((s32[32,1,256]{2,1,0:T(1,128)}), s32[32,1,256]{2,1,0:T(1,128)S(1)}, u32[]{:S(2)}, u32[]{:S(2)}) async-start(s32[32,1,256]{2,1,0:T(1,128)} %get-tuple-element.47), calls=%async_computation | async-start | bytes 65536 | tf_op jit(solution)/shard_map/all_to_all | solution.py:393
  12.6 1.8 %collective-permute-start.9 = (f32[256,256]{1,0:T(8,128)S(1)}, f32[256,256]{1,0:T(8,128)S(1)}, u32[]{:S(2)}, u32[]{:S(2)}) collective-permute-start(f32[256,256]{1,0:T(8,128)S(1)} %get-tuple-element.46.refs_4_.refs_0_), channel_id=1, source_target_pairs={{0,2},{1,3},{2,0},{3,1},{4,6},{5,7},{6,4},{7,5},{8,10},{9,11},{10,... | collective-permute-start | bytes 786440 | tf_op jit(solution)/shard_map/ppermute | solution.py:367
  14.5 8.3 %all-to-all-done.got.got_v = s32[32,1,256]{2,1,0:T(1,128)S(1)} async-done(((s32[32,1,256]{2,1,0:T(1,128)}), s32[32,1,256]{2,1,0:T(1,128)S(1)}, u32[]{:S(2)}, u32[]{:S(2)}) %all-to-all-start) | async-done | bytes 32800 | tf_op jit(solution)/shard_map/all_to_all | solution.py:393
  22.7 0.7 collective-permute-start.7
  23.4 0.5 collective-permute-start.6
  23.9 2.2 %copy-done = f32[4096,256]{1,0:T(8,128)S(1)} copy-done((f32[4096,256]{1,0:T(8,128)S(1)}, f32[4096,256]{1,0:T(8,128)}, u32[]{:S(2)}) %copy-start) | copy-done | bytes 4194328
  26.1 2.3 %gather_negatives.1 = (f32[128,256]{1,0:T(8,128)S(1)}, f32[128,256]{1,0:T(8,128)S(1)}, f32[128,256]{1,0:T(8,128)S(1)}, f32[128,256]{1,0:T(8,128)S(1)}) custom-call(s32[2]{0:T(128)S(1)} %pad_add_fusion.1.info, s32[32,1,256]{2,1,0:T(1,128)S(1)} %all-to-all-done.got.got_v, f32[4096,256]{1,0:T(8,128)S(1)} %copy-done, ...), custom_call_target="tpu_custom_call" | custom-call | tf_op jit(solution)/shard_map/gather_negatives/pallas_call | solution.py:26
  28.5 0.8 collective-permute-start.3
  29.3 1.1 %collective-permute-start.4 = (f32[128,256]{1,0:T(8,128)S(1)}, f32[128,256]{1,0:T(8,128)S(1)}, u32[]{:S(2)}, u32[]{:S(2)}) collective-permute-start(f32[128,256]{1,0:T(8,128)S(1)} %get-tuple-element.52), channel_id=1, source_target_pairs={{0,24},{8,16},{16,8},{24,0},{1,25},{9,17},{17,9},{25,1},{2,26},{10... | collective-permute-start | bytes 393224 | tf_op jit(solution)/shard_map/ppermute | solution.py:367
  30.3 1.4 %collective-permute-done.7.refs_6_.refs_10_ = f32[256,256]{1,0:T(8,128)S(1)} collective-permute-done((f32[256,256]{1,0:T(8,128)S(1)}, f32[256,256]{1,0:T(8,128)S(1)}, u32[]{:S(2)}, u32[]{:S(2)}) %collective-permute-start.7) | collective-permute-done | bytes 262176 | tf_op jit(solution)/shard_map/ppermute | solution.py:367
  31.9 1.5 %collective-permute-start.8 = (f32[256,256]{1,0:T(8,128)S(1)}, f32[256,256]{1,0:T(8,128)S(1)}, u32[]{:S(2)}, u32[]{:S(2)}) collective-permute-start(f32[256,256]{1,0:T(8,128)S(1)} %collective-permute-done.7.refs_6_.refs_10_), channel_id=1, source_target_pairs={{0,1},{1,0},{2,3},{3,2},{4,5},{5,4},{6,7},{7,6},{8,9},{9,8},{10,11... | collective-permute-start | bytes 786440 | tf_op jit(solution)/shard_map/ppermute | solution.py:367
  33.4 3.3 %gather_targets.1 = (f32[256,256]{1,0:T(8,128)S(1)}, f32[256,256]{1,0:T(8,128)S(1)}, f32[256,256]{1,0:T(8,128)S(1)}, f32[256,256]{1,0:T(8,128)S(1)}) custom-call(s32[2]{0:T(128)S(1)} %pad_add_fusion.1.info, s32[32,1,256]{2,1,0:T(1,128)S(1)} %all-to-all-done.got.got_v, f32[4096,256]{1,0:T(8,128)S(1)} %copy-done, ...), custom_call_target="tpu_custom_call" | custom-call | tf_op jit(solution)/shard_map/gather_targets/pallas_call | solution.py:26
  36.8 1.5 %collective-permute-start.11 = (f32[256,256]{1,0:T(8,128)S(1)}, f32[256,256]{1,0:T(8,128)S(1)}, u32[]{:S(2)}, u32[]{:S(2)}) collective-permute-start(f32[256,256]{1,0:T(8,128)S(1)} %get-tuple-element.59), channel_id=1, source_target_pairs={{0,16},{8,24},{16,0},{24,8},{1,17},{9,25},{17,1},{25,9},{2,18},{10... | collective-permute-start | bytes 786440 | tf_op jit(solution)/shard_map/ppermute | solution.py:367
  38.6 3.1 %score.2 = (f32[2,2048]{1,0:T(2,128)S(1)}, bf16[4,512,256]{2,1,0:T(8,128)(2,1)S(1)}, bf16[4,512,256]{2,1,0:T(8,128)(2,1)S(1)}) custom-call(s32[2]{0:T(128)S(1)} %pad_add_fusion.1.info, f32[128,256]{1,0:T(8,128)S(1)} %get-tuple-element.49.refs_0_, f32[128,256]{1,0:T(8,128)S(1)} %collective-permute-done.2.refs_1_, ...), custom_call_target="tpu_custom_call" | custom-call | flops 1610612736 | bytes 1048576 | tf_op jit(solution)/shard_map/score/pallas_call | solution.py:26
  41.7 1.6 %pick.1 = (f32[256,256]{1,0:T(8,128)S(1)}, f32[256,256]{1,0:T(8,128)S(1)}, f32[256,256]{1,0:T(8,128)S(1)}, f32[256,256]{1,0:T(8,128)S(1)}) custom-call(s32[2]{0:T(128)S(1)} %pad_add_fusion.1.info, s32[32,1,256]{2,1,0:T(1,128)S(1)} %all-to-all-done.got.got_v, f32[256,256]{1,0:T(8,128)S(1)} %get-tuple-element.46.refs_4_.refs_0_, ...), custom_call_target="tpu_custom_call" | custom-call | tf_op jit(solution)/shard_map/pick/pallas_call | solution.py:26
  43.3 0.4 collective-permute-start.16
  43.7 1.5 %collective-permute-start.17 = (f32[256,256]{1,0:T(8,128)S(1)}, f32[256,256]{1,0:T(8,128)S(1)}, u32[]{:S(2)}, u32[]{:S(2)}) collective-permute-start(f32[256,256]{1,0:T(8,128)S(1)} %get-tuple-element.63.refs_6_), channel_id=1, source_target_pairs={{0,16},{8,24},{16,0},{24,8},{1,17},{9,25},{17,1},{25,9},{2,18},{10... | collective-permute-start | bytes 786440 | tf_op jit(solution)/shard_map/ppermute | solution.py:367
  45.3 3.1 %score.3 = (f32[2,2048]{1,0:T(2,128)S(1)}, bf16[4,512,256]{2,1,0:T(8,128)(2,1)S(1)}, bf16[4,512,256]{2,1,0:T(8,128)(2,1)S(1)}) custom-call(s32[2]{0:T(128)S(1)} %pad_add_fusion.1.info, f32[128,256]{1,0:T(8,128)S(1)} %get-tuple-element.49.refs_0_, f32[128,256]{1,0:T(8,128)S(1)} %collective-permute-done.2.refs_1_, ...), custom_call_target="tpu_custom_call" | custom-call | flops 1610612736 | bytes 1048576 | tf_op jit(solution)/shard_map/score/pallas_call | solution.py:26
  48.3 2.3 %collective-permute-done.12.refs_3_.refs_7_ = f32[256,256]{1,0:T(8,128)S(1)} collective-permute-done((f32[256,256]{1,0:T(8,128)S(1)}, f32[256,256]{1,0:T(8,128)S(1)}, u32[]{:S(2)}, u32[]{:S(2)}) %collective-permute-start.12) | collective-permute-done | bytes 262176 | tf_op jit(solution)/shard_map/ppermute | solution.py:367
  50.6 1.2 %positive.1 = (f32[2,2048]{1,0:T(2,128)S(1)}, f32[2,2048]{1,0:T(2,128)S(1)}) custom-call(s32[2]{0:T(128)S(1)} %pad_add_fusion.1.info, s32[32,1,256]{2,1,0:T(1,128)S(1)} %all-to-all-done.got.got_v, f32[2,2048]{1,0:T(2,128)S(1)} %get-tuple-element.56.stats, f32[256,256]{1,0:T(8,128)S(1)} %get-tuple-element.57.refs_0_.refs_4_, ...), custom_call_target="tpu_custom_call" | custom-call | tf_op jit(solution)/shard_map/positive/pallas_call | solution.py:26
  51.8 0.6 collective-permute-start.13
  52.4 2.0 %pulled.2 = (f32[4,256,256]{2,1,0:T(8,128)S(1)}, f32[4,256,256]{2,1,0:T(8,128)S(1)}) custom-call(s32[2]{0:T(128)S(1)} %pad_add_fusion.1.info, s32[32,1,256]{2,1,0:T(1,128)S(1)} %all-to-all-done.got.got_v, f32[128,256]{1,0:T(8,128)S(1)} %get-tuple-element.49.refs_0_, f32[128,256]{1,0:T(8,128)S(1)} %collective-permute-done.2.refs_1_, ...), custom_call_target="tpu_custom_call" | custom-call | flops 805306368 | bytes 1048576 | tf_op jit(solution)/shard_map/pulled/pallas_call | solution.py:26
  54.4 1.3 %collective-permute-done.13.second = f32[2,2048]{1,0:T(2,128)S(1)} collective-permute-done((f32[2,2048]{1,0:T(2,128)S(1)}, f32[2,2048]{1,0:T(2,128)S(1)}, u32[]{:S(2)}, u32[]{:S(2)}) %collective-permute-start.13) | collective-permute-done | bytes 16416 | tf_op jit(solution)/shard_map/ppermute | solution.py:367
  55.7 2.1 %collective-permute-start.14 = (f32[2,2048]{1,0:T(2,128)S(1)}, f32[2,2048]{1,0:T(2,128)S(1)}, u32[]{:S(2)}, u32[]{:S(2)}) collective-permute-start(f32[2,2048]{1,0:T(2,128)S(1)} %join.3.first), channel_id=1, source_target_pairs={{0,2},{1,3},{2,0},{3,1},{4,6},{5,7},{6,4},{7,5},{8,10},{9,11},{10,... | collective-permute-start | bytes 49160 | tf_op jit(solution)/shard_map/ppermute | solution.py:367
  57.7 2.0 %pulled.3 = (f32[4,256,256]{2,1,0:T(8,128)S(1)}, f32[4,256,256]{2,1,0:T(8,128)S(1)}) custom-call(s32[2]{0:T(128)S(1)} %pad_add_fusion.1.info, s32[32,1,256]{2,1,0:T(1,128)S(1)} %all-to-all-done.got.got_v, f32[128,256]{1,0:T(8,128)S(1)} %get-tuple-element.49.refs_0_, f32[128,256]{1,0:T(8,128)S(1)} %collective-permute-done.2.refs_1_, ...), custom_call_target="tpu_custom_call" | custom-call | flops 805306368 | bytes 1048576 | tf_op jit(solution)/shard_map/pulled/pallas_call | solution.py:26
  59.8 3.9 %collective-permute-start.15 = (f32[2,2048]{1,0:T(2,128)S(1)}, f32[2,2048]{1,0:T(2,128)S(1)}, u32[]{:S(2)}, u32[]{:S(2)}) collective-permute-start(f32[2,2048]{1,0:T(2,128)S(1)} %join.4.first), channel_id=1, source_target_pairs={{0,4},{1,5},{2,6},{3,7},{4,0},{5,1},{6,2},{7,3},{8,12},{9,13},{10,... | collective-permute-start | bytes 49160 | tf_op jit(solution)/shard_map/ppermute | solution.py:367
  63.7 1.7 %collective-permute-done.15.second = f32[2,2048]{1,0:T(2,128)S(1)} collective-permute-done((f32[2,2048]{1,0:T(2,128)S(1)}, f32[2,2048]{1,0:T(2,128)S(1)}, u32[]{:S(2)}, u32[]{:S(2)}) %collective-permute-start.15) | collective-permute-done | bytes 16416 | tf_op jit(solution)/shard_map/ppermute | solution.py:367
  65.4 0.7 pull.3
  66.1 0.6 collective-permute-start.20
  66.7 0.7 collective-permute-start.21
  67.5 2.7 %grad.1 = (f32[136,256]{1,0:T(8,128)S(1)}, f32[136,256]{1,0:T(8,128)S(1)}, f32[136,256]{1,0:T(8,128)S(1)}, f32[136,256]{1,0:T(8,128)S(1)}) custom-call(s32[2]{0:T(128)S(1)} %pad_add_fusion.1.info, s32[32,1,256]{2,1,0:T(1,128)S(1)} %all-to-all-done.got.got_v, f32[2,2048]{1,0:T(2,128)S(1)} %join.5.final, f32[2,2048]{1,0:T(2,128)S(1)} %get-tuple-element.56.stats, ...), custom_call_target="tpu_custom_call" | custom-call | flops 1610612736 | bytes 8388608 | tf_op jit(solution)/shard_map/grad/pallas_call | solution.py:26
  70.2 1.6 %collective-permute-start.22 = (f32[136,256]{1,0:T(8,128)S(1)}, f32[136,256]{1,0:T(8,128)S(1)}, u32[]{:S(2)}, u32[]{:S(2)}) collective-permute-start(f32[136,256]{1,0:T(8,128)S(1)} %get-tuple-element.82), channel_id=1, source_target_pairs={{0,16},{8,24},{16,0},{24,8},{1,17},{9,25},{17,1},{25,9},{2,18},{10... | collective-permute-start | bytes 417800 | tf_op jit(solution)/shard_map/ppermute | solution.py:367
  72.1 0.7 pull.2
  73.2 1.1 %collective-permute-start.24 = (f32[256,256]{1,0:T(8,128)S(1)}, f32[256,256]{1,0:T(8,128)S(1)}, u32[]{:S(2)}, u32[]{:S(2)}) collective-permute-start(f32[256,256]{1,0:T(8,128)S(1)} %add.12.refs_4_), channel_id=1, source_target_pairs={{0,2},{1,3},{2,0},{3,1},{4,6},{5,7},{6,4},{7,5},{8,10},{9,11},{10,... | collective-permute-start | bytes 786440 | tf_op jit(solution)/shard_map/ppermute | solution.py:367
  74.2 1.5 %collective-permute-start.25 = (f32[256,256]{1,0:T(8,128)S(1)}, f32[256,256]{1,0:T(8,128)S(1)}, u32[]{:S(2)}, u32[]{:S(2)}) collective-permute-start(f32[256,256]{1,0:T(8,128)S(1)} %get-tuple-element.85), channel_id=1, source_target_pairs={{0,1},{1,0},{2,3},{3,2},{4,5},{5,4},{6,7},{7,6},{8,9},{9,8},{10,11... | collective-permute-start | bytes 786440 | tf_op jit(solution)/shard_map/ppermute | solution.py:367
  75.7 5.1 %scatter.2.refs_1_.refs_4_ = f32[4096,256]{1,0:T(8,128)S(1)} custom-call(s32[2]{0:T(128)S(1)} %pad_add_fusion.1.info, s32[32,1,256]{2,1,0:T(1,128)S(1)} %all-to-all-done.got.got_v, s32[32,1,256]{2,1,0:T(1,128)S(1)} %all-to-all-done.got.got_v, f32[136,256]{1,0:T(8,128)S(1)} %get-tuple-element.75.refs_4_.refs_2_.refs_0_, ...), custom_call_target="tpu_custom_call" | custom-call | flops 8589934592 | tf_op jit(solution)/shard_map/scatter/pallas_call | solution.py:26
  80.9 1.6 %collective-permute-done.25.refs_2_ = f32[256,256]{1,0:T(8,128)S(1)} collective-permute-done((f32[256,256]{1,0:T(8,128)S(1)}, f32[256,256]{1,0:T(8,128)S(1)}, u32[]{:S(2)}, u32[]{:S(2)}) %collective-permute-start.25) | collective-permute-done | bytes 262176 | tf_op jit(solution)/shard_map/ppermute | solution.py:367
  82.5 3.0 %collective-permute-start.28 = (f32[256,256]{1,0:T(8,128)S(1)}, f32[256,256]{1,0:T(8,128)S(1)}, u32[]{:S(2)}, u32[]{:S(2)}) collective-permute-start(f32[256,256]{1,0:T(8,128)S(1)} %add.14), channel_id=1, source_target_pairs={{0,4},{1,5},{2,6},{3,7},{4,0},{5,1},{6,2},{7,3},{8,12},{9,13},{10,... | collective-permute-start | bytes 786440 | tf_op jit(solution)/shard_map/ppermute | solution.py:367
  85.5 1.5 %collective-permute-start.26 = (f32[256,256]{1,0:T(8,128)S(1)}, f32[256,256]{1,0:T(8,128)S(1)}, u32[]{:S(2)}, u32[]{:S(2)}) collective-permute-start(f32[256,256]{1,0:T(8,128)S(1)} %get-tuple-element.86), channel_id=1, source_target_pairs={{0,1},{1,0},{2,3},{3,2},{4,5},{5,4},{6,7},{7,6},{8,9},{9,8},{10,11... | collective-permute-start | bytes 786440 | tf_op jit(solution)/shard_map/ppermute | solution.py:367
  87.4 7.0 %scatter.3 = f32[4096,256]{1,0:T(8,128)} custom-call(s32[2]{0:T(128)S(1)} %pad_add_fusion.1.info, s32[32,1,256]{2,1,0:T(1,128)S(1)} %all-to-all-done.got.got_v, s32[32,1,256]{2,1,0:T(1,128)S(1)} %all-to-all-done.got.got_v, f32[136,256]{1,0:T(8,128)S(1)} %collective-permute-done.22.refs_2_.refs_0_, f32[136,256]{1,0:T(8,128)S(1)} %collective-permute-done.23.refs_3_.refs_1_, ...), custom_call_target="tpu_custom_call" | custom-call | tf_op jit(solution)/shard_map/scatter/pallas_call | solution.py:26
  94.3 2.6 %collective-permute-done.28.refs_2_ = f32[256,256]{1,0:T(8,128)S(1)} collective-permute-done((f32[256,256]{1,0:T(8,128)S(1)}, f32[256,256]{1,0:T(8,128)S(1)}, u32[]{:S(2)}, u32[]{:S(2)}) %collective-permute-start.28) | collective-permute-done | bytes 262176 | tf_op jit(solution)/shard_map/ppermute | solution.py:367
  97.0 3.3 %collective-permute-done.27.refs_1_ = f32[256,256]{1,0:T(8,128)S(1)} collective-permute-done((f32[256,256]{1,0:T(8,128)S(1)}, f32[256,256]{1,0:T(8,128)S(1)}, u32[]{:S(2)}, u32[]{:S(2)}) %collective-permute-start.27) | collective-permute-done | bytes 262176 | tf_op jit(solution)/shard_map/ppermute | solution.py:367
  100.3 1.0 finish.1
  (43 shorter events, 2.0 us)
Async XLA Ops:
  1.5 1.0 copy-start.1
  4.2 18.5 %collective-permute-start = (f32[256,256]{1,0:T(8,128)S(1)}, f32[256,256]{1,0:T(8,128)S(1)}, u32[]{:S(2)}, u32[]{:S(2)}) collective-permute-start(f32[256,256]{1,0:T(8,128)S(1)} %get-tuple-element.46.refs_4_.refs_0_), channel_id=1, source_target_pairs={{0,4},{1,5},{2,6},{3,7},{4,0},{5,1},{6,2},{7,3},{8,12},{9,13},{10,... | collective-permute-start | bytes 786440 | tf_op jit(solution)/shard_map/ppermute | solution.py:367
  8.2 15.6 %collective-permute-start.1 = (f32[256,256]{1,0:T(8,128)S(1)}, f32[256,256]{1,0:T(8,128)S(1)}, u32[]{:S(2)}, u32[]{:S(2)}) collective-permute-start(f32[256,256]{1,0:T(8,128)S(1)} %get-tuple-element.46.refs_4_.refs_0_), channel_id=1, source_target_pairs={{0,1},{1,0},{2,3},{3,2},{4,5},{5,4},{6,7},{7,6},{8,9},{9,8},{10,11... | collective-permute-start | bytes 786440 | tf_op jit(solution)/shard_map/ppermute | solution.py:367
  9.7 13.0 %all-to-all-start = ((s32[32,1,256]{2,1,0:T(1,128)}), s32[32,1,256]{2,1,0:T(1,128)S(1)}, u32[]{:S(2)}, u32[]{:S(2)}) async-start(s32[32,1,256]{2,1,0:T(1,128)} %get-tuple-element.47), calls=%async_computation | async-start | bytes 65536 | tf_op jit(solution)/shard_map/all_to_all | solution.py:393
  12.6 16.6 %collective-permute-start.9 = (f32[256,256]{1,0:T(8,128)S(1)}, f32[256,256]{1,0:T(8,128)S(1)}, u32[]{:S(2)}, u32[]{:S(2)}) collective-permute-start(f32[256,256]{1,0:T(8,128)S(1)} %get-tuple-element.46.refs_4_.refs_0_), channel_id=1, source_target_pairs={{0,2},{1,3},{2,0},{3,1},{4,6},{5,7},{6,4},{7,5},{8,10},{9,11},{10,... | collective-permute-start | bytes 786440 | tf_op jit(solution)/shard_map/ppermute | solution.py:367
  22.7 9.0 %collective-permute-start.7 = (f32[256,256]{1,0:T(8,128)S(1)}, f32[256,256]{1,0:T(8,128)S(1)}, u32[]{:S(2)}, u32[]{:S(2)}) collective-permute-start(f32[256,256]{1,0:T(8,128)S(1)} %collective-permute-done.refs_1_.refs_7_.refs_4_.refs_8_), channel_id=1, source_target_pairs={{0,2},{1,3},{2,0},{3,1},{4,6},{5,7},{6,4},{7,5},{8,10},{9,11},{10,... | collective-permute-start | bytes 786440 | tf_op jit(solution)/shard_map/ppermute | solution.py:367
  23.4 8.5 %collective-permute-start.6 = (f32[256,256]{1,0:T(8,128)S(1)}, f32[256,256]{1,0:T(8,128)S(1)}, u32[]{:S(2)}, u32[]{:S(2)}) collective-permute-start(f32[256,256]{1,0:T(8,128)S(1)} %collective-permute-done.refs_1_.refs_7_.refs_4_.refs_8_), channel_id=1, source_target_pairs={{0,1},{1,0},{2,3},{3,2},{4,5},{5,4},{6,7},{7,6},{8,9},{9,8},{10,11... | collective-permute-start | bytes 786440 | tf_op jit(solution)/shard_map/ppermute | solution.py:367
  23.9 2.2 %copy-start = (f32[4096,256]{1,0:T(8,128)S(1)}, f32[4096,256]{1,0:T(8,128)}, u32[]{:S(2)}) copy-start(f32[4096,256]{1,0:T(8,128)} %table.3) | copy-start | bytes 12582916
  28.4 8.3 %collective-permute-start.2 = (f32[128,256]{1,0:T(8,128)S(1)}, f32[128,256]{1,0:T(8,128)S(1)}, u32[]{:S(2)}, u32[]{:S(2)}) collective-permute-start(f32[128,256]{1,0:T(8,128)S(1)} %get-tuple-element.50), channel_id=1, source_target_pairs={{0,8},{8,0},{16,24},{24,16},{1,9},{9,1},{17,25},{25,17},{2,10},{10... | collective-permute-start | bytes 393224 | tf_op jit(solution)/shard_map/ppermute | solution.py:367
  28.5 8.3 %collective-permute-start.3 = (f32[128,256]{1,0:T(8,128)S(1)}, f32[128,256]{1,0:T(8,128)S(1)}, u32[]{:S(2)}, u32[]{:S(2)}) collective-permute-start(f32[128,256]{1,0:T(8,128)S(1)} %get-tuple-element.51), channel_id=1, source_target_pairs={{0,16},{8,24},{16,0},{24,8},{1,17},{9,25},{17,1},{25,9},{2,18},{10... | collective-permute-start | bytes 393224 | tf_op jit(solution)/shard_map/ppermute | solution.py:367
  29.3 9.0 %collective-permute-start.4 = (f32[128,256]{1,0:T(8,128)S(1)}, f32[128,256]{1,0:T(8,128)S(1)}, u32[]{:S(2)}, u32[]{:S(2)}) collective-permute-start(f32[128,256]{1,0:T(8,128)S(1)} %get-tuple-element.52), channel_id=1, source_target_pairs={{0,24},{8,16},{16,8},{24,0},{1,25},{9,17},{17,9},{25,1},{2,26},{10... | collective-permute-start | bytes 393224 | tf_op jit(solution)/shard_map/ppermute | solution.py:367
  31.7 10.0 %collective-permute-start.5 = (f32[256,256]{1,0:T(8,128)S(1)}, f32[256,256]{1,0:T(8,128)S(1)}, u32[]{:S(2)}, u32[]{:S(2)}) collective-permute-start(f32[256,256]{1,0:T(8,128)S(1)} %collective-permute-done.1.refs_0_.refs_5_.refs_1_), channel_id=1, source_target_pairs={{0,2},{1,3},{2,0},{3,1},{4,6},{5,7},{6,4},{7,5},{8,10},{9,11},{10,... | collective-permute-start | bytes 786440 | tf_op jit(solution)/shard_map/ppermute | solution.py:367
  31.9 9.8 %collective-permute-start.8 = (f32[256,256]{1,0:T(8,128)S(1)}, f32[256,256]{1,0:T(8,128)S(1)}, u32[]{:S(2)}, u32[]{:S(2)}) collective-permute-start(f32[256,256]{1,0:T(8,128)S(1)} %collective-permute-done.7.refs_6_.refs_10_), channel_id=1, source_target_pairs={{0,1},{1,0},{2,3},{3,2},{4,5},{5,4},{6,7},{7,6},{8,9},{9,8},{10,11... | collective-permute-start | bytes 786440 | tf_op jit(solution)/shard_map/ppermute | solution.py:367
  36.7 8.6 %collective-permute-start.10 = (f32[256,256]{1,0:T(8,128)S(1)}, f32[256,256]{1,0:T(8,128)S(1)}, u32[]{:S(2)}, u32[]{:S(2)}) collective-permute-start(f32[256,256]{1,0:T(8,128)S(1)} %get-tuple-element.58), channel_id=1, source_target_pairs={{0,8},{8,0},{16,24},{24,16},{1,9},{9,1},{17,25},{25,17},{2,10},{10... | collective-permute-start | bytes 786440 | tf_op jit(solution)/shard_map/ppermute | solution.py:367
  36.8 11.6 %collective-permute-start.11 = (f32[256,256]{1,0:T(8,128)S(1)}, f32[256,256]{1,0:T(8,128)S(1)}, u32[]{:S(2)}, u32[]{:S(2)}) collective-permute-start(f32[256,256]{1,0:T(8,128)S(1)} %get-tuple-element.59), channel_id=1, source_target_pairs={{0,16},{8,24},{16,0},{24,8},{1,17},{9,25},{17,1},{25,9},{2,18},{10... | collective-permute-start | bytes 786440 | tf_op jit(solution)/shard_map/ppermute | solution.py:367
  38.3 12.3 %collective-permute-start.12 = (f32[256,256]{1,0:T(8,128)S(1)}, f32[256,256]{1,0:T(8,128)S(1)}, u32[]{:S(2)}, u32[]{:S(2)}) collective-permute-start(f32[256,256]{1,0:T(8,128)S(1)} %get-tuple-element.60), channel_id=1, source_target_pairs={{0,24},{8,16},{16,8},{24,0},{1,25},{9,17},{17,9},{25,1},{2,26},{10... | collective-permute-start | bytes 786440 | tf_op jit(solution)/shard_map/ppermute | solution.py:367
  43.3 24.1 %collective-permute-start.16 = (f32[256,256]{1,0:T(8,128)S(1)}, f32[256,256]{1,0:T(8,128)S(1)}, u32[]{:S(2)}, u32[]{:S(2)}) collective-permute-start(f32[256,256]{1,0:T(8,128)S(1)} %get-tuple-element.62.refs_5_), channel_id=1, source_target_pairs={{0,8},{8,0},{16,24},{24,16},{1,9},{9,1},{17,25},{25,17},{2,10},{10... | collective-permute-start | bytes 786440 | tf_op jit(solution)/shard_map/ppermute | solution.py:367
  43.7 23.7 %collective-permute-start.17 = (f32[256,256]{1,0:T(8,128)S(1)}, f32[256,256]{1,0:T(8,128)S(1)}, u32[]{:S(2)}, u32[]{:S(2)}) collective-permute-start(f32[256,256]{1,0:T(8,128)S(1)} %get-tuple-element.63.refs_6_), channel_id=1, source_target_pairs={{0,16},{8,24},{16,0},{24,8},{1,17},{9,25},{17,1},{25,9},{2,18},{10... | collective-permute-start | bytes 786440 | tf_op jit(solution)/shard_map/ppermute | solution.py:367
  45.2 22.2 %collective-permute-start.18 = (f32[256,256]{1,0:T(8,128)S(1)}, f32[256,256]{1,0:T(8,128)S(1)}, u32[]{:S(2)}, u32[]{:S(2)}) collective-permute-start(f32[256,256]{1,0:T(8,128)S(1)} %get-tuple-element.64.refs_7_), channel_id=1, source_target_pairs={{0,24},{8,16},{16,8},{24,0},{1,25},{9,17},{17,9},{25,1},{2,26},{10... | collective-permute-start | bytes 786440 | tf_op jit(solution)/shard_map/ppermute | solution.py:367
  51.8 3.8 %collective-permute-start.13 = (f32[2,2048]{1,0:T(2,128)S(1)}, f32[2,2048]{1,0:T(2,128)S(1)}, u32[]{:S(2)}, u32[]{:S(2)}) collective-permute-start(f32[2,2048]{1,0:T(2,128)S(1)} %get-tuple-element.65.first), channel_id=1, source_target_pairs={{0,1},{1,0},{2,3},{3,2},{4,5},{5,4},{6,7},{7,6},{8,9},{9,8},{10,11... | collective-permute-start | bytes 49160 | tf_op jit(solution)/shard_map/ppermute | solution.py:367
  55.7 4.1 %collective-permute-start.14 = (f32[2,2048]{1,0:T(2,128)S(1)}, f32[2,2048]{1,0:T(2,128)S(1)}, u32[]{:S(2)}, u32[]{:S(2)}) collective-permute-start(f32[2,2048]{1,0:T(2,128)S(1)} %join.3.first), channel_id=1, source_target_pairs={{0,2},{1,3},{2,0},{3,1},{4,6},{5,7},{6,4},{7,5},{8,10},{9,11},{10,... | collective-permute-start | bytes 49160 | tf_op jit(solution)/shard_map/ppermute | solution.py:367
  59.8 5.6 %collective-permute-start.15 = (f32[2,2048]{1,0:T(2,128)S(1)}, f32[2,2048]{1,0:T(2,128)S(1)}, u32[]{:S(2)}, u32[]{:S(2)}) collective-permute-start(f32[2,2048]{1,0:T(2,128)S(1)} %join.4.first), channel_id=1, source_target_pairs={{0,4},{1,5},{2,6},{3,7},{4,0},{5,1},{6,2},{7,3},{8,12},{9,13},{10,... | collective-permute-start | bytes 49160 | tf_op jit(solution)/shard_map/ppermute | solution.py:367
  66.1 6.7 %collective-permute-start.20 = (f32[256,256]{1,0:T(8,128)S(1)}, f32[256,256]{1,0:T(8,128)S(1)}, u32[]{:S(2)}, u32[]{:S(2)}) collective-permute-start(f32[256,256]{1,0:T(8,128)S(1)} %get-tuple-element.80), channel_id=1, source_target_pairs={{0,1},{1,0},{2,3},{3,2},{4,5},{5,4},{6,7},{7,6},{8,9},{9,8},{10,11... | collective-permute-start | bytes 786440 | tf_op jit(solution)/shard_map/ppermute | solution.py:367
  66.7 6.4 %collective-permute-start.21 = (f32[256,256]{1,0:T(8,128)S(1)}, f32[256,256]{1,0:T(8,128)S(1)}, u32[]{:S(2)}, u32[]{:S(2)}) collective-permute-start(f32[256,256]{1,0:T(8,128)S(1)} %get-tuple-element.81), channel_id=1, source_target_pairs={{0,2},{1,3},{2,0},{3,1},{4,6},{5,7},{6,4},{7,5},{8,10},{9,11},{10,... | collective-permute-start | bytes 786440 | tf_op jit(solution)/shard_map/ppermute | solution.py:367
  70.1 5.6 %collective-permute-start.19 = (f32[136,256]{1,0:T(8,128)S(1)}, f32[136,256]{1,0:T(8,128)S(1)}, u32[]{:S(2)}, u32[]{:S(2)}) collective-permute-start(f32[136,256]{1,0:T(8,128)S(1)} %get-tuple-element.78), channel_id=1, source_target_pairs={{0,8},{8,0},{16,24},{24,16},{1,9},{9,1},{17,25},{25,17},{2,10},{10... | collective-permute-start | bytes 417800 | tf_op jit(solution)/shard_map/ppermute | solution.py:367
  70.2 10.6 %collective-permute-start.22 = (f32[136,256]{1,0:T(8,128)S(1)}, f32[136,256]{1,0:T(8,128)S(1)}, u32[]{:S(2)}, u32[]{:S(2)}) collective-permute-start(f32[136,256]{1,0:T(8,128)S(1)} %get-tuple-element.82), channel_id=1, source_target_pairs={{0,16},{8,24},{16,0},{24,8},{1,17},{9,25},{17,1},{25,9},{2,18},{10... | collective-permute-start | bytes 417800 | tf_op jit(solution)/shard_map/ppermute | solution.py:367
  71.8 9.0 %collective-permute-start.23 = (f32[136,256]{1,0:T(8,128)S(1)}, f32[136,256]{1,0:T(8,128)S(1)}, u32[]{:S(2)}, u32[]{:S(2)}) collective-permute-start(f32[136,256]{1,0:T(8,128)S(1)} %get-tuple-element.83), channel_id=1, source_target_pairs={{0,24},{8,16},{16,8},{24,0},{1,25},{9,17},{17,9},{25,1},{2,26},{10... | collective-permute-start | bytes 417800 | tf_op jit(solution)/shard_map/ppermute | solution.py:367
  73.2 9.3 %collective-permute-start.24 = (f32[256,256]{1,0:T(8,128)S(1)}, f32[256,256]{1,0:T(8,128)S(1)}, u32[]{:S(2)}, u32[]{:S(2)}) collective-permute-start(f32[256,256]{1,0:T(8,128)S(1)} %add.12.refs_4_), channel_id=1, source_target_pairs={{0,2},{1,3},{2,0},{3,1},{4,6},{5,7},{6,4},{7,5},{8,10},{9,11},{10,... | collective-permute-start | bytes 786440 | tf_op jit(solution)/shard_map/ppermute | solution.py:367
  74.2 8.3 %collective-permute-start.25 = (f32[256,256]{1,0:T(8,128)S(1)}, f32[256,256]{1,0:T(8,128)S(1)}, u32[]{:S(2)}, u32[]{:S(2)}) collective-permute-start(f32[256,256]{1,0:T(8,128)S(1)} %get-tuple-element.85), channel_id=1, source_target_pairs={{0,1},{1,0},{2,3},{3,2},{4,5},{5,4},{6,7},{7,6},{8,9},{9,8},{10,11... | collective-permute-start | bytes 786440 | tf_op jit(solution)/shard_map/ppermute | solution.py:367
  82.5 14.4 %collective-permute-start.28 = (f32[256,256]{1,0:T(8,128)S(1)}, f32[256,256]{1,0:T(8,128)S(1)}, u32[]{:S(2)}, u32[]{:S(2)}) collective-permute-start(f32[256,256]{1,0:T(8,128)S(1)} %add.14), channel_id=1, source_target_pairs={{0,4},{1,5},{2,6},{3,7},{4,0},{5,1},{6,2},{7,3},{8,12},{9,13},{10,... | collective-permute-start | bytes 786440 | tf_op jit(solution)/shard_map/ppermute | solution.py:367
  85.5 14.8 %copy-start.2 = (s32[256]{0:T(256)S(1)}, s32[256]{0:T(256)}, u32[]{:S(2)}) copy-start(s32[256]{0:T(256)} %param.11) | copy-start | bytes 3076
  85.5 11.5 %collective-permute-start.26 = (f32[256,256]{1,0:T(8,128)S(1)}, f32[256,256]{1,0:T(8,128)S(1)}, u32[]{:S(2)}, u32[]{:S(2)}) collective-permute-start(f32[256,256]{1,0:T(8,128)S(1)} %get-tuple-element.86), channel_id=1, source_target_pairs={{0,1},{1,0},{2,3},{3,2},{4,5},{5,4},{6,7},{7,6},{8,9},{9,8},{10,11... | collective-permute-start | bytes 786440 | tf_op jit(solution)/shard_map/ppermute | solution.py:367
  87.0 13.3 %collective-permute-start.27 = (f32[256,256]{1,0:T(8,128)S(1)}, f32[256,256]{1,0:T(8,128)S(1)}, u32[]{:S(2)}, u32[]{:S(2)}) collective-permute-start(f32[256,256]{1,0:T(8,128)S(1)} %get-tuple-element.88), channel_id=1, source_target_pairs={{0,3},{1,2},{2,1},{3,0},{4,7},{5,6},{6,5},{7,4},{8,11},{9,10},{10,... | collective-permute-start | bytes 786440 | tf_op jit(solution)/shard_map/ppermute | solution.py:367

commit v9 on v8

--- a/solution.py
+++ b/solution.py
@@ -122,8 +122,8 @@
     out_ref[:, 0, LANES : 2 * LANES] = position.astype(I32)
 
 
-def gather_kernel(members, groups, part, count, info, got, table, *refs):
-    for d, out in enumerate(refs[-groups:]):
+def gather_kernel(members, chosen, part, count, info, got, table, *refs):
+    for d, out in zip(chosen, refs[-len(chosen) :]):
         first = (info[0] ^ d) * members
 
         def member(mr, carry, out=out, first=first):
@@ -134,11 +134,11 @@
         lax.fori_loop(0, members, member, 0)
 
 
-def score_kernel(blocks, groups, info, *refs):
+def score_kernel(blocks, groups, follows, info, *refs):
     rows, refs = refs[:groups], refs[groups:]
     encs, refs = refs[: len(blocks)], refs[len(blocks) :]
     stats, prob_hi, prob_lo = refs[-3:]
-    if len(refs) > 3:
+    if follows:
         stats[...] = refs[0][...]
     tokens = encs[0].shape[0]
     neg = split3(jnp.concatenate([row[...] for row in rows], axis=0))
@@ -406,35 +406,47 @@
     halves[1] = [d for d in range(members) if d not in halves[0]]
 
     early = [encs[d] for d in halves[0] if d and d != near]
-    gather = lambda part, many, deps, name: call(
-        functools.partial(gather_kernel, members, groups, part, many),
-        [sds(members * many, width)] * groups,
-        [SMEM, SMEM, VMEM] + [ANY] * len(deps),
-        [VMEM] * groups,
-        (info, got, item_table, *deps),
-        name=name,
-    )
-    negs = gather(slots, count, early, "gather_negatives")
+
+    def after(blocks, done):
+        return [lax.optimization_barrier((block, done))[0] for block in blocks]
+
+    def gather(chosen, part, many, deps, name):
+        return call(
+            functools.partial(gather_kernel, members, chosen, part, many),
+            [sds(members * many, width)] * len(chosen),
+            [SMEM, SMEM, VMEM] + [ANY] * len(deps),
+            [VMEM] * len(chosen),
+            (info, got, item_table, *deps),
+            name=name,
+        )
+
+    negs = gather(range(groups), slots, count, early, "gather_negatives")
     for x in range(1, near):
         encs[near + x] = swap(lax.optimization_barrier((encs[x], negs[0]))[0], "member", near)
     negs = [negs[0]] + [swap(negs[d], "group", d) for d in range(1, groups)]
-    rows = gather(0, slots, [encs[near], *encs[2 * near + 1 : 3 * near]], "gather_targets")
-    rows = [rows[0]] + [swap(rows[d], "group", d) for d in range(1, groups)]
+    waited = [encs[near], *encs[2 * near + 1 : 3 * near]]
+    rows = gather(range(2, groups), 0, slots, waited, "gather_far_targets")
+    gathered = rows
+    rows = [swap(row, "group", d) for d, row in enumerate(rows, 2)]
 
     stats, probs = [], []
     for blocks in halves:
         many = len(blocks)
         *stats, hi, lo = call(
-            functools.partial(score_kernel, blocks, groups),
+            functools.partial(score_kernel, blocks, groups, bool(stats)),
             [sds(2, everyone)] + [shape((many, negatives, tokens), BF16)] * 2,
-            [SMEM] + [VMEM] * (groups + many + len(stats)),
+            [SMEM] + [VMEM] * (groups + many + len(stats)) + [ANY] * len(gathered),
             [VMEM] * 3,
-            (info, *negs, *[encs[e] for e in blocks], *stats),
+            (info, *negs, *[encs[e] for e in blocks], *stats, *gathered),
             flops=12 * many * tokens * negatives * width,
             moved=MIB,
             name="score",
         )
         probs += [hi, lo]
+        if gathered:
+            gathered = []
+            kept, row = gather(range(2), 0, slots, stats, "gather_targets")
+            rows = [kept, swap(row, "group", 1), *rows]
     stats = stats[0]
     picked = call(
         functools.partial(pick_kernel, members, groups, slots),
@@ -445,7 +457,9 @@
         scratch=[pltpu.VMEM((members, LANES), I32), pltpu.VMEM((LANES, 1), I32)],
         name="pick",
     )
-    sent = [picked[0]] + [swap(picked[d], "group", d) for d in range(1, groups)]
+    sent = list(picked[:1]) + [
+        swap(b, "group", d) for d, b in enumerate(after(picked[1:], stats), 1)
+    ]
     joined, own = call(
         functools.partial(positive_kernel, members, groups, slots, tokens),
         [sds(2, everyone)] * 2,
@@ -541,9 +555,6 @@
             name="scatter",
         )
 
-    def after(blocks, done):
-        return [lax.optimization_barrier((block, done))[0] for block in blocks]
-
     close = [*along[1:], *[near + x for x in along[1:]]]
     farthest, *rest, nearest = scaled([3 * near + x for x in along] + [near], [])
     arrived = beside(rest)
@@ -555,8 +566,10 @@
     early_groups = list(range(2))
     table_own = scatter(early_groups, [], [total], 1 << 33)
     far = added([far], [table_own, *grads[2:]])
-    half = added([far, swap(total, "member", near), *beside(others)], [])
-    parts = [swap(b, "member", d) for d, b in zip(close, after(sends, half))]
+    others = beside(others)
+    half = added([far, swap(total, "member", near), *others], [])
+    held = after(sends[: near - 1], half) + after(sends[near - 1 :], others[0])
+    parts = [swap(b, "member", d) for d, b in zip(close, held)]
     parts.append(added([nearest, kept, swap(half, "member", 2 * near)], []))
 
     table_grad = scatter(list(range(2, groups)), [table_own], [], 0)

time: 102 us -> 97.9 us (0.960)
  waiting for transfers between devices: 22.8 us -> 16.1 us
  starting transfers between devices: 36.1 us -> 38.1 us
    ppermute x29, waiting for transfers between devices: 14.6 us -> 8.71 us  [swap(): lax.ppermute(value, axis, [(i, i ^ d) for i in range(lax.axis_size(axis))])]
    ppermute x29, starting transfers between devices: 33.2 us -> 34.3 us  [swap(): lax.ppermute(value, axis, [(i, i ^ d) for i in range(lax.axis_size(axis))])]
    pallas_call x22 -> x23, Pallas kernels: 37.6 us -> 38.6 us  [call(): pl.pallas_call(kernel, out_shape=out_shape, in_specs=ins, out_specs=outs,...]
    unnamed x6 -> x8, local copies, waits for them, and re-layouts: 3.14 us -> 3.15 us
  transfers between devices with their start and end apart: 30 -> 30, of which waited for: 9 -> 9; matrix products, arithmetic and copies ran while one was open for 0% -> 0% of each run, Pallas kernels for 34% -> 37%
where the time goes in v9:
time: 97.9 us; the launch traced here: 97.6 us
  Pallas kernels  38.6 us (39%)
  starting transfers between devices  38.1 us (39%)
  waiting for transfers between devices  16.1 us (16%)
  local copies, waits for them, and re-layouts  3.15 us (3%)
    pallas_call x23, Pallas kernels, call(): pl.pallas_call(kernel, out_shape=out_shape, in_specs=ins, out_specs=outs,...  38.6 us
    ppermute x29, starting transfers between devices, swap(): lax.ppermute(value, axis, [(i, i ^ d) for i in range(lax.axis_size(axis))])  34.3 us
    ppermute x29, waiting for transfers between devices, swap(): lax.ppermute(value, axis, [(i, i ^ d) for i in range(lax.axis_size(axis))])  8.71 us
    all_to_all x1, waiting for transfers between devices, shards(): lax.all_to_all(request, ('group', 'member'), split_axis=0, concat_axis=0,...  7.36 us
    all_to_all x1, starting transfers between devices, shards(): lax.all_to_all(request, ('group', 'member'), split_axis=0, concat_axis=0,...  3.82 us
    unnamed x8, local copies, waits for them, and re-layouts  3.15 us
  transfers between devices with their start and end apart: 30, of which 9 were waited for; matrix products, arithmetic and copies ran while one was open for 0% of the time, Pallas kernels for 37%

profile of v9, /device:TPU:0, one launch (start us, length us, event | category | flops | bytes accessed | tf_op | source)
XLA Modules:
  0.0 97.6 jit_solution(2430875291650205058)
XLA Ops:
  0.6 0.7 pad_add_fusion
  1.5 0.9 copy-done.2
  2.4 1.8 %front.1 = (s32[32,1,256]{2,1,0:T(1,128)}, f32[256,256]{1,0:T(8,128)S(1)}) custom-call(s32[2]{0:T(128)S(1)} %pad_add_fusion.1.info, s32[1,1280]{1,0:T(1,128)S(1)} %reshape.15.ints, f32[256,256]{1,0:T(8,128)S(1)} %copy-done.2), custom_call_target="tpu_custom_call" | custom-call | tf_op jit(solution)/shard_map/front/pallas_call | solution.py:26
  4.2 4.0 %collective-permute-start = (f32[256,256]{1,0:T(8,128)S(1)}, f32[256,256]{1,0:T(8,128)S(1)}, u32[]{:S(2)}, u32[]{:S(2)}) collective-permute-start(f32[256,256]{1,0:T(8,128)S(1)} %get-tuple-element.49.refs_4_.refs_0_), channel_id=1, source_target_pairs={{0,4},{1,5},{2,6},{3,7},{4,0},{5,1},{6,2},{7,3},{8,12},{9,13},{10,... | collective-permute-start | bytes 786440 | tf_op jit(solution)/shard_map/ppermute | solution.py:367
  8.2 3.8 %all-to-all-start = ((s32[32,1,256]{2,1,0:T(1,128)}), s32[32,1,256]{2,1,0:T(1,128)S(1)}, u32[]{:S(2)}, u32[]{:S(2)}) async-start(s32[32,1,256]{2,1,0:T(1,128)} %get-tuple-element.50), calls=%async_computation | async-start | bytes 65536 | tf_op jit(solution)/shard_map/all_to_all | solution.py:393
  12.1 1.8 %collective-permute-start.1 = (f32[256,256]{1,0:T(8,128)S(1)}, f32[256,256]{1,0:T(8,128)S(1)}, u32[]{:S(2)}, u32[]{:S(2)}) collective-permute-start(f32[256,256]{1,0:T(8,128)S(1)} %get-tuple-element.49.refs_4_.refs_0_), channel_id=1, source_target_pairs={{0,1},{1,0},{2,3},{3,2},{4,5},{5,4},{6,7},{7,6},{8,9},{9,8},{10,11... | collective-permute-start | bytes 786440 | tf_op jit(solution)/shard_map/ppermute | solution.py:367
  13.9 1.5 %collective-permute-start.9 = (f32[256,256]{1,0:T(8,128)S(1)}, f32[256,256]{1,0:T(8,128)S(1)}, u32[]{:S(2)}, u32[]{:S(2)}) collective-permute-start(f32[256,256]{1,0:T(8,128)S(1)} %get-tuple-element.49.refs_4_.refs_0_), channel_id=1, source_target_pairs={{0,2},{1,3},{2,0},{3,1},{4,6},{5,7},{6,4},{7,5},{8,10},{9,11},{10,... | collective-permute-start | bytes 786440 | tf_op jit(solution)/shard_map/ppermute | solution.py:367
  15.4 7.4 %all-to-all-done.got.got_v = s32[32,1,256]{2,1,0:T(1,128)S(1)} async-done(((s32[32,1,256]{2,1,0:T(1,128)}), s32[32,1,256]{2,1,0:T(1,128)S(1)}, u32[]{:S(2)}, u32[]{:S(2)}) %all-to-all-start) | async-done | bytes 32800 | tf_op jit(solution)/shard_map/all_to_all | solution.py:393
  22.7 0.7 collective-permute-start.7
  23.4 0.5 collective-permute-start.6
  23.9 2.2 %copy-done = f32[4096,256]{1,0:T(8,128)S(1)} copy-done((f32[4096,256]{1,0:T(8,128)S(1)}, f32[4096,256]{1,0:T(8,128)}, u32[]{:S(2)}) %copy-start) | copy-done | bytes 4194328
  26.1 2.3 %gather_negatives.1 = (f32[128,256]{1,0:T(8,128)S(1)}, f32[128,256]{1,0:T(8,128)S(1)}, f32[128,256]{1,0:T(8,128)S(1)}, f32[128,256]{1,0:T(8,128)S(1)}) custom-call(s32[2]{0:T(128)S(1)} %pad_add_fusion.1.info, s32[32,1,256]{2,1,0:T(1,128)S(1)} %all-to-all-done.got.got_v, f32[4096,256]{1,0:T(8,128)S(1)} %copy-done, ...), custom_call_target="tpu_custom_call" | custom-call | tf_op jit(solution)/shard_map/gather_negatives/pallas_call | solution.py:26
  28.5 0.8 collective-permute-start.3
  29.3 1.1 %collective-permute-start.4 = (f32[128,256]{1,0:T(8,128)S(1)}, f32[128,256]{1,0:T(8,128)S(1)}, u32[]{:S(2)}, u32[]{:S(2)}) collective-permute-start(f32[128,256]{1,0:T(8,128)S(1)} %get-tuple-element.55), channel_id=1, source_target_pairs={{0,24},{8,16},{16,8},{24,0},{1,25},{9,17},{17,9},{25,1},{2,26},{10... | collective-permute-start | bytes 393224 | tf_op jit(solution)/shard_map/ppermute | solution.py:367
  30.4 1.4 %collective-permute-done.7.refs_6_.refs_10_ = f32[256,256]{1,0:T(8,128)S(1)} collective-permute-done((f32[256,256]{1,0:T(8,128)S(1)}, f32[256,256]{1,0:T(8,128)S(1)}, u32[]{:S(2)}, u32[]{:S(2)}) %collective-permute-start.7) | collective-permute-done | bytes 262176 | tf_op jit(solution)/shard_map/ppermute | solution.py:367
  31.9 1.4 %collective-permute-start.8 = (f32[256,256]{1,0:T(8,128)S(1)}, f32[256,256]{1,0:T(8,128)S(1)}, u32[]{:S(2)}, u32[]{:S(2)}) collective-permute-start(f32[256,256]{1,0:T(8,128)S(1)} %collective-permute-done.7.refs_6_.refs_10_), channel_id=1, source_target_pairs={{0,1},{1,0},{2,3},{3,2},{4,5},{5,4},{6,7},{7,6},{8,9},{9,8},{10,11... | collective-permute-start | bytes 786440 | tf_op jit(solution)/shard_map/ppermute | solution.py:367
  33.2 2.2 %gather_far_targets.1 = (f32[256,256]{1,0:T(8,128)S(1)}, f32[256,256]{1,0:T(8,128)S(1)}) custom-call(s32[2]{0:T(128)S(1)} %pad_add_fusion.1.info, s32[32,1,256]{2,1,0:T(1,128)S(1)} %all-to-all-done.got.got_v, f32[4096,256]{1,0:T(8,128)S(1)} %copy-done, f32[256,256]{1,0:T(8,128)S(1)} %collective-permute-done.9.refs_0_.refs_6_.refs_2_, ...), custom_call_target="tpu_custom_call" | custom-call | tf_op jit(solution)/shard_map/gather_far_targets/pallas_call | solution.py:26
  35.4 1.4 %collective-permute-start.11 = (f32[256,256]{1,0:T(8,128)S(1)}, f32[256,256]{1,0:T(8,128)S(1)}, u32[]{:S(2)}, u32[]{:S(2)}) collective-permute-start(f32[256,256]{1,0:T(8,128)S(1)} %get-tuple-element.58.refs_8_), channel_id=1, source_target_pairs={{0,16},{8,24},{16,0},{24,8},{1,17},{9,25},{17,1},{25,9},{2,18},{10... | collective-permute-start | bytes 786440 | tf_op jit(solution)/shard_map/ppermute | solution.py:367
  36.8 3.1 %score.2 = (f32[2,2048]{1,0:T(2,128)S(1)}, bf16[4,512,256]{2,1,0:T(8,128)(2,1)S(1)}, bf16[4,512,256]{2,1,0:T(8,128)(2,1)S(1)}) custom-call(s32[2]{0:T(128)S(1)} %pad_add_fusion.1.info, f32[128,256]{1,0:T(8,128)S(1)} %get-tuple-element.52.refs_0_, f32[128,256]{1,0:T(8,128)S(1)} %collective-permute-done.2.refs_1_, ...), custom_call_target="tpu_custom_call" | custom-call | flops 1610612736 | bytes 1048576 | tf_op jit(solution)/shard_map/score/pallas_call | solution.py:26
  39.9 2.4 %gather_targets.1 = (f32[256,256]{1,0:T(8,128)S(1)}, f32[256,256]{1,0:T(8,128)S(1)}) custom-call(s32[2]{0:T(128)S(1)} %pad_add_fusion.1.info, s32[32,1,256]{2,1,0:T(1,128)S(1)} %all-to-all-done.got.got_v, f32[4096,256]{1,0:T(8,128)S(1)} %copy-done.1, f32[2,2048]{1,0:T(2,128)S(1)} %get-tuple-element.60.refs_8_.refs_0_), custom_call_target="tpu_custom_call" | custom-call | tf_op jit(solution)/shard_map/gather_targets/pallas_call | solution.py:26
  42.3 0.9 collective-permute-start.10
  43.2 1.6 %pick.1 = (f32[256,256]{1,0:T(8,128)S(1)}, f32[256,256]{1,0:T(8,128)S(1)}, f32[256,256]{1,0:T(8,128)S(1)}, f32[256,256]{1,0:T(8,128)S(1)}) custom-call(s32[2]{0:T(128)S(1)} %pad_add_fusion.1.info, s32[32,1,256]{2,1,0:T(1,128)S(1)} %all-to-all-done.got.got_v, f32[256,256]{1,0:T(8,128)S(1)} %get-tuple-element.49.refs_4_.refs_0_, ...), custom_call_target="tpu_custom_call" | custom-call | tf_op jit(solution)/shard_map/pick/pallas_call | solution.py:26
  44.8 3.1 %score.3 = (f32[2,2048]{1,0:T(2,128)S(1)}, bf16[4,512,256]{2,1,0:T(8,128)(2,1)S(1)}, bf16[4,512,256]{2,1,0:T(8,128)(2,1)S(1)}) custom-call(s32[2]{0:T(128)S(1)} %pad_add_fusion.1.info, f32[128,256]{1,0:T(8,128)S(1)} %get-tuple-element.52.refs_0_, f32[128,256]{1,0:T(8,128)S(1)} %collective-permute-done.2.refs_1_, ...), custom_call_target="tpu_custom_call" | custom-call | flops 1610612736 | bytes 1048576 | tf_op jit(solution)/shard_map/score/pallas_call | solution.py:26
  47.9 1.4 %collective-permute-start.17 = (f32[256,256]{1,0:T(8,128)S(1)}, f32[256,256]{1,0:T(8,128)S(1)}, u32[]{:S(2)}, u32[]{:S(2)}) collective-permute-start(f32[256,256]{1,0:T(8,128)S(1)} %get-tuple-element.79.refs_6_), channel_id=1, source_target_pairs={{0,16},{8,24},{16,0},{24,8},{1,17},{9,25},{17,1},{25,9},{2,18},{10... | collective-permute-start | bytes 786440 | tf_op jit(solution)/shard_map/ppermute | solution.py:367
  49.8 1.2 %positive.1 = (f32[2,2048]{1,0:T(2,128)S(1)}, f32[2,2048]{1,0:T(2,128)S(1)}) custom-call(s32[2]{0:T(128)S(1)} %pad_add_fusion.1.info, s32[32,1,256]{2,1,0:T(1,128)S(1)} %all-to-all-done.got.got_v, f32[2,2048]{1,0:T(2,128)S(1)} %get-tuple-element.61.stats, f32[256,256]{1,0:T(8,128)S(1)} %get-tuple-element.62.refs_0_.refs_4_, ...), custom_call_target="tpu_custom_call" | custom-call | tf_op jit(solution)/shard_map/positive/pallas_call | solution.py:26
  51.0 1.4 %collective-permute-start.13 = (f32[2,2048]{1,0:T(2,128)S(1)}, f32[2,2048]{1,0:T(2,128)S(1)}, u32[]{:S(2)}, u32[]{:S(2)}) collective-permute-start(f32[2,2048]{1,0:T(2,128)S(1)} %get-tuple-element.68.first), channel_id=1, source_target_pairs={{0,1},{1,0},{2,3},{3,2},{4,5},{5,4},{6,7},{7,6},{8,9},{9,8},{10,11... | collective-permute-start | bytes 49160 | tf_op jit(solution)/shard_map/ppermute | solution.py:367
  52.4 2.0 %pulled.2 = (f32[4,256,256]{2,1,0:T(8,128)S(1)}, f32[4,256,256]{2,1,0:T(8,128)S(1)}) custom-call(s32[2]{0:T(128)S(1)} %pad_add_fusion.1.info, s32[32,1,256]{2,1,0:T(1,128)S(1)} %all-to-all-done.got.got_v, f32[128,256]{1,0:T(8,128)S(1)} %get-tuple-element.52.refs_0_, f32[128,256]{1,0:T(8,128)S(1)} %collective-permute-done.2.refs_1_, ...), custom_call_target="tpu_custom_call" | custom-call | flops 805306368 | bytes 1048576 | tf_op jit(solution)/shard_map/pulled/pallas_call | solution.py:26
  54.8 1.7 %collective-permute-start.14 = (f32[2,2048]{1,0:T(2,128)S(1)}, f32[2,2048]{1,0:T(2,128)S(1)}, u32[]{:S(2)}, u32[]{:S(2)}) collective-permute-start(f32[2,2048]{1,0:T(2,128)S(1)} %join.3.first), channel_id=1, source_target_pairs={{0,2},{1,3},{2,0},{3,1},{4,6},{5,7},{6,4},{7,5},{8,10},{9,11},{10,... | collective-permute-start | bytes 49160 | tf_op jit(solution)/shard_map/ppermute | solution.py:367
  56.6 2.0 %pulled.3 = (f32[4,256,256]{2,1,0:T(8,128)S(1)}, f32[4,256,256]{2,1,0:T(8,128)S(1)}) custom-call(s32[2]{0:T(128)S(1)} %pad_add_fusion.1.info, s32[32,1,256]{2,1,0:T(1,128)S(1)} %all-to-all-done.got.got_v, f32[128,256]{1,0:T(8,128)S(1)} %get-tuple-element.52.refs_0_, f32[128,256]{1,0:T(8,128)S(1)} %collective-permute-done.2.refs_1_, ...), custom_call_target="tpu_custom_call" | custom-call | flops 805306368 | bytes 1048576 | tf_op jit(solution)/shard_map/pulled/pallas_call | solution.py:26
  58.7 4.3 %collective-permute-start.15 = (f32[2,2048]{1,0:T(2,128)S(1)}, f32[2,2048]{1,0:T(2,128)S(1)}, u32[]{:S(2)}, u32[]{:S(2)}) collective-permute-start(f32[2,2048]{1,0:T(2,128)S(1)} %join.4.first), channel_id=1, source_target_pairs={{0,4},{1,5},{2,6},{3,7},{4,0},{5,1},{6,2},{7,3},{8,12},{9,13},{10,... | collective-permute-start | bytes 49160 | tf_op jit(solution)/shard_map/ppermute | solution.py:367
  63.0 1.7 %collective-permute-done.15.second = f32[2,2048]{1,0:T(2,128)S(1)} collective-permute-done((f32[2,2048]{1,0:T(2,128)S(1)}, f32[2,2048]{1,0:T(2,128)S(1)}, u32[]{:S(2)}, u32[]{:S(2)}) %collective-permute-start.15) | collective-permute-done | bytes 16416 | tf_op jit(solution)/shard_map/ppermute | solution.py:367
  64.7 0.7 pull.3
  65.4 0.6 collective-permute-start.20
  66.0 0.7 collective-permute-start.21
  66.8 2.7 %grad.1 = (f32[136,256]{1,0:T(8,128)S(1)}, f32[136,256]{1,0:T(8,128)S(1)}, f32[136,256]{1,0:T(8,128)S(1)}, f32[136,256]{1,0:T(8,128)S(1)}) custom-call(s32[2]{0:T(128)S(1)} %pad_add_fusion.1.info, s32[32,1,256]{2,1,0:T(1,128)S(1)} %all-to-all-done.got.got_v, f32[2,2048]{1,0:T(2,128)S(1)} %join.5.final, f32[2,2048]{1,0:T(2,128)S(1)} %get-tuple-element.61.stats, ...), custom_call_target="tpu_custom_call" | custom-call | flops 1610612736 | bytes 8388608 | tf_op jit(solution)/shard_map/grad/pallas_call | solution.py:26
  69.5 1.6 %collective-permute-start.22 = (f32[136,256]{1,0:T(8,128)S(1)}, f32[136,256]{1,0:T(8,128)S(1)}, u32[]{:S(2)}, u32[]{:S(2)}) collective-permute-start(f32[136,256]{1,0:T(8,128)S(1)} %get-tuple-element.88), channel_id=1, source_target_pairs={{0,16},{8,24},{16,0},{24,8},{1,17},{9,25},{17,1},{25,9},{2,18},{10... | collective-permute-start | bytes 417800 | tf_op jit(solution)/shard_map/ppermute | solution.py:367
  71.4 0.7 pull.2
  72.4 1.1 %collective-permute-start.24 = (f32[256,256]{1,0:T(8,128)S(1)}, f32[256,256]{1,0:T(8,128)S(1)}, u32[]{:S(2)}, u32[]{:S(2)}) collective-permute-start(f32[256,256]{1,0:T(8,128)S(1)} %add.12.refs_4_), channel_id=1, source_target_pairs={{0,2},{1,3},{2,0},{3,1},{4,6},{5,7},{6,4},{7,5},{8,10},{9,11},{10,... | collective-permute-start | bytes 786440 | tf_op jit(solution)/shard_map/ppermute | solution.py:367
  73.5 1.5 %collective-permute-start.25 = (f32[256,256]{1,0:T(8,128)S(1)}, f32[256,256]{1,0:T(8,128)S(1)}, u32[]{:S(2)}, u32[]{:S(2)}) collective-permute-start(f32[256,256]{1,0:T(8,128)S(1)} %get-tuple-element.91), channel_id=1, source_target_pairs={{0,1},{1,0},{2,3},{3,2},{4,5},{5,4},{6,7},{7,6},{8,9},{9,8},{10,11... | collective-permute-start | bytes 786440 | tf_op jit(solution)/shard_map/ppermute | solution.py:367
  75.0 4.9 %scatter.2.refs_1_.refs_4_ = f32[4096,256]{1,0:T(8,128)S(1)} custom-call(s32[2]{0:T(128)S(1)} %pad_add_fusion.1.info, s32[32,1,256]{2,1,0:T(1,128)S(1)} %all-to-all-done.got.got_v, s32[32,1,256]{2,1,0:T(1,128)S(1)} %all-to-all-done.got.got_v, f32[136,256]{1,0:T(8,128)S(1)} %get-tuple-element.81.refs_4_.refs_2_.refs_0_, ...), custom_call_target="tpu_custom_call" | custom-call | flops 8589934592 | tf_op jit(solution)/shard_map/scatter/pallas_call | solution.py:26
  80.0 1.8 %collective-permute-done.25.refs_2_ = f32[256,256]{1,0:T(8,128)S(1)} collective-permute-done((f32[256,256]{1,0:T(8,128)S(1)}, f32[256,256]{1,0:T(8,128)S(1)}, u32[]{:S(2)}, u32[]{:S(2)}) %collective-permute-start.25) | collective-permute-done | bytes 262176 | tf_op jit(solution)/shard_map/ppermute | solution.py:367
  81.8 1.3 %collective-permute-start.27 = (f32[256,256]{1,0:T(8,128)S(1)}, f32[256,256]{1,0:T(8,128)S(1)}, u32[]{:S(2)}, u32[]{:S(2)}) collective-permute-start(f32[256,256]{1,0:T(8,128)S(1)} %get-tuple-element.94), channel_id=1, source_target_pairs={{0,3},{1,2},{2,1},{3,0},{4,7},{5,6},{6,5},{7,4},{8,11},{9,10},{10,... | collective-permute-start | bytes 786440 | tf_op jit(solution)/shard_map/ppermute | solution.py:367
  83.1 3.0 %collective-permute-start.28 = (f32[256,256]{1,0:T(8,128)S(1)}, f32[256,256]{1,0:T(8,128)S(1)}, u32[]{:S(2)}, u32[]{:S(2)}) collective-permute-start(f32[256,256]{1,0:T(8,128)S(1)} %add.14), channel_id=1, source_target_pairs={{0,4},{1,5},{2,6},{3,7},{4,0},{5,1},{6,2},{7,3},{8,12},{9,13},{10,... | collective-permute-start | bytes 786440 | tf_op jit(solution)/shard_map/ppermute | solution.py:367
  86.1 0.5 collective-permute-start.26
  86.6 7.0 %scatter.3 = f32[4096,256]{1,0:T(8,128)} custom-call(s32[2]{0:T(128)S(1)} %pad_add_fusion.1.info, s32[32,1,256]{2,1,0:T(1,128)S(1)} %all-to-all-done.got.got_v, s32[32,1,256]{2,1,0:T(1,128)S(1)} %all-to-all-done.got.got_v, f32[136,256]{1,0:T(8,128)S(1)} %collective-permute-done.22.refs_2_.refs_0_, f32[136,256]{1,0:T(8,128)S(1)} %collective-permute-done.23.refs_3_.refs_1_, ...), custom_call_target="tpu_custom_call" | custom-call | tf_op jit(solution)/shard_map/scatter/pallas_call | solution.py:26
  93.7 2.2 %collective-permute-done.27.refs_1_ = f32[256,256]{1,0:T(8,128)S(1)} collective-permute-done((f32[256,256]{1,0:T(8,128)S(1)}, f32[256,256]{1,0:T(8,128)S(1)}, u32[]{:S(2)}, u32[]{:S(2)}) %collective-permute-start.27) | collective-permute-done | bytes 262176 | tf_op jit(solution)/shard_map/ppermute | solution.py:367
  95.8 0.8 collective-permute-done.26.refs_0_
  96.7 1.0 finish.1
  (46 shorter events, 2.2 us)
Async XLA Ops:
  1.5 1.0 copy-start.2
  4.2 18.5 %collective-permute-start = (f32[256,256]{1,0:T(8,128)S(1)}, f32[256,256]{1,0:T(8,128)S(1)}, u32[]{:S(2)}, u32[]{:S(2)}) collective-permute-start(f32[256,256]{1,0:T(8,128)S(1)} %get-tuple-element.49.refs_4_.refs_0_), channel_id=1, source_target_pairs={{0,4},{1,5},{2,6},{3,7},{4,0},{5,1},{6,2},{7,3},{8,12},{9,13},{10,... | collective-permute-start | bytes 786440 | tf_op jit(solution)/shard_map/ppermute | solution.py:367
  8.2 14.5 %all-to-all-start = ((s32[32,1,256]{2,1,0:T(1,128)}), s32[32,1,256]{2,1,0:T(1,128)S(1)}, u32[]{:S(2)}, u32[]{:S(2)}) async-start(s32[32,1,256]{2,1,0:T(1,128)} %get-tuple-element.50), calls=%async_computation | async-start | bytes 65536 | tf_op jit(solution)/shard_map/all_to_all | solution.py:393
  12.1 11.9 %collective-permute-start.1 = (f32[256,256]{1,0:T(8,128)S(1)}, f32[256,256]{1,0:T(8,128)S(1)}, u32[]{:S(2)}, u32[]{:S(2)}) collective-permute-start(f32[256,256]{1,0:T(8,128)S(1)} %get-tuple-element.49.refs_4_.refs_0_), channel_id=1, source_target_pairs={{0,1},{1,0},{2,3},{3,2},{4,5},{5,4},{6,7},{7,6},{8,9},{9,8},{10,11... | collective-permute-start | bytes 786440 | tf_op jit(solution)/shard_map/ppermute | solution.py:367
  13.9 15.4 %collective-permute-start.9 = (f32[256,256]{1,0:T(8,128)S(1)}, f32[256,256]{1,0:T(8,128)S(1)}, u32[]{:S(2)}, u32[]{:S(2)}) collective-permute-start(f32[256,256]{1,0:T(8,128)S(1)} %get-tuple-element.49.refs_4_.refs_0_), channel_id=1, source_target_pairs={{0,2},{1,3},{2,0},{3,1},{4,6},{5,7},{6,4},{7,5},{8,10},{9,11},{10,... | collective-permute-start | bytes 786440 | tf_op jit(solution)/shard_map/ppermute | solution.py:367
  22.7 9.0 %collective-permute-start.7 = (f32[256,256]{1,0:T(8,128)S(1)}, f32[256,256]{1,0:T(8,128)S(1)}, u32[]{:S(2)}, u32[]{:S(2)}) collective-permute-start(f32[256,256]{1,0:T(8,128)S(1)} %collective-permute-done.refs_1_.refs_7_.refs_4_.refs_8_), channel_id=1, source_target_pairs={{0,2},{1,3},{2,0},{3,1},{4,6},{5,7},{6,4},{7,5},{8,10},{9,11},{10,... | collective-permute-start | bytes 786440 | tf_op jit(solution)/shard_map/ppermute | solution.py:367
  23.4 8.5 %collective-permute-start.6 = (f32[256,256]{1,0:T(8,128)S(1)}, f32[256,256]{1,0:T(8,128)S(1)}, u32[]{:S(2)}, u32[]{:S(2)}) collective-permute-start(f32[256,256]{1,0:T(8,128)S(1)} %collective-permute-done.refs_1_.refs_7_.refs_4_.refs_8_), channel_id=1, source_target_pairs={{0,1},{1,0},{2,3},{3,2},{4,5},{5,4},{6,7},{7,6},{8,9},{9,8},{10,11... | collective-permute-start | bytes 786440 | tf_op jit(solution)/shard_map/ppermute | solution.py:367
  23.9 2.2 %copy-start = (f32[4096,256]{1,0:T(8,128)S(1)}, f32[4096,256]{1,0:T(8,128)}, u32[]{:S(2)}) copy-start(f32[4096,256]{1,0:T(8,128)} %table.5) | copy-start | bytes 12582916
  28.4 7.0 %collective-permute-start.2 = (f32[128,256]{1,0:T(8,128)S(1)}, f32[128,256]{1,0:T(8,128)S(1)}, u32[]{:S(2)}, u32[]{:S(2)}) collective-permute-start(f32[128,256]{1,0:T(8,128)S(1)} %get-tuple-element.53), channel_id=1, source_target_pairs={{0,8},{8,0},{16,24},{24,16},{1,9},{9,1},{17,25},{25,17},{2,10},{10... | collective-permute-start | bytes 393224 | tf_op jit(solution)/shard_map/ppermute | solution.py:367
  28.5 8.3 %collective-permute-start.3 = (f32[128,256]{1,0:T(8,128)S(1)}, f32[128,256]{1,0:T(8,128)S(1)}, u32[]{:S(2)}, u32[]{:S(2)}) collective-permute-start(f32[128,256]{1,0:T(8,128)S(1)} %get-tuple-element.54), channel_id=1, source_target_pairs={{0,16},{8,24},{16,0},{24,8},{1,17},{9,25},{17,1},{25,9},{2,18},{10... | collective-permute-start | bytes 393224 | tf_op jit(solution)/shard_map/ppermute | solution.py:367
  29.3 7.5 %collective-permute-start.4 = (f32[128,256]{1,0:T(8,128)S(1)}, f32[128,256]{1,0:T(8,128)S(1)}, u32[]{:S(2)}, u32[]{:S(2)}) collective-permute-start(f32[128,256]{1,0:T(8,128)S(1)} %get-tuple-element.55), channel_id=1, source_target_pairs={{0,24},{8,16},{16,8},{24,0},{1,25},{9,17},{17,9},{25,1},{2,26},{10... | collective-permute-start | bytes 393224 | tf_op jit(solution)/shard_map/ppermute | solution.py:367
  30.4 9.5 %copy-start.1 = (f32[4096,256]{1,0:T(8,128)S(1)}, f32[4096,256]{1,0:T(8,128)}, u32[]{:S(2)}) copy-start(f32[4096,256]{1,0:T(8,128)} %table.5) | copy-start | bytes 12582916
  31.7 11.4 %collective-permute-start.5 = (f32[256,256]{1,0:T(8,128)S(1)}, f32[256,256]{1,0:T(8,128)S(1)}, u32[]{:S(2)}, u32[]{:S(2)}) collective-permute-start(f32[256,256]{1,0:T(8,128)S(1)} %collective-permute-done.1.refs_0_.refs_5_.refs_1_), channel_id=1, source_target_pairs={{0,2},{1,3},{2,0},{3,1},{4,6},{5,7},{6,4},{7,5},{8,10},{9,11},{10,... | collective-permute-start | bytes 786440 | tf_op jit(solution)/shard_map/ppermute | solution.py:367
  31.9 11.3 %collective-permute-start.8 = (f32[256,256]{1,0:T(8,128)S(1)}, f32[256,256]{1,0:T(8,128)S(1)}, u32[]{:S(2)}, u32[]{:S(2)}) collective-permute-start(f32[256,256]{1,0:T(8,128)S(1)} %collective-permute-done.7.refs_6_.refs_10_), channel_id=1, source_target_pairs={{0,1},{1,0},{2,3},{3,2},{4,5},{5,4},{6,7},{7,6},{8,9},{9,8},{10,11... | collective-permute-start | bytes 786440 | tf_op jit(solution)/shard_map/ppermute | solution.py:367
  35.4 13.9 %collective-permute-start.11 = (f32[256,256]{1,0:T(8,128)S(1)}, f32[256,256]{1,0:T(8,128)S(1)}, u32[]{:S(2)}, u32[]{:S(2)}) collective-permute-start(f32[256,256]{1,0:T(8,128)S(1)} %get-tuple-element.58.refs_8_), channel_id=1, source_target_pairs={{0,16},{8,24},{16,0},{24,8},{1,17},{9,25},{17,1},{25,9},{2,18},{10... | collective-permute-start | bytes 786440 | tf_op jit(solution)/shard_map/ppermute | solution.py:367
  36.8 13.0 %collective-permute-start.12 = (f32[256,256]{1,0:T(8,128)S(1)}, f32[256,256]{1,0:T(8,128)S(1)}, u32[]{:S(2)}, u32[]{:S(2)}) collective-permute-start(f32[256,256]{1,0:T(8,128)S(1)} %get-tuple-element.59.refs_9_), channel_id=1, source_target_pairs={{0,24},{8,16},{16,8},{24,0},{1,25},{9,17},{17,9},{25,1},{2,26},{10... | collective-permute-start | bytes 786440 | tf_op jit(solution)/shard_map/ppermute | solution.py:367
  42.3 7.5 %collective-permute-start.10 = (f32[256,256]{1,0:T(8,128)S(1)}, f32[256,256]{1,0:T(8,128)S(1)}, u32[]{:S(2)}, u32[]{:S(2)}) collective-permute-start(f32[256,256]{1,0:T(8,128)S(1)} %get-tuple-element.63), channel_id=1, source_target_pairs={{0,8},{8,0},{16,24},{24,16},{1,9},{9,1},{17,25},{25,17},{2,10},{10... | collective-permute-start | bytes 786440 | tf_op jit(solution)/shard_map/ppermute | solution.py:367
  47.9 18.9 %collective-permute-start.16 = (f32[256,256]{1,0:T(8,128)S(1)}, f32[256,256]{1,0:T(8,128)S(1)}, u32[]{:S(2)}, u32[]{:S(2)}) collective-permute-start(f32[256,256]{1,0:T(8,128)S(1)} %get-tuple-element.78.refs_5_), channel_id=1, source_target_pairs={{0,8},{8,0},{16,24},{24,16},{1,9},{9,1},{17,25},{25,17},{2,10},{10... | collective-permute-start | bytes 786440 | tf_op jit(solution)/shard_map/ppermute | solution.py:367
  47.9 18.8 %collective-permute-start.17 = (f32[256,256]{1,0:T(8,128)S(1)}, f32[256,256]{1,0:T(8,128)S(1)}, u32[]{:S(2)}, u32[]{:S(2)}) collective-permute-start(f32[256,256]{1,0:T(8,128)S(1)} %get-tuple-element.79.refs_6_), channel_id=1, source_target_pairs={{0,16},{8,24},{16,0},{24,8},{1,17},{9,25},{17,1},{25,9},{2,18},{10... | collective-permute-start | bytes 786440 | tf_op jit(solution)/shard_map/ppermute | solution.py:367
  49.3 17.4 %collective-permute-start.18 = (f32[256,256]{1,0:T(8,128)S(1)}, f32[256,256]{1,0:T(8,128)S(1)}, u32[]{:S(2)}, u32[]{:S(2)}) collective-permute-start(f32[256,256]{1,0:T(8,128)S(1)} %get-tuple-element.80.refs_7_), channel_id=1, source_target_pairs={{0,24},{8,16},{16,8},{24,0},{1,25},{9,17},{17,9},{25,1},{2,26},{10... | collective-permute-start | bytes 786440 | tf_op jit(solution)/shard_map/ppermute | solution.py:367
  51.0 3.8 %collective-permute-start.13 = (f32[2,2048]{1,0:T(2,128)S(1)}, f32[2,2048]{1,0:T(2,128)S(1)}, u32[]{:S(2)}, u32[]{:S(2)}) collective-permute-start(f32[2,2048]{1,0:T(2,128)S(1)} %get-tuple-element.68.first), channel_id=1, source_target_pairs={{0,1},{1,0},{2,3},{3,2},{4,5},{5,4},{6,7},{7,6},{8,9},{9,8},{10,11... | collective-permute-start | bytes 49160 | tf_op jit(solution)/shard_map/ppermute | solution.py:367
  54.8 3.8 %collective-permute-start.14 = (f32[2,2048]{1,0:T(2,128)S(1)}, f32[2,2048]{1,0:T(2,128)S(1)}, u32[]{:S(2)}, u32[]{:S(2)}) collective-permute-start(f32[2,2048]{1,0:T(2,128)S(1)} %join.3.first), channel_id=1, source_target_pairs={{0,2},{1,3},{2,0},{3,1},{4,6},{5,7},{6,4},{7,5},{8,10},{9,11},{10,... | collective-permute-start | bytes 49160 | tf_op jit(solution)/shard_map/ppermute | solution.py:367
  58.7 6.1 %collective-permute-start.15 = (f32[2,2048]{1,0:T(2,128)S(1)}, f32[2,2048]{1,0:T(2,128)S(1)}, u32[]{:S(2)}, u32[]{:S(2)}) collective-permute-start(f32[2,2048]{1,0:T(2,128)S(1)} %join.4.first), channel_id=1, source_target_pairs={{0,4},{1,5},{2,6},{3,7},{4,0},{5,1},{6,2},{7,3},{8,12},{9,13},{10,... | collective-permute-start | bytes 49160 | tf_op jit(solution)/shard_map/ppermute | solution.py:367
  65.4 6.7 %collective-permute-start.20 = (f32[256,256]{1,0:T(8,128)S(1)}, f32[256,256]{1,0:T(8,128)S(1)}, u32[]{:S(2)}, u32[]{:S(2)}) collective-permute-start(f32[256,256]{1,0:T(8,128)S(1)} %get-tuple-element.86), channel_id=1, source_target_pairs={{0,1},{1,0},{2,3},{3,2},{4,5},{5,4},{6,7},{7,6},{8,9},{9,8},{10,11... | collective-permute-start | bytes 786440 | tf_op jit(solution)/shard_map/ppermute | solution.py:367
  66.0 6.4 %collective-permute-start.21 = (f32[256,256]{1,0:T(8,128)S(1)}, f32[256,256]{1,0:T(8,128)S(1)}, u32[]{:S(2)}, u32[]{:S(2)}) collective-permute-start(f32[256,256]{1,0:T(8,128)S(1)} %get-tuple-element.87), channel_id=1, source_target_pairs={{0,2},{1,3},{2,0},{3,1},{4,6},{5,7},{6,4},{7,5},{8,10},{9,11},{10,... | collective-permute-start | bytes 786440 | tf_op jit(solution)/shard_map/ppermute | solution.py:367
  69.4 5.6 %collective-permute-start.19 = (f32[136,256]{1,0:T(8,128)S(1)}, f32[136,256]{1,0:T(8,128)S(1)}, u32[]{:S(2)}, u32[]{:S(2)}) collective-permute-start(f32[136,256]{1,0:T(8,128)S(1)} %get-tuple-element.84), channel_id=1, source_target_pairs={{0,8},{8,0},{16,24},{24,16},{1,9},{9,1},{17,25},{25,17},{2,10},{10... | collective-permute-start | bytes 417800 | tf_op jit(solution)/shard_map/ppermute | solution.py:367
  69.5 10.4 %collective-permute-start.22 = (f32[136,256]{1,0:T(8,128)S(1)}, f32[136,256]{1,0:T(8,128)S(1)}, u32[]{:S(2)}, u32[]{:S(2)}) collective-permute-start(f32[136,256]{1,0:T(8,128)S(1)} %get-tuple-element.88), channel_id=1, source_target_pairs={{0,16},{8,24},{16,0},{24,8},{1,17},{9,25},{17,1},{25,9},{2,18},{10... | collective-permute-start | bytes 417800 | tf_op jit(solution)/shard_map/ppermute | solution.py:367
  71.1 8.9 %collective-permute-start.23 = (f32[136,256]{1,0:T(8,128)S(1)}, f32[136,256]{1,0:T(8,128)S(1)}, u32[]{:S(2)}, u32[]{:S(2)}) collective-permute-start(f32[136,256]{1,0:T(8,128)S(1)} %get-tuple-element.89), channel_id=1, source_target_pairs={{0,24},{8,16},{16,8},{24,0},{1,25},{9,17},{17,9},{25,1},{2,26},{10... | collective-permute-start | bytes 417800 | tf_op jit(solution)/shard_map/ppermute | solution.py:367
  72.4 10.7 %collective-permute-start.24 = (f32[256,256]{1,0:T(8,128)S(1)}, f32[256,256]{1,0:T(8,128)S(1)}, u32[]{:S(2)}, u32[]{:S(2)}) collective-permute-start(f32[256,256]{1,0:T(8,128)S(1)} %add.12.refs_4_), channel_id=1, source_target_pairs={{0,2},{1,3},{2,0},{3,1},{4,6},{5,7},{6,4},{7,5},{8,10},{9,11},{10,... | collective-permute-start | bytes 786440 | tf_op jit(solution)/shard_map/ppermute | solution.py:367
  73.5 8.3 %collective-permute-start.25 = (f32[256,256]{1,0:T(8,128)S(1)}, f32[256,256]{1,0:T(8,128)S(1)}, u32[]{:S(2)}, u32[]{:S(2)}) collective-permute-start(f32[256,256]{1,0:T(8,128)S(1)} %get-tuple-element.91), channel_id=1, source_target_pairs={{0,1},{1,0},{2,3},{3,2},{4,5},{5,4},{6,7},{7,6},{8,9},{9,8},{10,11... | collective-permute-start | bytes 786440 | tf_op jit(solution)/shard_map/ppermute | solution.py:367
  81.8 14.1 %collective-permute-start.27 = (f32[256,256]{1,0:T(8,128)S(1)}, f32[256,256]{1,0:T(8,128)S(1)}, u32[]{:S(2)}, u32[]{:S(2)}) collective-permute-start(f32[256,256]{1,0:T(8,128)S(1)} %get-tuple-element.94), channel_id=1, source_target_pairs={{0,3},{1,2},{2,1},{3,0},{4,7},{5,6},{6,5},{7,4},{8,11},{9,10},{10,... | collective-permute-start | bytes 786440 | tf_op jit(solution)/shard_map/ppermute | solution.py:367
  83.1 10.5 %collective-permute-start.28 = (f32[256,256]{1,0:T(8,128)S(1)}, f32[256,256]{1,0:T(8,128)S(1)}, u32[]{:S(2)}, u32[]{:S(2)}) collective-permute-start(f32[256,256]{1,0:T(8,128)S(1)} %add.14), channel_id=1, source_target_pairs={{0,4},{1,5},{2,6},{3,7},{4,0},{5,1},{6,2},{7,3},{8,12},{9,13},{10,... | collective-permute-start | bytes 786440 | tf_op jit(solution)/shard_map/ppermute | solution.py:367
  86.1 10.6 %copy-start.3 = (s32[256]{0:T(256)S(1)}, s32[256]{0:T(256)}, u32[]{:S(2)}) copy-start(s32[256]{0:T(256)} %param.11) | copy-start | bytes 3076
  86.1 10.6 %collective-permute-start.26 = (f32[256,256]{1,0:T(8,128)S(1)}, f32[256,256]{1,0:T(8,128)S(1)}, u32[]{:S(2)}, u32[]{:S(2)}) collective-permute-start(f32[256,256]{1,0:T(8,128)S(1)} %get-tuple-element.92), channel_id=1, source_target_pairs={{0,1},{1,0},{2,3},{3,2},{4,5},{5,4},{6,7},{7,6},{8,9},{9,8},{10,11... | collective-permute-start | bytes 786440 | tf_op jit(solution)/shard_map/ppermute | solution.py:367

commit v10 on v9

--- a/solution.py
+++ b/solution.py
@@ -14,6 +14,7 @@
 VMEM = pl.BlockSpec(memory_space=pltpu.VMEM)
 ANY = pl.BlockSpec(memory_space=pl.ANY)
 SMEM = pl.BlockSpec(memory_space=pltpu.SMEM)
+
 MIB = 1 << 20
 BATCH = 8
 
@@ -122,8 +123,12 @@
     out_ref[:, 0, LANES : 2 * LANES] = position.astype(I32)
 
 
-def gather_kernel(members, chosen, part, count, info, got, table, *refs):
-    for d, out in zip(chosen, refs[-len(chosen) :]):
+def gather_kernel(members, chosen, part, count, info, requests, table, *refs):
+    got, arrived = refs[-2:]
+    copy = pltpu.make_async_copy(requests.at[:, :, 0:LANES], got, arrived)
+    copy.start()
+    copy.wait()
+    for d, out in zip(chosen, refs[-2 - len(chosen) : -2]):
         first = (info[0] ^ d) * members
 
         def member(mr, carry, out=out, first=first):
@@ -299,10 +304,12 @@
     return same.astype(F32)
 
 
-def scatter_kernel(members, groups, own, slots, count, info, got_v, got, *refs):
+def scatter_kernel(members, groups, own, slots, count, info, got_v, requests, *refs):
     size = len(own)
     grads, picked = refs[:size], refs[size : 2 * size]
-    out, negs, tgts = refs[-3:]
+    out, negs, tgts, got, arrived = refs[-5:]
+    copy = pltpu.make_async_copy(requests.at[:, :, 0:LANES], got, arrived)
+    copy.start()
     out[...] = refs[2 * size][...] if own[0] else jnp.zeros_like(out)
 
     def add_rows(asked, first, source, base, number):
@@ -315,6 +322,7 @@
             for k in range(BATCH):
                 out[pl.ds(rows[k], 1), :] = new[k]
 
+    copy.wait()
     for i, d in enumerate(own):
         g = info[0] ^ d
         asked = got_v[pl.ds(g * members, members), 0, 0:LANES]
@@ -380,6 +388,7 @@
     shape = jax.ShapeDtypeStruct
     sds = lambda *s: shape(s, F32)
 
+    scalars = [pltpu.SMEM((devices, 1, LANES), I32), pltpu.SemaphoreType.DMA]
     info = jnp.stack([lax.axis_index("group"), lax.axis_index("member")]).astype(I32)
     ints = jnp.concatenate([target_owner.reshape(-1), target_local, valid, negative_ids])
     request, masked = call(
@@ -414,9 +423,10 @@
         return call(
             functools.partial(gather_kernel, members, chosen, part, many),
             [sds(members * many, width)] * len(chosen),
-            [SMEM, SMEM, VMEM] + [ANY] * len(deps),
+            [SMEM, ANY, VMEM] + [ANY] * len(deps),
             [VMEM] * len(chosen),
             (info, got, item_table, *deps),
+            scratch=scalars,
             name=name,
         )
 
@@ -544,33 +554,37 @@
         return call(
             functools.partial(scatter_kernel, members, groups, own, slots, count),
             sds(rows_dev, width),
-            [SMEM, VMEM, SMEM] + [VMEM] * (2 * len(own) + len(base)) + [ANY] * len(deps),
+            [SMEM, VMEM, ANY] + [VMEM] * (2 * len(own) + len(base)) + [ANY] * len(deps),
             VMEM,
             (info, got, got, *[grads[d] for d in own], *[sent[d] for d in own], *base, *deps),
             scratch=[
                 pltpu.VMEM((members * count, width), F32),
                 pltpu.VMEM((members * slots, width), F32),
+                *scalars,
             ],
             flops=flops,
             name="scatter",
         )
 
-    close = [*along[1:], *[near + x for x in along[1:]]]
-    farthest, *rest, nearest = scaled([3 * near + x for x in along] + [near], [])
+    farthest, *rest = scaled([*[3 * near + x for x in along], *[near + x for x in along[1:]]], [])
+    rest, diagonal = rest[: near - 1], rest[near - 1 :]
     arrived = beside(rest)
-    nearest = swap(nearest, "member", near)
-    kept, far, *others = scaled([0, *[2 * near + x for x in along], *close], graded)
+    diagonal = [swap(block, "member", near) for block in diagonal]
+    near_blocks = [near, *along[1:]]
+    kept, far, *others = scaled(
+        [0, *[2 * near + x for x in along], *near_blocks], graded
+    )
     others, sends = others[: near - 1], others[near - 1 :]
-    total = added([farthest, *arrived], [*graded, nearest])
+    total = added([farthest, *arrived], [*graded, *diagonal])
+    sums = [added([sends[x], diagonal[x - 1]], []) for x in along[1:]]
     others = after(others, total)
-    early_groups = list(range(2))
-    table_own = scatter(early_groups, [], [total], 1 << 33)
+    table_own = scatter(list(range(2)), [], [total], 1 << 33)
     far = added([far], [table_own, *grads[2:]])
     others = beside(others)
     half = added([far, swap(total, "member", near), *others], [])
-    held = after(sends[: near - 1], half) + after(sends[near - 1 :], others[0])
-    parts = [swap(b, "member", d) for d, b in zip(close, held)]
-    parts.append(added([nearest, kept, swap(half, "member", 2 * near)], []))
+    held = after([sends[0], *sums], others[0])
+    parts = [swap(b, "member", d) for d, b in zip(near_blocks, held)]
+    parts.append(added([kept, swap(half, "member", 2 * near)], []))
 
     table_grad = scatter(list(range(2, groups)), [table_own], [], 0)
     encoded_grad = call(

time: 97.9 us -> 99.3 us (1.014)
  Pallas kernels: 38.6 us -> 40 us
    pallas_call x23 -> x24, Pallas kernels: 38.6 us -> 40 us  [call(): pl.pallas_call(kernel, out_shape=out_shape, in_specs=ins, out_specs=outs,...]
  transfers between devices with their start and end apart: 30 -> 30, of which waited for: 9 -> 9; matrix products, arithmetic and copies ran while one was open for 0% -> 0% of each run, Pallas kernels for 37% -> 38%
where the time goes in v10:
time: 99.3 us; the launch traced here: 99 us
  Pallas kernels  40 us (40%)
  starting transfers between devices  37.5 us (38%)
  waiting for transfers between devices  16.7 us (17%)
  local copies, waits for them, and re-layouts  3.15 us (3%)
    pallas_call x24, Pallas kernels, call(): pl.pallas_call(kernel, out_shape=out_shape, in_specs=ins, out_specs=outs,...  40 us
    ppermute x29, starting transfers between devices, swap(): lax.ppermute(value, axis, [(i, i ^ d) for i in range(lax.axis_size(axis))])  33.7 us
    ppermute x29, waiting for transfers between devices, swap(): lax.ppermute(value, axis, [(i, i ^ d) for i in range(lax.axis_size(axis))])  9.37 us
    all_to_all x1, waiting for transfers between devices, shards(): lax.all_to_all(request, ('group', 'member'), split_axis=0, concat_axis=0,...  7.36 us
    all_to_all x1, starting transfers between devices, shards(): lax.all_to_all(request, ('group', 'member'), split_axis=0, concat_axis=0,...  3.82 us
    unnamed x8, local copies, waits for them, and re-layouts  3.15 us
  transfers between devices with their start and end apart: 30, of which 9 were waited for; matrix products, arithmetic and copies ran while one was open for 0% of the time, Pallas kernels for 38%

profile of v10, /device:TPU:0, one launch (start us, length us, event | category | flops | bytes accessed | tf_op | source)
XLA Modules:
  0.0 99.0 jit_solution(9994767628381566063)
XLA Ops:
  0.6 0.7 pad_add_fusion
  1.5 0.9 copy-done.2
  2.4 1.8 %front.1 = (s32[32,1,256]{2,1,0:T(1,128)}, f32[256,256]{1,0:T(8,128)S(1)}) custom-call(s32[2]{0:T(128)S(1)} %pad_add_fusion.1.info, s32[1,1280]{1,0:T(1,128)S(1)} %reshape.15.ints, f32[256,256]{1,0:T(8,128)S(1)} %copy-done.2), custom_call_target="tpu_custom_call" | custom-call | tf_op jit(solution)/shard_map/front/pallas_call | solution.py:27
  4.2 4.0 %collective-permute-start = (f32[256,256]{1,0:T(8,128)S(1)}, f32[256,256]{1,0:T(8,128)S(1)}, u32[]{:S(2)}, u32[]{:S(2)}) collective-permute-start(f32[256,256]{1,0:T(8,128)S(1)} %get-tuple-element.49.refs_4_.refs_0_), channel_id=1, source_target_pairs={{0,4},{1,5},{2,6},{3,7},{4,0},{5,1},{6,2},{7,3},{8,12},{9,13},{10,... | collective-permute-start | bytes 786440 | tf_op jit(solution)/shard_map/ppermute | solution.py:375
  8.2 3.8 %all-to-all-start = ((s32[32,1,256]{2,1,0:T(1,128)}), s32[32,1,256]{2,1,0:T(1,128)S(1)}, u32[]{:S(2)}, u32[]{:S(2)}) async-start(s32[32,1,256]{2,1,0:T(1,128)} %get-tuple-element.50), calls=%async_computation | async-start | bytes 65536 | tf_op jit(solution)/shard_map/all_to_all | solution.py:402
  12.1 1.8 %collective-permute-start.1 = (f32[256,256]{1,0:T(8,128)S(1)}, f32[256,256]{1,0:T(8,128)S(1)}, u32[]{:S(2)}, u32[]{:S(2)}) collective-permute-start(f32[256,256]{1,0:T(8,128)S(1)} %get-tuple-element.49.refs_4_.refs_0_), channel_id=1, source_target_pairs={{0,1},{1,0},{2,3},{3,2},{4,5},{5,4},{6,7},{7,6},{8,9},{9,8},{10,11... | collective-permute-start | bytes 786440 | tf_op jit(solution)/shard_map/ppermute | solution.py:375
  13.9 1.5 %collective-permute-start.9 = (f32[256,256]{1,0:T(8,128)S(1)}, f32[256,256]{1,0:T(8,128)S(1)}, u32[]{:S(2)}, u32[]{:S(2)}) collective-permute-start(f32[256,256]{1,0:T(8,128)S(1)} %get-tuple-element.49.refs_4_.refs_0_), channel_id=1, source_target_pairs={{0,2},{1,3},{2,0},{3,1},{4,6},{5,7},{6,4},{7,5},{8,10},{9,11},{10,... | collective-permute-start | bytes 786440 | tf_op jit(solution)/shard_map/ppermute | solution.py:375
  15.4 7.4 %all-to-all-done.requests.got.got_v = s32[32,1,256]{2,1,0:T(1,128)S(1)} async-done(((s32[32,1,256]{2,1,0:T(1,128)}), s32[32,1,256]{2,1,0:T(1,128)S(1)}, u32[]{:S(2)}, u32[]{:S(2)}) %all-to-all-start) | async-done | bytes 32800 | tf_op jit(solution)/shard_map/all_to_all | solution.py:402
  22.7 0.7 collective-permute-start.7
  23.9 2.2 %copy-done = f32[4096,256]{1,0:T(8,128)S(1)} copy-done((f32[4096,256]{1,0:T(8,128)S(1)}, f32[4096,256]{1,0:T(8,128)}, u32[]{:S(2)}) %copy-start) | copy-done | bytes 4194328
  26.1 2.6 %gather_negatives.1 = (f32[128,256]{1,0:T(8,128)S(1)}, f32[128,256]{1,0:T(8,128)S(1)}, f32[128,256]{1,0:T(8,128)S(1)}, f32[128,256]{1,0:T(8,128)S(1)}) custom-call(s32[2]{0:T(128)S(1)} %pad_add_fusion.1.info, s32[32,1,256]{2,1,0:T(1,128)S(1)} %all-to-all-done.requests.got.got_v, f32[4096,256]{1,0:T(8,128)S(1)} %copy-done, ...), custom_call_target="tpu_custom_call" | custom-call | tf_op jit(solution)/shard_map/gather_negatives/pallas_call | solution.py:27
  28.8 0.8 collective-permute-start.3
  29.6 1.1 %collective-permute-start.4 = (f32[128,256]{1,0:T(8,128)S(1)}, f32[128,256]{1,0:T(8,128)S(1)}, u32[]{:S(2)}, u32[]{:S(2)}) collective-permute-start(f32[128,256]{1,0:T(8,128)S(1)} %get-tuple-element.55), channel_id=1, source_target_pairs={{0,24},{8,16},{16,8},{24,0},{1,25},{9,17},{17,9},{25,1},{2,26},{10... | collective-permute-start | bytes 393224 | tf_op jit(solution)/shard_map/ppermute | solution.py:375
  30.6 1.1 %collective-permute-done.7.refs_6_.refs_10_ = f32[256,256]{1,0:T(8,128)S(1)} collective-permute-done((f32[256,256]{1,0:T(8,128)S(1)}, f32[256,256]{1,0:T(8,128)S(1)}, u32[]{:S(2)}, u32[]{:S(2)}) %collective-permute-start.7) | collective-permute-done | bytes 262176 | tf_op jit(solution)/shard_map/ppermute | solution.py:375
  32.1 1.4 %collective-permute-start.8 = (f32[256,256]{1,0:T(8,128)S(1)}, f32[256,256]{1,0:T(8,128)S(1)}, u32[]{:S(2)}, u32[]{:S(2)}) collective-permute-start(f32[256,256]{1,0:T(8,128)S(1)} %collective-permute-done.7.refs_6_.refs_10_), channel_id=1, source_target_pairs={{0,1},{1,0},{2,3},{3,2},{4,5},{5,4},{6,7},{7,6},{8,9},{9,8},{10,11... | collective-permute-start | bytes 786440 | tf_op jit(solution)/shard_map/ppermute | solution.py:375
  33.5 2.4 %gather_far_targets.1 = (f32[256,256]{1,0:T(8,128)S(1)}, f32[256,256]{1,0:T(8,128)S(1)}) custom-call(s32[2]{0:T(128)S(1)} %pad_add_fusion.1.info, s32[32,1,256]{2,1,0:T(1,128)S(1)} %all-to-all-done.requests.got.got_v, f32[4096,256]{1,0:T(8,128)S(1)} %copy-done, f32[256,256]{1,0:T(8,128)S(1)} %collective-permute-done.9.refs_0_.refs_6_.refs_2_, ...), custom_call_target="tpu_custom_call" | custom-call | tf_op jit(solution)/shard_map/gather_far_targets/pallas_call | solution.py:27
  36.0 1.1 %collective-permute-start.11 = (f32[256,256]{1,0:T(8,128)S(1)}, f32[256,256]{1,0:T(8,128)S(1)}, u32[]{:S(2)}, u32[]{:S(2)}) collective-permute-start(f32[256,256]{1,0:T(8,128)S(1)} %get-tuple-element.58.refs_8_), channel_id=1, source_target_pairs={{0,16},{8,24},{16,0},{24,8},{1,17},{9,25},{17,1},{25,9},{2,18},{10... | collective-permute-start | bytes 786440 | tf_op jit(solution)/shard_map/ppermute | solution.py:375
  37.2 3.1 %score.2 = (f32[2,2048]{1,0:T(2,128)S(1)}, bf16[4,512,256]{2,1,0:T(8,128)(2,1)S(1)}, bf16[4,512,256]{2,1,0:T(8,128)(2,1)S(1)}) custom-call(s32[2]{0:T(128)S(1)} %pad_add_fusion.1.info, f32[128,256]{1,0:T(8,128)S(1)} %get-tuple-element.52.refs_0_, f32[128,256]{1,0:T(8,128)S(1)} %collective-permute-done.2.refs_1_, ...), custom_call_target="tpu_custom_call" | custom-call | flops 1610612736 | bytes 1048576 | tf_op jit(solution)/shard_map/score/pallas_call | solution.py:27
  40.3 2.6 %gather_targets.1 = (f32[256,256]{1,0:T(8,128)S(1)}, f32[256,256]{1,0:T(8,128)S(1)}) custom-call(s32[2]{0:T(128)S(1)} %pad_add_fusion.1.info, s32[32,1,256]{2,1,0:T(1,128)S(1)} %all-to-all-done.requests.got.got_v, f32[4096,256]{1,0:T(8,128)S(1)} %copy-done.1, f32[2,2048]{1,0:T(2,128)S(1)} %get-tuple-element.60.refs_8_.refs_0_), custom_call_target="tpu_custom_call" | custom-call | tf_op jit(solution)/shard_map/gather_targets/pallas_call | solution.py:27
  42.9 1.1 %collective-permute-start.10 = (f32[256,256]{1,0:T(8,128)S(1)}, f32[256,256]{1,0:T(8,128)S(1)}, u32[]{:S(2)}, u32[]{:S(2)}) collective-permute-start(f32[256,256]{1,0:T(8,128)S(1)} %get-tuple-element.63), channel_id=1, source_target_pairs={{0,8},{8,0},{16,24},{24,16},{1,9},{9,1},{17,25},{25,17},{2,10},{10... | collective-permute-start | bytes 786440 | tf_op jit(solution)/shard_map/ppermute | solution.py:375
  44.0 1.6 %pick.1 = (f32[256,256]{1,0:T(8,128)S(1)}, f32[256,256]{1,0:T(8,128)S(1)}, f32[256,256]{1,0:T(8,128)S(1)}, f32[256,256]{1,0:T(8,128)S(1)}) custom-call(s32[2]{0:T(128)S(1)} %pad_add_fusion.1.info, s32[32,1,256]{2,1,0:T(1,128)S(1)} %all-to-all-done.requests.got.got_v, f32[256,256]{1,0:T(8,128)S(1)} %get-tuple-element.49.refs_4_.refs_0_, ...), custom_call_target="tpu_custom_call" | custom-call | tf_op jit(solution)/shard_map/pick/pallas_call | solution.py:27
  45.6 3.1 %score.3 = (f32[2,2048]{1,0:T(2,128)S(1)}, bf16[4,512,256]{2,1,0:T(8,128)(2,1)S(1)}, bf16[4,512,256]{2,1,0:T(8,128)(2,1)S(1)}) custom-call(s32[2]{0:T(128)S(1)} %pad_add_fusion.1.info, f32[128,256]{1,0:T(8,128)S(1)} %get-tuple-element.52.refs_0_, f32[128,256]{1,0:T(8,128)S(1)} %collective-permute-done.2.refs_1_, ...), custom_call_target="tpu_custom_call" | custom-call | flops 1610612736 | bytes 1048576 | tf_op jit(solution)/shard_map/score/pallas_call | solution.py:27
  48.8 1.1 %collective-permute-start.17 = (f32[256,256]{1,0:T(8,128)S(1)}, f32[256,256]{1,0:T(8,128)S(1)}, u32[]{:S(2)}, u32[]{:S(2)}) collective-permute-start(f32[256,256]{1,0:T(8,128)S(1)} %get-tuple-element.79.refs_6_), channel_id=1, source_target_pairs={{0,16},{8,24},{16,0},{24,8},{1,17},{9,25},{17,1},{25,9},{2,18},{10... | collective-permute-start | bytes 786440 | tf_op jit(solution)/shard_map/ppermute | solution.py:375
  49.9 0.8 collective-permute-start.18
  50.6 1.2 %positive.1 = (f32[2,2048]{1,0:T(2,128)S(1)}, f32[2,2048]{1,0:T(2,128)S(1)}) custom-call(s32[2]{0:T(128)S(1)} %pad_add_fusion.1.info, s32[32,1,256]{2,1,0:T(1,128)S(1)} %all-to-all-done.requests.got.got_v, f32[2,2048]{1,0:T(2,128)S(1)} %get-tuple-element.61.stats, f32[256,256]{1,0:T(8,128)S(1)} %get-tuple-element.62.refs_0_.refs_4_, ...), custom_call_target="tpu_custom_call" | custom-call | tf_op jit(solution)/shard_map/positive/pallas_call | solution.py:27
  51.8 1.0 collective-permute-start.13
  52.8 2.0 %pulled.2 = (f32[4,256,256]{2,1,0:T(8,128)S(1)}, f32[4,256,256]{2,1,0:T(8,128)S(1)}) custom-call(s32[2]{0:T(128)S(1)} %pad_add_fusion.1.info, s32[32,1,256]{2,1,0:T(1,128)S(1)} %all-to-all-done.requests.got.got_v, f32[128,256]{1,0:T(8,128)S(1)} %get-tuple-element.52.refs_0_, f32[128,256]{1,0:T(8,128)S(1)} %collective-permute-done.2.refs_1_, ...), custom_call_target="tpu_custom_call" | custom-call | flops 805306368 | bytes 1048576 | tf_op jit(solution)/shard_map/pulled/pallas_call | solution.py:27
  54.8 0.8 collective-permute-done.13.second
  55.7 1.5 %collective-permute-start.14 = (f32[2,2048]{1,0:T(2,128)S(1)}, f32[2,2048]{1,0:T(2,128)S(1)}, u32[]{:S(2)}, u32[]{:S(2)}) collective-permute-start(f32[2,2048]{1,0:T(2,128)S(1)} %join.3.first), channel_id=1, source_target_pairs={{0,2},{1,3},{2,0},{3,1},{4,6},{5,7},{6,4},{7,5},{8,10},{9,11},{10,... | collective-permute-start | bytes 49160 | tf_op jit(solution)/shard_map/ppermute | solution.py:375
  57.1 2.0 %pulled.3 = (f32[4,256,256]{2,1,0:T(8,128)S(1)}, f32[4,256,256]{2,1,0:T(8,128)S(1)}) custom-call(s32[2]{0:T(128)S(1)} %pad_add_fusion.1.info, s32[32,1,256]{2,1,0:T(1,128)S(1)} %all-to-all-done.requests.got.got_v, f32[128,256]{1,0:T(8,128)S(1)} %get-tuple-element.52.refs_0_, f32[128,256]{1,0:T(8,128)S(1)} %collective-permute-done.2.refs_1_, ...), custom_call_target="tpu_custom_call" | custom-call | flops 805306368 | bytes 1048576 | tf_op jit(solution)/shard_map/pulled/pallas_call | solution.py:27
  59.5 4.1 %collective-permute-start.15 = (f32[2,2048]{1,0:T(2,128)S(1)}, f32[2,2048]{1,0:T(2,128)S(1)}, u32[]{:S(2)}, u32[]{:S(2)}) collective-permute-start(f32[2,2048]{1,0:T(2,128)S(1)} %join.4.first), channel_id=1, source_target_pairs={{0,4},{1,5},{2,6},{3,7},{4,0},{5,1},{6,2},{7,3},{8,12},{9,13},{10,... | collective-permute-start | bytes 49160 | tf_op jit(solution)/shard_map/ppermute | solution.py:375
  63.6 1.7 %collective-permute-done.15.second = f32[2,2048]{1,0:T(2,128)S(1)} collective-permute-done((f32[2,2048]{1,0:T(2,128)S(1)}, f32[2,2048]{1,0:T(2,128)S(1)}, u32[]{:S(2)}, u32[]{:S(2)}) %collective-permute-start.15) | collective-permute-done | bytes 16416 | tf_op jit(solution)/shard_map/ppermute | solution.py:375
  65.3 0.7 pull.3
  66.0 0.6 collective-permute-start.19
  66.6 0.7 collective-permute-start.20
  67.3 2.7 %grad.1 = (f32[136,256]{1,0:T(8,128)S(1)}, f32[136,256]{1,0:T(8,128)S(1)}, f32[136,256]{1,0:T(8,128)S(1)}, f32[136,256]{1,0:T(8,128)S(1)}) custom-call(s32[2]{0:T(128)S(1)} %pad_add_fusion.1.info, s32[32,1,256]{2,1,0:T(1,128)S(1)} %all-to-all-done.requests.got.got_v, f32[2,2048]{1,0:T(2,128)S(1)} %join.5.final, f32[2,2048]{1,0:T(2,128)S(1)} %get-tuple-element.61.stats, ...), custom_call_target="tpu_custom_call" | custom-call | flops 1610612736 | bytes 8388608 | tf_op jit(solution)/shard_map/grad/pallas_call | solution.py:27
  70.1 1.6 %collective-permute-start.25 = (f32[136,256]{1,0:T(8,128)S(1)}, f32[136,256]{1,0:T(8,128)S(1)}, u32[]{:S(2)}, u32[]{:S(2)}) collective-permute-start(f32[136,256]{1,0:T(8,128)S(1)} %get-tuple-element.94), channel_id=1, source_target_pairs={{0,16},{8,24},{16,0},{24,8},{1,17},{9,25},{17,1},{25,9},{2,18},{10... | collective-permute-start | bytes 417800 | tf_op jit(solution)/shard_map/ppermute | solution.py:375
  71.9 0.7 pull.2
  73.0 1.1 %collective-permute-start.27 = (f32[256,256]{1,0:T(8,128)S(1)}, f32[256,256]{1,0:T(8,128)S(1)}, u32[]{:S(2)}, u32[]{:S(2)}) collective-permute-start(f32[256,256]{1,0:T(8,128)S(1)} %add.13.refs_4_), channel_id=1, source_target_pairs={{0,2},{1,3},{2,0},{3,1},{4,6},{5,7},{6,4},{7,5},{8,10},{9,11},{10,... | collective-permute-start | bytes 786440 | tf_op jit(solution)/shard_map/ppermute | solution.py:375
  74.1 1.5 %collective-permute-start.21 = (f32[256,256]{1,0:T(8,128)S(1)}, f32[256,256]{1,0:T(8,128)S(1)}, u32[]{:S(2)}, u32[]{:S(2)}) collective-permute-start(f32[256,256]{1,0:T(8,128)S(1)} %get-tuple-element.87), channel_id=1, source_target_pairs={{0,1},{1,0},{2,3},{3,2},{4,5},{5,4},{6,7},{7,6},{8,9},{9,8},{10,11... | collective-permute-start | bytes 786440 | tf_op jit(solution)/shard_map/ppermute | solution.py:375
  75.6 5.3 %scatter.2.refs_1_.refs_4_ = f32[4096,256]{1,0:T(8,128)S(1)} custom-call(s32[2]{0:T(128)S(1)} %pad_add_fusion.1.info, s32[32,1,256]{2,1,0:T(1,128)S(1)} %all-to-all-done.requests.got.got_v, s32[32,1,256]{2,1,0:T(1,128)S(1)} %all-to-all-done.requests.got.got_v, f32[136,256]{1,0:T(8,128)S(1)} %get-tuple-element.81.refs_4_.refs_2_.refs_0_, ...), custom_call_target="tpu_custom_call" | custom-call | flops 8589934592 | tf_op jit(solution)/shard_map/scatter/pallas_call | solution.py:27
  81.0 1.4 %collective-permute-done.21.refs_2_ = f32[256,256]{1,0:T(8,128)S(1)} collective-permute-done((f32[256,256]{1,0:T(8,128)S(1)}, f32[256,256]{1,0:T(8,128)S(1)}, u32[]{:S(2)}, u32[]{:S(2)}) %collective-permute-start.21) | collective-permute-done | bytes 262176 | tf_op jit(solution)/shard_map/ppermute | solution.py:375
  82.4 3.0 %collective-permute-start.28 = (f32[256,256]{1,0:T(8,128)S(1)}, f32[256,256]{1,0:T(8,128)S(1)}, u32[]{:S(2)}, u32[]{:S(2)}) collective-permute-start(f32[256,256]{1,0:T(8,128)S(1)} %add.16), channel_id=1, source_target_pairs={{0,4},{1,5},{2,6},{3,7},{4,0},{5,1},{6,2},{7,3},{8,12},{9,13},{10,... | collective-permute-start | bytes 786440 | tf_op jit(solution)/shard_map/ppermute | solution.py:375
  85.8 1.5 %collective-permute-start.23 = (f32[256,256]{1,0:T(8,128)S(1)}, f32[256,256]{1,0:T(8,128)S(1)}, u32[]{:S(2)}, u32[]{:S(2)}) collective-permute-start(f32[256,256]{1,0:T(8,128)S(1)} %add.14), channel_id=1, source_target_pairs={{0,1},{1,0},{2,3},{3,2},{4,5},{5,4},{6,7},{7,6},{8,9},{9,8},{10,11... | collective-permute-start | bytes 786440 | tf_op jit(solution)/shard_map/ppermute | solution.py:375
  87.2 7.0 %scatter.3 = f32[4096,256]{1,0:T(8,128)} custom-call(s32[2]{0:T(128)S(1)} %pad_add_fusion.1.info, s32[32,1,256]{2,1,0:T(1,128)S(1)} %all-to-all-done.requests.got.got_v, s32[32,1,256]{2,1,0:T(1,128)S(1)} %all-to-all-done.requests.got.got_v, f32[136,256]{1,0:T(8,128)S(1)} %collective-permute-done.25.refs_2_.refs_0_, ...), custom_call_target="tpu_custom_call" | custom-call | tf_op jit(solution)/shard_map/scatter/pallas_call | solution.py:27
  94.3 2.5 %collective-permute-done.28.refs_1_ = f32[256,256]{1,0:T(8,128)S(1)} collective-permute-done((f32[256,256]{1,0:T(8,128)S(1)}, f32[256,256]{1,0:T(8,128)S(1)}, u32[]{:S(2)}, u32[]{:S(2)}) %collective-permute-start.28) | collective-permute-done | bytes 262176 | tf_op jit(solution)/shard_map/ppermute | solution.py:375
  96.9 1.2 %collective-permute-done.22.refs_0_ = f32[256,256]{1,0:T(8,128)S(1)} collective-permute-done((f32[256,256]{1,0:T(8,128)S(1)}, f32[256,256]{1,0:T(8,128)S(1)}, u32[]{:S(2)}, u32[]{:S(2)}) %collective-permute-start.22) | collective-permute-done | bytes 262176 | tf_op jit(solution)/shard_map/ppermute | solution.py:375
  98.0 1.0 finish.1
  (47 shorter events, 2.9 us)
Async XLA Ops:
  1.5 1.0 copy-start.2
  4.2 18.5 %collective-permute-start = (f32[256,256]{1,0:T(8,128)S(1)}, f32[256,256]{1,0:T(8,128)S(1)}, u32[]{:S(2)}, u32[]{:S(2)}) collective-permute-start(f32[256,256]{1,0:T(8,128)S(1)} %get-tuple-element.49.refs_4_.refs_0_), channel_id=1, source_target_pairs={{0,4},{1,5},{2,6},{3,7},{4,0},{5,1},{6,2},{7,3},{8,12},{9,13},{10,... | collective-permute-start | bytes 786440 | tf_op jit(solution)/shard_map/ppermute | solution.py:375
  8.2 14.5 %all-to-all-start = ((s32[32,1,256]{2,1,0:T(1,128)}), s32[32,1,256]{2,1,0:T(1,128)S(1)}, u32[]{:S(2)}, u32[]{:S(2)}) async-start(s32[32,1,256]{2,1,0:T(1,128)} %get-tuple-element.50), calls=%async_computation | async-start | bytes 65536 | tf_op jit(solution)/shard_map/all_to_all | solution.py:402
  12.1 11.9 %collective-permute-start.1 = (f32[256,256]{1,0:T(8,128)S(1)}, f32[256,256]{1,0:T(8,128)S(1)}, u32[]{:S(2)}, u32[]{:S(2)}) collective-permute-start(f32[256,256]{1,0:T(8,128)S(1)} %get-tuple-element.49.refs_4_.refs_0_), channel_id=1, source_target_pairs={{0,1},{1,0},{2,3},{3,2},{4,5},{5,4},{6,7},{7,6},{8,9},{9,8},{10,11... | collective-permute-start | bytes 786440 | tf_op jit(solution)/shard_map/ppermute | solution.py:375
  13.9 15.7 %collective-permute-start.9 = (f32[256,256]{1,0:T(8,128)S(1)}, f32[256,256]{1,0:T(8,128)S(1)}, u32[]{:S(2)}, u32[]{:S(2)}) collective-permute-start(f32[256,256]{1,0:T(8,128)S(1)} %get-tuple-element.49.refs_4_.refs_0_), channel_id=1, source_target_pairs={{0,2},{1,3},{2,0},{3,1},{4,6},{5,7},{6,4},{7,5},{8,10},{9,11},{10,... | collective-permute-start | bytes 786440 | tf_op jit(solution)/shard_map/ppermute | solution.py:375
  22.7 9.0 %collective-permute-start.7 = (f32[256,256]{1,0:T(8,128)S(1)}, f32[256,256]{1,0:T(8,128)S(1)}, u32[]{:S(2)}, u32[]{:S(2)}) collective-permute-start(f32[256,256]{1,0:T(8,128)S(1)} %collective-permute-done.refs_1_.refs_7_.refs_4_.refs_8_), channel_id=1, source_target_pairs={{0,2},{1,3},{2,0},{3,1},{4,6},{5,7},{6,4},{7,5},{8,10},{9,11},{10,... | collective-permute-start | bytes 786440 | tf_op jit(solution)/shard_map/ppermute | solution.py:375
  23.4 8.8 %collective-permute-start.6 = (f32[256,256]{1,0:T(8,128)S(1)}, f32[256,256]{1,0:T(8,128)S(1)}, u32[]{:S(2)}, u32[]{:S(2)}) collective-permute-start(f32[256,256]{1,0:T(8,128)S(1)} %collective-permute-done.refs_1_.refs_7_.refs_4_.refs_8_), channel_id=1, source_target_pairs={{0,1},{1,0},{2,3},{3,2},{4,5},{5,4},{6,7},{7,6},{8,9},{9,8},{10,11... | collective-permute-start | bytes 786440 | tf_op jit(solution)/shard_map/ppermute | solution.py:375
  23.9 2.2 %copy-start = (f32[4096,256]{1,0:T(8,128)S(1)}, f32[4096,256]{1,0:T(8,128)}, u32[]{:S(2)}) copy-start(f32[4096,256]{1,0:T(8,128)} %table.5) | copy-start | bytes 12582916
  28.7 7.3 %collective-permute-start.2 = (f32[128,256]{1,0:T(8,128)S(1)}, f32[128,256]{1,0:T(8,128)S(1)}, u32[]{:S(2)}, u32[]{:S(2)}) collective-permute-start(f32[128,256]{1,0:T(8,128)S(1)} %get-tuple-element.53), channel_id=1, source_target_pairs={{0,8},{8,0},{16,24},{24,16},{1,9},{9,1},{17,25},{25,17},{2,10},{10... | collective-permute-start | bytes 393224 | tf_op jit(solution)/shard_map/ppermute | solution.py:375
  28.8 8.3 %collective-permute-start.3 = (f32[128,256]{1,0:T(8,128)S(1)}, f32[128,256]{1,0:T(8,128)S(1)}, u32[]{:S(2)}, u32[]{:S(2)}) collective-permute-start(f32[128,256]{1,0:T(8,128)S(1)} %get-tuple-element.54), channel_id=1, source_target_pairs={{0,16},{8,24},{16,0},{24,8},{1,17},{9,25},{17,1},{25,9},{2,18},{10... | collective-permute-start | bytes 393224 | tf_op jit(solution)/shard_map/ppermute | solution.py:375
  29.6 7.6 %collective-permute-start.4 = (f32[128,256]{1,0:T(8,128)S(1)}, f32[128,256]{1,0:T(8,128)S(1)}, u32[]{:S(2)}, u32[]{:S(2)}) collective-permute-start(f32[128,256]{1,0:T(8,128)S(1)} %get-tuple-element.55), channel_id=1, source_target_pairs={{0,24},{8,16},{16,8},{24,0},{1,25},{9,17},{17,9},{25,1},{2,26},{10... | collective-permute-start | bytes 393224 | tf_op jit(solution)/shard_map/ppermute | solution.py:375
  30.6 9.6 %copy-start.1 = (f32[4096,256]{1,0:T(8,128)S(1)}, f32[4096,256]{1,0:T(8,128)}, u32[]{:S(2)}) copy-start(f32[4096,256]{1,0:T(8,128)} %table.5) | copy-start | bytes 12582916
  31.7 12.2 %collective-permute-start.5 = (f32[256,256]{1,0:T(8,128)S(1)}, f32[256,256]{1,0:T(8,128)S(1)}, u32[]{:S(2)}, u32[]{:S(2)}) collective-permute-start(f32[256,256]{1,0:T(8,128)S(1)} %collective-permute-done.1.refs_0_.refs_5_.refs_1_), channel_id=1, source_target_pairs={{0,2},{1,3},{2,0},{3,1},{4,6},{5,7},{6,4},{7,5},{8,10},{9,11},{10,... | collective-permute-start | bytes 786440 | tf_op jit(solution)/shard_map/ppermute | solution.py:375
  32.1 11.9 %collective-permute-start.8 = (f32[256,256]{1,0:T(8,128)S(1)}, f32[256,256]{1,0:T(8,128)S(1)}, u32[]{:S(2)}, u32[]{:S(2)}) collective-permute-start(f32[256,256]{1,0:T(8,128)S(1)} %collective-permute-done.7.refs_6_.refs_10_), channel_id=1, source_target_pairs={{0,1},{1,0},{2,3},{3,2},{4,5},{5,4},{6,7},{7,6},{8,9},{9,8},{10,11... | collective-permute-start | bytes 786440 | tf_op jit(solution)/shard_map/ppermute | solution.py:375
  36.0 13.9 %collective-permute-start.11 = (f32[256,256]{1,0:T(8,128)S(1)}, f32[256,256]{1,0:T(8,128)S(1)}, u32[]{:S(2)}, u32[]{:S(2)}) collective-permute-start(f32[256,256]{1,0:T(8,128)S(1)} %get-tuple-element.58.refs_8_), channel_id=1, source_target_pairs={{0,16},{8,24},{16,0},{24,8},{1,17},{9,25},{17,1},{25,9},{2,18},{10... | collective-permute-start | bytes 786440 | tf_op jit(solution)/shard_map/ppermute | solution.py:375
  37.1 13.5 %collective-permute-start.12 = (f32[256,256]{1,0:T(8,128)S(1)}, f32[256,256]{1,0:T(8,128)S(1)}, u32[]{:S(2)}, u32[]{:S(2)}) collective-permute-start(f32[256,256]{1,0:T(8,128)S(1)} %get-tuple-element.59.refs_9_), channel_id=1, source_target_pairs={{0,24},{8,16},{16,8},{24,0},{1,25},{9,17},{17,9},{25,1},{2,26},{10... | collective-permute-start | bytes 786440 | tf_op jit(solution)/shard_map/ppermute | solution.py:375
  42.9 7.7 %collective-permute-start.10 = (f32[256,256]{1,0:T(8,128)S(1)}, f32[256,256]{1,0:T(8,128)S(1)}, u32[]{:S(2)}, u32[]{:S(2)}) collective-permute-start(f32[256,256]{1,0:T(8,128)S(1)} %get-tuple-element.63), channel_id=1, source_target_pairs={{0,8},{8,0},{16,24},{24,16},{1,9},{9,1},{17,25},{25,17},{2,10},{10... | collective-permute-start | bytes 786440 | tf_op jit(solution)/shard_map/ppermute | solution.py:375
  48.7 18.6 %collective-permute-start.16 = (f32[256,256]{1,0:T(8,128)S(1)}, f32[256,256]{1,0:T(8,128)S(1)}, u32[]{:S(2)}, u32[]{:S(2)}) collective-permute-start(f32[256,256]{1,0:T(8,128)S(1)} %get-tuple-element.78.refs_5_), channel_id=1, source_target_pairs={{0,8},{8,0},{16,24},{24,16},{1,9},{9,1},{17,25},{25,17},{2,10},{10... | collective-permute-start | bytes 786440 | tf_op jit(solution)/shard_map/ppermute | solution.py:375
  48.8 18.5 %collective-permute-start.17 = (f32[256,256]{1,0:T(8,128)S(1)}, f32[256,256]{1,0:T(8,128)S(1)}, u32[]{:S(2)}, u32[]{:S(2)}) collective-permute-start(f32[256,256]{1,0:T(8,128)S(1)} %get-tuple-element.79.refs_6_), channel_id=1, source_target_pairs={{0,16},{8,24},{16,0},{24,8},{1,17},{9,25},{17,1},{25,9},{2,18},{10... | collective-permute-start | bytes 786440 | tf_op jit(solution)/shard_map/ppermute | solution.py:375
  49.9 17.4 %collective-permute-start.18 = (f32[256,256]{1,0:T(8,128)S(1)}, f32[256,256]{1,0:T(8,128)S(1)}, u32[]{:S(2)}, u32[]{:S(2)}) collective-permute-start(f32[256,256]{1,0:T(8,128)S(1)} %get-tuple-element.80.refs_7_), channel_id=1, source_target_pairs={{0,24},{8,16},{16,8},{24,0},{1,25},{9,17},{17,9},{25,1},{2,26},{10... | collective-permute-start | bytes 786440 | tf_op jit(solution)/shard_map/ppermute | solution.py:375
  51.8 3.8 %collective-permute-start.13 = (f32[2,2048]{1,0:T(2,128)S(1)}, f32[2,2048]{1,0:T(2,128)S(1)}, u32[]{:S(2)}, u32[]{:S(2)}) collective-permute-start(f32[2,2048]{1,0:T(2,128)S(1)} %get-tuple-element.68.first), channel_id=1, source_target_pairs={{0,1},{1,0},{2,3},{3,2},{4,5},{5,4},{6,7},{7,6},{8,9},{9,8},{10,11... | collective-permute-start | bytes 49160 | tf_op jit(solution)/shard_map/ppermute | solution.py:375
  55.7 3.8 %collective-permute-start.14 = (f32[2,2048]{1,0:T(2,128)S(1)}, f32[2,2048]{1,0:T(2,128)S(1)}, u32[]{:S(2)}, u32[]{:S(2)}) collective-permute-start(f32[2,2048]{1,0:T(2,128)S(1)} %join.3.first), channel_id=1, source_target_pairs={{0,2},{1,3},{2,0},{3,1},{4,6},{5,7},{6,4},{7,5},{8,10},{9,11},{10,... | collective-permute-start | bytes 49160 | tf_op jit(solution)/shard_map/ppermute | solution.py:375
  59.5 5.8 %collective-permute-start.15 = (f32[2,2048]{1,0:T(2,128)S(1)}, f32[2,2048]{1,0:T(2,128)S(1)}, u32[]{:S(2)}, u32[]{:S(2)}) collective-permute-start(f32[2,2048]{1,0:T(2,128)S(1)} %join.4.first), channel_id=1, source_target_pairs={{0,4},{1,5},{2,6},{3,7},{4,0},{5,1},{6,2},{7,3},{8,12},{9,13},{10,... | collective-permute-start | bytes 49160 | tf_op jit(solution)/shard_map/ppermute | solution.py:375
  66.0 6.7 %collective-permute-start.19 = (f32[256,256]{1,0:T(8,128)S(1)}, f32[256,256]{1,0:T(8,128)S(1)}, u32[]{:S(2)}, u32[]{:S(2)}) collective-permute-start(f32[256,256]{1,0:T(8,128)S(1)} %get-tuple-element.85), channel_id=1, source_target_pairs={{0,1},{1,0},{2,3},{3,2},{4,5},{5,4},{6,7},{7,6},{8,9},{9,8},{10,11... | collective-permute-start | bytes 786440 | tf_op jit(solution)/shard_map/ppermute | solution.py:375
  66.6 6.4 %collective-permute-start.20 = (f32[256,256]{1,0:T(8,128)S(1)}, f32[256,256]{1,0:T(8,128)S(1)}, u32[]{:S(2)}, u32[]{:S(2)}) collective-permute-start(f32[256,256]{1,0:T(8,128)S(1)} %get-tuple-element.86), channel_id=1, source_target_pairs={{0,2},{1,3},{2,0},{3,1},{4,6},{5,7},{6,4},{7,5},{8,10},{9,11},{10,... | collective-permute-start | bytes 786440 | tf_op jit(solution)/shard_map/ppermute | solution.py:375
  70.0 5.6 %collective-permute-start.24 = (f32[136,256]{1,0:T(8,128)S(1)}, f32[136,256]{1,0:T(8,128)S(1)}, u32[]{:S(2)}, u32[]{:S(2)}) collective-permute-start(f32[136,256]{1,0:T(8,128)S(1)} %get-tuple-element.93), channel_id=1, source_target_pairs={{0,8},{8,0},{16,24},{24,16},{1,9},{9,1},{17,25},{25,17},{2,10},{10... | collective-permute-start | bytes 417800 | tf_op jit(solution)/shard_map/ppermute | solution.py:375
  70.1 10.9 %collective-permute-start.25 = (f32[136,256]{1,0:T(8,128)S(1)}, f32[136,256]{1,0:T(8,128)S(1)}, u32[]{:S(2)}, u32[]{:S(2)}) collective-permute-start(f32[136,256]{1,0:T(8,128)S(1)} %get-tuple-element.94), channel_id=1, source_target_pairs={{0,16},{8,24},{16,0},{24,8},{1,17},{9,25},{17,1},{25,9},{2,18},{10... | collective-permute-start | bytes 417800 | tf_op jit(solution)/shard_map/ppermute | solution.py:375
  71.6 9.3 %collective-permute-start.26 = (f32[136,256]{1,0:T(8,128)S(1)}, f32[136,256]{1,0:T(8,128)S(1)}, u32[]{:S(2)}, u32[]{:S(2)}) collective-permute-start(f32[136,256]{1,0:T(8,128)S(1)} %get-tuple-element.95), channel_id=1, source_target_pairs={{0,24},{8,16},{16,8},{24,0},{1,25},{9,17},{17,9},{25,1},{2,26},{10... | collective-permute-start | bytes 417800 | tf_op jit(solution)/shard_map/ppermute | solution.py:375
  73.0 9.4 %collective-permute-start.27 = (f32[256,256]{1,0:T(8,128)S(1)}, f32[256,256]{1,0:T(8,128)S(1)}, u32[]{:S(2)}, u32[]{:S(2)}) collective-permute-start(f32[256,256]{1,0:T(8,128)S(1)} %add.13.refs_4_), channel_id=1, source_target_pairs={{0,2},{1,3},{2,0},{3,1},{4,6},{5,7},{6,4},{7,5},{8,10},{9,11},{10,... | collective-permute-start | bytes 786440 | tf_op jit(solution)/shard_map/ppermute | solution.py:375
  74.1 8.3 %collective-permute-start.21 = (f32[256,256]{1,0:T(8,128)S(1)}, f32[256,256]{1,0:T(8,128)S(1)}, u32[]{:S(2)}, u32[]{:S(2)}) collective-permute-start(f32[256,256]{1,0:T(8,128)S(1)} %get-tuple-element.87), channel_id=1, source_target_pairs={{0,1},{1,0},{2,3},{3,2},{4,5},{5,4},{6,7},{7,6},{8,9},{9,8},{10,11... | collective-permute-start | bytes 786440 | tf_op jit(solution)/shard_map/ppermute | solution.py:375
  82.4 15.6 %copy-start.3 = (s32[256]{0:T(256)S(1)}, s32[256]{0:T(256)}, u32[]{:S(2)}) copy-start(s32[256]{0:T(256)} %param.11) | copy-start | bytes 3076
  82.4 14.4 %collective-permute-start.28 = (f32[256,256]{1,0:T(8,128)S(1)}, f32[256,256]{1,0:T(8,128)S(1)}, u32[]{:S(2)}, u32[]{:S(2)}) collective-permute-start(f32[256,256]{1,0:T(8,128)S(1)} %add.16), channel_id=1, source_target_pairs={{0,4},{1,5},{2,6},{3,7},{4,0},{5,1},{6,2},{7,3},{8,12},{9,13},{10,... | collective-permute-start | bytes 786440 | tf_op jit(solution)/shard_map/ppermute | solution.py:375
  85.4 12.6 %collective-permute-start.22 = (f32[256,256]{1,0:T(8,128)S(1)}, f32[256,256]{1,0:T(8,128)S(1)}, u32[]{:S(2)}, u32[]{:S(2)}) collective-permute-start(f32[256,256]{1,0:T(8,128)S(1)} %get-tuple-element.88), channel_id=1, source_target_pairs={{0,2},{1,3},{2,0},{3,1},{4,6},{5,7},{6,4},{7,5},{8,10},{9,11},{10,... | collective-permute-start | bytes 786440 | tf_op jit(solution)/shard_map/ppermute | solution.py:375
  85.8 12.3 %collective-permute-start.23 = (f32[256,256]{1,0:T(8,128)S(1)}, f32[256,256]{1,0:T(8,128)S(1)}, u32[]{:S(2)}, u32[]{:S(2)}) collective-permute-start(f32[256,256]{1,0:T(8,128)S(1)} %add.14), channel_id=1, source_target_pairs={{0,1},{1,0},{2,3},{3,2},{4,5},{5,4},{6,7},{7,6},{8,9},{9,8},{10,11... | collective-permute-start | bytes 786440 | tf_op jit(solution)/shard_map/ppermute | solution.py:375

commit v11 on v9

--- a/solution.py
+++ b/solution.py
@@ -399,7 +399,7 @@
         encs[z] = swap(masked, "member", z)
     onward, got = lax.optimization_barrier((encs[2 * near], got))
     encs[3 * near] = swap(onward, "member", near)
-    for z in (0, 2 * near, 3 * near):
+    for z in (0, 2 * near):
         for x in range(1, near):
             encs[z ^ x] = swap(onward if z == 2 * near else encs[z], "member", x)
     halves = [[d for d in range(members) if (d < near) or d in (near, 2 * near)], []]
@@ -427,6 +427,8 @@
     waited = [encs[near], *encs[2 * near + 1 : 3 * near]]
     rows = gather(range(2, groups), 0, slots, waited, "gather_far_targets")
     gathered = rows
+    for x in range(1, near):
+        encs[3 * near + x] = swap(after([encs[3 * near]], rows[0])[0], "member", x)
     rows = [swap(row, "group", d) for d, row in enumerate(rows, 2)]
 
     stats, probs = [], []
@@ -555,22 +557,25 @@
             name="scatter",
         )
 
-    close = [*along[1:], *[near + x for x in along[1:]]]
-    farthest, *rest, nearest = scaled([3 * near + x for x in along] + [near], [])
+    farthest, *rest = scaled([*[3 * near + x for x in along], *[near + x for x in along[1:]]], [])
+    rest, diagonal = rest[: near - 1], rest[near - 1 :]
     arrived = beside(rest)
-    nearest = swap(nearest, "member", near)
-    kept, far, *others = scaled([0, *[2 * near + x for x in along], *close], graded)
+    diagonal = [swap(block, "member", near) for block in diagonal]
+    near_blocks = [near, *along[1:]]
+    kept, far, *others = scaled(
+        [0, *[2 * near + x for x in along], *near_blocks], graded
+    )
     others, sends = others[: near - 1], others[near - 1 :]
-    total = added([farthest, *arrived], [*graded, nearest])
+    total = added([farthest, *arrived], [*graded, *diagonal])
+    sums = [added([sends[x], diagonal[x - 1]], []) for x in along[1:]]
     others = after(others, total)
-    early_groups = list(range(2))
-    table_own = scatter(early_groups, [], [total], 1 << 33)
+    table_own = scatter(list(range(2)), [], [total], 1 << 33)
     far = added([far], [table_own, *grads[2:]])
     others = beside(others)
     half = added([far, swap(total, "member", near), *others], [])
-    held = after(sends[: near - 1], half) + after(sends[near - 1 :], others[0])
-    parts = [swap(b, "member", d) for d, b in zip(close, held)]
-    parts.append(added([nearest, kept, swap(half, "member", 2 * near)], []))
+    held = after(sends[:1], others[0]) + after(sums, half)
+    parts = [swap(b, "member", d) for d, b in zip(near_blocks, held)]
+    parts.append(added([kept, swap(half, "member", 2 * near)], []))
 
     table_grad = scatter(list(range(2, groups)), [table_own], [], 0)
     encoded_grad = call(

time: 97.9 us -> 96.4 us (0.985)
  starting transfers between devices: 38.1 us -> 36.9 us
    ppermute x29, starting transfers between devices: 34.3 us -> 33.1 us  [swap(): lax.ppermute(value, axis, [(i, i ^ d) for i in range(lax.axis_size(axis))])]
    pallas_call x23 -> x24, Pallas kernels: 38.6 us -> 38.7 us  [call(): pl.pallas_call(kernel, out_shape=out_shape, in_specs=ins, out_specs=outs,...]
where the time goes in v11:
time: 96.4 us; the launch traced here: 96 us
  Pallas kernels  38.7 us (40%)
  starting transfers between devices  36.9 us (38%)
  waiting for transfers between devices  15.5 us (16%)
  local copies, waits for them, and re-layouts  3.15 us (3%)
    pallas_call x24, Pallas kernels, call(): pl.pallas_call(kernel, out_shape=out_shape, in_specs=ins, out_specs=outs,...  38.7 us
    ppermute x29, starting transfers between devices, swap(): lax.ppermute(value, axis, [(i, i ^ d) for i in range(lax.axis_size(axis))])  33.1 us
    ppermute x29, waiting for transfers between devices, swap(): lax.ppermute(value, axis, [(i, i ^ d) for i in range(lax.axis_size(axis))])  8.18 us
    all_to_all x1, waiting for transfers between devices, shards(): lax.all_to_all(request, ('group', 'member'), split_axis=0, concat_axis=0,...  7.36 us
    all_to_all x1, starting transfers between devices, shards(): lax.all_to_all(request, ('group', 'member'), split_axis=0, concat_axis=0,...  3.82 us
    unnamed x8, local copies, waits for them, and re-layouts  3.15 us
  transfers between devices with their start and end apart: 30, of which 9 were waited for; matrix products, arithmetic and copies ran while one was open for 0% of the time, Pallas kernels for 37%

profile of v11, /device:TPU:0, one launch (start us, length us, event | category | flops | bytes accessed | tf_op | source)
XLA Modules:
  0.0 96.0 jit_solution(15289586766068865453)
XLA Ops:
  0.6 0.7 pad_add_fusion
  1.5 0.9 copy-done.2
  2.4 1.8 %front.1 = (s32[32,1,256]{2,1,0:T(1,128)}, f32[256,256]{1,0:T(8,128)S(1)}) custom-call(s32[2]{0:T(128)S(1)} %pad_add_fusion.1.info, s32[1,1280]{1,0:T(1,128)S(1)} %reshape.15.ints, f32[256,256]{1,0:T(8,128)S(1)} %copy-done.2), custom_call_target="tpu_custom_call" | custom-call | tf_op jit(solution)/shard_map/front/pallas_call | solution.py:26
  4.2 4.0 %collective-permute-start = (f32[256,256]{1,0:T(8,128)S(1)}, f32[256,256]{1,0:T(8,128)S(1)}, u32[]{:S(2)}, u32[]{:S(2)}) collective-permute-start(f32[256,256]{1,0:T(8,128)S(1)} %get-tuple-element.50.refs_4_.refs_0_), channel_id=1, source_target_pairs={{0,4},{1,5},{2,6},{3,7},{4,0},{5,1},{6,2},{7,3},{8,12},{9,13},{10,... | collective-permute-start | bytes 786440 | tf_op jit(solution)/shard_map/ppermute | solution.py:367
  8.2 3.8 %all-to-all-start = ((s32[32,1,256]{2,1,0:T(1,128)}), s32[32,1,256]{2,1,0:T(1,128)S(1)}, u32[]{:S(2)}, u32[]{:S(2)}) async-start(s32[32,1,256]{2,1,0:T(1,128)} %get-tuple-element.51), calls=%async_computation | async-start | bytes 65536 | tf_op jit(solution)/shard_map/all_to_all | solution.py:393
  12.1 1.8 %collective-permute-start.1 = (f32[256,256]{1,0:T(8,128)S(1)}, f32[256,256]{1,0:T(8,128)S(1)}, u32[]{:S(2)}, u32[]{:S(2)}) collective-permute-start(f32[256,256]{1,0:T(8,128)S(1)} %get-tuple-element.50.refs_4_.refs_0_), channel_id=1, source_target_pairs={{0,1},{1,0},{2,3},{3,2},{4,5},{5,4},{6,7},{7,6},{8,9},{9,8},{10,11... | collective-permute-start | bytes 786440 | tf_op jit(solution)/shard_map/ppermute | solution.py:367
  13.9 1.5 %collective-permute-start.8 = (f32[256,256]{1,0:T(8,128)S(1)}, f32[256,256]{1,0:T(8,128)S(1)}, u32[]{:S(2)}, u32[]{:S(2)}) collective-permute-start(f32[256,256]{1,0:T(8,128)S(1)} %get-tuple-element.50.refs_4_.refs_0_), channel_id=1, source_target_pairs={{0,2},{1,3},{2,0},{3,1},{4,6},{5,7},{6,4},{7,5},{8,10},{9,11},{10,... | collective-permute-start | bytes 786440 | tf_op jit(solution)/shard_map/ppermute | solution.py:367
  15.4 7.4 %all-to-all-done.got.got_v = s32[32,1,256]{2,1,0:T(1,128)S(1)} async-done(((s32[32,1,256]{2,1,0:T(1,128)}), s32[32,1,256]{2,1,0:T(1,128)S(1)}, u32[]{:S(2)}, u32[]{:S(2)}) %all-to-all-start) | async-done | bytes 32800 | tf_op jit(solution)/shard_map/all_to_all | solution.py:393
  22.7 0.6 collective-permute-start.6
  23.9 2.2 %copy-done = f32[4096,256]{1,0:T(8,128)S(1)} copy-done((f32[4096,256]{1,0:T(8,128)S(1)}, f32[4096,256]{1,0:T(8,128)}, u32[]{:S(2)}) %copy-start) | copy-done | bytes 4194328
  26.1 2.3 %gather_negatives.1 = (f32[128,256]{1,0:T(8,128)S(1)}, f32[128,256]{1,0:T(8,128)S(1)}, f32[128,256]{1,0:T(8,128)S(1)}, f32[128,256]{1,0:T(8,128)S(1)}) custom-call(s32[2]{0:T(128)S(1)} %pad_add_fusion.1.info, s32[32,1,256]{2,1,0:T(1,128)S(1)} %all-to-all-done.got.got_v, f32[4096,256]{1,0:T(8,128)S(1)} %copy-done, ...), custom_call_target="tpu_custom_call" | custom-call | tf_op jit(solution)/shard_map/gather_negatives/pallas_call | solution.py:26
  28.5 0.8 collective-permute-start.3
  29.3 1.1 %collective-permute-start.4 = (f32[128,256]{1,0:T(8,128)S(1)}, f32[128,256]{1,0:T(8,128)S(1)}, u32[]{:S(2)}, u32[]{:S(2)}) collective-permute-start(f32[128,256]{1,0:T(8,128)S(1)} %get-tuple-element.56), channel_id=1, source_target_pairs={{0,24},{8,16},{16,8},{24,0},{1,25},{9,17},{17,9},{25,1},{2,26},{10... | collective-permute-start | bytes 393224 | tf_op jit(solution)/shard_map/ppermute | solution.py:367
  30.4 0.6 collective-permute-done.6.refs_1_.refs_5_.refs_9_
  31.0 0.8 collective-permute-start.5
  31.9 2.2 %gather_far_targets.1 = (f32[256,256]{1,0:T(8,128)S(1)}, f32[256,256]{1,0:T(8,128)S(1)}) custom-call(s32[2]{0:T(128)S(1)} %pad_add_fusion.1.info, s32[32,1,256]{2,1,0:T(1,128)S(1)} %all-to-all-done.got.got_v, f32[4096,256]{1,0:T(8,128)S(1)} %copy-done, f32[256,256]{1,0:T(8,128)S(1)} %collective-permute-done.8.refs_0_.refs_6_.refs_2_, ...), custom_call_target="tpu_custom_call" | custom-call | tf_op jit(solution)/shard_map/gather_far_targets/pallas_call | solution.py:26
  34.0 1.5 %collective-permute-start.9 = (f32[256,256]{1,0:T(8,128)S(1)}, f32[256,256]{1,0:T(8,128)S(1)}, u32[]{:S(2)}, u32[]{:S(2)}) collective-permute-start(f32[256,256]{1,0:T(8,128)S(1)} %collective-permute-done.7.refs_6_.refs_10_), channel_id=1, source_target_pairs={{0,1},{1,0},{2,3},{3,2},{4,5},{5,4},{6,7},{7,6},{8,9},{9,8},{10,11... | collective-permute-start | bytes 786440 | tf_op jit(solution)/shard_map/ppermute | solution.py:367
  35.5 0.6 collective-permute-start.11
  36.8 3.1 %score.2 = (f32[2,2048]{1,0:T(2,128)S(1)}, bf16[4,512,256]{2,1,0:T(8,128)(2,1)S(1)}, bf16[4,512,256]{2,1,0:T(8,128)(2,1)S(1)}) custom-call(s32[2]{0:T(128)S(1)} %pad_add_fusion.1.info, f32[128,256]{1,0:T(8,128)S(1)} %get-tuple-element.53.refs_0_, f32[128,256]{1,0:T(8,128)S(1)} %collective-permute-done.2.refs_1_, ...), custom_call_target="tpu_custom_call" | custom-call | flops 1610612736 | bytes 1048576 | tf_op jit(solution)/shard_map/score/pallas_call | solution.py:26
  39.8 2.4 %gather_targets.1 = (f32[256,256]{1,0:T(8,128)S(1)}, f32[256,256]{1,0:T(8,128)S(1)}) custom-call(s32[2]{0:T(128)S(1)} %pad_add_fusion.1.info, s32[32,1,256]{2,1,0:T(1,128)S(1)} %all-to-all-done.got.got_v, f32[4096,256]{1,0:T(8,128)S(1)} %copy-done.1, f32[2,2048]{1,0:T(2,128)S(1)} %get-tuple-element.62.refs_8_.refs_0_), custom_call_target="tpu_custom_call" | custom-call | tf_op jit(solution)/shard_map/gather_targets/pallas_call | solution.py:26
  42.2 0.9 collective-permute-start.10
  43.2 1.6 %pick.1 = (f32[256,256]{1,0:T(8,128)S(1)}, f32[256,256]{1,0:T(8,128)S(1)}, f32[256,256]{1,0:T(8,128)S(1)}, f32[256,256]{1,0:T(8,128)S(1)}) custom-call(s32[2]{0:T(128)S(1)} %pad_add_fusion.1.info, s32[32,1,256]{2,1,0:T(1,128)S(1)} %all-to-all-done.got.got_v, f32[256,256]{1,0:T(8,128)S(1)} %get-tuple-element.50.refs_4_.refs_0_, ...), custom_call_target="tpu_custom_call" | custom-call | tf_op jit(solution)/shard_map/pick/pallas_call | solution.py:26
  44.8 3.1 %score.3 = (f32[2,2048]{1,0:T(2,128)S(1)}, bf16[4,512,256]{2,1,0:T(8,128)(2,1)S(1)}, bf16[4,512,256]{2,1,0:T(8,128)(2,1)S(1)}) custom-call(s32[2]{0:T(128)S(1)} %pad_add_fusion.1.info, f32[128,256]{1,0:T(8,128)S(1)} %get-tuple-element.53.refs_0_, f32[128,256]{1,0:T(8,128)S(1)} %collective-permute-done.2.refs_1_, ...), custom_call_target="tpu_custom_call" | custom-call | flops 1610612736 | bytes 1048576 | tf_op jit(solution)/shard_map/score/pallas_call | solution.py:26
  48.0 0.6 collective-permute-start.17
  48.6 1.2 %collective-permute-start.18 = (f32[256,256]{1,0:T(8,128)S(1)}, f32[256,256]{1,0:T(8,128)S(1)}, u32[]{:S(2)}, u32[]{:S(2)}) collective-permute-start(f32[256,256]{1,0:T(8,128)S(1)} %get-tuple-element.82.refs_7_), channel_id=1, source_target_pairs={{0,24},{8,16},{16,8},{24,0},{1,25},{9,17},{17,9},{25,1},{2,26},{10... | collective-permute-start | bytes 786440 | tf_op jit(solution)/shard_map/ppermute | solution.py:367
  49.8 1.2 %positive.1 = (f32[2,2048]{1,0:T(2,128)S(1)}, f32[2,2048]{1,0:T(2,128)S(1)}) custom-call(s32[2]{0:T(128)S(1)} %pad_add_fusion.1.info, s32[32,1,256]{2,1,0:T(1,128)S(1)} %all-to-all-done.got.got_v, f32[2,2048]{1,0:T(2,128)S(1)} %get-tuple-element.63.stats, f32[256,256]{1,0:T(8,128)S(1)} %get-tuple-element.64.refs_0_.refs_4_, ...), custom_call_target="tpu_custom_call" | custom-call | tf_op jit(solution)/shard_map/positive/pallas_call | solution.py:26
  51.0 1.4 %collective-permute-start.13 = (f32[2,2048]{1,0:T(2,128)S(1)}, f32[2,2048]{1,0:T(2,128)S(1)}, u32[]{:S(2)}, u32[]{:S(2)}) collective-permute-start(f32[2,2048]{1,0:T(2,128)S(1)} %get-tuple-element.70.first), channel_id=1, source_target_pairs={{0,1},{1,0},{2,3},{3,2},{4,5},{5,4},{6,7},{7,6},{8,9},{9,8},{10,11... | collective-permute-start | bytes 49160 | tf_op jit(solution)/shard_map/ppermute | solution.py:367
  52.4 2.0 %pulled.2 = (f32[4,256,256]{2,1,0:T(8,128)S(1)}, f32[4,256,256]{2,1,0:T(8,128)S(1)}) custom-call(s32[2]{0:T(128)S(1)} %pad_add_fusion.1.info, s32[32,1,256]{2,1,0:T(1,128)S(1)} %all-to-all-done.got.got_v, f32[128,256]{1,0:T(8,128)S(1)} %get-tuple-element.53.refs_0_, f32[128,256]{1,0:T(8,128)S(1)} %collective-permute-done.2.refs_1_, ...), custom_call_target="tpu_custom_call" | custom-call | flops 805306368 | bytes 1048576 | tf_op jit(solution)/shard_map/pulled/pallas_call | solution.py:26
  54.8 1.4 %collective-permute-start.14 = (f32[2,2048]{1,0:T(2,128)S(1)}, f32[2,2048]{1,0:T(2,128)S(1)}, u32[]{:S(2)}, u32[]{:S(2)}) collective-permute-start(f32[2,2048]{1,0:T(2,128)S(1)} %join.3.first), channel_id=1, source_target_pairs={{0,2},{1,3},{2,0},{3,1},{4,6},{5,7},{6,4},{7,5},{8,10},{9,11},{10,... | collective-permute-start | bytes 49160 | tf_op jit(solution)/shard_map/ppermute | solution.py:367
  56.2 2.0 %pulled.3 = (f32[4,256,256]{2,1,0:T(8,128)S(1)}, f32[4,256,256]{2,1,0:T(8,128)S(1)}) custom-call(s32[2]{0:T(128)S(1)} %pad_add_fusion.1.info, s32[32,1,256]{2,1,0:T(1,128)S(1)} %all-to-all-done.got.got_v, f32[128,256]{1,0:T(8,128)S(1)} %get-tuple-element.53.refs_0_, f32[128,256]{1,0:T(8,128)S(1)} %collective-permute-done.2.refs_1_, ...), custom_call_target="tpu_custom_call" | custom-call | flops 805306368 | bytes 1048576 | tf_op jit(solution)/shard_map/pulled/pallas_call | solution.py:26
  58.7 3.4 %collective-permute-start.15 = (f32[2,2048]{1,0:T(2,128)S(1)}, f32[2,2048]{1,0:T(2,128)S(1)}, u32[]{:S(2)}, u32[]{:S(2)}) collective-permute-start(f32[2,2048]{1,0:T(2,128)S(1)} %join.4.first), channel_id=1, source_target_pairs={{0,4},{1,5},{2,6},{3,7},{4,0},{5,1},{6,2},{7,3},{8,12},{9,13},{10,... | collective-permute-start | bytes 49160 | tf_op jit(solution)/shard_map/ppermute | solution.py:367
  62.1 1.7 %collective-permute-done.15.second = f32[2,2048]{1,0:T(2,128)S(1)} collective-permute-done((f32[2,2048]{1,0:T(2,128)S(1)}, f32[2,2048]{1,0:T(2,128)S(1)}, u32[]{:S(2)}, u32[]{:S(2)}) %collective-permute-start.15) | collective-permute-done | bytes 16416 | tf_op jit(solution)/shard_map/ppermute | solution.py:367
  63.9 0.7 pull.3
  64.5 1.6 %collective-permute-start.19 = (f32[256,256]{1,0:T(8,128)S(1)}, f32[256,256]{1,0:T(8,128)S(1)}, u32[]{:S(2)}, u32[]{:S(2)}) collective-permute-start(f32[256,256]{1,0:T(8,128)S(1)} %get-tuple-element.87), channel_id=1, source_target_pairs={{0,1},{1,0},{2,3},{3,2},{4,5},{5,4},{6,7},{7,6},{8,9},{9,8},{10,11... | collective-permute-start | bytes 786440 | tf_op jit(solution)/shard_map/ppermute | solution.py:367
  66.1 1.0 %collective-permute-start.20 = (f32[256,256]{1,0:T(8,128)S(1)}, f32[256,256]{1,0:T(8,128)S(1)}, u32[]{:S(2)}, u32[]{:S(2)}) collective-permute-start(f32[256,256]{1,0:T(8,128)S(1)} %get-tuple-element.88), channel_id=1, source_target_pairs={{0,2},{1,3},{2,0},{3,1},{4,6},{5,7},{6,4},{7,5},{8,10},{9,11},{10,... | collective-permute-start | bytes 786440 | tf_op jit(solution)/shard_map/ppermute | solution.py:367
  67.1 2.7 %grad.1 = (f32[136,256]{1,0:T(8,128)S(1)}, f32[136,256]{1,0:T(8,128)S(1)}, f32[136,256]{1,0:T(8,128)S(1)}, f32[136,256]{1,0:T(8,128)S(1)}) custom-call(s32[2]{0:T(128)S(1)} %pad_add_fusion.1.info, s32[32,1,256]{2,1,0:T(1,128)S(1)} %all-to-all-done.got.got_v, f32[2,2048]{1,0:T(2,128)S(1)} %join.5.final, f32[2,2048]{1,0:T(2,128)S(1)} %get-tuple-element.63.stats, ...), custom_call_target="tpu_custom_call" | custom-call | flops 1610612736 | bytes 8388608 | tf_op jit(solution)/shard_map/grad/pallas_call | solution.py:26
  69.9 0.6 collective-permute-start.24
  70.5 1.2 %collective-permute-start.25 = (f32[136,256]{1,0:T(8,128)S(1)}, f32[136,256]{1,0:T(8,128)S(1)}, u32[]{:S(2)}, u32[]{:S(2)}) collective-permute-start(f32[136,256]{1,0:T(8,128)S(1)} %get-tuple-element.95), channel_id=1, source_target_pairs={{0,24},{8,16},{16,8},{24,0},{1,25},{9,17},{17,9},{25,1},{2,26},{10... | collective-permute-start | bytes 417800 | tf_op jit(solution)/shard_map/ppermute | solution.py:367
  71.7 0.7 pull.2
  72.5 1.1 %collective-permute-start.26 = (f32[256,256]{1,0:T(8,128)S(1)}, f32[256,256]{1,0:T(8,128)S(1)}, u32[]{:S(2)}, u32[]{:S(2)}) collective-permute-start(f32[256,256]{1,0:T(8,128)S(1)} %add.13.refs_4_), channel_id=1, source_target_pairs={{0,2},{1,3},{2,0},{3,1},{4,6},{5,7},{6,4},{7,5},{8,10},{9,11},{10,... | collective-permute-start | bytes 786440 | tf_op jit(solution)/shard_map/ppermute | solution.py:367
  74.2 4.9 %scatter.2.refs_1_.refs_4_ = f32[4096,256]{1,0:T(8,128)S(1)} custom-call(s32[2]{0:T(128)S(1)} %pad_add_fusion.1.info, s32[32,1,256]{2,1,0:T(1,128)S(1)} %all-to-all-done.got.got_v, s32[32,1,256]{2,1,0:T(1,128)S(1)} %all-to-all-done.got.got_v, f32[136,256]{1,0:T(8,128)S(1)} %get-tuple-element.83.refs_4_.refs_2_.refs_0_, ...), custom_call_target="tpu_custom_call" | custom-call | flops 8589934592 | tf_op jit(solution)/shard_map/scatter/pallas_call | solution.py:26
  79.2 2.8 %collective-permute-done.21.refs_2_ = f32[256,256]{1,0:T(8,128)S(1)} collective-permute-done((f32[256,256]{1,0:T(8,128)S(1)}, f32[256,256]{1,0:T(8,128)S(1)}, u32[]{:S(2)}, u32[]{:S(2)}) %collective-permute-start.21) | collective-permute-done | bytes 262176 | tf_op jit(solution)/shard_map/ppermute | solution.py:367
  81.9 1.0 %collective-permute-start.22 = (f32[256,256]{1,0:T(8,128)S(1)}, f32[256,256]{1,0:T(8,128)S(1)}, u32[]{:S(2)}, u32[]{:S(2)}) collective-permute-start(f32[256,256]{1,0:T(8,128)S(1)} %get-tuple-element.90), channel_id=1, source_target_pairs={{0,2},{1,3},{2,0},{3,1},{4,6},{5,7},{6,4},{7,5},{8,10},{9,11},{10,... | collective-permute-start | bytes 786440 | tf_op jit(solution)/shard_map/ppermute | solution.py:367
  83.0 2.4 %collective-permute-start.28 = (f32[256,256]{1,0:T(8,128)S(1)}, f32[256,256]{1,0:T(8,128)S(1)}, u32[]{:S(2)}, u32[]{:S(2)}) collective-permute-start(f32[256,256]{1,0:T(8,128)S(1)} %add.16), channel_id=1, source_target_pairs={{0,4},{1,5},{2,6},{3,7},{4,0},{5,1},{6,2},{7,3},{8,12},{9,13},{10,... | collective-permute-start | bytes 786440 | tf_op jit(solution)/shard_map/ppermute | solution.py:367
  85.3 0.7 collective-permute-start.27
  86.0 7.0 %scatter.3 = f32[4096,256]{1,0:T(8,128)} custom-call(s32[2]{0:T(128)S(1)} %pad_add_fusion.1.info, s32[32,1,256]{2,1,0:T(1,128)S(1)} %all-to-all-done.got.got_v, s32[32,1,256]{2,1,0:T(1,128)S(1)} %all-to-all-done.got.got_v, f32[136,256]{1,0:T(8,128)S(1)} %collective-permute-done.24.refs_2_.refs_0_, f32[136,256]{1,0:T(8,128)S(1)} %collective-permute-done.25.refs_3_.refs_1_, ...), custom_call_target="tpu_custom_call" | custom-call | tf_op jit(solution)/shard_map/scatter/pallas_call | solution.py:26
  93.5 1.4 %collective-permute-done.22.refs_0_ = f32[256,256]{1,0:T(8,128)S(1)} collective-permute-done((f32[256,256]{1,0:T(8,128)S(1)}, f32[256,256]{1,0:T(8,128)S(1)}, u32[]{:S(2)}, u32[]{:S(2)}) %collective-permute-start.22) | collective-permute-done | bytes 262176 | tf_op jit(solution)/shard_map/ppermute | solution.py:367
  95.0 1.0 %finish.1 = f32[256,256]{1,0:T(8,128)} custom-call(s32[1,256]{1,0:T(1,128)S(1)} %bitcast.4, f32[256,256]{1,0:T(8,128)S(1)} %collective-permute-done.22.refs_0_, f32[256,256]{1,0:T(8,128)S(1)} %collective-permute-done.27.refs_1_, f32[256,256]{1,0:T(8,128)S(1)} %add.17.refs_2_), custom_call_target="tpu_custom_call" | custom-call | tf_op jit(solution)/shard_map/finish/pallas_call | solution.py:26
  (47 shorter events, 3.8 us)
Async XLA Ops:
  1.5 1.0 copy-start.2
  4.2 18.5 %collective-permute-start = (f32[256,256]{1,0:T(8,128)S(1)}, f32[256,256]{1,0:T(8,128)S(1)}, u32[]{:S(2)}, u32[]{:S(2)}) collective-permute-start(f32[256,256]{1,0:T(8,128)S(1)} %get-tuple-element.50.refs_4_.refs_0_), channel_id=1, source_target_pairs={{0,4},{1,5},{2,6},{3,7},{4,0},{5,1},{6,2},{7,3},{8,12},{9,13},{10,... | collective-permute-start | bytes 786440 | tf_op jit(solution)/shard_map/ppermute | solution.py:367
  8.2 14.5 %all-to-all-start = ((s32[32,1,256]{2,1,0:T(1,128)}), s32[32,1,256]{2,1,0:T(1,128)S(1)}, u32[]{:S(2)}, u32[]{:S(2)}) async-start(s32[32,1,256]{2,1,0:T(1,128)} %get-tuple-element.51), calls=%async_computation | async-start | bytes 65536 | tf_op jit(solution)/shard_map/all_to_all | solution.py:393
  12.1 11.9 %collective-permute-start.1 = (f32[256,256]{1,0:T(8,128)S(1)}, f32[256,256]{1,0:T(8,128)S(1)}, u32[]{:S(2)}, u32[]{:S(2)}) collective-permute-start(f32[256,256]{1,0:T(8,128)S(1)} %get-tuple-element.50.refs_4_.refs_0_), channel_id=1, source_target_pairs={{0,1},{1,0},{2,3},{3,2},{4,5},{5,4},{6,7},{7,6},{8,9},{9,8},{10,11... | collective-permute-start | bytes 786440 | tf_op jit(solution)/shard_map/ppermute | solution.py:367
  13.9 15.4 %collective-permute-start.8 = (f32[256,256]{1,0:T(8,128)S(1)}, f32[256,256]{1,0:T(8,128)S(1)}, u32[]{:S(2)}, u32[]{:S(2)}) collective-permute-start(f32[256,256]{1,0:T(8,128)S(1)} %get-tuple-element.50.refs_4_.refs_0_), channel_id=1, source_target_pairs={{0,2},{1,3},{2,0},{3,1},{4,6},{5,7},{6,4},{7,5},{8,10},{9,11},{10,... | collective-permute-start | bytes 786440 | tf_op jit(solution)/shard_map/ppermute | solution.py:367
  22.7 8.3 %collective-permute-start.6 = (f32[256,256]{1,0:T(8,128)S(1)}, f32[256,256]{1,0:T(8,128)S(1)}, u32[]{:S(2)}, u32[]{:S(2)}) collective-permute-start(f32[256,256]{1,0:T(8,128)S(1)} %collective-permute-done.refs_1_.refs_7_.refs_4_.refs_8_), channel_id=1, source_target_pairs={{0,1},{1,0},{2,3},{3,2},{4,5},{5,4},{6,7},{7,6},{8,9},{9,8},{10,11... | collective-permute-start | bytes 786440 | tf_op jit(solution)/shard_map/ppermute | solution.py:367
  23.4 10.7 %collective-permute-start.7 = (f32[256,256]{1,0:T(8,128)S(1)}, f32[256,256]{1,0:T(8,128)S(1)}, u32[]{:S(2)}, u32[]{:S(2)}) collective-permute-start(f32[256,256]{1,0:T(8,128)S(1)} %collective-permute-done.refs_1_.refs_7_.refs_4_.refs_8_), channel_id=1, source_target_pairs={{0,2},{1,3},{2,0},{3,1},{4,6},{5,7},{6,4},{7,5},{8,10},{9,11},{10,... | collective-permute-start | bytes 786440 | tf_op jit(solution)/shard_map/ppermute | solution.py:367
  23.9 2.2 %copy-start = (f32[4096,256]{1,0:T(8,128)S(1)}, f32[4096,256]{1,0:T(8,128)}, u32[]{:S(2)}) copy-start(f32[4096,256]{1,0:T(8,128)} %table.5) | copy-start | bytes 12582916
  28.4 7.1 %collective-permute-start.2 = (f32[128,256]{1,0:T(8,128)S(1)}, f32[128,256]{1,0:T(8,128)S(1)}, u32[]{:S(2)}, u32[]{:S(2)}) collective-permute-start(f32[128,256]{1,0:T(8,128)S(1)} %get-tuple-element.54), channel_id=1, source_target_pairs={{0,8},{8,0},{16,24},{24,16},{1,9},{9,1},{17,25},{25,17},{2,10},{10... | collective-permute-start | bytes 393224 | tf_op jit(solution)/shard_map/ppermute | solution.py:367
  28.5 7.6 %collective-permute-start.3 = (f32[128,256]{1,0:T(8,128)S(1)}, f32[128,256]{1,0:T(8,128)S(1)}, u32[]{:S(2)}, u32[]{:S(2)}) collective-permute-start(f32[128,256]{1,0:T(8,128)S(1)} %get-tuple-element.55), channel_id=1, source_target_pairs={{0,16},{8,24},{16,0},{24,8},{1,17},{9,25},{17,1},{25,9},{2,18},{10... | collective-permute-start | bytes 393224 | tf_op jit(solution)/shard_map/ppermute | solution.py:367
  29.3 7.5 %collective-permute-start.4 = (f32[128,256]{1,0:T(8,128)S(1)}, f32[128,256]{1,0:T(8,128)S(1)}, u32[]{:S(2)}, u32[]{:S(2)}) collective-permute-start(f32[128,256]{1,0:T(8,128)S(1)} %get-tuple-element.56), channel_id=1, source_target_pairs={{0,24},{8,16},{16,8},{24,0},{1,25},{9,17},{17,9},{25,1},{2,26},{10... | collective-permute-start | bytes 393224 | tf_op jit(solution)/shard_map/ppermute | solution.py:367
  30.4 9.5 %copy-start.1 = (f32[4096,256]{1,0:T(8,128)S(1)}, f32[4096,256]{1,0:T(8,128)}, u32[]{:S(2)}) copy-start(f32[4096,256]{1,0:T(8,128)} %table.5) | copy-start | bytes 12582916
  31.0 12.2 %collective-permute-start.5 = (f32[256,256]{1,0:T(8,128)S(1)}, f32[256,256]{1,0:T(8,128)S(1)}, u32[]{:S(2)}, u32[]{:S(2)}) collective-permute-start(f32[256,256]{1,0:T(8,128)S(1)} %collective-permute-done.1.refs_0_.refs_5_.refs_1_), channel_id=1, source_target_pairs={{0,2},{1,3},{2,0},{3,1},{4,6},{5,7},{6,4},{7,5},{8,10},{9,11},{10,... | collective-permute-start | bytes 786440 | tf_op jit(solution)/shard_map/ppermute | solution.py:367
  34.0 9.1 %collective-permute-start.9 = (f32[256,256]{1,0:T(8,128)S(1)}, f32[256,256]{1,0:T(8,128)S(1)}, u32[]{:S(2)}, u32[]{:S(2)}) collective-permute-start(f32[256,256]{1,0:T(8,128)S(1)} %collective-permute-done.7.refs_6_.refs_10_), channel_id=1, source_target_pairs={{0,1},{1,0},{2,3},{3,2},{4,5},{5,4},{6,7},{7,6},{8,9},{9,8},{10,11... | collective-permute-start | bytes 786440 | tf_op jit(solution)/shard_map/ppermute | solution.py:367
  35.5 14.3 %collective-permute-start.11 = (f32[256,256]{1,0:T(8,128)S(1)}, f32[256,256]{1,0:T(8,128)S(1)}, u32[]{:S(2)}, u32[]{:S(2)}) collective-permute-start(f32[256,256]{1,0:T(8,128)S(1)} %get-tuple-element.59.refs_8_), channel_id=1, source_target_pairs={{0,16},{8,24},{16,0},{24,8},{1,17},{9,25},{17,1},{25,9},{2,18},{10... | collective-permute-start | bytes 786440 | tf_op jit(solution)/shard_map/ppermute | solution.py:367
  36.1 12.5 %collective-permute-start.12 = (f32[256,256]{1,0:T(8,128)S(1)}, f32[256,256]{1,0:T(8,128)S(1)}, u32[]{:S(2)}, u32[]{:S(2)}) collective-permute-start(f32[256,256]{1,0:T(8,128)S(1)} %get-tuple-element.61.refs_9_), channel_id=1, source_target_pairs={{0,24},{8,16},{16,8},{24,0},{1,25},{9,17},{17,9},{25,1},{2,26},{10... | collective-permute-start | bytes 786440 | tf_op jit(solution)/shard_map/ppermute | solution.py:367
  42.2 7.6 %collective-permute-start.10 = (f32[256,256]{1,0:T(8,128)S(1)}, f32[256,256]{1,0:T(8,128)S(1)}, u32[]{:S(2)}, u32[]{:S(2)}) collective-permute-start(f32[256,256]{1,0:T(8,128)S(1)} %get-tuple-element.65), channel_id=1, source_target_pairs={{0,8},{8,0},{16,24},{24,16},{1,9},{9,1},{17,25},{25,17},{2,10},{10... | collective-permute-start | bytes 786440 | tf_op jit(solution)/shard_map/ppermute | solution.py:367
  47.9 19.3 %collective-permute-start.16 = (f32[256,256]{1,0:T(8,128)S(1)}, f32[256,256]{1,0:T(8,128)S(1)}, u32[]{:S(2)}, u32[]{:S(2)}) collective-permute-start(f32[256,256]{1,0:T(8,128)S(1)} %get-tuple-element.80.refs_5_), channel_id=1, source_target_pairs={{0,8},{8,0},{16,24},{24,16},{1,9},{9,1},{17,25},{25,17},{2,10},{10... | collective-permute-start | bytes 786440 | tf_op jit(solution)/shard_map/ppermute | solution.py:367
  48.0 19.2 %collective-permute-start.17 = (f32[256,256]{1,0:T(8,128)S(1)}, f32[256,256]{1,0:T(8,128)S(1)}, u32[]{:S(2)}, u32[]{:S(2)}) collective-permute-start(f32[256,256]{1,0:T(8,128)S(1)} %get-tuple-element.81.refs_6_), channel_id=1, source_target_pairs={{0,16},{8,24},{16,0},{24,8},{1,17},{9,25},{17,1},{25,9},{2,18},{10... | collective-permute-start | bytes 786440 | tf_op jit(solution)/shard_map/ppermute | solution.py:367
  48.6 18.6 %collective-permute-start.18 = (f32[256,256]{1,0:T(8,128)S(1)}, f32[256,256]{1,0:T(8,128)S(1)}, u32[]{:S(2)}, u32[]{:S(2)}) collective-permute-start(f32[256,256]{1,0:T(8,128)S(1)} %get-tuple-element.82.refs_7_), channel_id=1, source_target_pairs={{0,24},{8,16},{16,8},{24,0},{1,25},{9,17},{17,9},{25,1},{2,26},{10... | collective-permute-start | bytes 786440 | tf_op jit(solution)/shard_map/ppermute | solution.py:367
  51.0 3.8 %collective-permute-start.13 = (f32[2,2048]{1,0:T(2,128)S(1)}, f32[2,2048]{1,0:T(2,128)S(1)}, u32[]{:S(2)}, u32[]{:S(2)}) collective-permute-start(f32[2,2048]{1,0:T(2,128)S(1)} %get-tuple-element.70.first), channel_id=1, source_target_pairs={{0,1},{1,0},{2,3},{3,2},{4,5},{5,4},{6,7},{7,6},{8,9},{9,8},{10,11... | collective-permute-start | bytes 49160 | tf_op jit(solution)/shard_map/ppermute | solution.py:367
  54.8 3.8 %collective-permute-start.14 = (f32[2,2048]{1,0:T(2,128)S(1)}, f32[2,2048]{1,0:T(2,128)S(1)}, u32[]{:S(2)}, u32[]{:S(2)}) collective-permute-start(f32[2,2048]{1,0:T(2,128)S(1)} %join.3.first), channel_id=1, source_target_pairs={{0,2},{1,3},{2,0},{3,1},{4,6},{5,7},{6,4},{7,5},{8,10},{9,11},{10,... | collective-permute-start | bytes 49160 | tf_op jit(solution)/shard_map/ppermute | solution.py:367
  58.7 5.2 %collective-permute-start.15 = (f32[2,2048]{1,0:T(2,128)S(1)}, f32[2,2048]{1,0:T(2,128)S(1)}, u32[]{:S(2)}, u32[]{:S(2)}) collective-permute-start(f32[2,2048]{1,0:T(2,128)S(1)} %join.4.first), channel_id=1, source_target_pairs={{0,4},{1,5},{2,6},{3,7},{4,0},{5,1},{6,2},{7,3},{8,12},{9,13},{10,... | collective-permute-start | bytes 49160 | tf_op jit(solution)/shard_map/ppermute | solution.py:367
  64.5 8.0 %collective-permute-start.19 = (f32[256,256]{1,0:T(8,128)S(1)}, f32[256,256]{1,0:T(8,128)S(1)}, u32[]{:S(2)}, u32[]{:S(2)}) collective-permute-start(f32[256,256]{1,0:T(8,128)S(1)} %get-tuple-element.87), channel_id=1, source_target_pairs={{0,1},{1,0},{2,3},{3,2},{4,5},{5,4},{6,7},{7,6},{8,9},{9,8},{10,11... | collective-permute-start | bytes 786440 | tf_op jit(solution)/shard_map/ppermute | solution.py:367
  66.1 6.4 %collective-permute-start.20 = (f32[256,256]{1,0:T(8,128)S(1)}, f32[256,256]{1,0:T(8,128)S(1)}, u32[]{:S(2)}, u32[]{:S(2)}) collective-permute-start(f32[256,256]{1,0:T(8,128)S(1)} %get-tuple-element.88), channel_id=1, source_target_pairs={{0,2},{1,3},{2,0},{3,1},{4,6},{5,7},{6,4},{7,5},{8,10},{9,11},{10,... | collective-permute-start | bytes 786440 | tf_op jit(solution)/shard_map/ppermute | solution.py:367
  69.8 4.3 %collective-permute-start.23 = (f32[136,256]{1,0:T(8,128)S(1)}, f32[136,256]{1,0:T(8,128)S(1)}, u32[]{:S(2)}, u32[]{:S(2)}) collective-permute-start(f32[136,256]{1,0:T(8,128)S(1)} %get-tuple-element.93), channel_id=1, source_target_pairs={{0,8},{8,0},{16,24},{24,16},{1,9},{9,1},{17,25},{25,17},{2,10},{10... | collective-permute-start | bytes 417800 | tf_op jit(solution)/shard_map/ppermute | solution.py:367
  69.9 9.2 %collective-permute-start.24 = (f32[136,256]{1,0:T(8,128)S(1)}, f32[136,256]{1,0:T(8,128)S(1)}, u32[]{:S(2)}, u32[]{:S(2)}) collective-permute-start(f32[136,256]{1,0:T(8,128)S(1)} %get-tuple-element.94), channel_id=1, source_target_pairs={{0,16},{8,24},{16,0},{24,8},{1,17},{9,25},{17,1},{25,9},{2,18},{10... | collective-permute-start | bytes 417800 | tf_op jit(solution)/shard_map/ppermute | solution.py:367
  70.5 8.6 %collective-permute-start.25 = (f32[136,256]{1,0:T(8,128)S(1)}, f32[136,256]{1,0:T(8,128)S(1)}, u32[]{:S(2)}, u32[]{:S(2)}) collective-permute-start(f32[136,256]{1,0:T(8,128)S(1)} %get-tuple-element.95), channel_id=1, source_target_pairs={{0,24},{8,16},{16,8},{24,0},{1,25},{9,17},{17,9},{25,1},{2,26},{10... | collective-permute-start | bytes 417800 | tf_op jit(solution)/shard_map/ppermute | solution.py:367
  72.5 10.4 %collective-permute-start.26 = (f32[256,256]{1,0:T(8,128)S(1)}, f32[256,256]{1,0:T(8,128)S(1)}, u32[]{:S(2)}, u32[]{:S(2)}) collective-permute-start(f32[256,256]{1,0:T(8,128)S(1)} %add.13.refs_4_), channel_id=1, source_target_pairs={{0,2},{1,3},{2,0},{3,1},{4,6},{5,7},{6,4},{7,5},{8,10},{9,11},{10,... | collective-permute-start | bytes 786440 | tf_op jit(solution)/shard_map/ppermute | solution.py:367
  73.6 8.3 %collective-permute-start.21 = (f32[256,256]{1,0:T(8,128)S(1)}, f32[256,256]{1,0:T(8,128)S(1)}, u32[]{:S(2)}, u32[]{:S(2)}) collective-permute-start(f32[256,256]{1,0:T(8,128)S(1)} %get-tuple-element.89), channel_id=1, source_target_pairs={{0,1},{1,0},{2,3},{3,2},{4,5},{5,4},{6,7},{7,6},{8,9},{9,8},{10,11... | collective-permute-start | bytes 786440 | tf_op jit(solution)/shard_map/ppermute | solution.py:367
  81.9 13.1 %collective-permute-start.22 = (f32[256,256]{1,0:T(8,128)S(1)}, f32[256,256]{1,0:T(8,128)S(1)}, u32[]{:S(2)}, u32[]{:S(2)}) collective-permute-start(f32[256,256]{1,0:T(8,128)S(1)} %get-tuple-element.90), channel_id=1, source_target_pairs={{0,2},{1,3},{2,0},{3,1},{4,6},{5,7},{6,4},{7,5},{8,10},{9,11},{10,... | collective-permute-start | bytes 786440 | tf_op jit(solution)/shard_map/ppermute | solution.py:367
  83.0 12.0 %copy-start.3 = (s32[256]{0:T(256)S(1)}, s32[256]{0:T(256)}, u32[]{:S(2)}) copy-start(s32[256]{0:T(256)} %param.11) | copy-start | bytes 3076
  83.0 10.5 %collective-permute-start.28 = (f32[256,256]{1,0:T(8,128)S(1)}, f32[256,256]{1,0:T(8,128)S(1)}, u32[]{:S(2)}, u32[]{:S(2)}) collective-permute-start(f32[256,256]{1,0:T(8,128)S(1)} %add.16), channel_id=1, source_target_pairs={{0,4},{1,5},{2,6},{3,7},{4,0},{5,1},{6,2},{7,3},{8,12},{9,13},{10,... | collective-permute-start | bytes 786440 | tf_op jit(solution)/shard_map/ppermute | solution.py:367
  85.3 9.6 %collective-permute-start.27 = (f32[256,256]{1,0:T(8,128)S(1)}, f32[256,256]{1,0:T(8,128)S(1)}, u32[]{:S(2)}, u32[]{:S(2)}) collective-permute-start(f32[256,256]{1,0:T(8,128)S(1)} %add.14), channel_id=1, source_target_pairs={{0,1},{1,0},{2,3},{3,2},{4,5},{5,4},{6,7},{7,6},{8,9},{9,8},{10,11... | collective-permute-start | bytes 786440 | tf_op jit(solution)/shard_map/ppermute | solution.py:367

commit v12 on v11

--- a/solution.py
+++ b/solution.py
@@ -22,7 +22,19 @@
 TN = (((0,), (0,)), ((), ()))
 
 
+PLACE = object()
+
+
+def located(kernel):
+    def run(*refs):
+        kernel((lax.axis_index("group"), lax.axis_index("member")), *refs)
+
+    return run
+
+
 def call(kernel, out_shape, ins, outs, args, scratch=(), limit=10, flops=0, moved=0, name=None):
+    if args[0] is PLACE:
+        kernel, ins, args = located(kernel), ins[1:], args[1:]
     return pl.pallas_call(
         kernel,
         out_shape=out_shape,
@@ -380,7 +392,7 @@
     shape = jax.ShapeDtypeStruct
     sds = lambda *s: shape(s, F32)
 
-    info = jnp.stack([lax.axis_index("group"), lax.axis_index("member")]).astype(I32)
+    info = PLACE
     ints = jnp.concatenate([target_owner.reshape(-1), target_local, valid, negative_ids])
     request, masked = call(
         functools.partial(front_kernel, members, rows_dev, slots, tokens, negatives),

time: 96.4 us -> 91.7 us (0.951)
  Pallas kernels: 38.7 us -> 33.2 us
  waiting for transfers between devices: 15.5 us -> 16.9 us
    pallas_call x24, Pallas kernels: 38.7 us -> 33.2 us  [call(): pl.pallas_call(kernel, out_shape=out_shape, in_specs=ins, out_specs=outs,...]
    ppermute x29, waiting for transfers between devices: 8.18 us -> 9.55 us  [swap(): lax.ppermute(value, axis, [(i, i ^ d) for i in range(lax.axis_size(axis))])]
  transfers between devices with their start and end apart: 30 -> 30, of which waited for: 9 -> 10; matrix products, arithmetic and copies ran while one was open for 0% -> 0% of each run, Pallas kernels for 37% -> 34%
where the time goes in v12:
time: 91.7 us; the launch traced here: 90.8 us
  starting transfers between devices  36 us (39%)
  Pallas kernels  33.2 us (36%)
  waiting for transfers between devices  16.9 us (18%)
  local copies, waits for them, and re-layouts  3.15 us (3%)
    pallas_call x24, Pallas kernels, call(): pl.pallas_call(kernel, out_shape=out_shape, in_specs=ins, out_specs=outs,...  33.2 us
    ppermute x29, starting transfers between devices, swap(): lax.ppermute(value, axis, [(i, i ^ d) for i in range(lax.axis_size(axis))])  32.2 us
    ppermute x29, waiting for transfers between devices, swap(): lax.ppermute(value, axis, [(i, i ^ d) for i in range(lax.axis_size(axis))])  9.55 us
    all_to_all x1, waiting for transfers between devices, shards(): lax.all_to_all(request, ('group', 'member'), split_axis=0, concat_axis=0,...  7.36 us
    all_to_all x1, starting transfers between devices, shards(): lax.all_to_all(request, ('group', 'member'), split_axis=0, concat_axis=0,...  3.82 us
    unnamed x8, local copies, waits for them, and re-layouts  3.14 us
  transfers between devices with their start and end apart: 30, of which 10 were waited for; matrix products, arithmetic and copies ran while one was open for 0% of the time, Pallas kernels for 34%

profile of v12, /device:TPU:0, one launch (start us, length us, event | category | flops | bytes accessed | tf_op | source)
XLA Modules:
  0.0 90.8 jit_solution(15830516862607451375)
XLA Ops:
  0.6 0.7 pad_add_fusion
  1.4 0.9 %copy-done.2 = f32[256,256]{1,0:T(8,128)S(1)} copy-done((f32[256,256]{1,0:T(8,128)S(1)}, f32[256,256]{1,0:T(8,128)}, u32[]{:S(2)}) %copy-start.2) | copy-done | bytes 262168
  2.3 1.2 %front.1 = (s32[32,1,256]{2,1,0:T(1,128)}, f32[256,256]{1,0:T(8,128)S(1)}) custom-call(s32[1,1280]{1,0:T(1,128)S(1)} %reshape.15.refs_0_, f32[256,256]{1,0:T(8,128)S(1)} %copy-done.2), custom_call_target="tpu_custom_call" | custom-call | tf_op jit(solution)/shard_map/front/pallas_call | solution.py:38
  3.6 4.0 %collective-permute-start = (f32[256,256]{1,0:T(8,128)S(1)}, f32[256,256]{1,0:T(8,128)S(1)}, u32[]{:S(2)}, u32[]{:S(2)}) collective-permute-start(f32[256,256]{1,0:T(8,128)S(1)} %get-tuple-element.50.refs_4_.refs_1_.refs_8_), channel_id=1, source_target_pairs={{0,4},{1,5},{2,6},{3,7},{4,0},{5,1},{6,2},{7,3},{8,12},{9,13},{10,... | collective-permute-start | bytes 786440 | tf_op jit(solution)/shard_map/ppermute | solution.py:379
  7.6 3.8 %all-to-all-start = ((s32[32,1,256]{2,1,0:T(1,128)}), s32[32,1,256]{2,1,0:T(1,128)S(1)}, u32[]{:S(2)}, u32[]{:S(2)}) async-start(s32[32,1,256]{2,1,0:T(1,128)} %get-tuple-element.51), calls=%async_computation | async-start | bytes 65536 | tf_op jit(solution)/shard_map/all_to_all | solution.py:405
  11.4 1.8 %collective-permute-start.1 = (f32[256,256]{1,0:T(8,128)S(1)}, f32[256,256]{1,0:T(8,128)S(1)}, u32[]{:S(2)}, u32[]{:S(2)}) collective-permute-start(f32[256,256]{1,0:T(8,128)S(1)} %get-tuple-element.50.refs_4_.refs_1_.refs_8_), channel_id=1, source_target_pairs={{0,1},{1,0},{2,3},{3,2},{4,5},{5,4},{6,7},{7,6},{8,9},{9,8},{10,11... | collective-permute-start | bytes 786440 | tf_op jit(solution)/shard_map/ppermute | solution.py:379
  13.3 1.5 %collective-permute-start.8 = (f32[256,256]{1,0:T(8,128)S(1)}, f32[256,256]{1,0:T(8,128)S(1)}, u32[]{:S(2)}, u32[]{:S(2)}) collective-permute-start(f32[256,256]{1,0:T(8,128)S(1)} %get-tuple-element.50.refs_4_.refs_1_.refs_8_), channel_id=1, source_target_pairs={{0,2},{1,3},{2,0},{3,1},{4,6},{5,7},{6,4},{7,5},{8,10},{9,11},{10,... | collective-permute-start | bytes 786440 | tf_op jit(solution)/shard_map/ppermute | solution.py:379
  14.7 7.4 %all-to-all-done.refs_0_.refs_1_ = s32[32,1,256]{2,1,0:T(1,128)S(1)} async-done(((s32[32,1,256]{2,1,0:T(1,128)}), s32[32,1,256]{2,1,0:T(1,128)S(1)}, u32[]{:S(2)}, u32[]{:S(2)}) %all-to-all-start) | async-done | bytes 32800 | tf_op jit(solution)/shard_map/all_to_all | solution.py:405
  22.1 0.6 collective-permute-start.6
  23.3 2.2 %copy-done = f32[4096,256]{1,0:T(8,128)S(1)} copy-done((f32[4096,256]{1,0:T(8,128)S(1)}, f32[4096,256]{1,0:T(8,128)}, u32[]{:S(2)}) %copy-start) | copy-done | bytes 4194328
  25.5 2.3 %gather_negatives.1 = (f32[128,256]{1,0:T(8,128)S(1)}, f32[128,256]{1,0:T(8,128)S(1)}, f32[128,256]{1,0:T(8,128)S(1)}, f32[128,256]{1,0:T(8,128)S(1)}) custom-call(s32[32,1,256]{2,1,0:T(1,128)S(1)} %all-to-all-done.refs_0_.refs_1_, f32[4096,256]{1,0:T(8,128)S(1)} %copy-done, f32[256,256]{1,0:T(8,128)S(1)} %collective-permute-done.1.refs_2_.refs_5_.refs_9_, ...), custom_call_target="tpu_custom_call" | custom-call | tf_op jit(solution)/shard_map/gather_negatives/pallas_call | solution.py:38
  27.9 0.8 collective-permute-start.3
  28.7 1.1 %collective-permute-start.4 = (f32[128,256]{1,0:T(8,128)S(1)}, f32[128,256]{1,0:T(8,128)S(1)}, u32[]{:S(2)}, u32[]{:S(2)}) collective-permute-start(f32[128,256]{1,0:T(8,128)S(1)} %get-tuple-element.56), channel_id=1, source_target_pairs={{0,24},{8,16},{16,8},{24,0},{1,25},{9,17},{17,9},{25,1},{2,26},{10... | collective-permute-start | bytes 393224 | tf_op jit(solution)/shard_map/ppermute | solution.py:379
  29.7 0.7 collective-permute-done.6.refs_3_.refs_5_.refs_6_.refs_13_
  30.4 0.8 collective-permute-start.5
  31.2 2.2 %gather_far_targets.1 = (f32[256,256]{1,0:T(8,128)S(1)}, f32[256,256]{1,0:T(8,128)S(1)}) custom-call(s32[32,1,256]{2,1,0:T(1,128)S(1)} %all-to-all-done.refs_0_.refs_1_, f32[4096,256]{1,0:T(8,128)S(1)} %copy-done, f32[256,256]{1,0:T(8,128)S(1)} %collective-permute-done.8.refs_2_.refs_6_.refs_3_.refs_10_, ...), custom_call_target="tpu_custom_call" | custom-call | tf_op jit(solution)/shard_map/gather_far_targets/pallas_call | solution.py:38
  33.4 1.5 %collective-permute-start.9 = (f32[256,256]{1,0:T(8,128)S(1)}, f32[256,256]{1,0:T(8,128)S(1)}, u32[]{:S(2)}, u32[]{:S(2)}) collective-permute-start(f32[256,256]{1,0:T(8,128)S(1)} %collective-permute-done.7.refs_6_.refs_7_.refs_14_), channel_id=1, source_target_pairs={{0,1},{1,0},{2,3},{3,2},{4,5},{5,4},{6,7},{7,6},{8,9},{9,8},{10,11... | collective-permute-start | bytes 786440 | tf_op jit(solution)/shard_map/ppermute | solution.py:379
  36.1 2.5 %score.2 = (f32[2,2048]{1,0:T(2,128)S(1)}, bf16[4,512,256]{2,1,0:T(8,128)(2,1)S(1)}, bf16[4,512,256]{2,1,0:T(8,128)(2,1)S(1)}) custom-call(f32[128,256]{1,0:T(8,128)S(1)} %get-tuple-element.53.refs_0_.refs_1_, f32[128,256]{1,0:T(8,128)S(1)} %collective-permute-done.2.refs_1_.refs_2_, f32[128,256]{1,0:T(8,128)S(1)} %collective-permute-done.3.refs_2_.refs_3_, ...), custom_call_target="tpu_custom_call" | custom-call | flops 1610612736 | bytes 1048576 | tf_op jit(solution)/shard_map/score/pallas_call | solution.py:38
  38.7 2.4 %gather_targets.1 = (f32[256,256]{1,0:T(8,128)S(1)}, f32[256,256]{1,0:T(8,128)S(1)}) custom-call(s32[32,1,256]{2,1,0:T(1,128)S(1)} %all-to-all-done.refs_0_.refs_1_, f32[4096,256]{1,0:T(8,128)S(1)} %copy-done.1, f32[2,2048]{1,0:T(2,128)S(1)} %get-tuple-element.62.refs_8_.refs_2_), custom_call_target="tpu_custom_call" | custom-call | tf_op jit(solution)/shard_map/gather_targets/pallas_call | solution.py:38
  41.0 0.9 %collective-permute-start.10 = (f32[256,256]{1,0:T(8,128)S(1)}, f32[256,256]{1,0:T(8,128)S(1)}, u32[]{:S(2)}, u32[]{:S(2)}) collective-permute-start(f32[256,256]{1,0:T(8,128)S(1)} %get-tuple-element.65), channel_id=1, source_target_pairs={{0,8},{8,0},{16,24},{24,16},{1,9},{9,1},{17,25},{25,17},{2,10},{10... | collective-permute-start | bytes 786440 | tf_op jit(solution)/shard_map/ppermute | solution.py:379
  42.0 1.1 %pick.1 = (f32[256,256]{1,0:T(8,128)S(1)}, f32[256,256]{1,0:T(8,128)S(1)}, f32[256,256]{1,0:T(8,128)S(1)}, f32[256,256]{1,0:T(8,128)S(1)}) custom-call(s32[32,1,256]{2,1,0:T(1,128)S(1)} %all-to-all-done.refs_0_.refs_1_, f32[256,256]{1,0:T(8,128)S(1)} %get-tuple-element.50.refs_4_.refs_1_.refs_8_, ...), custom_call_target="tpu_custom_call" | custom-call | tf_op jit(solution)/shard_map/pick/pallas_call | solution.py:38
  43.1 2.5 %score.3 = (f32[2,2048]{1,0:T(2,128)S(1)}, bf16[4,512,256]{2,1,0:T(8,128)(2,1)S(1)}, bf16[4,512,256]{2,1,0:T(8,128)(2,1)S(1)}) custom-call(f32[128,256]{1,0:T(8,128)S(1)} %get-tuple-element.53.refs_0_.refs_1_, f32[128,256]{1,0:T(8,128)S(1)} %collective-permute-done.2.refs_1_.refs_2_, f32[128,256]{1,0:T(8,128)S(1)} %collective-permute-done.3.refs_2_.refs_3_, ...), custom_call_target="tpu_custom_call" | custom-call | flops 1610612736 | bytes 1048576 | tf_op jit(solution)/shard_map/score/pallas_call | solution.py:38
  45.7 0.6 collective-permute-start.17
  46.3 0.9 %collective-permute-done.12.refs_5_.refs_8_ = f32[256,256]{1,0:T(8,128)S(1)} collective-permute-done((f32[256,256]{1,0:T(8,128)S(1)}, f32[256,256]{1,0:T(8,128)S(1)}, u32[]{:S(2)}, u32[]{:S(2)}) %collective-permute-start.12) | collective-permute-done | bytes 262176 | tf_op jit(solution)/shard_map/ppermute | solution.py:379
  47.3 1.2 %collective-permute-start.18 = (f32[256,256]{1,0:T(8,128)S(1)}, f32[256,256]{1,0:T(8,128)S(1)}, u32[]{:S(2)}, u32[]{:S(2)}) collective-permute-start(f32[256,256]{1,0:T(8,128)S(1)} %get-tuple-element.82.refs_9_), channel_id=1, source_target_pairs={{0,24},{8,16},{16,8},{24,0},{1,25},{9,17},{17,9},{25,1},{2,26},{10... | collective-permute-start | bytes 786440 | tf_op jit(solution)/shard_map/ppermute | solution.py:379
  48.5 0.7 positive.1
  49.2 0.8 collective-permute-start.13
  50.0 1.5 %pulled.2 = (f32[4,256,256]{2,1,0:T(8,128)S(1)}, f32[4,256,256]{2,1,0:T(8,128)S(1)}) custom-call(s32[32,1,256]{2,1,0:T(1,128)S(1)} %all-to-all-done.refs_0_.refs_1_, f32[128,256]{1,0:T(8,128)S(1)} %get-tuple-element.53.refs_0_.refs_1_, f32[128,256]{1,0:T(8,128)S(1)} %collective-permute-done.2.refs_1_.refs_2_, ...), custom_call_target="tpu_custom_call" | custom-call | flops 805306368 | bytes 1048576 | tf_op jit(solution)/shard_map/pulled/pallas_call | solution.py:38
  51.5 1.5 %collective-permute-done.13.second = f32[2,2048]{1,0:T(2,128)S(1)} collective-permute-done((f32[2,2048]{1,0:T(2,128)S(1)}, f32[2,2048]{1,0:T(2,128)S(1)}, u32[]{:S(2)}, u32[]{:S(2)}) %collective-permute-start.13) | collective-permute-done | bytes 16416 | tf_op jit(solution)/shard_map/ppermute | solution.py:379
  53.0 0.9 collective-permute-start.14
  53.9 1.5 %pulled.3 = (f32[4,256,256]{2,1,0:T(8,128)S(1)}, f32[4,256,256]{2,1,0:T(8,128)S(1)}) custom-call(s32[32,1,256]{2,1,0:T(1,128)S(1)} %all-to-all-done.refs_0_.refs_1_, f32[128,256]{1,0:T(8,128)S(1)} %get-tuple-element.53.refs_0_.refs_1_, f32[128,256]{1,0:T(8,128)S(1)} %collective-permute-done.2.refs_1_.refs_2_, ...), custom_call_target="tpu_custom_call" | custom-call | flops 805306368 | bytes 1048576 | tf_op jit(solution)/shard_map/pulled/pallas_call | solution.py:38
  55.3 1.5 %collective-permute-done.14.second = f32[2,2048]{1,0:T(2,128)S(1)} collective-permute-done((f32[2,2048]{1,0:T(2,128)S(1)}, f32[2,2048]{1,0:T(2,128)S(1)}, u32[]{:S(2)}, u32[]{:S(2)}) %collective-permute-start.14) | collective-permute-done | bytes 16416 | tf_op jit(solution)/shard_map/ppermute | solution.py:379
  56.8 2.8 %collective-permute-start.15 = (f32[2,2048]{1,0:T(2,128)S(1)}, f32[2,2048]{1,0:T(2,128)S(1)}, u32[]{:S(2)}, u32[]{:S(2)}) collective-permute-start(f32[2,2048]{1,0:T(2,128)S(1)} %join.4.first), channel_id=1, source_target_pairs={{0,4},{1,5},{2,6},{3,7},{4,0},{5,1},{6,2},{7,3},{8,12},{9,13},{10,... | collective-permute-start | bytes 49160 | tf_op jit(solution)/shard_map/ppermute | solution.py:379
  59.7 1.9 %collective-permute-done.15.second = f32[2,2048]{1,0:T(2,128)S(1)} collective-permute-done((f32[2,2048]{1,0:T(2,128)S(1)}, f32[2,2048]{1,0:T(2,128)S(1)}, u32[]{:S(2)}, u32[]{:S(2)}) %collective-permute-start.15) | collective-permute-done | bytes 16416 | tf_op jit(solution)/shard_map/ppermute | solution.py:379
  61.7 1.5 %collective-permute-start.19 = (f32[256,256]{1,0:T(8,128)S(1)}, f32[256,256]{1,0:T(8,128)S(1)}, u32[]{:S(2)}, u32[]{:S(2)}) collective-permute-start(f32[256,256]{1,0:T(8,128)S(1)} %get-tuple-element.87), channel_id=1, source_target_pairs={{0,1},{1,0},{2,3},{3,2},{4,5},{5,4},{6,7},{7,6},{8,9},{9,8},{10,11... | collective-permute-start | bytes 786440 | tf_op jit(solution)/shard_map/ppermute | solution.py:379
  63.2 0.8 collective-permute-start.20
  64.0 2.0 %grad.1 = (f32[136,256]{1,0:T(8,128)S(1)}, f32[136,256]{1,0:T(8,128)S(1)}, f32[136,256]{1,0:T(8,128)S(1)}, f32[136,256]{1,0:T(8,128)S(1)}) custom-call(s32[32,1,256]{2,1,0:T(1,128)S(1)} %all-to-all-done.refs_0_.refs_1_, f32[2,2048]{1,0:T(2,128)S(1)} %join.5.refs_1_.refs_0_, f32[2,2048]{1,0:T(2,128)S(1)} %get-tuple-element.63.refs_1_.refs_2_, ...), custom_call_target="tpu_custom_call" | custom-call | flops 1610612736 | bytes 8388608 | tf_op jit(solution)/shard_map/grad/pallas_call | solution.py:38
  66.1 1.5 %collective-permute-start.24 = (f32[136,256]{1,0:T(8,128)S(1)}, f32[136,256]{1,0:T(8,128)S(1)}, u32[]{:S(2)}, u32[]{:S(2)}) collective-permute-start(f32[136,256]{1,0:T(8,128)S(1)} %get-tuple-element.94), channel_id=1, source_target_pairs={{0,16},{8,24},{16,0},{24,8},{1,17},{9,25},{17,1},{25,9},{2,18},{10... | collective-permute-start | bytes 417800 | tf_op jit(solution)/shard_map/ppermute | solution.py:379
  68.1 1.4 %collective-permute-done.20.refs_3_.refs_1_ = f32[256,256]{1,0:T(8,128)S(1)} collective-permute-done((f32[256,256]{1,0:T(8,128)S(1)}, f32[256,256]{1,0:T(8,128)S(1)}, u32[]{:S(2)}, u32[]{:S(2)}) %collective-permute-start.20) | collective-permute-done | bytes 262176 | tf_op jit(solution)/shard_map/ppermute | solution.py:379
  69.6 0.8 collective-permute-start.26
  70.4 1.0 %collective-permute-start.21 = (f32[256,256]{1,0:T(8,128)S(1)}, f32[256,256]{1,0:T(8,128)S(1)}, u32[]{:S(2)}, u32[]{:S(2)}) collective-permute-start(f32[256,256]{1,0:T(8,128)S(1)} %get-tuple-element.89), channel_id=1, source_target_pairs={{0,1},{1,0},{2,3},{3,2},{4,5},{5,4},{6,7},{7,6},{8,9},{9,8},{10,11... | collective-permute-start | bytes 786440 | tf_op jit(solution)/shard_map/ppermute | solution.py:379
  71.5 4.9 %scatter.2.refs_1_.refs_6_ = f32[4096,256]{1,0:T(8,128)S(1)} custom-call(s32[32,1,256]{2,1,0:T(1,128)S(1)} %all-to-all-done.refs_0_.refs_1_, s32[32,1,256]{2,1,0:T(1,128)S(1)} %all-to-all-done.refs_0_.refs_1_, f32[136,256]{1,0:T(8,128)S(1)} %get-tuple-element.83.refs_7_.refs_2_, f32[136,256]{1,0:T(8,128)S(1)} %collective-permute-done.23.refs_3_, ...), custom_call_target="tpu_custom_call" | custom-call | flops 8589934592 | tf_op jit(solution)/shard_map/scatter/pallas_call | solution.py:38
  76.5 1.3 %collective-permute-done.21.refs_2_ = f32[256,256]{1,0:T(8,128)S(1)} collective-permute-done((f32[256,256]{1,0:T(8,128)S(1)}, f32[256,256]{1,0:T(8,128)S(1)}, u32[]{:S(2)}, u32[]{:S(2)}) %collective-permute-start.21) | collective-permute-done | bytes 262176 | tf_op jit(solution)/shard_map/ppermute | solution.py:379
  77.8 0.8 collective-permute-start.22
  78.6 2.7 %collective-permute-start.28 = (f32[256,256]{1,0:T(8,128)S(1)}, f32[256,256]{1,0:T(8,128)S(1)}, u32[]{:S(2)}, u32[]{:S(2)}) collective-permute-start(f32[256,256]{1,0:T(8,128)S(1)} %add.14), channel_id=1, source_target_pairs={{0,4},{1,5},{2,6},{3,7},{4,0},{5,1},{6,2},{7,3},{8,12},{9,13},{10,... | collective-permute-start | bytes 786440 | tf_op jit(solution)/shard_map/ppermute | solution.py:379
  81.3 1.4 %collective-permute-start.27 = (f32[256,256]{1,0:T(8,128)S(1)}, f32[256,256]{1,0:T(8,128)S(1)}, u32[]{:S(2)}, u32[]{:S(2)}) collective-permute-start(f32[256,256]{1,0:T(8,128)S(1)} %add.12), channel_id=1, source_target_pairs={{0,1},{1,0},{2,3},{3,2},{4,5},{5,4},{6,7},{7,6},{8,9},{9,8},{10,11... | collective-permute-start | bytes 786440 | tf_op jit(solution)/shard_map/ppermute | solution.py:379
  82.7 7.0 %scatter.3 = f32[4096,256]{1,0:T(8,128)} custom-call(s32[32,1,256]{2,1,0:T(1,128)S(1)} %all-to-all-done.refs_0_.refs_1_, s32[32,1,256]{2,1,0:T(1,128)S(1)} %all-to-all-done.refs_0_.refs_1_, f32[136,256]{1,0:T(8,128)S(1)} %collective-permute-done.24.refs_2_, f32[136,256]{1,0:T(8,128)S(1)} %collective-permute-done.25.refs_3_, ...), custom_call_target="tpu_custom_call" | custom-call | tf_op jit(solution)/shard_map/scatter/pallas_call | solution.py:38
  89.9 1.0 %finish.1 = f32[256,256]{1,0:T(8,128)} custom-call(s32[1,256]{1,0:T(1,128)S(1)} %bitcast.2, f32[256,256]{1,0:T(8,128)S(1)} %collective-permute-done.22.refs_0_, f32[256,256]{1,0:T(8,128)S(1)} %collective-permute-done.27.refs_1_, f32[256,256]{1,0:T(8,128)S(1)} %add.15.refs_2_), custom_call_target="tpu_custom_call" | custom-call | tf_op jit(solution)/shard_map/finish/pallas_call | solution.py:38
  (46 shorter events, 3.2 us)
Async XLA Ops:
  1.4 1.0 %copy-start.2 = (f32[256,256]{1,0:T(8,128)S(1)}, f32[256,256]{1,0:T(8,128)}, u32[]{:S(2)}) copy-start(f32[256,256]{1,0:T(8,128)} %refs_1_.4) | copy-start | bytes 786436
  3.6 18.5 %collective-permute-start = (f32[256,256]{1,0:T(8,128)S(1)}, f32[256,256]{1,0:T(8,128)S(1)}, u32[]{:S(2)}, u32[]{:S(2)}) collective-permute-start(f32[256,256]{1,0:T(8,128)S(1)} %get-tuple-element.50.refs_4_.refs_1_.refs_8_), channel_id=1, source_target_pairs={{0,4},{1,5},{2,6},{3,7},{4,0},{5,1},{6,2},{7,3},{8,12},{9,13},{10,... | collective-permute-start | bytes 786440 | tf_op jit(solution)/shard_map/ppermute | solution.py:379
  7.6 14.5 %all-to-all-start = ((s32[32,1,256]{2,1,0:T(1,128)}), s32[32,1,256]{2,1,0:T(1,128)S(1)}, u32[]{:S(2)}, u32[]{:S(2)}) async-start(s32[32,1,256]{2,1,0:T(1,128)} %get-tuple-element.51), calls=%async_computation | async-start | bytes 65536 | tf_op jit(solution)/shard_map/all_to_all | solution.py:405
  11.4 11.9 %collective-permute-start.1 = (f32[256,256]{1,0:T(8,128)S(1)}, f32[256,256]{1,0:T(8,128)S(1)}, u32[]{:S(2)}, u32[]{:S(2)}) collective-permute-start(f32[256,256]{1,0:T(8,128)S(1)} %get-tuple-element.50.refs_4_.refs_1_.refs_8_), channel_id=1, source_target_pairs={{0,1},{1,0},{2,3},{3,2},{4,5},{5,4},{6,7},{7,6},{8,9},{9,8},{10,11... | collective-permute-start | bytes 786440 | tf_op jit(solution)/shard_map/ppermute | solution.py:379
  13.3 15.4 %collective-permute-start.8 = (f32[256,256]{1,0:T(8,128)S(1)}, f32[256,256]{1,0:T(8,128)S(1)}, u32[]{:S(2)}, u32[]{:S(2)}) collective-permute-start(f32[256,256]{1,0:T(8,128)S(1)} %get-tuple-element.50.refs_4_.refs_1_.refs_8_), channel_id=1, source_target_pairs={{0,2},{1,3},{2,0},{3,1},{4,6},{5,7},{6,4},{7,5},{8,10},{9,11},{10,... | collective-permute-start | bytes 786440 | tf_op jit(solution)/shard_map/ppermute | solution.py:379
  22.1 8.3 %collective-permute-start.6 = (f32[256,256]{1,0:T(8,128)S(1)}, f32[256,256]{1,0:T(8,128)S(1)}, u32[]{:S(2)}, u32[]{:S(2)}) collective-permute-start(f32[256,256]{1,0:T(8,128)S(1)} %collective-permute-done.refs_3_.refs_7_.refs_5_.refs_12_), channel_id=1, source_target_pairs={{0,1},{1,0},{2,3},{3,2},{4,5},{5,4},{6,7},{7,6},{8,9},{9,8},{10,11... | collective-permute-start | bytes 786440 | tf_op jit(solution)/shard_map/ppermute | solution.py:379
  22.7 10.7 %collective-permute-start.7 = (f32[256,256]{1,0:T(8,128)S(1)}, f32[256,256]{1,0:T(8,128)S(1)}, u32[]{:S(2)}, u32[]{:S(2)}) collective-permute-start(f32[256,256]{1,0:T(8,128)S(1)} %collective-permute-done.refs_3_.refs_7_.refs_5_.refs_12_), channel_id=1, source_target_pairs={{0,2},{1,3},{2,0},{3,1},{4,6},{5,7},{6,4},{7,5},{8,10},{9,11},{10,... | collective-permute-start | bytes 786440 | tf_op jit(solution)/shard_map/ppermute | solution.py:379
  23.3 2.2 %copy-start = (f32[4096,256]{1,0:T(8,128)S(1)}, f32[4096,256]{1,0:T(8,128)}, u32[]{:S(2)}) copy-start(f32[4096,256]{1,0:T(8,128)} %refs_1_.7) | copy-start | bytes 12582916
  27.8 7.1 %collective-permute-start.2 = (f32[128,256]{1,0:T(8,128)S(1)}, f32[128,256]{1,0:T(8,128)S(1)}, u32[]{:S(2)}, u32[]{:S(2)}) collective-permute-start(f32[128,256]{1,0:T(8,128)S(1)} %get-tuple-element.54), channel_id=1, source_target_pairs={{0,8},{8,0},{16,24},{24,16},{1,9},{9,1},{17,25},{25,17},{2,10},{10... | collective-permute-start | bytes 393224 | tf_op jit(solution)/shard_map/ppermute | solution.py:379
  27.9 7.6 %collective-permute-start.3 = (f32[128,256]{1,0:T(8,128)S(1)}, f32[128,256]{1,0:T(8,128)S(1)}, u32[]{:S(2)}, u32[]{:S(2)}) collective-permute-start(f32[128,256]{1,0:T(8,128)S(1)} %get-tuple-element.55), channel_id=1, source_target_pairs={{0,16},{8,24},{16,0},{24,8},{1,17},{9,25},{17,1},{25,9},{2,18},{10... | collective-permute-start | bytes 393224 | tf_op jit(solution)/shard_map/ppermute | solution.py:379
  28.7 7.5 %collective-permute-start.4 = (f32[128,256]{1,0:T(8,128)S(1)}, f32[128,256]{1,0:T(8,128)S(1)}, u32[]{:S(2)}, u32[]{:S(2)}) collective-permute-start(f32[128,256]{1,0:T(8,128)S(1)} %get-tuple-element.56), channel_id=1, source_target_pairs={{0,24},{8,16},{16,8},{24,0},{1,25},{9,17},{17,9},{25,1},{2,26},{10... | collective-permute-start | bytes 393224 | tf_op jit(solution)/shard_map/ppermute | solution.py:379
  29.7 8.9 %copy-start.1 = (f32[4096,256]{1,0:T(8,128)S(1)}, f32[4096,256]{1,0:T(8,128)}, u32[]{:S(2)}) copy-start(f32[4096,256]{1,0:T(8,128)} %refs_1_.7) | copy-start | bytes 12582916
  30.4 11.6 %collective-permute-start.5 = (f32[256,256]{1,0:T(8,128)S(1)}, f32[256,256]{1,0:T(8,128)S(1)}, u32[]{:S(2)}, u32[]{:S(2)}) collective-permute-start(f32[256,256]{1,0:T(8,128)S(1)} %collective-permute-done.1.refs_2_.refs_5_.refs_9_), channel_id=1, source_target_pairs={{0,2},{1,3},{2,0},{3,1},{4,6},{5,7},{6,4},{7,5},{8,10},{9,11},{10,... | collective-permute-start | bytes 786440 | tf_op jit(solution)/shard_map/ppermute | solution.py:379
  33.4 8.6 %collective-permute-start.9 = (f32[256,256]{1,0:T(8,128)S(1)}, f32[256,256]{1,0:T(8,128)S(1)}, u32[]{:S(2)}, u32[]{:S(2)}) collective-permute-start(f32[256,256]{1,0:T(8,128)S(1)} %collective-permute-done.7.refs_6_.refs_7_.refs_14_), channel_id=1, source_target_pairs={{0,1},{1,0},{2,3},{3,2},{4,5},{5,4},{6,7},{7,6},{8,9},{9,8},{10,11... | collective-permute-start | bytes 786440 | tf_op jit(solution)/shard_map/ppermute | solution.py:379
  34.9 13.6 %collective-permute-start.11 = (f32[256,256]{1,0:T(8,128)S(1)}, f32[256,256]{1,0:T(8,128)S(1)}, u32[]{:S(2)}, u32[]{:S(2)}) collective-permute-start(f32[256,256]{1,0:T(8,128)S(1)} %get-tuple-element.59.refs_8_), channel_id=1, source_target_pairs={{0,16},{8,24},{16,0},{24,8},{1,17},{9,25},{17,1},{25,9},{2,18},{10... | collective-permute-start | bytes 786440 | tf_op jit(solution)/shard_map/ppermute | solution.py:379
  35.5 11.8 %collective-permute-start.12 = (f32[256,256]{1,0:T(8,128)S(1)}, f32[256,256]{1,0:T(8,128)S(1)}, u32[]{:S(2)}, u32[]{:S(2)}) collective-permute-start(f32[256,256]{1,0:T(8,128)S(1)} %get-tuple-element.61.refs_9_), channel_id=1, source_target_pairs={{0,24},{8,16},{16,8},{24,0},{1,25},{9,17},{17,9},{25,1},{2,26},{10... | collective-permute-start | bytes 786440 | tf_op jit(solution)/shard_map/ppermute | solution.py:379
  41.0 7.5 %collective-permute-start.10 = (f32[256,256]{1,0:T(8,128)S(1)}, f32[256,256]{1,0:T(8,128)S(1)}, u32[]{:S(2)}, u32[]{:S(2)}) collective-permute-start(f32[256,256]{1,0:T(8,128)S(1)} %get-tuple-element.65), channel_id=1, source_target_pairs={{0,8},{8,0},{16,24},{24,16},{1,9},{9,1},{17,25},{25,17},{2,10},{10... | collective-permute-start | bytes 786440 | tf_op jit(solution)/shard_map/ppermute | solution.py:379
  45.6 18.3 %collective-permute-start.16 = (f32[256,256]{1,0:T(8,128)S(1)}, f32[256,256]{1,0:T(8,128)S(1)}, u32[]{:S(2)}, u32[]{:S(2)}) collective-permute-start(f32[256,256]{1,0:T(8,128)S(1)} %get-tuple-element.80.refs_7_), channel_id=1, source_target_pairs={{0,8},{8,0},{16,24},{24,16},{1,9},{9,1},{17,25},{25,17},{2,10},{10... | collective-permute-start | bytes 786440 | tf_op jit(solution)/shard_map/ppermute | solution.py:379
  45.7 18.2 %collective-permute-start.17 = (f32[256,256]{1,0:T(8,128)S(1)}, f32[256,256]{1,0:T(8,128)S(1)}, u32[]{:S(2)}, u32[]{:S(2)}) collective-permute-start(f32[256,256]{1,0:T(8,128)S(1)} %get-tuple-element.81.refs_8_), channel_id=1, source_target_pairs={{0,16},{8,24},{16,0},{24,8},{1,17},{9,25},{17,1},{25,9},{2,18},{10... | collective-permute-start | bytes 786440 | tf_op jit(solution)/shard_map/ppermute | solution.py:379
  47.3 16.7 %collective-permute-start.18 = (f32[256,256]{1,0:T(8,128)S(1)}, f32[256,256]{1,0:T(8,128)S(1)}, u32[]{:S(2)}, u32[]{:S(2)}) collective-permute-start(f32[256,256]{1,0:T(8,128)S(1)} %get-tuple-element.82.refs_9_), channel_id=1, source_target_pairs={{0,24},{8,16},{16,8},{24,0},{1,25},{9,17},{17,9},{25,1},{2,26},{10... | collective-permute-start | bytes 786440 | tf_op jit(solution)/shard_map/ppermute | solution.py:379
  49.2 3.8 %collective-permute-start.13 = (f32[2,2048]{1,0:T(2,128)S(1)}, f32[2,2048]{1,0:T(2,128)S(1)}, u32[]{:S(2)}, u32[]{:S(2)}) collective-permute-start(f32[2,2048]{1,0:T(2,128)S(1)} %get-tuple-element.70.first), channel_id=1, source_target_pairs={{0,1},{1,0},{2,3},{3,2},{4,5},{5,4},{6,7},{7,6},{8,9},{9,8},{10,11... | collective-permute-start | bytes 49160 | tf_op jit(solution)/shard_map/ppermute | solution.py:379
  53.0 3.8 %collective-permute-start.14 = (f32[2,2048]{1,0:T(2,128)S(1)}, f32[2,2048]{1,0:T(2,128)S(1)}, u32[]{:S(2)}, u32[]{:S(2)}) collective-permute-start(f32[2,2048]{1,0:T(2,128)S(1)} %join.3.first), channel_id=1, source_target_pairs={{0,2},{1,3},{2,0},{3,1},{4,6},{5,7},{6,4},{7,5},{8,10},{9,11},{10,... | collective-permute-start | bytes 49160 | tf_op jit(solution)/shard_map/ppermute | solution.py:379
  56.8 4.7 %collective-permute-start.15 = (f32[2,2048]{1,0:T(2,128)S(1)}, f32[2,2048]{1,0:T(2,128)S(1)}, u32[]{:S(2)}, u32[]{:S(2)}) collective-permute-start(f32[2,2048]{1,0:T(2,128)S(1)} %join.4.first), channel_id=1, source_target_pairs={{0,4},{1,5},{2,6},{3,7},{4,0},{5,1},{6,2},{7,3},{8,12},{9,13},{10,... | collective-permute-start | bytes 49160 | tf_op jit(solution)/shard_map/ppermute | solution.py:379
  61.7 6.5 %collective-permute-start.19 = (f32[256,256]{1,0:T(8,128)S(1)}, f32[256,256]{1,0:T(8,128)S(1)}, u32[]{:S(2)}, u32[]{:S(2)}) collective-permute-start(f32[256,256]{1,0:T(8,128)S(1)} %get-tuple-element.87), channel_id=1, source_target_pairs={{0,1},{1,0},{2,3},{3,2},{4,5},{5,4},{6,7},{7,6},{8,9},{9,8},{10,11... | collective-permute-start | bytes 786440 | tf_op jit(solution)/shard_map/ppermute | solution.py:379
  63.2 6.4 %collective-permute-start.20 = (f32[256,256]{1,0:T(8,128)S(1)}, f32[256,256]{1,0:T(8,128)S(1)}, u32[]{:S(2)}, u32[]{:S(2)}) collective-permute-start(f32[256,256]{1,0:T(8,128)S(1)} %get-tuple-element.88), channel_id=1, source_target_pairs={{0,2},{1,3},{2,0},{3,1},{4,6},{5,7},{6,4},{7,5},{8,10},{9,11},{10,... | collective-permute-start | bytes 786440 | tf_op jit(solution)/shard_map/ppermute | solution.py:379
  66.0 5.5 %collective-permute-start.23 = (f32[136,256]{1,0:T(8,128)S(1)}, f32[136,256]{1,0:T(8,128)S(1)}, u32[]{:S(2)}, u32[]{:S(2)}) collective-permute-start(f32[136,256]{1,0:T(8,128)S(1)} %get-tuple-element.93), channel_id=1, source_target_pairs={{0,8},{8,0},{16,24},{24,16},{1,9},{9,1},{17,25},{25,17},{2,10},{10... | collective-permute-start | bytes 417800 | tf_op jit(solution)/shard_map/ppermute | solution.py:379
  66.1 10.3 %collective-permute-start.24 = (f32[136,256]{1,0:T(8,128)S(1)}, f32[136,256]{1,0:T(8,128)S(1)}, u32[]{:S(2)}, u32[]{:S(2)}) collective-permute-start(f32[136,256]{1,0:T(8,128)S(1)} %get-tuple-element.94), channel_id=1, source_target_pairs={{0,16},{8,24},{16,0},{24,8},{1,17},{9,25},{17,1},{25,9},{2,18},{10... | collective-permute-start | bytes 417800 | tf_op jit(solution)/shard_map/ppermute | solution.py:379
  67.6 8.9 %collective-permute-start.25 = (f32[136,256]{1,0:T(8,128)S(1)}, f32[136,256]{1,0:T(8,128)S(1)}, u32[]{:S(2)}, u32[]{:S(2)}) collective-permute-start(f32[136,256]{1,0:T(8,128)S(1)} %get-tuple-element.95), channel_id=1, source_target_pairs={{0,24},{8,16},{16,8},{24,0},{1,25},{9,17},{17,9},{25,1},{2,26},{10... | collective-permute-start | bytes 417800 | tf_op jit(solution)/shard_map/ppermute | solution.py:379
  69.6 9.0 %collective-permute-start.26 = (f32[256,256]{1,0:T(8,128)S(1)}, f32[256,256]{1,0:T(8,128)S(1)}, u32[]{:S(2)}, u32[]{:S(2)}) collective-permute-start(f32[256,256]{1,0:T(8,128)S(1)} %add.11.refs_6_), channel_id=1, source_target_pairs={{0,2},{1,3},{2,0},{3,1},{4,6},{5,7},{6,4},{7,5},{8,10},{9,11},{10,... | collective-permute-start | bytes 786440 | tf_op jit(solution)/shard_map/ppermute | solution.py:379
  70.4 7.4 %collective-permute-start.21 = (f32[256,256]{1,0:T(8,128)S(1)}, f32[256,256]{1,0:T(8,128)S(1)}, u32[]{:S(2)}, u32[]{:S(2)}) collective-permute-start(f32[256,256]{1,0:T(8,128)S(1)} %get-tuple-element.89), channel_id=1, source_target_pairs={{0,1},{1,0},{2,3},{3,2},{4,5},{5,4},{6,7},{7,6},{8,9},{9,8},{10,11... | collective-permute-start | bytes 786440 | tf_op jit(solution)/shard_map/ppermute | solution.py:379
  77.8 12.1 %collective-permute-start.22 = (f32[256,256]{1,0:T(8,128)S(1)}, f32[256,256]{1,0:T(8,128)S(1)}, u32[]{:S(2)}, u32[]{:S(2)}) collective-permute-start(f32[256,256]{1,0:T(8,128)S(1)} %get-tuple-element.90), channel_id=1, source_target_pairs={{0,2},{1,3},{2,0},{3,1},{4,6},{5,7},{6,4},{7,5},{8,10},{9,11},{10,... | collective-permute-start | bytes 786440 | tf_op jit(solution)/shard_map/ppermute | solution.py:379
  78.6 11.3 %copy-start.3 = (s32[256]{0:T(256)S(1)}, s32[256]{0:T(256)}, u32[]{:S(2)}) copy-start(s32[256]{0:T(256)} %param.11) | copy-start | bytes 3076
  78.6 11.0 %collective-permute-start.28 = (f32[256,256]{1,0:T(8,128)S(1)}, f32[256,256]{1,0:T(8,128)S(1)}, u32[]{:S(2)}, u32[]{:S(2)}) collective-permute-start(f32[256,256]{1,0:T(8,128)S(1)} %add.14), channel_id=1, source_target_pairs={{0,4},{1,5},{2,6},{3,7},{4,0},{5,1},{6,2},{7,3},{8,12},{9,13},{10,... | collective-permute-start | bytes 786440 | tf_op jit(solution)/shard_map/ppermute | solution.py:379
  81.3 8.6 %collective-permute-start.27 = (f32[256,256]{1,0:T(8,128)S(1)}, f32[256,256]{1,0:T(8,128)S(1)}, u32[]{:S(2)}, u32[]{:S(2)}) collective-permute-start(f32[256,256]{1,0:T(8,128)S(1)} %add.12), channel_id=1, source_target_pairs={{0,1},{1,0},{2,3},{3,2},{4,5},{5,4},{6,7},{7,6},{8,9},{9,8},{10,11... | collective-permute-start | bytes 786440 | tf_op jit(solution)/shard_map/ppermute | solution.py:379

commit v13 on v12

--- a/solution.py
+++ b/solution.py
@@ -311,10 +311,12 @@
     return same.astype(F32)
 
 
-def scatter_kernel(members, groups, own, slots, count, info, got_v, got, *refs):
+def scatter_kernel(members, groups, own, slots, count, info, got_v, requests, *refs):
     size = len(own)
     grads, picked = refs[:size], refs[size : 2 * size]
-    out, negs, tgts = refs[-3:]
+    out, negs, tgts, got, arrived = refs[-5:]
+    copy = pltpu.make_async_copy(requests, got, arrived)
+    copy.start()
     out[...] = refs[2 * size][...] if own[0] else jnp.zeros_like(out)
 
     def add_rows(asked, first, source, base, number):
@@ -327,6 +329,7 @@
             for k in range(BATCH):
                 out[pl.ds(rows[k], 1), :] = new[k]
 
+    copy.wait()
     for i, d in enumerate(own):
         g = info[0] ^ d
         asked = got_v[pl.ds(g * members, members), 0, 0:LANES]
@@ -558,12 +561,14 @@
         return call(
             functools.partial(scatter_kernel, members, groups, own, slots, count),
             sds(rows_dev, width),
-            [SMEM, VMEM, SMEM] + [VMEM] * (2 * len(own) + len(base)) + [ANY] * len(deps),
+            [SMEM, VMEM, ANY] + [VMEM] * (2 * len(own) + len(base)) + [ANY] * len(deps),
             VMEM,
             (info, got, got, *[grads[d] for d in own], *[sent[d] for d in own], *base, *deps),
             scratch=[
                 pltpu.VMEM((members * count, width), F32),
                 pltpu.VMEM((members * slots, width), F32),
+                pltpu.SMEM(got.shape, I32),
+                pltpu.SemaphoreType.DMA,
             ],
             flops=flops,
             name="scatter",

time: 91.7 us -> 91.7 us (level)
  no operation moved by 1% of the time
where the time goes in v13:
time: 91.7 us; the launch traced here: 90.8 us
  starting transfers between devices  36 us (39%)
  Pallas kernels  32.8 us (36%)
  waiting for transfers between devices  17.3 us (19%)
  local copies, waits for them, and re-layouts  3.15 us (3%)
    pallas_call x24, Pallas kernels, call(): pl.pallas_call(kernel, out_shape=out_shape, in_specs=ins, out_specs=outs,...  32.8 us
    ppermute x29, starting transfers between devices, swap(): lax.ppermute(value, axis, [(i, i ^ d) for i in range(lax.axis_size(axis))])  32.2 us
    ppermute x29, waiting for transfers between devices, swap(): lax.ppermute(value, axis, [(i, i ^ d) for i in range(lax.axis_size(axis))])  9.89 us
    all_to_all x1, waiting for transfers between devices, shards(): lax.all_to_all(request, ('group', 'member'), split_axis=0, concat_axis=0,...  7.36 us
    all_to_all x1, starting transfers between devices, shards(): lax.all_to_all(request, ('group', 'member'), split_axis=0, concat_axis=0,...  3.82 us
    unnamed x8, local copies, waits for them, and re-layouts  3.14 us
  transfers between devices with their start and end apart: 30, of which 10 were waited for; matrix products, arithmetic and copies ran while one was open for 0% of the time, Pallas kernels for 34%

profile of v13, /device:TPU:0, one launch (start us, length us, event | category | flops | bytes accessed | tf_op | source)
XLA Modules:
  0.0 90.8 jit_solution(12798292978135542572)
XLA Ops:
  0.6 0.7 pad_add_fusion
  1.4 0.9 %copy-done.2 = f32[256,256]{1,0:T(8,128)S(1)} copy-done((f32[256,256]{1,0:T(8,128)S(1)}, f32[256,256]{1,0:T(8,128)}, u32[]{:S(2)}) %copy-start.2) | copy-done | bytes 262168
  2.3 1.2 %front.1 = (s32[32,1,256]{2,1,0:T(1,128)}, f32[256,256]{1,0:T(8,128)S(1)}) custom-call(s32[1,1280]{1,0:T(1,128)S(1)} %reshape.15.refs_0_, f32[256,256]{1,0:T(8,128)S(1)} %copy-done.2), custom_call_target="tpu_custom_call" | custom-call | tf_op jit(solution)/shard_map/front/pallas_call | solution.py:38
  3.6 4.0 %collective-permute-start = (f32[256,256]{1,0:T(8,128)S(1)}, f32[256,256]{1,0:T(8,128)S(1)}, u32[]{:S(2)}, u32[]{:S(2)}) collective-permute-start(f32[256,256]{1,0:T(8,128)S(1)} %get-tuple-element.50.refs_4_.refs_1_.refs_8_), channel_id=1, source_target_pairs={{0,4},{1,5},{2,6},{3,7},{4,0},{5,1},{6,2},{7,3},{8,12},{9,13},{10,... | collective-permute-start | bytes 786440 | tf_op jit(solution)/shard_map/ppermute | solution.py:382
  7.6 3.8 %all-to-all-start = ((s32[32,1,256]{2,1,0:T(1,128)}), s32[32,1,256]{2,1,0:T(1,128)S(1)}, u32[]{:S(2)}, u32[]{:S(2)}) async-start(s32[32,1,256]{2,1,0:T(1,128)} %get-tuple-element.51), calls=%async_computation | async-start | bytes 65536 | tf_op jit(solution)/shard_map/all_to_all | solution.py:408
  11.4 1.8 %collective-permute-start.1 = (f32[256,256]{1,0:T(8,128)S(1)}, f32[256,256]{1,0:T(8,128)S(1)}, u32[]{:S(2)}, u32[]{:S(2)}) collective-permute-start(f32[256,256]{1,0:T(8,128)S(1)} %get-tuple-element.50.refs_4_.refs_1_.refs_8_), channel_id=1, source_target_pairs={{0,1},{1,0},{2,3},{3,2},{4,5},{5,4},{6,7},{7,6},{8,9},{9,8},{10,11... | collective-permute-start | bytes 786440 | tf_op jit(solution)/shard_map/ppermute | solution.py:382
  13.3 1.5 %collective-permute-start.8 = (f32[256,256]{1,0:T(8,128)S(1)}, f32[256,256]{1,0:T(8,128)S(1)}, u32[]{:S(2)}, u32[]{:S(2)}) collective-permute-start(f32[256,256]{1,0:T(8,128)S(1)} %get-tuple-element.50.refs_4_.refs_1_.refs_8_), channel_id=1, source_target_pairs={{0,2},{1,3},{2,0},{3,1},{4,6},{5,7},{6,4},{7,5},{8,10},{9,11},{10,... | collective-permute-start | bytes 786440 | tf_op jit(solution)/shard_map/ppermute | solution.py:382
  14.7 7.4 %all-to-all-done.refs_0_.refs_1_ = s32[32,1,256]{2,1,0:T(1,128)S(1)} async-done(((s32[32,1,256]{2,1,0:T(1,128)}), s32[32,1,256]{2,1,0:T(1,128)S(1)}, u32[]{:S(2)}, u32[]{:S(2)}) %all-to-all-start) | async-done | bytes 32800 | tf_op jit(solution)/shard_map/all_to_all | solution.py:408
  22.1 0.6 collective-permute-start.6
  23.3 2.2 %copy-done = f32[4096,256]{1,0:T(8,128)S(1)} copy-done((f32[4096,256]{1,0:T(8,128)S(1)}, f32[4096,256]{1,0:T(8,128)}, u32[]{:S(2)}) %copy-start) | copy-done | bytes 4194328
  25.5 2.3 %gather_negatives.1 = (f32[128,256]{1,0:T(8,128)S(1)}, f32[128,256]{1,0:T(8,128)S(1)}, f32[128,256]{1,0:T(8,128)S(1)}, f32[128,256]{1,0:T(8,128)S(1)}) custom-call(s32[32,1,256]{2,1,0:T(1,128)S(1)} %all-to-all-done.refs_0_.refs_1_, f32[4096,256]{1,0:T(8,128)S(1)} %copy-done, f32[256,256]{1,0:T(8,128)S(1)} %collective-permute-done.1.refs_2_.refs_5_.refs_9_, ...), custom_call_target="tpu_custom_call" | custom-call | tf_op jit(solution)/shard_map/gather_negatives/pallas_call | solution.py:38
  27.9 0.8 collective-permute-start.3
  28.7 1.1 %collective-permute-start.4 = (f32[128,256]{1,0:T(8,128)S(1)}, f32[128,256]{1,0:T(8,128)S(1)}, u32[]{:S(2)}, u32[]{:S(2)}) collective-permute-start(f32[128,256]{1,0:T(8,128)S(1)} %get-tuple-element.56), channel_id=1, source_target_pairs={{0,24},{8,16},{16,8},{24,0},{1,25},{9,17},{17,9},{25,1},{2,26},{10... | collective-permute-start | bytes 393224 | tf_op jit(solution)/shard_map/ppermute | solution.py:382
  29.7 0.7 collective-permute-done.6.refs_3_.refs_5_.refs_6_.refs_13_
  30.4 0.8 collective-permute-start.5
  31.2 2.2 %gather_far_targets.1 = (f32[256,256]{1,0:T(8,128)S(1)}, f32[256,256]{1,0:T(8,128)S(1)}) custom-call(s32[32,1,256]{2,1,0:T(1,128)S(1)} %all-to-all-done.refs_0_.refs_1_, f32[4096,256]{1,0:T(8,128)S(1)} %copy-done, f32[256,256]{1,0:T(8,128)S(1)} %collective-permute-done.8.refs_2_.refs_6_.refs_3_.refs_10_, ...), custom_call_target="tpu_custom_call" | custom-call | tf_op jit(solution)/shard_map/gather_far_targets/pallas_call | solution.py:38
  33.4 1.5 %collective-permute-start.9 = (f32[256,256]{1,0:T(8,128)S(1)}, f32[256,256]{1,0:T(8,128)S(1)}, u32[]{:S(2)}, u32[]{:S(2)}) collective-permute-start(f32[256,256]{1,0:T(8,128)S(1)} %collective-permute-done.7.refs_6_.refs_7_.refs_14_), channel_id=1, source_target_pairs={{0,1},{1,0},{2,3},{3,2},{4,5},{5,4},{6,7},{7,6},{8,9},{9,8},{10,11... | collective-permute-start | bytes 786440 | tf_op jit(solution)/shard_map/ppermute | solution.py:382
  36.1 2.5 %score.2 = (f32[2,2048]{1,0:T(2,128)S(1)}, bf16[4,512,256]{2,1,0:T(8,128)(2,1)S(1)}, bf16[4,512,256]{2,1,0:T(8,128)(2,1)S(1)}) custom-call(f32[128,256]{1,0:T(8,128)S(1)} %get-tuple-element.53.refs_0_.refs_1_, f32[128,256]{1,0:T(8,128)S(1)} %collective-permute-done.2.refs_1_.refs_2_, f32[128,256]{1,0:T(8,128)S(1)} %collective-permute-done.3.refs_2_.refs_3_, ...), custom_call_target="tpu_custom_call" | custom-call | flops 1610612736 | bytes 1048576 | tf_op jit(solution)/shard_map/score/pallas_call | solution.py:38
  38.7 2.4 %gather_targets.1 = (f32[256,256]{1,0:T(8,128)S(1)}, f32[256,256]{1,0:T(8,128)S(1)}) custom-call(s32[32,1,256]{2,1,0:T(1,128)S(1)} %all-to-all-done.refs_0_.refs_1_, f32[4096,256]{1,0:T(8,128)S(1)} %copy-done.1, f32[2,2048]{1,0:T(2,128)S(1)} %get-tuple-element.62.refs_8_.refs_2_), custom_call_target="tpu_custom_call" | custom-call | tf_op jit(solution)/shard_map/gather_targets/pallas_call | solution.py:38
  41.0 0.9 %collective-permute-start.10 = (f32[256,256]{1,0:T(8,128)S(1)}, f32[256,256]{1,0:T(8,128)S(1)}, u32[]{:S(2)}, u32[]{:S(2)}) collective-permute-start(f32[256,256]{1,0:T(8,128)S(1)} %get-tuple-element.65), channel_id=1, source_target_pairs={{0,8},{8,0},{16,24},{24,16},{1,9},{9,1},{17,25},{25,17},{2,10},{10... | collective-permute-start | bytes 786440 | tf_op jit(solution)/shard_map/ppermute | solution.py:382
  42.0 1.1 %pick.1 = (f32[256,256]{1,0:T(8,128)S(1)}, f32[256,256]{1,0:T(8,128)S(1)}, f32[256,256]{1,0:T(8,128)S(1)}, f32[256,256]{1,0:T(8,128)S(1)}) custom-call(s32[32,1,256]{2,1,0:T(1,128)S(1)} %all-to-all-done.refs_0_.refs_1_, f32[256,256]{1,0:T(8,128)S(1)} %get-tuple-element.50.refs_4_.refs_1_.refs_8_, ...), custom_call_target="tpu_custom_call" | custom-call | tf_op jit(solution)/shard_map/pick/pallas_call | solution.py:38
  43.1 2.5 %score.3 = (f32[2,2048]{1,0:T(2,128)S(1)}, bf16[4,512,256]{2,1,0:T(8,128)(2,1)S(1)}, bf16[4,512,256]{2,1,0:T(8,128)(2,1)S(1)}) custom-call(f32[128,256]{1,0:T(8,128)S(1)} %get-tuple-element.53.refs_0_.refs_1_, f32[128,256]{1,0:T(8,128)S(1)} %collective-permute-done.2.refs_1_.refs_2_, f32[128,256]{1,0:T(8,128)S(1)} %collective-permute-done.3.refs_2_.refs_3_, ...), custom_call_target="tpu_custom_call" | custom-call | flops 1610612736 | bytes 1048576 | tf_op jit(solution)/shard_map/score/pallas_call | solution.py:38
  45.7 0.6 collective-permute-start.17
  46.3 0.9 %collective-permute-done.12.refs_5_.refs_8_ = f32[256,256]{1,0:T(8,128)S(1)} collective-permute-done((f32[256,256]{1,0:T(8,128)S(1)}, f32[256,256]{1,0:T(8,128)S(1)}, u32[]{:S(2)}, u32[]{:S(2)}) %collective-permute-start.12) | collective-permute-done | bytes 262176 | tf_op jit(solution)/shard_map/ppermute | solution.py:382
  47.3 1.2 %collective-permute-start.18 = (f32[256,256]{1,0:T(8,128)S(1)}, f32[256,256]{1,0:T(8,128)S(1)}, u32[]{:S(2)}, u32[]{:S(2)}) collective-permute-start(f32[256,256]{1,0:T(8,128)S(1)} %get-tuple-element.82.refs_9_), channel_id=1, source_target_pairs={{0,24},{8,16},{16,8},{24,0},{1,25},{9,17},{17,9},{25,1},{2,26},{10... | collective-permute-start | bytes 786440 | tf_op jit(solution)/shard_map/ppermute | solution.py:382
  48.5 0.7 positive.1
  49.2 0.8 collective-permute-start.13
  50.0 1.5 %pulled.2 = (f32[4,256,256]{2,1,0:T(8,128)S(1)}, f32[4,256,256]{2,1,0:T(8,128)S(1)}) custom-call(s32[32,1,256]{2,1,0:T(1,128)S(1)} %all-to-all-done.refs_0_.refs_1_, f32[128,256]{1,0:T(8,128)S(1)} %get-tuple-element.53.refs_0_.refs_1_, f32[128,256]{1,0:T(8,128)S(1)} %collective-permute-done.2.refs_1_.refs_2_, ...), custom_call_target="tpu_custom_call" | custom-call | flops 805306368 | bytes 1048576 | tf_op jit(solution)/shard_map/pulled/pallas_call | solution.py:38
  51.5 1.5 %collective-permute-done.13.second = f32[2,2048]{1,0:T(2,128)S(1)} collective-permute-done((f32[2,2048]{1,0:T(2,128)S(1)}, f32[2,2048]{1,0:T(2,128)S(1)}, u32[]{:S(2)}, u32[]{:S(2)}) %collective-permute-start.13) | collective-permute-done | bytes 16416 | tf_op jit(solution)/shard_map/ppermute | solution.py:382
  53.0 0.9 collective-permute-start.14
  53.9 1.5 %pulled.3 = (f32[4,256,256]{2,1,0:T(8,128)S(1)}, f32[4,256,256]{2,1,0:T(8,128)S(1)}) custom-call(s32[32,1,256]{2,1,0:T(1,128)S(1)} %all-to-all-done.refs_0_.refs_1_, f32[128,256]{1,0:T(8,128)S(1)} %get-tuple-element.53.refs_0_.refs_1_, f32[128,256]{1,0:T(8,128)S(1)} %collective-permute-done.2.refs_1_.refs_2_, ...), custom_call_target="tpu_custom_call" | custom-call | flops 805306368 | bytes 1048576 | tf_op jit(solution)/shard_map/pulled/pallas_call | solution.py:38
  55.3 1.5 %collective-permute-done.14.second = f32[2,2048]{1,0:T(2,128)S(1)} collective-permute-done((f32[2,2048]{1,0:T(2,128)S(1)}, f32[2,2048]{1,0:T(2,128)S(1)}, u32[]{:S(2)}, u32[]{:S(2)}) %collective-permute-start.14) | collective-permute-done | bytes 16416 | tf_op jit(solution)/shard_map/ppermute | solution.py:382
  56.8 2.8 %collective-permute-start.15 = (f32[2,2048]{1,0:T(2,128)S(1)}, f32[2,2048]{1,0:T(2,128)S(1)}, u32[]{:S(2)}, u32[]{:S(2)}) collective-permute-start(f32[2,2048]{1,0:T(2,128)S(1)} %join.4.first), channel_id=1, source_target_pairs={{0,4},{1,5},{2,6},{3,7},{4,0},{5,1},{6,2},{7,3},{8,12},{9,13},{10,... | collective-permute-start | bytes 49160 | tf_op jit(solution)/shard_map/ppermute | solution.py:382
  59.7 1.9 %collective-permute-done.15.second = f32[2,2048]{1,0:T(2,128)S(1)} collective-permute-done((f32[2,2048]{1,0:T(2,128)S(1)}, f32[2,2048]{1,0:T(2,128)S(1)}, u32[]{:S(2)}, u32[]{:S(2)}) %collective-permute-start.15) | collective-permute-done | bytes 16416 | tf_op jit(solution)/shard_map/ppermute | solution.py:382
  61.7 1.5 %collective-permute-start.19 = (f32[256,256]{1,0:T(8,128)S(1)}, f32[256,256]{1,0:T(8,128)S(1)}, u32[]{:S(2)}, u32[]{:S(2)}) collective-permute-start(f32[256,256]{1,0:T(8,128)S(1)} %get-tuple-element.87), channel_id=1, source_target_pairs={{0,1},{1,0},{2,3},{3,2},{4,5},{5,4},{6,7},{7,6},{8,9},{9,8},{10,11... | collective-permute-start | bytes 786440 | tf_op jit(solution)/shard_map/ppermute | solution.py:382
  63.2 0.8 collective-permute-start.20
  64.0 2.0 %grad.1 = (f32[136,256]{1,0:T(8,128)S(1)}, f32[136,256]{1,0:T(8,128)S(1)}, f32[136,256]{1,0:T(8,128)S(1)}, f32[136,256]{1,0:T(8,128)S(1)}) custom-call(s32[32,1,256]{2,1,0:T(1,128)S(1)} %all-to-all-done.refs_0_.refs_1_, f32[2,2048]{1,0:T(2,128)S(1)} %join.5.refs_1_.refs_0_, f32[2,2048]{1,0:T(2,128)S(1)} %get-tuple-element.63.refs_1_.refs_2_, ...), custom_call_target="tpu_custom_call" | custom-call | flops 1610612736 | bytes 8388608 | tf_op jit(solution)/shard_map/grad/pallas_call | solution.py:38
  66.1 1.5 %collective-permute-start.24 = (f32[136,256]{1,0:T(8,128)S(1)}, f32[136,256]{1,0:T(8,128)S(1)}, u32[]{:S(2)}, u32[]{:S(2)}) collective-permute-start(f32[136,256]{1,0:T(8,128)S(1)} %get-tuple-element.94), channel_id=1, source_target_pairs={{0,16},{8,24},{16,0},{24,8},{1,17},{9,25},{17,1},{25,9},{2,18},{10... | collective-permute-start | bytes 417800 | tf_op jit(solution)/shard_map/ppermute | solution.py:382
  68.1 1.4 %collective-permute-done.20.refs_3_.refs_1_ = f32[256,256]{1,0:T(8,128)S(1)} collective-permute-done((f32[256,256]{1,0:T(8,128)S(1)}, f32[256,256]{1,0:T(8,128)S(1)}, u32[]{:S(2)}, u32[]{:S(2)}) %collective-permute-start.20) | collective-permute-done | bytes 262176 | tf_op jit(solution)/shard_map/ppermute | solution.py:382
  69.6 0.8 collective-permute-start.26
  70.4 1.0 %collective-permute-start.21 = (f32[256,256]{1,0:T(8,128)S(1)}, f32[256,256]{1,0:T(8,128)S(1)}, u32[]{:S(2)}, u32[]{:S(2)}) collective-permute-start(f32[256,256]{1,0:T(8,128)S(1)} %get-tuple-element.89), channel_id=1, source_target_pairs={{0,1},{1,0},{2,3},{3,2},{4,5},{5,4},{6,7},{7,6},{8,9},{9,8},{10,11... | collective-permute-start | bytes 786440 | tf_op jit(solution)/shard_map/ppermute | solution.py:382
  71.5 4.8 %scatter.2.refs_1_.refs_6_ = f32[4096,256]{1,0:T(8,128)S(1)} custom-call(s32[32,1,256]{2,1,0:T(1,128)S(1)} %all-to-all-done.refs_0_.refs_1_, s32[32,1,256]{2,1,0:T(1,128)S(1)} %all-to-all-done.refs_0_.refs_1_, f32[136,256]{1,0:T(8,128)S(1)} %get-tuple-element.83.refs_7_.refs_2_, f32[136,256]{1,0:T(8,128)S(1)} %collective-permute-done.23.refs_3_, ...), custom_call_target="tpu_custom_call" | custom-call | flops 8589934592 | tf_op jit(solution)/shard_map/scatter/pallas_call | solution.py:38
  76.3 1.5 %collective-permute-done.21.refs_2_ = f32[256,256]{1,0:T(8,128)S(1)} collective-permute-done((f32[256,256]{1,0:T(8,128)S(1)}, f32[256,256]{1,0:T(8,128)S(1)}, u32[]{:S(2)}, u32[]{:S(2)}) %collective-permute-start.21) | collective-permute-done | bytes 262176 | tf_op jit(solution)/shard_map/ppermute | solution.py:382
  77.8 0.8 collective-permute-start.22
  78.6 2.7 %collective-permute-start.28 = (f32[256,256]{1,0:T(8,128)S(1)}, f32[256,256]{1,0:T(8,128)S(1)}, u32[]{:S(2)}, u32[]{:S(2)}) collective-permute-start(f32[256,256]{1,0:T(8,128)S(1)} %add.14), channel_id=1, source_target_pairs={{0,4},{1,5},{2,6},{3,7},{4,0},{5,1},{6,2},{7,3},{8,12},{9,13},{10,... | collective-permute-start | bytes 786440 | tf_op jit(solution)/shard_map/ppermute | solution.py:382
  81.3 1.4 %collective-permute-start.27 = (f32[256,256]{1,0:T(8,128)S(1)}, f32[256,256]{1,0:T(8,128)S(1)}, u32[]{:S(2)}, u32[]{:S(2)}) collective-permute-start(f32[256,256]{1,0:T(8,128)S(1)} %add.12), channel_id=1, source_target_pairs={{0,1},{1,0},{2,3},{3,2},{4,5},{5,4},{6,7},{7,6},{8,9},{9,8},{10,11... | collective-permute-start | bytes 786440 | tf_op jit(solution)/shard_map/ppermute | solution.py:382
  82.7 6.8 %scatter.3 = f32[4096,256]{1,0:T(8,128)} custom-call(s32[32,1,256]{2,1,0:T(1,128)S(1)} %all-to-all-done.refs_0_.refs_1_, s32[32,1,256]{2,1,0:T(1,128)S(1)} %all-to-all-done.refs_0_.refs_1_, f32[136,256]{1,0:T(8,128)S(1)} %collective-permute-done.24.refs_2_, f32[136,256]{1,0:T(8,128)S(1)} %collective-permute-done.25.refs_3_, ...), custom_call_target="tpu_custom_call" | custom-call | tf_op jit(solution)/shard_map/scatter/pallas_call | solution.py:38
  89.9 1.0 %finish.1 = f32[256,256]{1,0:T(8,128)} custom-call(s32[1,256]{1,0:T(1,128)S(1)} %bitcast.2, f32[256,256]{1,0:T(8,128)S(1)} %collective-permute-done.22.refs_0_, f32[256,256]{1,0:T(8,128)S(1)} %collective-permute-done.27.refs_1_, f32[256,256]{1,0:T(8,128)S(1)} %add.15.refs_2_), custom_call_target="tpu_custom_call" | custom-call | tf_op jit(solution)/shard_map/finish/pallas_call | solution.py:38
  (46 shorter events, 3.4 us)
Async XLA Ops:
  1.4 1.0 %copy-start.2 = (f32[256,256]{1,0:T(8,128)S(1)}, f32[256,256]{1,0:T(8,128)}, u32[]{:S(2)}) copy-start(f32[256,256]{1,0:T(8,128)} %refs_1_.4) | copy-start | bytes 786436
  3.6 18.5 %collective-permute-start = (f32[256,256]{1,0:T(8,128)S(1)}, f32[256,256]{1,0:T(8,128)S(1)}, u32[]{:S(2)}, u32[]{:S(2)}) collective-permute-start(f32[256,256]{1,0:T(8,128)S(1)} %get-tuple-element.50.refs_4_.refs_1_.refs_8_), channel_id=1, source_target_pairs={{0,4},{1,5},{2,6},{3,7},{4,0},{5,1},{6,2},{7,3},{8,12},{9,13},{10,... | collective-permute-start | bytes 786440 | tf_op jit(solution)/shard_map/ppermute | solution.py:382
  7.6 14.5 %all-to-all-start = ((s32[32,1,256]{2,1,0:T(1,128)}), s32[32,1,256]{2,1,0:T(1,128)S(1)}, u32[]{:S(2)}, u32[]{:S(2)}) async-start(s32[32,1,256]{2,1,0:T(1,128)} %get-tuple-element.51), calls=%async_computation | async-start | bytes 65536 | tf_op jit(solution)/shard_map/all_to_all | solution.py:408
  11.4 11.9 %collective-permute-start.1 = (f32[256,256]{1,0:T(8,128)S(1)}, f32[256,256]{1,0:T(8,128)S(1)}, u32[]{:S(2)}, u32[]{:S(2)}) collective-permute-start(f32[256,256]{1,0:T(8,128)S(1)} %get-tuple-element.50.refs_4_.refs_1_.refs_8_), channel_id=1, source_target_pairs={{0,1},{1,0},{2,3},{3,2},{4,5},{5,4},{6,7},{7,6},{8,9},{9,8},{10,11... | collective-permute-start | bytes 786440 | tf_op jit(solution)/shard_map/ppermute | solution.py:382
  13.3 15.4 %collective-permute-start.8 = (f32[256,256]{1,0:T(8,128)S(1)}, f32[256,256]{1,0:T(8,128)S(1)}, u32[]{:S(2)}, u32[]{:S(2)}) collective-permute-start(f32[256,256]{1,0:T(8,128)S(1)} %get-tuple-element.50.refs_4_.refs_1_.refs_8_), channel_id=1, source_target_pairs={{0,2},{1,3},{2,0},{3,1},{4,6},{5,7},{6,4},{7,5},{8,10},{9,11},{10,... | collective-permute-start | bytes 786440 | tf_op jit(solution)/shard_map/ppermute | solution.py:382
  22.1 8.3 %collective-permute-start.6 = (f32[256,256]{1,0:T(8,128)S(1)}, f32[256,256]{1,0:T(8,128)S(1)}, u32[]{:S(2)}, u32[]{:S(2)}) collective-permute-start(f32[256,256]{1,0:T(8,128)S(1)} %collective-permute-done.refs_3_.refs_7_.refs_5_.refs_12_), channel_id=1, source_target_pairs={{0,1},{1,0},{2,3},{3,2},{4,5},{5,4},{6,7},{7,6},{8,9},{9,8},{10,11... | collective-permute-start | bytes 786440 | tf_op jit(solution)/shard_map/ppermute | solution.py:382
  22.7 10.7 %collective-permute-start.7 = (f32[256,256]{1,0:T(8,128)S(1)}, f32[256,256]{1,0:T(8,128)S(1)}, u32[]{:S(2)}, u32[]{:S(2)}) collective-permute-start(f32[256,256]{1,0:T(8,128)S(1)} %collective-permute-done.refs_3_.refs_7_.refs_5_.refs_12_), channel_id=1, source_target_pairs={{0,2},{1,3},{2,0},{3,1},{4,6},{5,7},{6,4},{7,5},{8,10},{9,11},{10,... | collective-permute-start | bytes 786440 | tf_op jit(solution)/shard_map/ppermute | solution.py:382
  23.3 2.2 %copy-start = (f32[4096,256]{1,0:T(8,128)S(1)}, f32[4096,256]{1,0:T(8,128)}, u32[]{:S(2)}) copy-start(f32[4096,256]{1,0:T(8,128)} %refs_1_.7) | copy-start | bytes 12582916
  27.8 7.1 %collective-permute-start.2 = (f32[128,256]{1,0:T(8,128)S(1)}, f32[128,256]{1,0:T(8,128)S(1)}, u32[]{:S(2)}, u32[]{:S(2)}) collective-permute-start(f32[128,256]{1,0:T(8,128)S(1)} %get-tuple-element.54), channel_id=1, source_target_pairs={{0,8},{8,0},{16,24},{24,16},{1,9},{9,1},{17,25},{25,17},{2,10},{10... | collective-permute-start | bytes 393224 | tf_op jit(solution)/shard_map/ppermute | solution.py:382
  27.9 7.6 %collective-permute-start.3 = (f32[128,256]{1,0:T(8,128)S(1)}, f32[128,256]{1,0:T(8,128)S(1)}, u32[]{:S(2)}, u32[]{:S(2)}) collective-permute-start(f32[128,256]{1,0:T(8,128)S(1)} %get-tuple-element.55), channel_id=1, source_target_pairs={{0,16},{8,24},{16,0},{24,8},{1,17},{9,25},{17,1},{25,9},{2,18},{10... | collective-permute-start | bytes 393224 | tf_op jit(solution)/shard_map/ppermute | solution.py:382
  28.7 7.5 %collective-permute-start.4 = (f32[128,256]{1,0:T(8,128)S(1)}, f32[128,256]{1,0:T(8,128)S(1)}, u32[]{:S(2)}, u32[]{:S(2)}) collective-permute-start(f32[128,256]{1,0:T(8,128)S(1)} %get-tuple-element.56), channel_id=1, source_target_pairs={{0,24},{8,16},{16,8},{24,0},{1,25},{9,17},{17,9},{25,1},{2,26},{10... | collective-permute-start | bytes 393224 | tf_op jit(solution)/shard_map/ppermute | solution.py:382
  29.7 8.9 %copy-start.1 = (f32[4096,256]{1,0:T(8,128)S(1)}, f32[4096,256]{1,0:T(8,128)}, u32[]{:S(2)}) copy-start(f32[4096,256]{1,0:T(8,128)} %refs_1_.7) | copy-start | bytes 12582916
  30.4 11.6 %collective-permute-start.5 = (f32[256,256]{1,0:T(8,128)S(1)}, f32[256,256]{1,0:T(8,128)S(1)}, u32[]{:S(2)}, u32[]{:S(2)}) collective-permute-start(f32[256,256]{1,0:T(8,128)S(1)} %collective-permute-done.1.refs_2_.refs_5_.refs_9_), channel_id=1, source_target_pairs={{0,2},{1,3},{2,0},{3,1},{4,6},{5,7},{6,4},{7,5},{8,10},{9,11},{10,... | collective-permute-start | bytes 786440 | tf_op jit(solution)/shard_map/ppermute | solution.py:382
  33.4 8.6 %collective-permute-start.9 = (f32[256,256]{1,0:T(8,128)S(1)}, f32[256,256]{1,0:T(8,128)S(1)}, u32[]{:S(2)}, u32[]{:S(2)}) collective-permute-start(f32[256,256]{1,0:T(8,128)S(1)} %collective-permute-done.7.refs_6_.refs_7_.refs_14_), channel_id=1, source_target_pairs={{0,1},{1,0},{2,3},{3,2},{4,5},{5,4},{6,7},{7,6},{8,9},{9,8},{10,11... | collective-permute-start | bytes 786440 | tf_op jit(solution)/shard_map/ppermute | solution.py:382
  34.9 13.6 %collective-permute-start.11 = (f32[256,256]{1,0:T(8,128)S(1)}, f32[256,256]{1,0:T(8,128)S(1)}, u32[]{:S(2)}, u32[]{:S(2)}) collective-permute-start(f32[256,256]{1,0:T(8,128)S(1)} %get-tuple-element.59.refs_8_), channel_id=1, source_target_pairs={{0,16},{8,24},{16,0},{24,8},{1,17},{9,25},{17,1},{25,9},{2,18},{10... | collective-permute-start | bytes 786440 | tf_op jit(solution)/shard_map/ppermute | solution.py:382
  35.5 11.8 %collective-permute-start.12 = (f32[256,256]{1,0:T(8,128)S(1)}, f32[256,256]{1,0:T(8,128)S(1)}, u32[]{:S(2)}, u32[]{:S(2)}) collective-permute-start(f32[256,256]{1,0:T(8,128)S(1)} %get-tuple-element.61.refs_9_), channel_id=1, source_target_pairs={{0,24},{8,16},{16,8},{24,0},{1,25},{9,17},{17,9},{25,1},{2,26},{10... | collective-permute-start | bytes 786440 | tf_op jit(solution)/shard_map/ppermute | solution.py:382
  41.0 7.5 %collective-permute-start.10 = (f32[256,256]{1,0:T(8,128)S(1)}, f32[256,256]{1,0:T(8,128)S(1)}, u32[]{:S(2)}, u32[]{:S(2)}) collective-permute-start(f32[256,256]{1,0:T(8,128)S(1)} %get-tuple-element.65), channel_id=1, source_target_pairs={{0,8},{8,0},{16,24},{24,16},{1,9},{9,1},{17,25},{25,17},{2,10},{10... | collective-permute-start | bytes 786440 | tf_op jit(solution)/shard_map/ppermute | solution.py:382
  45.6 18.3 %collective-permute-start.16 = (f32[256,256]{1,0:T(8,128)S(1)}, f32[256,256]{1,0:T(8,128)S(1)}, u32[]{:S(2)}, u32[]{:S(2)}) collective-permute-start(f32[256,256]{1,0:T(8,128)S(1)} %get-tuple-element.80.refs_7_), channel_id=1, source_target_pairs={{0,8},{8,0},{16,24},{24,16},{1,9},{9,1},{17,25},{25,17},{2,10},{10... | collective-permute-start | bytes 786440 | tf_op jit(solution)/shard_map/ppermute | solution.py:382
  45.7 18.2 %collective-permute-start.17 = (f32[256,256]{1,0:T(8,128)S(1)}, f32[256,256]{1,0:T(8,128)S(1)}, u32[]{:S(2)}, u32[]{:S(2)}) collective-permute-start(f32[256,256]{1,0:T(8,128)S(1)} %get-tuple-element.81.refs_8_), channel_id=1, source_target_pairs={{0,16},{8,24},{16,0},{24,8},{1,17},{9,25},{17,1},{25,9},{2,18},{10... | collective-permute-start | bytes 786440 | tf_op jit(solution)/shard_map/ppermute | solution.py:382
  47.3 16.7 %collective-permute-start.18 = (f32[256,256]{1,0:T(8,128)S(1)}, f32[256,256]{1,0:T(8,128)S(1)}, u32[]{:S(2)}, u32[]{:S(2)}) collective-permute-start(f32[256,256]{1,0:T(8,128)S(1)} %get-tuple-element.82.refs_9_), channel_id=1, source_target_pairs={{0,24},{8,16},{16,8},{24,0},{1,25},{9,17},{17,9},{25,1},{2,26},{10... | collective-permute-start | bytes 786440 | tf_op jit(solution)/shard_map/ppermute | solution.py:382
  49.2 3.8 %collective-permute-start.13 = (f32[2,2048]{1,0:T(2,128)S(1)}, f32[2,2048]{1,0:T(2,128)S(1)}, u32[]{:S(2)}, u32[]{:S(2)}) collective-permute-start(f32[2,2048]{1,0:T(2,128)S(1)} %get-tuple-element.70.first), channel_id=1, source_target_pairs={{0,1},{1,0},{2,3},{3,2},{4,5},{5,4},{6,7},{7,6},{8,9},{9,8},{10,11... | collective-permute-start | bytes 49160 | tf_op jit(solution)/shard_map/ppermute | solution.py:382
  53.0 3.8 %collective-permute-start.14 = (f32[2,2048]{1,0:T(2,128)S(1)}, f32[2,2048]{1,0:T(2,128)S(1)}, u32[]{:S(2)}, u32[]{:S(2)}) collective-permute-start(f32[2,2048]{1,0:T(2,128)S(1)} %join.3.first), channel_id=1, source_target_pairs={{0,2},{1,3},{2,0},{3,1},{4,6},{5,7},{6,4},{7,5},{8,10},{9,11},{10,... | collective-permute-start | bytes 49160 | tf_op jit(solution)/shard_map/ppermute | solution.py:382
  56.8 4.7 %collective-permute-start.15 = (f32[2,2048]{1,0:T(2,128)S(1)}, f32[2,2048]{1,0:T(2,128)S(1)}, u32[]{:S(2)}, u32[]{:S(2)}) collective-permute-start(f32[2,2048]{1,0:T(2,128)S(1)} %join.4.first), channel_id=1, source_target_pairs={{0,4},{1,5},{2,6},{3,7},{4,0},{5,1},{6,2},{7,3},{8,12},{9,13},{10,... | collective-permute-start | bytes 49160 | tf_op jit(solution)/shard_map/ppermute | solution.py:382
  61.7 6.5 %collective-permute-start.19 = (f32[256,256]{1,0:T(8,128)S(1)}, f32[256,256]{1,0:T(8,128)S(1)}, u32[]{:S(2)}, u32[]{:S(2)}) collective-permute-start(f32[256,256]{1,0:T(8,128)S(1)} %get-tuple-element.87), channel_id=1, source_target_pairs={{0,1},{1,0},{2,3},{3,2},{4,5},{5,4},{6,7},{7,6},{8,9},{9,8},{10,11... | collective-permute-start | bytes 786440 | tf_op jit(solution)/shard_map/ppermute | solution.py:382
  63.2 6.4 %collective-permute-start.20 = (f32[256,256]{1,0:T(8,128)S(1)}, f32[256,256]{1,0:T(8,128)S(1)}, u32[]{:S(2)}, u32[]{:S(2)}) collective-permute-start(f32[256,256]{1,0:T(8,128)S(1)} %get-tuple-element.88), channel_id=1, source_target_pairs={{0,2},{1,3},{2,0},{3,1},{4,6},{5,7},{6,4},{7,5},{8,10},{9,11},{10,... | collective-permute-start | bytes 786440 | tf_op jit(solution)/shard_map/ppermute | solution.py:382
  66.0 5.5 %collective-permute-start.23 = (f32[136,256]{1,0:T(8,128)S(1)}, f32[136,256]{1,0:T(8,128)S(1)}, u32[]{:S(2)}, u32[]{:S(2)}) collective-permute-start(f32[136,256]{1,0:T(8,128)S(1)} %get-tuple-element.93), channel_id=1, source_target_pairs={{0,8},{8,0},{16,24},{24,16},{1,9},{9,1},{17,25},{25,17},{2,10},{10... | collective-permute-start | bytes 417800 | tf_op jit(solution)/shard_map/ppermute | solution.py:382
  66.1 10.2 %collective-permute-start.24 = (f32[136,256]{1,0:T(8,128)S(1)}, f32[136,256]{1,0:T(8,128)S(1)}, u32[]{:S(2)}, u32[]{:S(2)}) collective-permute-start(f32[136,256]{1,0:T(8,128)S(1)} %get-tuple-element.94), channel_id=1, source_target_pairs={{0,16},{8,24},{16,0},{24,8},{1,17},{9,25},{17,1},{25,9},{2,18},{10... | collective-permute-start | bytes 417800 | tf_op jit(solution)/shard_map/ppermute | solution.py:382
  67.6 8.7 %collective-permute-start.25 = (f32[136,256]{1,0:T(8,128)S(1)}, f32[136,256]{1,0:T(8,128)S(1)}, u32[]{:S(2)}, u32[]{:S(2)}) collective-permute-start(f32[136,256]{1,0:T(8,128)S(1)} %get-tuple-element.95), channel_id=1, source_target_pairs={{0,24},{8,16},{16,8},{24,0},{1,25},{9,17},{17,9},{25,1},{2,26},{10... | collective-permute-start | bytes 417800 | tf_op jit(solution)/shard_map/ppermute | solution.py:382
  69.6 9.0 %collective-permute-start.26 = (f32[256,256]{1,0:T(8,128)S(1)}, f32[256,256]{1,0:T(8,128)S(1)}, u32[]{:S(2)}, u32[]{:S(2)}) collective-permute-start(f32[256,256]{1,0:T(8,128)S(1)} %add.11.refs_6_), channel_id=1, source_target_pairs={{0,2},{1,3},{2,0},{3,1},{4,6},{5,7},{6,4},{7,5},{8,10},{9,11},{10,... | collective-permute-start | bytes 786440 | tf_op jit(solution)/shard_map/ppermute | solution.py:382
  70.4 7.4 %collective-permute-start.21 = (f32[256,256]{1,0:T(8,128)S(1)}, f32[256,256]{1,0:T(8,128)S(1)}, u32[]{:S(2)}, u32[]{:S(2)}) collective-permute-start(f32[256,256]{1,0:T(8,128)S(1)} %get-tuple-element.89), channel_id=1, source_target_pairs={{0,1},{1,0},{2,3},{3,2},{4,5},{5,4},{6,7},{7,6},{8,9},{9,8},{10,11... | collective-permute-start | bytes 786440 | tf_op jit(solution)/shard_map/ppermute | solution.py:382
  77.8 12.1 %collective-permute-start.22 = (f32[256,256]{1,0:T(8,128)S(1)}, f32[256,256]{1,0:T(8,128)S(1)}, u32[]{:S(2)}, u32[]{:S(2)}) collective-permute-start(f32[256,256]{1,0:T(8,128)S(1)} %get-tuple-element.90), channel_id=1, source_target_pairs={{0,2},{1,3},{2,0},{3,1},{4,6},{5,7},{6,4},{7,5},{8,10},{9,11},{10,... | collective-permute-start | bytes 786440 | tf_op jit(solution)/shard_map/ppermute | solution.py:382
  78.6 11.3 %copy-start.3 = (s32[256]{0:T(256)S(1)}, s32[256]{0:T(256)}, u32[]{:S(2)}) copy-start(s32[256]{0:T(256)} %param.11) | copy-start | bytes 3076
  78.6 10.8 %collective-permute-start.28 = (f32[256,256]{1,0:T(8,128)S(1)}, f32[256,256]{1,0:T(8,128)S(1)}, u32[]{:S(2)}, u32[]{:S(2)}) collective-permute-start(f32[256,256]{1,0:T(8,128)S(1)} %add.14), channel_id=1, source_target_pairs={{0,4},{1,5},{2,6},{3,7},{4,0},{5,1},{6,2},{7,3},{8,12},{9,13},{10,... | collective-permute-start | bytes 786440 | tf_op jit(solution)/shard_map/ppermute | solution.py:382
  81.3 8.6 %collective-permute-start.27 = (f32[256,256]{1,0:T(8,128)S(1)}, f32[256,256]{1,0:T(8,128)S(1)}, u32[]{:S(2)}, u32[]{:S(2)}) collective-permute-start(f32[256,256]{1,0:T(8,128)S(1)} %add.12), channel_id=1, source_target_pairs={{0,1},{1,0},{2,3},{3,2},{4,5},{5,4},{6,7},{7,6},{8,9},{9,8},{10,11... | collective-permute-start | bytes 786440 | tf_op jit(solution)/shard_map/ppermute | solution.py:382

commit v14 on v13

--- a/solution.py
+++ b/solution.py
@@ -474,8 +474,8 @@
         scratch=[pltpu.VMEM((members, LANES), I32), pltpu.VMEM((LANES, 1), I32)],
         name="pick",
     )
-    sent = list(picked[:1]) + [
-        swap(b, "group", d) for d, b in enumerate(after(picked[1:], stats), 1)
+    sent = list(picked[:2]) + [
+        swap(b, "group", d) for d, b in enumerate(after(picked[2:], stats), 2)
     ]
     joined, own = call(
         functools.partial(positive_kernel, members, groups, slots, tokens),
@@ -518,9 +518,9 @@
     grads = call(
         functools.partial(grad_kernel, members, groups, slots, halves),
         [sds(members * count + 8, width)] * groups,
-        [SMEM] + [VMEM] * (4 + len(probs) + members) + [ANY] * (groups - 1),
+        [SMEM] + [VMEM] * (4 + len(probs) + members) + [ANY] * (groups - 2),
         [VMEM] * groups,
-        (info, got, final, stats, own, *probs, *encs, *sent[1:]),
+        (info, got, final, stats, own, *probs, *encs, *sent[2:]),
         scratch=[
             pltpu.VMEM((negatives, width), F32),
             pltpu.VMEM((members, LANES), F32),
@@ -542,6 +542,7 @@
         )
 
     graded = [grads[0]]
+    sent[1] = swap(after([sent[1]], grads[0])[0], "group", 1)
     grads = graded + [swap(grads[d], "group", d) for d in range(1, groups)]
     def scaled(blocks, deps):
         return call(

time: 91.7 us -> 92.7 us (1.011); the launches traced: 90.8 us -> 90.8 us
  transfers between devices with their start and end apart: 30 -> 30, of which waited for: 10 -> 11; matrix products, arithmetic and copies ran while one was open for 0% -> 0% of each run, Pallas kernels for 34% -> 34%
where the time goes in v14:
time: 92.7 us; the launch traced here: 90.8 us
  starting transfers between devices  36.8 us (40%)
  Pallas kernels  32.8 us (35%)
  waiting for transfers between devices  16.5 us (18%)
  local copies, waits for them, and re-layouts  3.15 us (3%)
    ppermute x29, starting transfers between devices, swap(): lax.ppermute(value, axis, [(i, i ^ d) for i in range(lax.axis_size(axis))])  32.9 us
    pallas_call x24, Pallas kernels, call(): pl.pallas_call(kernel, out_shape=out_shape, in_specs=ins, out_specs=outs,...  32.8 us
    ppermute x29, waiting for transfers between devices, swap(): lax.ppermute(value, axis, [(i, i ^ d) for i in range(lax.axis_size(axis))])  9.12 us
    all_to_all x1, waiting for transfers between devices, shards(): lax.all_to_all(request, ('group', 'member'), split_axis=0, concat_axis=0,...  7.36 us
    all_to_all x1, starting transfers between devices, shards(): lax.all_to_all(request, ('group', 'member'), split_axis=0, concat_axis=0,...  3.82 us
    unnamed x8, local copies, waits for them, and re-layouts  3.14 us
  transfers between devices with their start and end apart: 30, of which 11 were waited for; matrix products, arithmetic and copies ran while one was open for 0% of the time, Pallas kernels for 34%

profile of v14, /device:TPU:0, one launch (start us, length us, event | category | flops | bytes accessed | tf_op | source)
XLA Modules:
  0.0 90.8 jit_solution(14935987416393654256)
XLA Ops:
  0.6 0.7 pad_add_fusion
  1.4 0.9 %copy-done.2 = f32[256,256]{1,0:T(8,128)S(1)} copy-done((f32[256,256]{1,0:T(8,128)S(1)}, f32[256,256]{1,0:T(8,128)}, u32[]{:S(2)}) %copy-start.2) | copy-done | bytes 262168
  2.3 1.2 %front.1 = (s32[32,1,256]{2,1,0:T(1,128)}, f32[256,256]{1,0:T(8,128)S(1)}) custom-call(s32[1,1280]{1,0:T(1,128)S(1)} %reshape.15.refs_0_, f32[256,256]{1,0:T(8,128)S(1)} %copy-done.2), custom_call_target="tpu_custom_call" | custom-call | tf_op jit(solution)/shard_map/front/pallas_call | solution.py:38
  3.6 4.0 %collective-permute-start = (f32[256,256]{1,0:T(8,128)S(1)}, f32[256,256]{1,0:T(8,128)S(1)}, u32[]{:S(2)}, u32[]{:S(2)}) collective-permute-start(f32[256,256]{1,0:T(8,128)S(1)} %get-tuple-element.50.refs_4_.refs_1_.refs_8_), channel_id=1, source_target_pairs={{0,4},{1,5},{2,6},{3,7},{4,0},{5,1},{6,2},{7,3},{8,12},{9,13},{10,... | collective-permute-start | bytes 786440 | tf_op jit(solution)/shard_map/ppermute | solution.py:382
  7.6 3.8 %all-to-all-start = ((s32[32,1,256]{2,1,0:T(1,128)}), s32[32,1,256]{2,1,0:T(1,128)S(1)}, u32[]{:S(2)}, u32[]{:S(2)}) async-start(s32[32,1,256]{2,1,0:T(1,128)} %get-tuple-element.51), calls=%async_computation | async-start | bytes 65536 | tf_op jit(solution)/shard_map/all_to_all | solution.py:408
  11.4 1.8 %collective-permute-start.1 = (f32[256,256]{1,0:T(8,128)S(1)}, f32[256,256]{1,0:T(8,128)S(1)}, u32[]{:S(2)}, u32[]{:S(2)}) collective-permute-start(f32[256,256]{1,0:T(8,128)S(1)} %get-tuple-element.50.refs_4_.refs_1_.refs_8_), channel_id=1, source_target_pairs={{0,1},{1,0},{2,3},{3,2},{4,5},{5,4},{6,7},{7,6},{8,9},{9,8},{10,11... | collective-permute-start | bytes 786440 | tf_op jit(solution)/shard_map/ppermute | solution.py:382
  13.3 1.5 %collective-permute-start.8 = (f32[256,256]{1,0:T(8,128)S(1)}, f32[256,256]{1,0:T(8,128)S(1)}, u32[]{:S(2)}, u32[]{:S(2)}) collective-permute-start(f32[256,256]{1,0:T(8,128)S(1)} %get-tuple-element.50.refs_4_.refs_1_.refs_8_), channel_id=1, source_target_pairs={{0,2},{1,3},{2,0},{3,1},{4,6},{5,7},{6,4},{7,5},{8,10},{9,11},{10,... | collective-permute-start | bytes 786440 | tf_op jit(solution)/shard_map/ppermute | solution.py:382
  14.7 7.4 %all-to-all-done.refs_0_.refs_1_ = s32[32,1,256]{2,1,0:T(1,128)S(1)} async-done(((s32[32,1,256]{2,1,0:T(1,128)}), s32[32,1,256]{2,1,0:T(1,128)S(1)}, u32[]{:S(2)}, u32[]{:S(2)}) %all-to-all-start) | async-done | bytes 32800 | tf_op jit(solution)/shard_map/all_to_all | solution.py:408
  22.1 0.6 collective-permute-start.6
  23.3 2.2 %copy-done = f32[4096,256]{1,0:T(8,128)S(1)} copy-done((f32[4096,256]{1,0:T(8,128)S(1)}, f32[4096,256]{1,0:T(8,128)}, u32[]{:S(2)}) %copy-start) | copy-done | bytes 4194328
  25.5 2.3 %gather_negatives.1 = (f32[128,256]{1,0:T(8,128)S(1)}, f32[128,256]{1,0:T(8,128)S(1)}, f32[128,256]{1,0:T(8,128)S(1)}, f32[128,256]{1,0:T(8,128)S(1)}) custom-call(s32[32,1,256]{2,1,0:T(1,128)S(1)} %all-to-all-done.refs_0_.refs_1_, f32[4096,256]{1,0:T(8,128)S(1)} %copy-done, f32[256,256]{1,0:T(8,128)S(1)} %collective-permute-done.1.refs_2_.refs_5_.refs_9_, ...), custom_call_target="tpu_custom_call" | custom-call | tf_op jit(solution)/shard_map/gather_negatives/pallas_call | solution.py:38
  27.9 0.8 collective-permute-start.3
  28.7 1.1 %collective-permute-start.4 = (f32[128,256]{1,0:T(8,128)S(1)}, f32[128,256]{1,0:T(8,128)S(1)}, u32[]{:S(2)}, u32[]{:S(2)}) collective-permute-start(f32[128,256]{1,0:T(8,128)S(1)} %get-tuple-element.56), channel_id=1, source_target_pairs={{0,24},{8,16},{16,8},{24,0},{1,25},{9,17},{17,9},{25,1},{2,26},{10... | collective-permute-start | bytes 393224 | tf_op jit(solution)/shard_map/ppermute | solution.py:382
  29.7 0.7 collective-permute-done.6.refs_3_.refs_5_.refs_6_.refs_13_
  30.4 0.8 collective-permute-start.5
  31.2 2.2 %gather_far_targets.1 = (f32[256,256]{1,0:T(8,128)S(1)}, f32[256,256]{1,0:T(8,128)S(1)}) custom-call(s32[32,1,256]{2,1,0:T(1,128)S(1)} %all-to-all-done.refs_0_.refs_1_, f32[4096,256]{1,0:T(8,128)S(1)} %copy-done, f32[256,256]{1,0:T(8,128)S(1)} %collective-permute-done.8.refs_2_.refs_6_.refs_3_.refs_10_, ...), custom_call_target="tpu_custom_call" | custom-call | tf_op jit(solution)/shard_map/gather_far_targets/pallas_call | solution.py:38
  33.4 1.5 %collective-permute-start.9 = (f32[256,256]{1,0:T(8,128)S(1)}, f32[256,256]{1,0:T(8,128)S(1)}, u32[]{:S(2)}, u32[]{:S(2)}) collective-permute-start(f32[256,256]{1,0:T(8,128)S(1)} %collective-permute-done.7.refs_6_.refs_7_.refs_14_), channel_id=1, source_target_pairs={{0,1},{1,0},{2,3},{3,2},{4,5},{5,4},{6,7},{7,6},{8,9},{9,8},{10,11... | collective-permute-start | bytes 786440 | tf_op jit(solution)/shard_map/ppermute | solution.py:382
  34.9 0.6 collective-permute-start.11
  35.5 0.6 collective-permute-start.12
  36.1 2.5 %score.2 = (f32[2,2048]{1,0:T(2,128)S(1)}, bf16[4,512,256]{2,1,0:T(8,128)(2,1)S(1)}, bf16[4,512,256]{2,1,0:T(8,128)(2,1)S(1)}) custom-call(f32[128,256]{1,0:T(8,128)S(1)} %get-tuple-element.53.refs_0_.refs_1_, f32[128,256]{1,0:T(8,128)S(1)} %collective-permute-done.2.refs_1_.refs_2_, f32[128,256]{1,0:T(8,128)S(1)} %collective-permute-done.3.refs_2_.refs_3_, ...), custom_call_target="tpu_custom_call" | custom-call | flops 1610612736 | bytes 1048576 | tf_op jit(solution)/shard_map/score/pallas_call | solution.py:38
  38.7 2.4 %gather_targets.1 = (f32[256,256]{1,0:T(8,128)S(1)}, f32[256,256]{1,0:T(8,128)S(1)}) custom-call(s32[32,1,256]{2,1,0:T(1,128)S(1)} %all-to-all-done.refs_0_.refs_1_, f32[4096,256]{1,0:T(8,128)S(1)} %copy-done.1, f32[2,2048]{1,0:T(2,128)S(1)} %get-tuple-element.62.refs_8_.refs_2_), custom_call_target="tpu_custom_call" | custom-call | tf_op jit(solution)/shard_map/gather_targets/pallas_call | solution.py:38
  41.0 1.0 %collective-permute-start.10 = (f32[256,256]{1,0:T(8,128)S(1)}, f32[256,256]{1,0:T(8,128)S(1)}, u32[]{:S(2)}, u32[]{:S(2)}) collective-permute-start(f32[256,256]{1,0:T(8,128)S(1)} %get-tuple-element.65), channel_id=1, source_target_pairs={{0,8},{8,0},{16,24},{24,16},{1,9},{9,1},{17,25},{25,17},{2,10},{10... | collective-permute-start | bytes 786440 | tf_op jit(solution)/shard_map/ppermute | solution.py:382
  42.0 1.1 %pick.1 = (f32[256,256]{1,0:T(8,128)S(1)}, f32[256,256]{1,0:T(8,128)S(1)}, f32[256,256]{1,0:T(8,128)S(1)}, f32[256,256]{1,0:T(8,128)S(1)}) custom-call(s32[32,1,256]{2,1,0:T(1,128)S(1)} %all-to-all-done.refs_0_.refs_1_, f32[256,256]{1,0:T(8,128)S(1)} %get-tuple-element.50.refs_4_.refs_1_.refs_8_, ...), custom_call_target="tpu_custom_call" | custom-call | tf_op jit(solution)/shard_map/pick/pallas_call | solution.py:38
  43.1 2.5 %score.3 = (f32[2,2048]{1,0:T(2,128)S(1)}, bf16[4,512,256]{2,1,0:T(8,128)(2,1)S(1)}, bf16[4,512,256]{2,1,0:T(8,128)(2,1)S(1)}) custom-call(f32[128,256]{1,0:T(8,128)S(1)} %get-tuple-element.53.refs_0_.refs_1_, f32[128,256]{1,0:T(8,128)S(1)} %collective-permute-done.2.refs_1_.refs_2_, f32[128,256]{1,0:T(8,128)S(1)} %collective-permute-done.3.refs_2_.refs_3_, ...), custom_call_target="tpu_custom_call" | custom-call | flops 1610612736 | bytes 1048576 | tf_op jit(solution)/shard_map/score/pallas_call | solution.py:38
  45.6 0.6 collective-permute-start.16
  46.3 0.8 collective-permute-start.17
  47.3 0.7 positive.1
  48.0 1.2 %collective-permute-start.13 = (f32[2,2048]{1,0:T(2,128)S(1)}, f32[2,2048]{1,0:T(2,128)S(1)}, u32[]{:S(2)}, u32[]{:S(2)}) collective-permute-start(f32[2,2048]{1,0:T(2,128)S(1)} %get-tuple-element.70.first), channel_id=1, source_target_pairs={{0,1},{1,0},{2,3},{3,2},{4,5},{5,4},{6,7},{7,6},{8,9},{9,8},{10,11... | collective-permute-start | bytes 49160 | tf_op jit(solution)/shard_map/ppermute | solution.py:382
  49.1 1.5 %pulled.2 = (f32[4,256,256]{2,1,0:T(8,128)S(1)}, f32[4,256,256]{2,1,0:T(8,128)S(1)}) custom-call(s32[32,1,256]{2,1,0:T(1,128)S(1)} %all-to-all-done.refs_0_.refs_1_, f32[128,256]{1,0:T(8,128)S(1)} %get-tuple-element.53.refs_0_.refs_1_, f32[128,256]{1,0:T(8,128)S(1)} %collective-permute-done.2.refs_1_.refs_2_, ...), custom_call_target="tpu_custom_call" | custom-call | flops 805306368 | bytes 1048576 | tf_op jit(solution)/shard_map/pulled/pallas_call | solution.py:38
  50.6 1.2 %collective-permute-done.13.second = f32[2,2048]{1,0:T(2,128)S(1)} collective-permute-done((f32[2,2048]{1,0:T(2,128)S(1)}, f32[2,2048]{1,0:T(2,128)S(1)}, u32[]{:S(2)}, u32[]{:S(2)}) %collective-permute-start.13) | collective-permute-done | bytes 16416 | tf_op jit(solution)/shard_map/ppermute | solution.py:382
  51.8 1.1 %collective-permute-start.14 = (f32[2,2048]{1,0:T(2,128)S(1)}, f32[2,2048]{1,0:T(2,128)S(1)}, u32[]{:S(2)}, u32[]{:S(2)}) collective-permute-start(f32[2,2048]{1,0:T(2,128)S(1)} %join.3.first), channel_id=1, source_target_pairs={{0,2},{1,3},{2,0},{3,1},{4,6},{5,7},{6,4},{7,5},{8,10},{9,11},{10,... | collective-permute-start | bytes 49160 | tf_op jit(solution)/shard_map/ppermute | solution.py:382
  52.9 1.5 %pulled.3 = (f32[4,256,256]{2,1,0:T(8,128)S(1)}, f32[4,256,256]{2,1,0:T(8,128)S(1)}) custom-call(s32[32,1,256]{2,1,0:T(1,128)S(1)} %all-to-all-done.refs_0_.refs_1_, f32[128,256]{1,0:T(8,128)S(1)} %get-tuple-element.53.refs_0_.refs_1_, f32[128,256]{1,0:T(8,128)S(1)} %collective-permute-done.2.refs_1_.refs_2_, ...), custom_call_target="tpu_custom_call" | custom-call | flops 805306368 | bytes 1048576 | tf_op jit(solution)/shard_map/pulled/pallas_call | solution.py:38
  54.4 1.2 %collective-permute-done.14.second = f32[2,2048]{1,0:T(2,128)S(1)} collective-permute-done((f32[2,2048]{1,0:T(2,128)S(1)}, f32[2,2048]{1,0:T(2,128)S(1)}, u32[]{:S(2)}, u32[]{:S(2)}) %collective-permute-start.14) | collective-permute-done | bytes 16416 | tf_op jit(solution)/shard_map/ppermute | solution.py:382
  55.6 3.3 %collective-permute-start.15 = (f32[2,2048]{1,0:T(2,128)S(1)}, f32[2,2048]{1,0:T(2,128)S(1)}, u32[]{:S(2)}, u32[]{:S(2)}) collective-permute-start(f32[2,2048]{1,0:T(2,128)S(1)} %join.4.first), channel_id=1, source_target_pairs={{0,4},{1,5},{2,6},{3,7},{4,0},{5,1},{6,2},{7,3},{8,12},{9,13},{10,... | collective-permute-start | bytes 49160 | tf_op jit(solution)/shard_map/ppermute | solution.py:382
  58.9 1.7 %collective-permute-done.15.second = f32[2,2048]{1,0:T(2,128)S(1)} collective-permute-done((f32[2,2048]{1,0:T(2,128)S(1)}, f32[2,2048]{1,0:T(2,128)S(1)}, u32[]{:S(2)}, u32[]{:S(2)}) %collective-permute-start.15) | collective-permute-done | bytes 16416 | tf_op jit(solution)/shard_map/ppermute | solution.py:382
  60.7 1.6 %collective-permute-start.18 = (f32[256,256]{1,0:T(8,128)S(1)}, f32[256,256]{1,0:T(8,128)S(1)}, u32[]{:S(2)}, u32[]{:S(2)}) collective-permute-start(f32[256,256]{1,0:T(8,128)S(1)} %get-tuple-element.86), channel_id=1, source_target_pairs={{0,1},{1,0},{2,3},{3,2},{4,5},{5,4},{6,7},{7,6},{8,9},{9,8},{10,11... | collective-permute-start | bytes 786440 | tf_op jit(solution)/shard_map/ppermute | solution.py:382
  62.4 1.0 %collective-permute-start.19 = (f32[256,256]{1,0:T(8,128)S(1)}, f32[256,256]{1,0:T(8,128)S(1)}, u32[]{:S(2)}, u32[]{:S(2)}) collective-permute-start(f32[256,256]{1,0:T(8,128)S(1)} %get-tuple-element.87), channel_id=1, source_target_pairs={{0,2},{1,3},{2,0},{3,1},{4,6},{5,7},{6,4},{7,5},{8,10},{9,11},{10,... | collective-permute-start | bytes 786440 | tf_op jit(solution)/shard_map/ppermute | solution.py:382
  63.3 2.0 %grad.1 = (f32[136,256]{1,0:T(8,128)S(1)}, f32[136,256]{1,0:T(8,128)S(1)}, f32[136,256]{1,0:T(8,128)S(1)}, f32[136,256]{1,0:T(8,128)S(1)}) custom-call(s32[32,1,256]{2,1,0:T(1,128)S(1)} %all-to-all-done.refs_0_.refs_1_, f32[2,2048]{1,0:T(2,128)S(1)} %join.5.refs_1_.refs_0_, f32[2,2048]{1,0:T(2,128)S(1)} %get-tuple-element.63.refs_1_.refs_2_, ...), custom_call_target="tpu_custom_call" | custom-call | flops 1610612736 | bytes 8388608 | tf_op jit(solution)/shard_map/grad/pallas_call | solution.py:38
  66.1 0.7 collective-permute-start.24
  67.6 1.1 %collective-permute-done.19.refs_3_.refs_1_ = f32[256,256]{1,0:T(8,128)S(1)} collective-permute-done((f32[256,256]{1,0:T(8,128)S(1)}, f32[256,256]{1,0:T(8,128)S(1)}, u32[]{:S(2)}, u32[]{:S(2)}) %collective-permute-start.19) | collective-permute-done | bytes 262176 | tf_op jit(solution)/shard_map/ppermute | solution.py:382
  68.8 1.0 %collective-permute-start.26 = (f32[256,256]{1,0:T(8,128)S(1)}, f32[256,256]{1,0:T(8,128)S(1)}, u32[]{:S(2)}, u32[]{:S(2)}) collective-permute-start(f32[256,256]{1,0:T(8,128)S(1)} %add.11.refs_6_), channel_id=1, source_target_pairs={{0,2},{1,3},{2,0},{3,1},{4,6},{5,7},{6,4},{7,5},{8,10},{9,11},{10,... | collective-permute-start | bytes 786440 | tf_op jit(solution)/shard_map/ppermute | solution.py:382
  70.3 4.8 %scatter.2.refs_1_.refs_6_ = f32[4096,256]{1,0:T(8,128)S(1)} custom-call(s32[32,1,256]{2,1,0:T(1,128)S(1)} %all-to-all-done.refs_0_.refs_1_, s32[32,1,256]{2,1,0:T(1,128)S(1)} %all-to-all-done.refs_0_.refs_1_, f32[136,256]{1,0:T(8,128)S(1)} %get-tuple-element.82.refs_7_.refs_2_, f32[136,256]{1,0:T(8,128)S(1)} %collective-permute-done.22.refs_3_, ...), custom_call_target="tpu_custom_call" | custom-call | flops 8589934592 | tf_op jit(solution)/shard_map/scatter/pallas_call | solution.py:38
  75.1 2.4 %collective-permute-done.20.refs_2_ = f32[256,256]{1,0:T(8,128)S(1)} collective-permute-done((f32[256,256]{1,0:T(8,128)S(1)}, f32[256,256]{1,0:T(8,128)S(1)}, u32[]{:S(2)}, u32[]{:S(2)}) %collective-permute-start.20) | collective-permute-done | bytes 262176 | tf_op jit(solution)/shard_map/ppermute | solution.py:382
  77.5 1.0 %collective-permute-start.21 = (f32[256,256]{1,0:T(8,128)S(1)}, f32[256,256]{1,0:T(8,128)S(1)}, u32[]{:S(2)}, u32[]{:S(2)}) collective-permute-start(f32[256,256]{1,0:T(8,128)S(1)} %get-tuple-element.89), channel_id=1, source_target_pairs={{0,2},{1,3},{2,0},{3,1},{4,6},{5,7},{6,4},{7,5},{8,10},{9,11},{10,... | collective-permute-start | bytes 786440 | tf_op jit(solution)/shard_map/ppermute | solution.py:382
  78.6 2.6 %collective-permute-start.28 = (f32[256,256]{1,0:T(8,128)S(1)}, f32[256,256]{1,0:T(8,128)S(1)}, u32[]{:S(2)}, u32[]{:S(2)}) collective-permute-start(f32[256,256]{1,0:T(8,128)S(1)} %add.14), channel_id=1, source_target_pairs={{0,4},{1,5},{2,6},{3,7},{4,0},{5,1},{6,2},{7,3},{8,12},{9,13},{10,... | collective-permute-start | bytes 786440 | tf_op jit(solution)/shard_map/ppermute | solution.py:382
  81.2 1.7 %collective-permute-start.27 = (f32[256,256]{1,0:T(8,128)S(1)}, f32[256,256]{1,0:T(8,128)S(1)}, u32[]{:S(2)}, u32[]{:S(2)}) collective-permute-start(f32[256,256]{1,0:T(8,128)S(1)} %add.12), channel_id=1, source_target_pairs={{0,1},{1,0},{2,3},{3,2},{4,5},{5,4},{6,7},{7,6},{8,9},{9,8},{10,11... | collective-permute-start | bytes 786440 | tf_op jit(solution)/shard_map/ppermute | solution.py:382
  82.8 6.8 %scatter.3 = f32[4096,256]{1,0:T(8,128)} custom-call(s32[32,1,256]{2,1,0:T(1,128)S(1)} %all-to-all-done.refs_0_.refs_1_, s32[32,1,256]{2,1,0:T(1,128)S(1)} %all-to-all-done.refs_0_.refs_1_, f32[136,256]{1,0:T(8,128)S(1)} %collective-permute-done.24.refs_2_, f32[136,256]{1,0:T(8,128)S(1)} %collective-permute-done.25.refs_3_, ...), custom_call_target="tpu_custom_call" | custom-call | tf_op jit(solution)/shard_map/scatter/pallas_call | solution.py:38
  89.9 1.0 %finish.1 = f32[256,256]{1,0:T(8,128)} custom-call(s32[1,256]{1,0:T(1,128)S(1)} %bitcast.2, f32[256,256]{1,0:T(8,128)S(1)} %collective-permute-done.21.refs_0_, f32[256,256]{1,0:T(8,128)S(1)} %collective-permute-done.27.refs_1_, f32[256,256]{1,0:T(8,128)S(1)} %add.15.refs_2_), custom_call_target="tpu_custom_call" | custom-call | tf_op jit(solution)/shard_map/finish/pallas_call | solution.py:38
  (46 shorter events, 3.5 us)
Async XLA Ops:
  1.4 1.0 %copy-start.2 = (f32[256,256]{1,0:T(8,128)S(1)}, f32[256,256]{1,0:T(8,128)}, u32[]{:S(2)}) copy-start(f32[256,256]{1,0:T(8,128)} %refs_1_.4) | copy-start | bytes 786436
  3.6 18.5 %collective-permute-start = (f32[256,256]{1,0:T(8,128)S(1)}, f32[256,256]{1,0:T(8,128)S(1)}, u32[]{:S(2)}, u32[]{:S(2)}) collective-permute-start(f32[256,256]{1,0:T(8,128)S(1)} %get-tuple-element.50.refs_4_.refs_1_.refs_8_), channel_id=1, source_target_pairs={{0,4},{1,5},{2,6},{3,7},{4,0},{5,1},{6,2},{7,3},{8,12},{9,13},{10,... | collective-permute-start | bytes 786440 | tf_op jit(solution)/shard_map/ppermute | solution.py:382
  7.6 14.5 %all-to-all-start = ((s32[32,1,256]{2,1,0:T(1,128)}), s32[32,1,256]{2,1,0:T(1,128)S(1)}, u32[]{:S(2)}, u32[]{:S(2)}) async-start(s32[32,1,256]{2,1,0:T(1,128)} %get-tuple-element.51), calls=%async_computation | async-start | bytes 65536 | tf_op jit(solution)/shard_map/all_to_all | solution.py:408
  11.4 11.9 %collective-permute-start.1 = (f32[256,256]{1,0:T(8,128)S(1)}, f32[256,256]{1,0:T(8,128)S(1)}, u32[]{:S(2)}, u32[]{:S(2)}) collective-permute-start(f32[256,256]{1,0:T(8,128)S(1)} %get-tuple-element.50.refs_4_.refs_1_.refs_8_), channel_id=1, source_target_pairs={{0,1},{1,0},{2,3},{3,2},{4,5},{5,4},{6,7},{7,6},{8,9},{9,8},{10,11... | collective-permute-start | bytes 786440 | tf_op jit(solution)/shard_map/ppermute | solution.py:382
  13.3 15.4 %collective-permute-start.8 = (f32[256,256]{1,0:T(8,128)S(1)}, f32[256,256]{1,0:T(8,128)S(1)}, u32[]{:S(2)}, u32[]{:S(2)}) collective-permute-start(f32[256,256]{1,0:T(8,128)S(1)} %get-tuple-element.50.refs_4_.refs_1_.refs_8_), channel_id=1, source_target_pairs={{0,2},{1,3},{2,0},{3,1},{4,6},{5,7},{6,4},{7,5},{8,10},{9,11},{10,... | collective-permute-start | bytes 786440 | tf_op jit(solution)/shard_map/ppermute | solution.py:382
  22.1 8.3 %collective-permute-start.6 = (f32[256,256]{1,0:T(8,128)S(1)}, f32[256,256]{1,0:T(8,128)S(1)}, u32[]{:S(2)}, u32[]{:S(2)}) collective-permute-start(f32[256,256]{1,0:T(8,128)S(1)} %collective-permute-done.refs_3_.refs_7_.refs_5_.refs_12_), channel_id=1, source_target_pairs={{0,1},{1,0},{2,3},{3,2},{4,5},{5,4},{6,7},{7,6},{8,9},{9,8},{10,11... | collective-permute-start | bytes 786440 | tf_op jit(solution)/shard_map/ppermute | solution.py:382
  22.7 10.7 %collective-permute-start.7 = (f32[256,256]{1,0:T(8,128)S(1)}, f32[256,256]{1,0:T(8,128)S(1)}, u32[]{:S(2)}, u32[]{:S(2)}) collective-permute-start(f32[256,256]{1,0:T(8,128)S(1)} %collective-permute-done.refs_3_.refs_7_.refs_5_.refs_12_), channel_id=1, source_target_pairs={{0,2},{1,3},{2,0},{3,1},{4,6},{5,7},{6,4},{7,5},{8,10},{9,11},{10,... | collective-permute-start | bytes 786440 | tf_op jit(solution)/shard_map/ppermute | solution.py:382
  23.3 2.2 %copy-start = (f32[4096,256]{1,0:T(8,128)S(1)}, f32[4096,256]{1,0:T(8,128)}, u32[]{:S(2)}) copy-start(f32[4096,256]{1,0:T(8,128)} %refs_1_.7) | copy-start | bytes 12582916
  27.8 7.1 %collective-permute-start.2 = (f32[128,256]{1,0:T(8,128)S(1)}, f32[128,256]{1,0:T(8,128)S(1)}, u32[]{:S(2)}, u32[]{:S(2)}) collective-permute-start(f32[128,256]{1,0:T(8,128)S(1)} %get-tuple-element.54), channel_id=1, source_target_pairs={{0,8},{8,0},{16,24},{24,16},{1,9},{9,1},{17,25},{25,17},{2,10},{10... | collective-permute-start | bytes 393224 | tf_op jit(solution)/shard_map/ppermute | solution.py:382
  27.9 7.6 %collective-permute-start.3 = (f32[128,256]{1,0:T(8,128)S(1)}, f32[128,256]{1,0:T(8,128)S(1)}, u32[]{:S(2)}, u32[]{:S(2)}) collective-permute-start(f32[128,256]{1,0:T(8,128)S(1)} %get-tuple-element.55), channel_id=1, source_target_pairs={{0,16},{8,24},{16,0},{24,8},{1,17},{9,25},{17,1},{25,9},{2,18},{10... | collective-permute-start | bytes 393224 | tf_op jit(solution)/shard_map/ppermute | solution.py:382
  28.7 7.5 %collective-permute-start.4 = (f32[128,256]{1,0:T(8,128)S(1)}, f32[128,256]{1,0:T(8,128)S(1)}, u32[]{:S(2)}, u32[]{:S(2)}) collective-permute-start(f32[128,256]{1,0:T(8,128)S(1)} %get-tuple-element.56), channel_id=1, source_target_pairs={{0,24},{8,16},{16,8},{24,0},{1,25},{9,17},{17,9},{25,1},{2,26},{10... | collective-permute-start | bytes 393224 | tf_op jit(solution)/shard_map/ppermute | solution.py:382
  29.7 8.9 %copy-start.1 = (f32[4096,256]{1,0:T(8,128)S(1)}, f32[4096,256]{1,0:T(8,128)}, u32[]{:S(2)}) copy-start(f32[4096,256]{1,0:T(8,128)} %refs_1_.7) | copy-start | bytes 12582916
  30.4 11.6 %collective-permute-start.5 = (f32[256,256]{1,0:T(8,128)S(1)}, f32[256,256]{1,0:T(8,128)S(1)}, u32[]{:S(2)}, u32[]{:S(2)}) collective-permute-start(f32[256,256]{1,0:T(8,128)S(1)} %collective-permute-done.1.refs_2_.refs_5_.refs_9_), channel_id=1, source_target_pairs={{0,2},{1,3},{2,0},{3,1},{4,6},{5,7},{6,4},{7,5},{8,10},{9,11},{10,... | collective-permute-start | bytes 786440 | tf_op jit(solution)/shard_map/ppermute | solution.py:382
  33.4 8.6 %collective-permute-start.9 = (f32[256,256]{1,0:T(8,128)S(1)}, f32[256,256]{1,0:T(8,128)S(1)}, u32[]{:S(2)}, u32[]{:S(2)}) collective-permute-start(f32[256,256]{1,0:T(8,128)S(1)} %collective-permute-done.7.refs_6_.refs_7_.refs_14_), channel_id=1, source_target_pairs={{0,1},{1,0},{2,3},{3,2},{4,5},{5,4},{6,7},{7,6},{8,9},{9,8},{10,11... | collective-permute-start | bytes 786440 | tf_op jit(solution)/shard_map/ppermute | solution.py:382
  34.9 12.4 %collective-permute-start.11 = (f32[256,256]{1,0:T(8,128)S(1)}, f32[256,256]{1,0:T(8,128)S(1)}, u32[]{:S(2)}, u32[]{:S(2)}) collective-permute-start(f32[256,256]{1,0:T(8,128)S(1)} %get-tuple-element.59.refs_8_), channel_id=1, source_target_pairs={{0,16},{8,24},{16,0},{24,8},{1,17},{9,25},{17,1},{25,9},{2,18},{10... | collective-permute-start | bytes 786440 | tf_op jit(solution)/shard_map/ppermute | solution.py:382
  35.5 11.8 %collective-permute-start.12 = (f32[256,256]{1,0:T(8,128)S(1)}, f32[256,256]{1,0:T(8,128)S(1)}, u32[]{:S(2)}, u32[]{:S(2)}) collective-permute-start(f32[256,256]{1,0:T(8,128)S(1)} %get-tuple-element.61.refs_9_), channel_id=1, source_target_pairs={{0,24},{8,16},{16,8},{24,0},{1,25},{9,17},{17,9},{25,1},{2,26},{10... | collective-permute-start | bytes 786440 | tf_op jit(solution)/shard_map/ppermute | solution.py:382
  41.0 6.2 %collective-permute-start.10 = (f32[256,256]{1,0:T(8,128)S(1)}, f32[256,256]{1,0:T(8,128)S(1)}, u32[]{:S(2)}, u32[]{:S(2)}) collective-permute-start(f32[256,256]{1,0:T(8,128)S(1)} %get-tuple-element.65), channel_id=1, source_target_pairs={{0,8},{8,0},{16,24},{24,16},{1,9},{9,1},{17,25},{25,17},{2,10},{10... | collective-permute-start | bytes 786440 | tf_op jit(solution)/shard_map/ppermute | solution.py:382
  45.6 17.7 %collective-permute-start.16 = (f32[256,256]{1,0:T(8,128)S(1)}, f32[256,256]{1,0:T(8,128)S(1)}, u32[]{:S(2)}, u32[]{:S(2)}) collective-permute-start(f32[256,256]{1,0:T(8,128)S(1)} %get-tuple-element.80.refs_8_), channel_id=1, source_target_pairs={{0,16},{8,24},{16,0},{24,8},{1,17},{9,25},{17,1},{25,9},{2,18},{10... | collective-permute-start | bytes 786440 | tf_op jit(solution)/shard_map/ppermute | solution.py:382
  46.3 17.1 %collective-permute-start.17 = (f32[256,256]{1,0:T(8,128)S(1)}, f32[256,256]{1,0:T(8,128)S(1)}, u32[]{:S(2)}, u32[]{:S(2)}) collective-permute-start(f32[256,256]{1,0:T(8,128)S(1)} %get-tuple-element.81.refs_9_), channel_id=1, source_target_pairs={{0,24},{8,16},{16,8},{24,0},{1,25},{9,17},{17,9},{25,1},{2,26},{10... | collective-permute-start | bytes 786440 | tf_op jit(solution)/shard_map/ppermute | solution.py:382
  48.0 3.8 %collective-permute-start.13 = (f32[2,2048]{1,0:T(2,128)S(1)}, f32[2,2048]{1,0:T(2,128)S(1)}, u32[]{:S(2)}, u32[]{:S(2)}) collective-permute-start(f32[2,2048]{1,0:T(2,128)S(1)} %get-tuple-element.70.first), channel_id=1, source_target_pairs={{0,1},{1,0},{2,3},{3,2},{4,5},{5,4},{6,7},{7,6},{8,9},{9,8},{10,11... | collective-permute-start | bytes 49160 | tf_op jit(solution)/shard_map/ppermute | solution.py:382
  51.8 3.8 %collective-permute-start.14 = (f32[2,2048]{1,0:T(2,128)S(1)}, f32[2,2048]{1,0:T(2,128)S(1)}, u32[]{:S(2)}, u32[]{:S(2)}) collective-permute-start(f32[2,2048]{1,0:T(2,128)S(1)} %join.3.first), channel_id=1, source_target_pairs={{0,2},{1,3},{2,0},{3,1},{4,6},{5,7},{6,4},{7,5},{8,10},{9,11},{10,... | collective-permute-start | bytes 49160 | tf_op jit(solution)/shard_map/ppermute | solution.py:382
  55.6 5.0 %collective-permute-start.15 = (f32[2,2048]{1,0:T(2,128)S(1)}, f32[2,2048]{1,0:T(2,128)S(1)}, u32[]{:S(2)}, u32[]{:S(2)}) collective-permute-start(f32[2,2048]{1,0:T(2,128)S(1)} %join.4.first), channel_id=1, source_target_pairs={{0,4},{1,5},{2,6},{3,7},{4,0},{5,1},{6,2},{7,3},{8,12},{9,13},{10,... | collective-permute-start | bytes 49160 | tf_op jit(solution)/shard_map/ppermute | solution.py:382
  60.7 6.5 %collective-permute-start.18 = (f32[256,256]{1,0:T(8,128)S(1)}, f32[256,256]{1,0:T(8,128)S(1)}, u32[]{:S(2)}, u32[]{:S(2)}) collective-permute-start(f32[256,256]{1,0:T(8,128)S(1)} %get-tuple-element.86), channel_id=1, source_target_pairs={{0,1},{1,0},{2,3},{3,2},{4,5},{5,4},{6,7},{7,6},{8,9},{9,8},{10,11... | collective-permute-start | bytes 786440 | tf_op jit(solution)/shard_map/ppermute | solution.py:382
  62.4 6.4 %collective-permute-start.19 = (f32[256,256]{1,0:T(8,128)S(1)}, f32[256,256]{1,0:T(8,128)S(1)}, u32[]{:S(2)}, u32[]{:S(2)}) collective-permute-start(f32[256,256]{1,0:T(8,128)S(1)} %get-tuple-element.87), channel_id=1, source_target_pairs={{0,2},{1,3},{2,0},{3,1},{4,6},{5,7},{6,4},{7,5},{8,10},{9,11},{10,... | collective-permute-start | bytes 786440 | tf_op jit(solution)/shard_map/ppermute | solution.py:382
  65.4 4.9 %collective-permute-start.23 = (f32[256,256]{1,0:T(8,128)S(1)}, f32[256,256]{1,0:T(8,128)S(1)}, u32[]{:S(2)}, u32[]{:S(2)}) collective-permute-start(f32[256,256]{1,0:T(8,128)S(1)} %get-tuple-element.93.refs_7_), channel_id=1, source_target_pairs={{0,8},{8,0},{16,24},{24,16},{1,9},{9,1},{17,25},{25,17},{2,10},{10... | collective-permute-start | bytes 786440 | tf_op jit(solution)/shard_map/ppermute | solution.py:382
  65.5 4.4 %collective-permute-start.22 = (f32[136,256]{1,0:T(8,128)S(1)}, f32[136,256]{1,0:T(8,128)S(1)}, u32[]{:S(2)}, u32[]{:S(2)}) collective-permute-start(f32[136,256]{1,0:T(8,128)S(1)} %get-tuple-element.92), channel_id=1, source_target_pairs={{0,8},{8,0},{16,24},{24,16},{1,9},{9,1},{17,25},{25,17},{2,10},{10... | collective-permute-start | bytes 417800 | tf_op jit(solution)/shard_map/ppermute | solution.py:382
  66.1 9.0 %collective-permute-start.24 = (f32[136,256]{1,0:T(8,128)S(1)}, f32[136,256]{1,0:T(8,128)S(1)}, u32[]{:S(2)}, u32[]{:S(2)}) collective-permute-start(f32[136,256]{1,0:T(8,128)S(1)} %get-tuple-element.94), channel_id=1, source_target_pairs={{0,16},{8,24},{16,0},{24,8},{1,17},{9,25},{17,1},{25,9},{2,18},{10... | collective-permute-start | bytes 417800 | tf_op jit(solution)/shard_map/ppermute | solution.py:382
  67.2 7.9 %collective-permute-start.25 = (f32[136,256]{1,0:T(8,128)S(1)}, f32[136,256]{1,0:T(8,128)S(1)}, u32[]{:S(2)}, u32[]{:S(2)}) collective-permute-start(f32[136,256]{1,0:T(8,128)S(1)} %get-tuple-element.95), channel_id=1, source_target_pairs={{0,24},{8,16},{16,8},{24,0},{1,25},{9,17},{17,9},{25,1},{2,26},{10... | collective-permute-start | bytes 417800 | tf_op jit(solution)/shard_map/ppermute | solution.py:382
  68.8 9.8 %collective-permute-start.26 = (f32[256,256]{1,0:T(8,128)S(1)}, f32[256,256]{1,0:T(8,128)S(1)}, u32[]{:S(2)}, u32[]{:S(2)}) collective-permute-start(f32[256,256]{1,0:T(8,128)S(1)} %add.11.refs_6_), channel_id=1, source_target_pairs={{0,2},{1,3},{2,0},{3,1},{4,6},{5,7},{6,4},{7,5},{8,10},{9,11},{10,... | collective-permute-start | bytes 786440 | tf_op jit(solution)/shard_map/ppermute | solution.py:382
  69.8 7.7 %collective-permute-start.20 = (f32[256,256]{1,0:T(8,128)S(1)}, f32[256,256]{1,0:T(8,128)S(1)}, u32[]{:S(2)}, u32[]{:S(2)}) collective-permute-start(f32[256,256]{1,0:T(8,128)S(1)} %get-tuple-element.88), channel_id=1, source_target_pairs={{0,1},{1,0},{2,3},{3,2},{4,5},{5,4},{6,7},{7,6},{8,9},{9,8},{10,11... | collective-permute-start | bytes 786440 | tf_op jit(solution)/shard_map/ppermute | solution.py:382
  77.5 12.3 %collective-permute-start.21 = (f32[256,256]{1,0:T(8,128)S(1)}, f32[256,256]{1,0:T(8,128)S(1)}, u32[]{:S(2)}, u32[]{:S(2)}) collective-permute-start(f32[256,256]{1,0:T(8,128)S(1)} %get-tuple-element.89), channel_id=1, source_target_pairs={{0,2},{1,3},{2,0},{3,1},{4,6},{5,7},{6,4},{7,5},{8,10},{9,11},{10,... | collective-permute-start | bytes 786440 | tf_op jit(solution)/shard_map/ppermute | solution.py:382
  78.6 11.3 %copy-start.3 = (s32[256]{0:T(256)S(1)}, s32[256]{0:T(256)}, u32[]{:S(2)}) copy-start(s32[256]{0:T(256)} %param.11) | copy-start | bytes 3076
  78.6 11.0 %collective-permute-start.28 = (f32[256,256]{1,0:T(8,128)S(1)}, f32[256,256]{1,0:T(8,128)S(1)}, u32[]{:S(2)}, u32[]{:S(2)}) collective-permute-start(f32[256,256]{1,0:T(8,128)S(1)} %add.14), channel_id=1, source_target_pairs={{0,4},{1,5},{2,6},{3,7},{4,0},{5,1},{6,2},{7,3},{8,12},{9,13},{10,... | collective-permute-start | bytes 786440 | tf_op jit(solution)/shard_map/ppermute | solution.py:382
  81.2 8.7 %collective-permute-start.27 = (f32[256,256]{1,0:T(8,128)S(1)}, f32[256,256]{1,0:T(8,128)S(1)}, u32[]{:S(2)}, u32[]{:S(2)}) collective-permute-start(f32[256,256]{1,0:T(8,128)S(1)} %add.12), channel_id=1, source_target_pairs={{0,1},{1,0},{2,3},{3,2},{4,5},{5,4},{6,7},{7,6},{8,9},{9,8},{10,11... | collective-permute-start | bytes 786440 | tf_op jit(solution)/shard_map/ppermute | solution.py:382
